TPU v7x, 256 devices: a whole 4x4x8 slice. The times are simulated.
256 devices in a mesh: ens: 8 (over z_hi, x), space: 32 (over y, z_lo, core).
Axes of the slice: x: 4, y: 4, z: 8 (z_hi: 2, z_lo: 4; z = z_hi * 4 + z_lo), core: 2. Of those that a mesh axis runs over, the one named last changes fastest.
Arguments:
- mesh_feats: bfloat16 [8, 2048, 1024], P('ens', 'space'), may hold values from -6 to 6
- grid_embed: bfloat16 [16384, 1024], P('space'), may hold values from -6 to 6
- w_src: bfloat16 [1024, 1024], replicated, may hold values from -0.1875 to 0.1875
- w_dst: bfloat16 [1024, 1024], replicated, may hold values from -0.1875 to 0.1875
- w_out: bfloat16 [1024, 32], replicated, may hold values from -0.1875 to 0.1875
- truth: float32 [16384, 32], P('space'), may hold values from -6 to 6
- area_weight: float32 [16384], P('space'), may hold values from 0.3 to 3
- var_weight: float32 [32], replicated, may hold values from 0.5 to 2
- neighbour: int32 [16384, 16], P('space'), may hold values from 0 to 2047, as said below
- edge_mask: int32 [16384, 16], P('space'), may hold values from 0 to 1, as said below
Outputs:
- grad_mesh: bfloat16 [8, 2048, 1024], P('ens', 'space')
- grad_w_src: float32 [1024, 1024], P(('ens', 'space'))
- grad_w_dst: float32 [1024, 1024], P(('ens', 'space'))
- grad_w_out: float32 [1024, 32], P(('ens', 'space'))
Inputs may be any that keep to these rules, and one draw needn't show every extreme that they name: `neighbour`: A grid point g in block b = g // 512 names only mesh nodes of blocks b-1, b and b+1 of 64 nodes each, counted cyclically over the 2048 nodes. `edge_mask`: the first slot of every grid point is used.
All inputs are finite; a program needn't handle non-finite values.
Results may differ from a plain program's by a relative error of at most 0.008.
Values may be sent and summed in bfloat16 or wider, within the bound.
No kernel may reach another device: no remote copies, remote signals or barrier semaphores. Data moves between devices by JAX's collectives and lax.ppermute only.
A program may use at most 128 MiB of HBM per device.

v0:
```python
import jax
import jax.numpy as jnp
from jax import lax
from jax.sharding import PartitionSpec as P

loss_scale = 8.0
smooth_sq = 0.01


def extended(cells, sides, width):
    for axis, dim in sides:
        count = lax.axis_size(axis)
        head = lax.slice_in_dim(cells, 0, width, axis=dim)
        tail = lax.slice_in_dim(cells, cells.shape[dim] - width, cells.shape[dim], axis=dim)
        cells = jnp.concatenate(
            [
                lax.ppermute(tail, axis, [(i, (i + 1) % count) for i in range(count)]),
                cells,
                lax.ppermute(head, axis, [((i + 1) % count, i) for i in range(count)]),
            ],
            axis=dim,
        )
    return cells


def passed_along(block, axis, distance):
    devices = range(lax.axis_size(axis))
    route = [((i - distance) % len(devices), i) for i in devices]
    return lax.ppermute(block, axis, route)


def gelu(v):
    return 0.5 * v * (1.0 + jnp.tanh(0.7978845608 * (v + 0.044715 * v * v * v)))


def gelu_grad(v):
    inner = 0.7978845608 * (v + 0.044715 * v * v * v)
    tval = jnp.tanh(inner)
    return 0.5 * (1.0 + tval) + 0.5 * v * (1.0 - tval * tval) * 0.7978845608 * (
        1.0 + 3.0 * 0.044715 * v * v
    )


def smooth_grad(diff):
    return diff / jnp.sqrt(diff * diff + smooth_sq)


def contract_first(left, right):
    return lax.dot_general(
        left, right, (((0,), (0,)), ((), ())), preferred_element_type=jnp.float32
    )


def body(
    mesh_feats,
    grid_embed,
    w_src,
    w_dst,
    w_out,
    truth,
    area_weight,
    var_weight,
    neighbour,
    edge_mask,
):
    f32 = jnp.float32
    own = mesh_feats[0]
    node_rows = own.shape[0]
    width = own.shape[1]
    grid_rows = grid_embed.shape[0]
    slots = neighbour.shape[1]
    space_count = lax.axis_size("space")
    block_id = lax.axis_index("space")
    members = lax.axis_size("ens")
    proj = jnp.dot(own, w_src, preferred_element_type=f32).astype(jnp.bfloat16)
    widened = extended(proj, (("space", 0),), node_rows)
    local = jnp.mod(neighbour - (block_id - 1) * node_rows, node_rows * space_count)
    flat = local.reshape(-1)
    dst = jnp.dot(grid_embed, w_dst, preferred_element_type=f32)
    gathered = jnp.take(widened, flat, axis=0).reshape(grid_rows, slots, width)
    pre = gathered.astype(f32) + dst[:, None, :]
    maskf = edge_mask.astype(f32)
    deg = jnp.sum(maskf, axis=1)
    wgt = maskf / deg[:, None]
    agg = jnp.sum(gelu(pre) * wgt[:, :, None], axis=1).astype(jnp.bfloat16)
    pred = jnp.dot(agg, w_out, preferred_element_type=f32)
    everyone = lax.all_gather(pred[None], "ens", axis=0, tiled=True)
    pair = jnp.sum(smooth_grad(pred[None] - everyone), axis=0)
    weighting = loss_scale * area_weight[:, None] * var_weight[None, :]
    dpred = (
        weighting * (smooth_grad(pred - truth) / members - pair / (members * (members - 1)))
    ).astype(jnp.bfloat16)
    dagg = lax.dot_general(dpred, w_out, (((1,), (1,)), ((), ())), preferred_element_type=f32)
    dpre = (gelu_grad(pre) * wgt[:, :, None] * dagg[:, None, :]).astype(jnp.bfloat16)
    ddst = jnp.sum(dpre, axis=1, dtype=f32).astype(jnp.bfloat16)
    onehot = (jnp.arange(3 * node_rows, dtype=jnp.int32)[:, None] == flat[None, :]).astype(
        jnp.bfloat16
    )
    dwide = jnp.dot(onehot, dpre.reshape(grid_rows * slots, width), preferred_element_type=f32)
    from_above = passed_along(dwide[:node_rows], "space", -1)
    from_below = passed_along(dwide[2 * node_rows :], "space", 1)
    dproj = (dwide[node_rows : 2 * node_rows] + from_above + from_below).astype(jnp.bfloat16)
    grad_mesh = lax.dot_general(
        dproj, w_src, (((1,), (1,)), ((), ())), preferred_element_type=f32
    ).astype(jnp.bfloat16)
    totals = lax.psum_scatter(
        jnp.concatenate(
            [
                contract_first(own, dproj),
                contract_first(grid_embed, ddst),
                contract_first(agg, dpred),
            ],
            axis=1,
        ),
        ("ens", "space"),
        scatter_dimension=0,
        tiled=True,
    )
    return (
        grad_mesh[None],
        totals[:, :width],
        totals[:, width : 2 * width],
        totals[:, 2 * width :],
    )


def solution(mesh):
    in_specs = (
        P("ens", "space", None),
        P("space", None),
        P(),
        P(),
        P(),
        P("space", None),
        P("space"),
        P(),
        P("space", None),
        P("space", None),
    )
    out_specs = (
        P("ens", "space", None),
        P(("ens", "space"), None),
        P(("ens", "space"), None),
        P(("ens", "space"), None),
    )
    return jax.shard_map(body, mesh=mesh, in_specs=in_specs, out_specs=out_specs, check_vma=False)
```

profile of v0, /device:TPU:1, one launch (start us, length us, event | category | flops | bytes accessed | tf_op | source)
XLA Modules:
  0.0 502.3 jit_solution(9321656368319369773)
XLA Ops:
  7.2 2.3 convolution_convert_fusion.1
  9.5 3.3 collective-permute-start.1
  12.8 0.8 compare_and_fusion
  13.9 0.1 reshape.68
  14.0 0.8 convert_reduce_fusion
  14.8 0.8 convert_divide_fusion
  15.6 0.2 copy.30
  16.1 3.8 fusion.33
  19.9 0.7 broadcast_multiply_fusion
  20.7 35.4 %gather_fusion = bf16[8192,1024]{1,0:T(8,128)(2,1)} fusion(bf16[192,1024]{1,0:T(8,128)(2,1)S(1)} %pad_maximum_fusion.1, s32[8192]{0:T(1024)S(1)} %broadcast_clamp_fusion), kind=kCustom, calls=%fused_computation | custom fusion | bytes 33587200 | tf_op jit(solution)/shard_map/jit(_take)/gather | solution.py:80
  56.1 22.6 %multiply_reduce_fusion = bf16[512,1024]{1,0:T(8,128)(2,1)S(1)} fusion(f32[512,16]{1,0:T(8,128)S(1)} %copy.29, f32[512,1024]{1,0:T(8,128)} %fusion.33, pred[512,16]{1,0:T(8,128)(4,1)S(1)} %copy.30, bf16[8192,1024]{1,0:T(8,128)(2,1)} %gather_fusion), kind=kLoop, calls=%fused_computation.22 | loop fusion | flops 108527616 | bytes 19963904 | tf_op jit(solution)/shard_map/reduce_sum | solution.py:85
  78.7 0.4 fusion.36
  79.1 40.2 %all-gather = f32[4096,32]{0,1:T(8,128)S(1)} all-gather(f32[512,32]{0,1:T(8,128)S(1)} %fusion.36), channel_id=2, replica_groups=mesh['ens'=8,'space'=32] {'ens'}, dimensions={0}, use_global_device_ids=true | all-gather | bytes 589824 | tf_op jit(solution)/shard_map/all_gather | solution.py:87
  119.3 0.3 copy.37
  119.6 0.2 multiply_reduce_fusion.1
  119.9 0.5 fusion.34
  120.4 33.8 %fusion.18 = bf16[512,1024]{1,0:T(8,128)(2,1)S(1)} fusion(f32[512,1024]{1,0:T(8,128)S(1)} %fusion.34, f32[512,16]{1,0:T(8,128)S(1)} %copy.29, f32[512,1024]{1,0:T(8,128)S(1)} %copy-done.2, pred[512,16]{1,0:T(8,128)(4,1)S(1)} %copy.30, bf16[8192,1024]{1,0:T(8,128)(2,1)} %gather_fusion), kind=kLoop, calls=%fused_computation.26 | loop fusion | flops 200802304 | bytes 22061056 | tf_op jit(solution)/shard_map/reduce_sum | solution.py:95
  154.2 30.8 %fusion.7 = bf16[8192,1024]{1,0:T(8,128)(2,1)} fusion(f32[512,1024]{1,0:T(8,128)S(1)} %fusion.34, f32[8192]{0:T(1024)S(1)} %mul.165, f32[512,1024]{1,0:T(8,128)S(1)} %copy-done.2, bf16[8192,1024]{1,0:T(8,128)(2,1)} %gather_fusion, pred[8192]{0:T(1024)(128)(4,1)S(1)} %compare_and_fusion.1), kind=kLoop, calls=%fused_computation.12 | loop fusion | flops 192937984 | bytes 37789696 | tf_op jit(solution)/shard_map/convert_element_type | solution.py:94
  185.0 7.7 %fusion.19 = f32[192,1024]{1,0:T(8,128)S(1)} fusion(bf16[8192,1024]{1,0:T(8,128)(2,1)} %fusion.7, s32[8192]{0:T(1024)S(1)} %eq.18), kind=kOutput, calls=%fused_computation.30 | convolution fusion | flops 3222798336 | bytes 17596416 | tf_op jit(solution)/shard_map/dot_general | solution.py:99
  192.7 10.2 %collective-permute-start.2 = (f32[64,1024]{1,0:T(8,128)S(1)}, f32[64,1024]{1,0:T(8,128)S(1)}, u32[]{:S(2)}, u32[]{:S(2)}) collective-permute-start(f32[64,1024]{1,0:T(8,128)S(1)} %get-tuple-element.20), channel_id=1, source_target_pairs={{1,0},{2,1},{3,2},{4,3},{5,4},{6,5},{7,6},{8,7},{9,8},{10,9},{11,1... | collective-permute-start | bytes 786440 | tf_op jit(solution)/shard_map/ppermute | solution.py:29
  202.9 1.3 convolution_bitcast_fusion
  204.2 0.3 fusion.35
  204.5 4.3 collective-permute-done.3
  208.9 0.7 convolution_bitcast_fusion.1
  209.7 4.0 pad_maximum_fusion
  213.7 3.0 fusion.21
  216.7 274.2 %all-reduce.3.cloned.1.call-done = f32[1024,2080]{0,1:T(8,128)} async-done(((f32[1024,2080]{0,1:T(8,128)}), f32[1024,2080]{0,1:T(8,128)}) %all-reduce.3.cloned.1.call-update) | async-done | bytes 8519696
  490.9 0.8 dynamic-slice.3
  491.7 0.7 copy.34
  492.3 1.5 fusion.31
  493.9 0.8 copy.33
  494.7 0.8 copy.32
  (34 shorter events, 0.9 us)
Async XLA Ops:
  7.2 9.0 %copy-start = (bf16[1024,1024]{1,0:T(8,128)(2,1)S(1)}, bf16[1024,1024]{1,0:T(8,128)(2,1)}, u32[]{:S(2)}) copy-start(bf16[1024,1024]{1,0:T(8,128)(2,1)} %param.13) | copy-start | bytes 6291460
  7.2 483.7 %all-reduce.3.cloned.1.call-start = ((), (), s32[]{:S(2)}) async-start(), calls=%async_computation | async-start | bytes 17039360
  9.5 11.1 %collective-permute-start.1 = (bf16[64,1024]{1,0:T(8,128)(2,1)S(1)}, bf16[64,1024]{1,0:T(8,128)(2,1)S(1)}, u32[]{:S(2)}, u32[]{:S(2)}) collective-permute-start(bf16[64,1024]{1,0:T(8,128)(2,1)S(1)} %convolution_convert_fusion.1), channel_id=1, source_target_pairs={{1,0},{2,1},{3,2},{4,3},{5,4},{6,5},{7,6},{8,7},{9,8},{10,9},{11,1... | collective-permute-start | bytes 393224 | tf_op jit(solution)/shard_map/ppermute | solution.py:19
  12.8 7.8 %collective-permute-start = (bf16[64,1024]{1,0:T(8,128)(2,1)S(1)}, bf16[64,1024]{1,0:T(8,128)(2,1)S(1)}, u32[]{:S(2)}, u32[]{:S(2)}) collective-permute-start(bf16[64,1024]{1,0:T(8,128)(2,1)S(1)} %convolution_convert_fusion.1), channel_id=1, source_target_pairs={{0,1},{1,2},{2,3},{3,4},{4,5},{5,6},{6,7},{7,8},{8,9},{9,10},{10,1... | collective-permute-start | bytes 393224 | tf_op jit(solution)/shard_map/ppermute | solution.py:17
  56.1 22.6 %copy-start.5 = (bf16[1024,32]{0,1:T(8,128)(2,1)S(1)}, bf16[1024,32]{0,1:T(8,128)(2,1)}, u32[]{:S(2)}) copy-start(bf16[1024,32]{0,1:T(8,128)(2,1)} %param.14) | copy-start | bytes 196612
  56.1 63.7 %copy-start.6 = (f32[512,32]{0,1:T(8,128)S(1)}, f32[512,32]{0,1:T(8,128)}, u32[]{:S(2)}) copy-start(f32[512,32]{0,1:T(8,128)} %param.15) | copy-start | bytes 196612
  56.1 63.7 %copy-start.7 = (f32[32]{0:T(128)S(1)}, f32[32]{0:T(128)}, u32[]{:S(2)}) copy-start(f32[32]{0:T(128)} %param.17) | copy-start | bytes 388
  56.1 64.3 %copy-start.2 = (f32[512,1024]{1,0:T(8,128)S(1)}, f32[512,1024]{1,0:T(8,128)}, u32[]{:S(2)}) copy-start(f32[512,1024]{1,0:T(8,128)} %fusion.33) | copy-start | bytes 6291460
  185.0 17.9 %copy-start.3 = (bf16[512,1024]{1,0:T(8,128)(2,1)S(1)}, bf16[512,1024]{1,0:T(8,128)(2,1)}, u32[]{:S(2)}) copy-start(bf16[512,1024]{1,0:T(8,128)(2,1)} %param.11) | copy-start | bytes 3145732
  185.0 23.9 %copy-start.4 = (bf16[1,64,1024]{2,1,0:T(8,128)(2,1)S(1)}, bf16[1,64,1024]{2,1,0:T(8,128)(2,1)}, u32[]{:S(2)}) copy-start(bf16[1,64,1024]{2,1,0:T(8,128)(2,1)} %param.10) | copy-start | bytes 393220
  192.7 11.8 %collective-permute-start.2 = (f32[64,1024]{1,0:T(8,128)S(1)}, f32[64,1024]{1,0:T(8,128)S(1)}, u32[]{:S(2)}, u32[]{:S(2)}) collective-permute-start(f32[64,1024]{1,0:T(8,128)S(1)} %get-tuple-element.20), channel_id=1, source_target_pairs={{1,0},{2,1},{3,2},{4,3},{5,4},{6,5},{7,6},{8,7},{9,8},{10,9},{11,1... | collective-permute-start | bytes 786440 | tf_op jit(solution)/shard_map/ppermute | solution.py:29
  202.9 5.9 %collective-permute-start.3 = (f32[64,1024]{1,0:T(8,128)S(1)}, f32[64,1024]{1,0:T(8,128)S(1)}, u32[]{:S(2)}, u32[]{:S(2)}) collective-permute-start(f32[64,1024]{1,0:T(8,128)S(1)} %get-tuple-element.21), channel_id=1, source_target_pairs={{31,0},{0,1},{1,2},{2,3},{3,4},{4,5},{5,6},{6,7},{7,8},{8,9},{9,10... | collective-permute-start | bytes 786440 | tf_op jit(solution)/shard_map/ppermute | solution.py:29
  208.9 286.6 %copy-start.1 = (bf16[1024,1024]{1,0:T(8,128)(2,1)S(1)}, bf16[1024,1024]{1,0:T(8,128)(2,1)}, u32[]{:S(2)}) copy-start(bf16[1024,1024]{1,0:T(8,128)(2,1)} %param.13) | copy-start | bytes 6291460
Sparse Core Ops, SparseCore 0:
  213.8 277.0 all-reduce.2
where the time goes:
time: 503 us; the launch traced here: 502 us
  waiting for transfers between devices  279 us (55%)
  other arithmetic  94.6 us (19%)
  local copies, waits for them, and re-layouts  41.2 us (8%)
  blocking collectives  40.2 us (8%)
  matrix products  19.9 us (4%)
  between operations  14.2 us (3%)
  starting transfers between devices  13.5 us (3%)
    unnamed x2, waiting for transfers between devices  274 us
    all_gather x1, blocking collectives, body(): everyone = lax.all_gather(pred[None], 'ens', axis=0, tiled=True)  40.2 us
    gather x1, local copies, waits for them, and re-layouts, body(): gathered = jnp.take(widened, flat, axis=0).reshape(grid_rows, slots, width)  35.4 us
    reduce_sum x1, other arithmetic, body(): ddst = jnp.sum(dpre, axis=1, dtype=f32).astype(jnp.bfloat16)  33.8 us
    convert_element_type x1, other arithmetic, body(): (gelu_grad(pre) * wgt[:, :, None] * dagg[:, None, :]).astype(jnp.bfloat16)  30.8 us
    reduce_sum x1, other arithmetic, body(): agg = jnp.sum(gelu(pre) * wgt[:, :, None], axis=1).astype(jnp.bfloat16)  22.6 us
    ppermute x2, starting transfers between devices, passed_along(): return lax.ppermute(block, axis, route)  10.2 us
  transfers between devices with their start and end apart: 5, of which 2 were waited for; matrix products, arithmetic and copies ran while one was open for 2% of the time, Pallas kernels for 0%

commit v1 on v0

v1 whole, which is shorter than its diff:
```python
import functools
import jax
import jax.numpy as jnp
from jax import lax
from jax.experimental import pallas as pl
from jax.experimental.pallas import tpu as pltpu
from jax.sharding import Mesh, PartitionSpec as P

loss_scale = 8.0
smooth_sq = 0.01
TILE = 64
LANES = 128
NCOL = 256
f32 = jnp.float32
bf16 = jnp.bfloat16
SPACE = ("y", "zl", "c")
ENS = ("zh", "x")
LATE = ("zh", "y", "zl")


def shifted(block, axes, distance):
    count = lax.axis_size(axes)
    return lax.ppermute(block, axes, [(i, (i + distance) % count) for i in range(count)])


def smooth_grad(diff):
    return diff / jnp.sqrt(diff * diff + smooth_sq)


def gelu_parts(v):
    c0 = 0.7978845608
    c1 = c0 * 0.044715
    sq = v * v
    inner = v * (c0 + c1 * sq)
    t = jnp.tanh(inner)
    u = 1.0 + t
    slope = v * (c0 + (3.0 * c1) * sq)
    return v * u, u * (1.0 + (1.0 - t) * slope)


def forward_kernel(slots, wide_ref, dst_ref, idx_ref, scale_ref, gp_ref, agg_ref, sum_ref, rhs, hot, pre):
    nodes = wide_ref.shape[0]
    tile = dst_ref.shape[0]
    width = dst_ref.shape[1]
    depth = rhs.shape[0]

    @pl.when(pl.program_id(0) == 0)
    def _():
        rhs[:nodes, :] = wide_ref[...]

    rhs[nodes:, :] = dst_ref[...]
    lane = lax.broadcasted_iota(jnp.int32, (tile, depth), 1)
    row = lax.broadcasted_iota(jnp.int32, (tile, depth), 0)
    eye = lane == row + nodes
    for k in range(slots):
        col = idx_ref[:, k : k + 1]
        hit = (lane == col) | (eye & (col >= 0))
        hot[k * tile : (k + 1) * tile, :] = jnp.where(hit, 1.0, 0.0).astype(bf16)
    scale = scale_ref[...]
    for n in range(width // NCOL):
        pre[n % 2] = jnp.dot(
            hot[...], rhs[:, n * NCOL : (n + 1) * NCOL], preferred_element_type=f32
        )
        for half in range(NCOL // LANES):
            here = slice(half * LANES, (half + 1) * LANES)
            cols = slice(n * NCOL + half * LANES, n * NCOL + (half + 1) * LANES)
            acc_g = jnp.zeros((tile, LANES), f32)
            acc_s = jnp.zeros((tile, LANES), f32)
            for k in range(slots):
                rows = slice(k * tile, (k + 1) * tile)
                value, grad = gelu_parts(pre[n % 2, rows, here])
                acc_g = acc_g + value
                acc_s = acc_s + jnp.where(idx_ref[:, k : k + 1] >= 0, grad, 0.0)
                gp_ref[rows, cols] = grad.astype(bf16)
            agg_ref[:, cols] = (acc_g * scale).astype(bf16)
            sum_ref[:, cols] = acc_s.astype(bf16)


def forward(wide, dst, idx, scale):
    grid_rows, width = dst.shape
    nodes = wide.shape[0]
    slots = idx.shape[1]
    tiles = grid_rows // TILE
    whole = lambda t: (0, 0)
    step = lambda t: (t, 0)
    return pl.pallas_call(
        functools.partial(forward_kernel, slots),
        grid=(tiles,),
        in_specs=[
            pl.BlockSpec((nodes, width), whole),
            pl.BlockSpec((TILE, width), step),
            pl.BlockSpec((TILE, slots), step),
            pl.BlockSpec((TILE, 1), step),
        ],
        out_specs=[
            pl.BlockSpec((TILE * slots, width), step),
            pl.BlockSpec((TILE, width), step),
            pl.BlockSpec((TILE, width), step),
        ],
        out_shape=[
            jax.ShapeDtypeStruct((grid_rows * slots, width), bf16),
            jax.ShapeDtypeStruct((grid_rows, width), bf16),
            jax.ShapeDtypeStruct((grid_rows, width), bf16),
        ],
        scratch_shapes=[
            pltpu.VMEM((nodes + TILE, width), bf16),
            pltpu.VMEM((TILE * slots, nodes + TILE), bf16),
            pltpu.VMEM((2, TILE * slots, NCOL), f32),
        ],
        compiler_params=pltpu.CompilerParams(vmem_limit_bytes=40 * 1024 * 1024),
        cost_estimate=pl.CostEstimate(
            flops=2 * grid_rows * slots * 256 * width,
            bytes_accessed=2 * grid_rows * slots * width,
            transcendentals=grid_rows * slots * width,
        ),
    )(wide, dst, idx, scale)


def backward_kernel(slots, gp_ref, sum_ref, dpred_ref, wout_ref, scale_ref, idx_ref, out_ref, lead, prod, acc):
    step = pl.program_id(0)
    nodes = acc.shape[0]
    tile = gp_ref.shape[0] // slots
    width = gp_ref.shape[1]

    @pl.when(step == 0)
    def _():
        for n in range(width // NCOL):
            cols = slice(n * NCOL, (n + 1) * NCOL)
            dagg = lax.dot_general(
                dpred_ref[...], wout_ref[:, cols], (((0,), (0,)), ((), ())), preferred_element_type=f32
            )
            dagg = dagg * scale_ref[...]
            lead[:, cols] = dagg.astype(bf16)
            out_ref[nodes:, cols] = (dagg * sum_ref[:, cols].astype(f32)).astype(bf16)
        acc[...] = jnp.zeros_like(acc)

    node = lax.broadcasted_iota(jnp.int32, (nodes, tile * slots), 0)
    hot = jnp.where(node == idx_ref[0], 1.0, 0.0).astype(bf16)
    here = pl.ds(pl.multiple_of(step * tile, tile), tile)
    for k in range(slots):
        rows = slice(k * tile, (k + 1) * tile)
        prod[rows, :] = gp_ref[rows, :] * lead[here, :]
    for n in range(width // NCOL):
        cols = slice(n * NCOL, (n + 1) * NCOL)
        acc[:, cols] += jnp.dot(hot, prod[:, cols], preferred_element_type=f32)

    @pl.when(step == pl.num_programs(0) - 1)
    def _():
        out_ref[:nodes, :] = acc[...].astype(bf16)


def backward(gp, sums, dpred_t, wout_t, scale, idx_rows, nodes):
    grid_rows, width = sums.shape
    slots = gp.shape[0] // grid_rows
    tiles = grid_rows // TILE
    whole = lambda t: (0, 0)
    return pl.pallas_call(
        functools.partial(backward_kernel, slots),
        grid=(tiles,),
        in_specs=[
            pl.BlockSpec((TILE * slots, width), lambda t: (t, 0)),
            pl.BlockSpec((grid_rows, width), whole),
            pl.BlockSpec(dpred_t.shape, whole),
            pl.BlockSpec(wout_t.shape, whole),
            pl.BlockSpec((grid_rows, 1), whole),
            pl.BlockSpec((1, 1, TILE * slots), lambda t: (t, 0, 0)),
        ],
        out_specs=pl.BlockSpec((nodes + grid_rows, width), whole),
        out_shape=jax.ShapeDtypeStruct((nodes + grid_rows, width), bf16),
        scratch_shapes=[
            pltpu.VMEM((grid_rows, width), bf16),
            pltpu.VMEM((TILE * slots, width), bf16),
            pltpu.VMEM((nodes, width), f32),
        ],
        compiler_params=pltpu.CompilerParams(vmem_limit_bytes=40 * 1024 * 1024),
        cost_estimate=pl.CostEstimate(
            flops=2 * grid_rows * slots * 256 * width,
            bytes_accessed=2 * grid_rows * slots * width,
            transcendentals=0,
        ),
    )(gp, sums, dpred_t, wout_t, scale, idx_rows)


def contract_first(left, right):
    return lax.dot_general(left, right, (((0,), (0,)), ((), ())), preferred_element_type=f32)


def body(
    mesh_feats,
    grid_embed,
    w_src,
    w_dst,
    w_out,
    truth,
    area_weight,
    var_weight,
    neighbour,
    edge_mask,
):
    own = mesh_feats[0]
    node_rows, width = own.shape
    grid_rows, slots = neighbour.shape
    nodes = 3 * node_rows
    tiles = grid_rows // TILE
    space_count = lax.axis_size(SPACE)
    block_id = lax.axis_index(SPACE)
    members = lax.axis_size(ENS)
    swap = [(0, 1), (1, 0)]
    core = lax.axis_index("c")

    below = shifted(own, SPACE, 1)
    above = shifted(own, SPACE, -1)
    feats = jnp.concatenate([below, own, above], axis=0)

    h = jnp.arange(width, dtype=jnp.int32)
    half = width // 2
    source = (h % half // 4) * 8 + (h // half) * 4 + h % 4
    order = (h[:, None] == source[None, :]).astype(bf16)

    dst = jnp.dot(grid_embed, w_dst, preferred_element_type=f32).astype(bf16)
    local = jnp.mod(neighbour - (block_id - 1) * node_rows, node_rows * space_count)
    idx = jnp.where(edge_mask > 0, local, -1)
    idx_rows = idx.reshape(tiles, TILE, slots).transpose(0, 2, 1).reshape(tiles, 1, slots * TILE)
    scale = 0.5 / jnp.sum(edge_mask.astype(f32), axis=1, keepdims=True)
    wide = jnp.dot(feats, w_src, preferred_element_type=f32).astype(bf16)

    left = jnp.concatenate([feats, grid_embed], axis=0)
    left = jnp.dot(left, order, preferred_element_type=f32).astype(bf16)
    left = left.reshape(left.shape[0], 2, half)
    left_own = lax.dynamic_index_in_dim(left, core, 1, keepdims=False)
    left_far = lax.ppermute(lax.dynamic_index_in_dim(left, 1 - core, 1, keepdims=False), "c", swap)

    gp, agg, sums = forward(wide, dst, idx, scale)

    pred = lax.dot_general(w_out, agg, (((0,), (1,)), ((), ())), preferred_element_type=f32)
    everyone = lax.all_to_all(
        jnp.broadcast_to(pred[None], (members,) + pred.shape), ENS, 0, 0, tiled=True
    )
    pair = jnp.sum(smooth_grad(pred[None] - everyone), axis=0)
    weighting = loss_scale * area_weight[None, :] * var_weight[:, None]
    dpred = (
        weighting * (smooth_grad(pred - truth.T) / members - pair / (members * (members - 1)))
    ).astype(bf16)

    right_own = backward(gp, sums, dpred, w_out.T, scale, idx_rows, nodes)
    right_far = lax.ppermute(right_own, "c", swap)

    from_above = shifted(right_own[:node_rows], SPACE, -1)
    from_below = shifted(right_own[2 * node_rows : nodes], SPACE, 1)
    dproj = (
        right_own[node_rows : 2 * node_rows].astype(f32)
        + from_above.astype(f32)
        + from_below.astype(f32)
    ).astype(bf16)
    grad_mesh = lax.dot_general(
        dproj, w_src, (((1,), (1,)), ((), ())), preferred_element_type=f32
    ).astype(bf16)

    out_part = jnp.dot(dpred, agg, preferred_element_type=f32).astype(bf16)
    out_part = jnp.dot(out_part, order, preferred_element_type=f32).T.reshape(2, half, -1)
    out_own = lax.dynamic_index_in_dim(out_part, core, 0, keepdims=False)
    out_far = lax.ppermute(
        lax.dynamic_index_in_dim(out_part, 1 - core, 0, keepdims=False).astype(bf16), "c", swap
    )
    total = jnp.concatenate(
        [
            contract_first(left_own[:nodes], right_own[:nodes])
            + contract_first(left_far[:nodes], right_far[:nodes]),
            contract_first(left_own[nodes:], right_own[nodes:])
            + contract_first(left_far[nodes:], right_far[nodes:]),
            out_own + out_far.astype(f32),
        ],
        axis=1,
    )
    columns = total.shape[1]
    total = total.reshape(2, lax.axis_size("x"), -1, columns)
    along = lax.axis_index("x")
    total_x = lax.dynamic_index_in_dim(total, along, 1, keepdims=False)
    count = lax.axis_size("x")
    for d in (1, 3, 2):
        piece = lax.dynamic_index_in_dim(total, (along + d) % count, 1, keepdims=False)
        total_x = total_x + shifted(piece.astype(bf16), "x", d).astype(f32)
    pieces = lax.all_to_all(total_x.reshape(-1, columns).astype(bf16), LATE, 0, 0, tiled=True)
    total = jnp.sum(pieces.reshape(lax.axis_size(LATE), -1, columns).astype(f32), axis=0)
    return (
        grad_mesh[None],
        total[:, :width],
        total[:, width : 2 * width],
        total[:, 2 * width :],
    )


def solution(mesh):
    fine = Mesh(mesh.devices.reshape(2, 4, 4, 4, 2), ("zh", "x", "y", "zl", "c"))
    everywhere = ENS + SPACE
    in_specs = (
        P(ENS, SPACE, None),
        P(SPACE, None),
        P(),
        P(),
        P(),
        P(SPACE, None),
        P(SPACE),
        P(),
        P(SPACE, None),
        P(SPACE, None),
    )
    out_specs = (
        P(ENS, SPACE, None),
        P(everywhere, None),
        P(everywhere, None),
        P(everywhere, None),
    )
    return jax.shard_map(body, mesh=fine, in_specs=in_specs, out_specs=out_specs, check_vma=False)
```

time: 503 us -> 171 us (0.34)
  waiting for transfers between devices: 279 us -> 38.7 us
  other arithmetic: 94.6 us -> 8.28 us
  blocking collectives: 40.2 us -> 0 us
  Pallas kernels: 0 us -> 39.9 us
  starting transfers between devices: 13.5 us -> 35.1 us
  local copies, waits for them, and re-layouts: 41.2 us -> 27 us
  between operations: 14.2 us -> 1.01 us
    unnamed x2 -> x0, waiting for transfers between devices: 274 us -> none
    reduce_sum x3 -> x2, other arithmetic: 57.1 us -> 2.07 us  [the longest x1 1.3 us: body(): jnp.sum(pieces.reshape(lax.axis_size(LATE), -1, columns).astype(f32), axi...]
    all_gather x1 -> x0, blocking collectives: 40.2 us -> none  [body(): everyone = lax.all_gather(pred[None], 'ens', axis=0, tiled=True)]
    pallas_call x0 -> x2, Pallas kernels: none -> 39.9 us  [the longest x1 29.3 us: forward(): pl.pallas_call(functools.partial(forward_kernel, slots), grid=(tiles,), i...]
    gather x1 -> x0, local copies, waits for them, and re-layouts: 35.4 us -> none  [body(): gathered = jnp.take(widened, flat, axis=0).reshape(grid_rows, slots, width)]
    ppermute x4 -> x10, waiting for transfers between devices: 4.36 us -> 38.7 us  [the longest x7 38.7 us: shifted(): lax.ppermute(block, axes, [(i, (i + distance) % count) for i in range(cou...]
    convert_element_type x3 -> x2, other arithmetic: 31 us -> 3.76 us  [the longest x1 2.81 us: body(): total_x.reshape(-1, columns).astype(bf16)]
    all_to_all x0 -> x2, starting transfers between devices: none -> 18 us  [the longest x1 9.42 us: body(): lax.all_to_all(jnp.broadcast_to(pred[None], (members,) + pred.shape), ENS...]
  transfers between devices with their start and end apart: 5 -> 12, of which waited for: 2 -> 4; matrix products, arithmetic and copies ran while one was open for 2% -> 19% of each run, Pallas kernels for 0% -> 6%
where the time goes in v1:
time: 171 us; the launch traced here: 170 us
  Pallas kernels  39.9 us (23%)
  waiting for transfers between devices  38.7 us (23%)
  starting transfers between devices  35.1 us (21%)
  local copies, waits for them, and re-layouts  27 us (16%)
  matrix products  19.6 us (11%)
  other arithmetic  8.28 us (5%)
    ppermute x7, waiting for transfers between devices, shifted(): lax.ppermute(block, axes, [(i, (i + distance) % count) for i in range(cou...  38.7 us
    pallas_call x1, Pallas kernels, forward(): pl.pallas_call(functools.partial(forward_kernel, slots), grid=(tiles,), i...  29.3 us
    unnamed x48, local copies, waits for them, and re-layouts  11 us
    pallas_call x1, Pallas kernels, backward(): pl.pallas_call(functools.partial(backward_kernel, slots), grid=(tiles,),...  10.7 us
    ppermute x7, starting transfers between devices, shifted(): lax.ppermute(block, axes, [(i, (i + distance) % count) for i in range(cou...  10 us
    all_to_all x1, starting transfers between devices, body(): lax.all_to_all(jnp.broadcast_to(pred[None], (members,) + pred.shape), ENS...  9.42 us
    all_to_all x1, starting transfers between devices, body(): lax.all_to_all(total_x.reshape(-1, columns).astype(bf16), LATE, 0, 0, til...  8.55 us
    dot_general x4, matrix products, contract_first(): lax.dot_general(left, right, (((0,), (0,)), ((), ())), preferred_element_...  6.13 us
  transfers between devices with their start and end apart: 12, of which 4 were waited for; matrix products, arithmetic and copies ran while one was open for 19% of the time, Pallas kernels for 6%

profile of v1, /device:TPU:1, one launch (start us, length us, event | category | flops | bytes accessed | tf_op | source)
XLA Modules:
  0.0 169.7 jit_solution(11356176848513200619)
XLA Ops:
  0.6 3.1 %collective-permute-start = (bf16[64,1024]{1,0:T(8,128)(2,1)}, bf16[64,1024]{1,0:T(8,128)(2,1)S(1)}, u32[]{:S(2)}, u32[]{:S(2)}) collective-permute-start(bf16[64,1024]{1,0:T(8,128)(2,1)} %bitcast.66), channel_id=1, source_target_pairs={{0,1},{1,2},{2,3},{3,4},{4,5},{5,6},{6,7},{7,8},{8,9},{9,10},{10,1... | collective-permute-start | bytes 393224 | tf_op jit(solution)/shard_map/ppermute | solution.py:23
  6.9 2.6 %convolution_convert_fusion.dst_ref = bf16[512,1024]{1,0:T(8,128)(2,1)S(1)} fusion(bf16[512,1024]{1,0:T(8,128)(2,1)} %param.11, bf16[1024,1024]{1,0:T(8,128)(2,1)S(1)} %copy-done), kind=kOutput, calls=%fused_computation.10 | convolution fusion | flops 1074266112 | bytes 4194304 | tf_op jit(solution)/shard_map/dot_general | solution.py:220
  10.4 29.3 %shard_map.129 = (bf16[8192,1024]{1,0:T(8,128)(2,1)}, bf16[512,1024]{1,0:T(8,128)(2,1)S(1)}, bf16[512,1024]{1,0:T(8,128)(2,1)S(1)}) custom-call(bf16[192,1024]{1,0:T(8,128)(2,1)S(1)} %convolution_convert_fusion.1.wide_ref, bf16[512,1024]{1,0:T(8,128)(2,1)S(1)} %convolution_convert_fusion.dst_ref, s32[512,16]{1,0:T(8,128)S(1)} %fusion.34.idx_ref, ...), custom_call_target="tpu_custom_call" | custom-call | flops 4294967296 | bytes 16777216 | tf_op jit(solution)/shard_map/pallas_call | solution.py:86
  43.6 9.4 %all-to-all-start = ((f32[8,32,512]{2,1,0:T(8,128)}), f32[8,32,512]{2,1,0:T(8,128)}, u32[]{:S(2)}, u32[]{:S(2)}) async-start(f32[8,32,512]{2,1,0:T(8,128)} %sub.45), calls=%async_computation | async-start | bytes 1048576 | tf_op jit(solution)/shard_map/all_to_all | solution.py:236
  53.9 3.9 %fusion.6 = bf16[704,1024]{1,0:T(8,128)(2,1)} fusion(s32[1024]{0:T(1024)S(1)} %fusion.51, bf16[512,1024]{1,0:T(8,128)(2,1)S(1)} %copy-done.19, bf16[64,1024]{1,0:T(8,128)(2,1)} %copy-done.22, bf16[64,1024]{1,0:T(8,128)(2,1)} %bitcast.68, bf16[64,1024]{1,0:T(8,128)(2,1)} %copy-done.21), kind=kOutput, calls=%fused_computation.7 | convolution fusion | flops 1483931648 | bytes 2887680 | tf_op jit(solution)/shard_map/dot_general | solution.py:228
  57.8 3.8 %reshape.98 = bf16[704,2,512]{2,1,0:T(2,128)(2,1)S(1)} reshape(bf16[704,1024]{1,0:T(8,128)(2,1)} %fusion.6) | data formatting | bytes 2883584 | tf_op jit(solution)/shard_map/reshape | solution.py:229
  61.6 1.5 constant_dynamic-slice_fusion.1
  64.1 5.3 %collective-permute-start.4 = (bf16[704,512]{1,0:T(8,128)(2,1)}, bf16[704,512]{1,0:T(8,128)(2,1)}, u32[]{:S(2)}, u32[]{:S(2)}) collective-permute-start(bf16[704,512]{1,0:T(8,128)(2,1)} %bitcast.57), channel_id=1, source_target_pairs={{0,1},{1,0},{2,3},{3,2},{4,5},{5,4},{6,7},{7,6},{8,9},{9,8},{10,11... | collective-permute-start | bytes 2162696 | tf_op jit(solution)/shard_map/ppermute | solution.py:231
  69.4 1.2 multiply_reduce_fusion
  72.5 1.2 copy-done.4
  75.4 10.7 %shard_map.130 = bf16[704,1024]{1,0:T(8,128)(2,1)S(1)} custom-call(bf16[8192,1024]{1,0:T(8,128)(2,1)} %get-tuple-element.7.gp_ref, bf16[512,1024]{1,0:T(8,128)(2,1)S(1)} %copy-done.4, bf16[32,512]{1,0:T(8,128)(2,1)S(1)} %multiply_convert_fusion.dpred_ref, bf16[32,1024]{1,0:T(8,128)(2,1)S(1)} %bitcast.59, f32[512,1]{1,0:T(8,128)S(1)} %copy-done.2, ...), custom_call_target="tpu_custom_call" | custom-call | flops 4294967296 | bytes 16777216 | tf_op jit(solution)/shard_map/pallas_call | solution.py:157
  86.0 1.5 collective-permute-start.5
  87.6 1.1 constant_dynamic-slice_fusion
  88.7 2.1 %constant_dynamic-slice_fusion.2 = bf16[512,1,512]{2,1,0:T(2,128)(2,1)} fusion(bf16[704,2,512]{2,1,0:T(2,128)(2,1)S(1)} %copy-done.11, s32[]{:T(128)S(6)} %add.173, s32[]{:T(128)S(6)} %select_n.96), kind=kLoop, calls=%fused_computation.97 | loop fusion | bytes 1048584 | tf_op jit(solution)/shard_map/slice | solution.py:269
  90.8 3.0 %fusion.2 = f32[1024,32]{1,0:T(8,128)} fusion(s32[1024]{0:T(1024)S(1)} %fusion.51, bf16[32,512]{1,0:T(8,128)(2,1)} %copy-done.9, bf16[512,1024]{1,0:T(8,128)(2,1)} %copy-done.5), kind=kOutput, calls=%fused_computation.4 | convolution fusion | flops 102793216 | bytes 1216512 | tf_op jit(solution)/shard_map/dot_general | solution.py:260
  95.1 2.0 %fusion.19 = f32[512,1024]{1,0:T(8,128)S(1)} fusion(bf16[704,1024]{1,0:T(8,128)(2,1)S(1)} %shard_map.130, bf16[512,1,512]{2,1,0:T(2,128)(2,1)} %constant_dynamic-slice_fusion.2), kind=kOutput, calls=%fused_computation.32 | convolution fusion | flops 536870912 | bytes 3670016 | tf_op jit(solution)/shard_map/dot_general | solution.py:185
  98.2 1.6 convolution_add_fusion.1
  99.8 2.1 %convolution_add_fusion = f32[512,1024]{1,0:T(8,128)S(1)} fusion(f32[512,1024]{1,0:T(8,128)S(1)} %fusion.19, bf16[704,1024]{1,0:T(8,128)(2,1)} %collective-permute-done.5, bf16[704,512]{1,0:T(8,128)(2,1)} %collective-permute-done.4), kind=kOutput, calls=%fused_computation.8 | convolution fusion | flops 537395200 | bytes 5767168 | tf_op jit(solution)/shard_map/dot_general | solution.py:185
  102.3 2.0 %copy-done.12 = f32[512,2080]{1,0:T(8,128)} copy-done((f32[512,2080]{1,0:T(8,128)}, f32[512,2080]{1,0:T(8,128)S(1)}, u32[]{:S(2)}) %copy-start.12) | copy-done | bytes 4259864
  104.3 1.3 fusion.22
  106.7 1.6 collective-permute-start.8
  108.3 1.3 collective-permute-start.9
  109.6 11.2 %collective-permute-done.7 = bf16[2,64,2080]{2,1,0:T(8,128)(2,1)} collective-permute-done((bf16[2,64,2080]{2,1,0:T(8,128)(2,1)}, bf16[2,64,2080]{2,1,0:T(8,128)(2,1)}, u32[]{:S(2)}, u32[]{:S(2)}) %collective-permute-start.7) | collective-permute-done | bytes 532512 | tf_op jit(solution)/shard_map/ppermute | solution.py:23
  120.8 12.7 %collective-permute-done.9 = bf16[2,64,2080]{2,1,0:T(8,128)(2,1)} collective-permute-done((bf16[2,64,2080]{2,1,0:T(8,128)(2,1)}, bf16[2,64,2080]{2,1,0:T(8,128)(2,1)}, u32[]{:S(2)}, u32[]{:S(2)}) %collective-permute-start.9) | collective-permute-done | bytes 532512 | tf_op jit(solution)/shard_map/ppermute | solution.py:23
  133.5 2.8 %fusion.17 = bf16[2,64,2080]{2,1,0:T(8,128)(2,1)} fusion(bf16[2,64,2080]{2,1,0:T(8,128)(2,1)} %collective-permute-done.9, bf16[2,64,2080]{2,1,0:T(8,128)(2,1)} %collective-permute-done.8, bf16[2,64,2080]{2,1,0:T(8,128)(2,1)} %collective-permute-done.7, f32[2,4,64,2080]{3,2,1,0:T(8,128)} %bitcast.61, s32[]{:T(128)S(6)} %select_n.98), kind=kLoop, calls=%fused_computation.28 | loop fusion | flops 1863680 | bytes 3194884 | tf_op jit(solution)/shard_map/convert_element_type | solution.py:283
  136.4 2.0 %convert_element_type.104 = bf16[32,4,2080]{2,1,0:T(4,128)(2,1)} reshape(bf16[2,64,2080]{2,1,0:T(8,128)(2,1)} %fusion.17) | data formatting | bytes 1064960 | tf_op jit(solution)/shard_map/convert_element_type | solution.py:283
  138.4 8.5 %all-to-all-start.1 = ((bf16[32,4,2080]{2,1,0:T(4,128)(2,1)}), bf16[32,4,2080]{2,1,0:T(4,128)(2,1)}, u32[]{:S(2)}, u32[]{:S(2)}) async-start(bf16[32,4,2080]{2,1,0:T(4,128)(2,1)} %convert_element_type.104), calls=%async_computation.1 | async-start | bytes 1114112 | tf_op jit(solution)/shard_map/all_to_all | solution.py:283
  146.9 1.2 collective-permute-start.2
  148.1 1.4 collective-permute-start.3
  149.5 14.7 %collective-permute-done.2 = bf16[64,1024]{1,0:T(8,128)(2,1)S(1)} collective-permute-done((bf16[64,1024]{1,0:T(8,128)(2,1)S(1)}, bf16[64,1024]{1,0:T(8,128)(2,1)S(1)}, u32[]{:S(2)}, u32[]{:S(2)}) %collective-permute-start.2) | collective-permute-done | bytes 131104 | tf_op jit(solution)/shard_map/ppermute | solution.py:23
  164.2 3.0 %fusion.14 = bf16[1,64,1024]{2,1,0:T(8,128)(2,1)} fusion(bf16[1024,1024]{1,0:T(8,128)(2,1)} %param.12, bf16[64,1024]{1,0:T(8,128)(2,1)S(1)} %collective-permute-done.3, bf16[64,1024]{1,0:T(8,128)(2,1)S(1)} %collective-permute-done.2, bf16[704,1024]{1,0:T(8,128)(2,1)S(1)} %shard_map.130), kind=kOutput, calls=%fused_computation.20 | convolution fusion | flops 134676480 | bytes 2621440 | tf_op jit(solution)/shard_map/dot_general | solution.py:255
  167.2 1.3 convert_reduce_fusion
  (79 shorter events, 18.2 us)
Async XLA Ops:
  0.6 6.2 %copy-start = (bf16[1024,1024]{1,0:T(8,128)(2,1)S(1)}, bf16[1024,1024]{1,0:T(8,128)(2,1)}, u32[]{:S(2)}) copy-start(bf16[1024,1024]{1,0:T(8,128)(2,1)} %param.13) | copy-start | bytes 6291460
  0.6 9.0 %collective-permute-start = (bf16[64,1024]{1,0:T(8,128)(2,1)}, bf16[64,1024]{1,0:T(8,128)(2,1)S(1)}, u32[]{:S(2)}, u32[]{:S(2)}) collective-permute-start(bf16[64,1024]{1,0:T(8,128)(2,1)} %bitcast.66), channel_id=1, source_target_pairs={{0,1},{1,2},{2,3},{3,4},{4,5},{5,6},{6,7},{7,8},{8,9},{9,10},{10,1... | collective-permute-start | bytes 393224 | tf_op jit(solution)/shard_map/ppermute | solution.py:23
  3.8 6.0 %collective-permute-start.1 = (bf16[64,1024]{1,0:T(8,128)(2,1)}, bf16[64,1024]{1,0:T(8,128)(2,1)S(1)}, u32[]{:S(2)}, u32[]{:S(2)}) collective-permute-start(bf16[64,1024]{1,0:T(8,128)(2,1)} %bitcast.67), channel_id=1, source_target_pairs={{0,31},{1,0},{2,1},{3,2},{4,3},{5,4},{6,5},{7,6},{8,7},{9,8},{10,9... | collective-permute-start | bytes 393224 | tf_op jit(solution)/shard_map/ppermute | solution.py:23
  6.8 3.5 %copy-start.1 = (f32[512,1]{1,0:T(8,128)}, f32[512,1]{1,0:T(8,128)S(1)}, u32[]{:S(2)}) copy-start(f32[512,1]{1,0:T(8,128)S(1)} %copy.35.scale_ref) | copy-start | bytes 6148
  6.9 2.9 %copy-start.13 = (bf16[1024,1024]{1,0:T(8,128)(2,1)S(1)}, bf16[1024,1024]{1,0:T(8,128)(2,1)}, u32[]{:S(2)}) copy-start(bf16[1024,1024]{1,0:T(8,128)(2,1)} %param.12) | copy-start | bytes 6291460
  6.9 2.9 %copy-start.20 = (bf16[1,64,1024]{2,1,0:T(8,128)(2,1)S(1)}, bf16[1,64,1024]{2,1,0:T(8,128)(2,1)}, u32[]{:S(2)}) copy-start(bf16[1,64,1024]{2,1,0:T(8,128)(2,1)} %param.10) | copy-start | bytes 393220
  10.4 31.3 %copy-start.6 = (bf16[1024,32]{0,1:T(8,128)(2,1)S(1)}, bf16[1024,32]{0,1:T(8,128)(2,1)}, u32[]{:S(2)}) copy-start(bf16[1024,32]{0,1:T(8,128)(2,1)} %param.14) | copy-start | bytes 196612
  39.7 1.0 copy-start.3
  40.7 1.0 copy-start.5
  40.7 13.2 %copy-start.17 = (f32[512]{0:T(512)S(1)}, f32[512]{0:T(512)}, u32[]{:S(2)}) copy-start(f32[512]{0:T(512)} %param.16) | copy-start | bytes 6148
  40.7 13.2 %copy-start.19 = (bf16[512,1024]{1,0:T(8,128)(2,1)S(1)}, bf16[512,1024]{1,0:T(8,128)(2,1)}, u32[]{:S(2)}) copy-start(bf16[512,1024]{1,0:T(8,128)(2,1)} %param.11) | copy-start | bytes 3145732
  43.6 25.8 %all-to-all-start = ((f32[8,32,512]{2,1,0:T(8,128)}), f32[8,32,512]{2,1,0:T(8,128)}, u32[]{:S(2)}, u32[]{:S(2)}) async-start(f32[8,32,512]{2,1,0:T(8,128)} %sub.45), calls=%async_computation | async-start | bytes 1048576 | tf_op jit(solution)/shard_map/all_to_all | solution.py:236
  61.6 2.6 %copy-start.10 = (bf16[704,2,512]{2,1,0:T(2,128)(2,1)}, bf16[704,2,512]{2,1,0:T(2,128)(2,1)S(1)}, u32[]{:S(2)}) copy-start(bf16[704,2,512]{2,1,0:T(2,128)(2,1)S(1)} %reshape.98) | copy-start | bytes 4325380
  63.1 7.5 %copy-start.18 = (f32[32]{0:T(128)S(1)}, f32[32]{0:T(128)}, u32[]{:S(2)}) copy-start(f32[32]{0:T(128)} %param.17) | copy-start | bytes 388
  64.1 34.1 %collective-permute-start.4 = (bf16[704,512]{1,0:T(8,128)(2,1)}, bf16[704,512]{1,0:T(8,128)(2,1)}, u32[]{:S(2)}, u32[]{:S(2)}) collective-permute-start(bf16[704,512]{1,0:T(8,128)(2,1)} %bitcast.57), channel_id=1, source_target_pairs={{0,1},{1,0},{2,3},{3,2},{4,5},{5,4},{6,7},{7,6},{8,9},{9,8},{10,11... | collective-permute-start | bytes 2162696 | tf_op jit(solution)/shard_map/ppermute | solution.py:231
  71.6 14.5 %copy-start.9 = (bf16[32,512]{1,0:T(8,128)(2,1)}, bf16[32,512]{1,0:T(8,128)(2,1)S(1)}, u32[]{:S(2)}) copy-start(bf16[32,512]{1,0:T(8,128)(2,1)S(1)} %multiply_convert_fusion.dpred_ref) | copy-start | bytes 98308
  71.6 1.0 copy-start.2
  72.5 1.2 copy-start.4
  73.8 0.8 copy-start.7
  74.6 0.8 copy-start.8
  75.4 12.2 %copy-start.11 = (bf16[704,2,512]{2,1,0:T(2,128)(2,1)S(1)}, bf16[704,2,512]{2,1,0:T(2,128)(2,1)}, u32[]{:S(2)}) copy-start(bf16[704,2,512]{2,1,0:T(2,128)(2,1)} %copy-done.10) | copy-start | bytes 4325380
  86.0 12.2 %collective-permute-start.5 = (bf16[704,1024]{1,0:T(8,128)(2,1)S(1)}, bf16[704,1024]{1,0:T(8,128)(2,1)}, u32[]{:S(2)}, u32[]{:S(2)}) collective-permute-start(bf16[704,1024]{1,0:T(8,128)(2,1)S(1)} %shard_map.130), channel_id=1, source_target_pairs={{0,1},{1,0},{2,3},{3,2},{4,5},{5,4},{6,7},{7,6},{8,9},{9,8},{10,11... | collective-permute-start | bytes 4325384 | tf_op jit(solution)/shard_map/ppermute | solution.py:246
  93.8 3.3 %copy-start.15 = (bf16[192,1,512]{2,1,0:T(2,128)(2,1)S(1)}, bf16[192,1,512]{2,1,0:T(2,128)(2,1)}, u32[]{:S(2)}) copy-start(bf16[192,1,512]{2,1,0:T(2,128)(2,1)} %constant_dynamic-slice_fusion) | copy-start | bytes 589828
  94.8 2.8 %collective-permute-start.6 = (bf16[512,32]{1,0:T(8,128)(2,1)S(1)}, bf16[512,32]{1,0:T(8,128)(2,1)S(1)}, u32[]{:S(2)}, u32[]{:S(2)}) collective-permute-start(bf16[512,32]{1,0:T(8,128)(2,1)S(1)} %fusion.36), channel_id=1, source_target_pairs={{0,1},{1,0},{2,3},{3,2},{4,5},{5,4},{6,7},{7,6},{8,9},{9,8},{10,11... | collective-permute-start | bytes 98312 | tf_op jit(solution)/shard_map/ppermute | solution.py:262
  97.1 1.0 copy-start.16
  102.3 2.1 %copy-start.12 = (f32[512,2080]{1,0:T(8,128)}, f32[512,2080]{1,0:T(8,128)S(1)}, u32[]{:S(2)}) copy-start(f32[512,2080]{1,0:T(8,128)S(1)} %pad_maximum_fusion) | copy-start | bytes 12779524
  105.6 15.2 %collective-permute-start.7 = (bf16[2,64,2080]{2,1,0:T(8,128)(2,1)}, bf16[2,64,2080]{2,1,0:T(8,128)(2,1)}, u32[]{:S(2)}, u32[]{:S(2)}) collective-permute-start(bf16[2,64,2080]{2,1,0:T(8,128)(2,1)} %get-tuple-element.10), channel_id=1, source_target_pairs={{0,32},{32,64},{64,96},{96,0},{1,33},{33,65},{65,97},{97,1},{2,34}... | collective-permute-start | bytes 1597448 | tf_op jit(solution)/shard_map/ppermute | solution.py:23
  106.7 14.2 %collective-permute-start.8 = (bf16[2,64,2080]{2,1,0:T(8,128)(2,1)}, bf16[2,64,2080]{2,1,0:T(8,128)(2,1)}, u32[]{:S(2)}, u32[]{:S(2)}) collective-permute-start(bf16[2,64,2080]{2,1,0:T(8,128)(2,1)} %get-tuple-element.12), channel_id=1, source_target_pairs={{0,96},{32,0},{64,32},{96,64},{1,97},{33,1},{65,33},{97,65},{2,98}... | collective-permute-start | bytes 1597448 | tf_op jit(solution)/shard_map/ppermute | solution.py:23
  108.3 25.3 %collective-permute-start.9 = (bf16[2,64,2080]{2,1,0:T(8,128)(2,1)}, bf16[2,64,2080]{2,1,0:T(8,128)(2,1)}, u32[]{:S(2)}, u32[]{:S(2)}) collective-permute-start(bf16[2,64,2080]{2,1,0:T(8,128)(2,1)} %get-tuple-element.11), channel_id=1, source_target_pairs={{0,64},{32,96},{64,0},{96,32},{1,65},{33,97},{65,1},{97,33},{2,66}... | collective-permute-start | bytes 1597448 | tf_op jit(solution)/shard_map/ppermute | solution.py:23
  138.4 28.9 %all-to-all-start.1 = ((bf16[32,4,2080]{2,1,0:T(4,128)(2,1)}), bf16[32,4,2080]{2,1,0:T(4,128)(2,1)}, u32[]{:S(2)}, u32[]{:S(2)}) async-start(bf16[32,4,2080]{2,1,0:T(4,128)(2,1)} %convert_element_type.104), calls=%async_computation.1 | async-start | bytes 1114112 | tf_op jit(solution)/shard_map/all_to_all | solution.py:283
  146.9 17.3 %collective-permute-start.2 = (bf16[64,1024]{1,0:T(8,128)(2,1)S(1)}, bf16[64,1024]{1,0:T(8,128)(2,1)S(1)}, u32[]{:S(2)}, u32[]{:S(2)}) collective-permute-start(bf16[64,1024]{1,0:T(8,128)(2,1)S(1)} %get-tuple-element.13), channel_id=1, source_target_pairs={{0,31},{1,0},{2,1},{3,2},{4,3},{5,4},{6,5},{7,6},{8,7},{9,8},{10,9... | collective-permute-start | bytes 393224 | tf_op jit(solution)/shard_map/ppermute | solution.py:23
  148.1 16.1 %collective-permute-start.3 = (bf16[64,1024]{1,0:T(8,128)(2,1)S(1)}, bf16[64,1024]{1,0:T(8,128)(2,1)S(1)}, u32[]{:S(2)}, u32[]{:S(2)}) collective-permute-start(bf16[64,1024]{1,0:T(8,128)(2,1)S(1)} %get-tuple-element.14), channel_id=1, source_target_pairs={{0,1},{1,2},{2,3},{3,4},{4,5},{5,6},{6,7},{7,8},{8,9},{9,10},{10,1... | collective-permute-start | bytes 393224 | tf_op jit(solution)/shard_map/ppermute | solution.py:23
  (3 other events, 2.0 us)

commit v2 on v1

v2 whole, which is shorter than its diff:
```python
import functools
import jax
import jax.numpy as jnp
from jax import lax
from jax.experimental import pallas as pl
from jax.experimental.pallas import tpu as pltpu
from jax.sharding import Mesh, PartitionSpec as P

loss_scale = 8.0
smooth_sq = 0.01
TILE = 64
NCOL = 256
ROWS = 32
GROUP = 4
VMEM_LIMIT = 56 * 1024 * 1024
f32 = jnp.float32
bf16 = jnp.bfloat16
SPACE = ("y", "zl", "c")
ENS = ("zh", "x")
LATE = ("zh", "y", "zl", "c")


def shifted(block, axes, distance):
    count = lax.axis_size(axes)
    return lax.ppermute(block, axes, [(i, (i + distance) % count) for i in range(count)])


def smooth_grad(diff):
    return diff / jnp.sqrt(diff * diff + smooth_sq)


def gelu_parts(v):
    c0 = 0.7978845608
    c1 = c0 * 0.044715
    sq = v * v
    t = jnp.tanh(v * (c0 + c1 * sq))
    u = 1.0 + t
    slope = v * (c0 + (3.0 * c1) * sq)
    return v * u, u * (1.0 + (1.0 - t) * slope)


def forward_kernel(
    slots, wide_ref, dst_ref, idx_ref, scale_ref, wout_ref, gp_ref, agg_ref, sum_ref, pred_ref, rhs, hot, pre
):
    step = pl.program_id(0)
    nodes = wide_ref.shape[0]
    tile, width = dst_ref.shape
    depth = rhs.shape[0]

    @pl.when(step == 0)
    def _():
        rhs[:nodes, :] = wide_ref[...]

    rhs[nodes:, :] = dst_ref[...]
    lane = lax.broadcasted_iota(jnp.int32, (tile, depth), 1)
    row = lax.broadcasted_iota(jnp.int32, (tile, depth), 0)
    eye = lane == row + nodes
    for k in range(slots):
        col = idx_ref[:, k : k + 1]
        hit = (lane == col) | (eye & (col >= 0))
        hot[k * tile : (k + 1) * tile, :] = jnp.where(hit, 1.0, 0.0).astype(bf16)
    for n in range(width // NCOL):
        cols = slice(n * NCOL, (n + 1) * NCOL)
        pre[n % 2] = jnp.dot(hot[...], rhs[:, cols], preferred_element_type=f32).astype(bf16)
        for r in range(0, tile, ROWS):
            acc_g = jnp.zeros((ROWS, NCOL), f32)
            acc_s = jnp.zeros((ROWS, NCOL), f32)
            for k in range(slots):
                rows = slice(k * tile + r, k * tile + r + ROWS)
                value, grad = gelu_parts(pre[n % 2, rows, :])
                gp_ref[rows, cols] = grad
                if k % GROUP == 0:
                    some_g, some_s = value, grad
                else:
                    some_g, some_s = some_g + value, some_s + grad
                if k % GROUP == GROUP - 1:
                    acc_g = acc_g + some_g.astype(f32)
                    acc_s = acc_s + some_s.astype(f32)
            scale = scale_ref[r : r + ROWS, :]
            here = pl.ds(pl.multiple_of(step * tile + r, ROWS), ROWS)
            agg_ref[here, cols] = (acc_g * scale).astype(bf16)
            sum_ref[r : r + ROWS, cols] = (acc_s - (slots - 0.5 / scale)).astype(bf16)

    @pl.when(step == pl.num_programs(0) - 1)
    def _():
        pred_ref[...] = lax.dot_general(
            wout_ref[...], agg_ref[...], (((1,), (1,)), ((), ())), preferred_element_type=f32
        )


def forward(wide, dst, idx, scale, wout_t):
    grid_rows, width = dst.shape
    nodes = wide.shape[0]
    slots = idx.shape[1]
    outs = wout_t.shape[0]
    whole = lambda t: (0, 0)
    step = lambda t: (t, 0)
    return pl.pallas_call(
        functools.partial(forward_kernel, slots),
        grid=(grid_rows // TILE,),
        in_specs=[
            pl.BlockSpec((nodes, width), whole),
            pl.BlockSpec((TILE, width), step),
            pl.BlockSpec((TILE, slots), step),
            pl.BlockSpec((TILE, 1), step),
            pl.BlockSpec((outs, width), whole),
        ],
        out_specs=[
            pl.BlockSpec((TILE * slots, width), step),
            pl.BlockSpec((grid_rows, width), whole),
            pl.BlockSpec((TILE, width), step),
            pl.BlockSpec((outs, grid_rows), whole),
        ],
        out_shape=[
            jax.ShapeDtypeStruct((grid_rows * slots, width), bf16),
            jax.ShapeDtypeStruct((grid_rows, width), bf16),
            jax.ShapeDtypeStruct((grid_rows, width), bf16),
            jax.ShapeDtypeStruct((outs, grid_rows), f32),
        ],
        scratch_shapes=[
            pltpu.VMEM((nodes + TILE, width), bf16),
            pltpu.VMEM((TILE * slots, nodes + TILE), bf16),
            pltpu.VMEM((2, TILE * slots, NCOL), bf16),
        ],
        compiler_params=pltpu.CompilerParams(vmem_limit_bytes=VMEM_LIMIT),
        cost_estimate=pl.CostEstimate(
            flops=2 * grid_rows * slots * 256 * width,
            bytes_accessed=2 * grid_rows * slots * width,
            transcendentals=grid_rows * slots * width,
        ),
        name="forward",
    )(wide, dst, idx, scale, wout_t)


def middle_kernel(
    core_ref,
    every_ref,
    pred_ref,
    truth_ref,
    area_ref,
    var_ref,
    wout_ref,
    scale_ref,
    sum_ref,
    agg_ref,
    grid_ref,
    lead_ref,
    own_ref,
    far_ref,
    dpred,
    ddst,
    part,
):
    width = sum_ref.shape[1]
    half = width // 2
    members = every_ref.shape[0]
    outs = pred_ref.shape[0]
    core = core_ref[0]

    @pl.when(pl.program_id(0) == 0)
    def _():
        pred = pred_ref[...]
        pair = jnp.zeros_like(pred)
        for e in range(members):
            pair = pair + smooth_grad(pred - every_ref[e])
        weighting = loss_scale * area_ref[...] * var_ref[...]
        dpred[...] = (
            weighting
            * (smooth_grad(pred - truth_ref[...]) / members - pair / (members * (members - 1)))
        ).astype(bf16)
        for n in range(width // NCOL):
            cols = slice(n * NCOL, (n + 1) * NCOL)
            dagg = lax.dot_general(
                dpred[...], wout_ref[:, cols], (((0,), (0,)), ((), ())), preferred_element_type=f32
            )
            dagg = dagg * scale_ref[...]
            lead_ref[:, cols] = dagg.astype(bf16)
            ddst[:, cols] = (dagg * sum_ref[:, cols].astype(f32)).astype(bf16)

    first = (((0,), (0,)), ((), ()))
    mine = pl.ds(pl.multiple_of(core * half, half), half)
    other = pl.ds(pl.multiple_of((1 - core) * half, half), half)
    part[...] = jnp.dot(dpred[...], agg_ref[...], preferred_element_type=f32)
    few = outs // 2
    rows = far_ref.shape[1] - few
    for chunk in range(far_ref.shape[0]):
        here = slice(chunk * rows, (chunk + 1) * rows)
        for ref, columns, which in ((far_ref, other, 1 - core), (own_ref, mine, core)):
            ref[chunk, :rows, :] = lax.dot_general(
                grid_ref[:, here], ddst[:, columns], first, preferred_element_type=f32
            ).astype(ref.dtype)
            ref[chunk, rows:, :] = jnp.zeros((few, half), ref.dtype)
            ref[chunk, rows:, :rows] = part[
                pl.ds(pl.multiple_of(which * few, few), few), here
            ].astype(ref.dtype)


def middle(core, everyone, pred, truth_t, area, var, wout_t, scale, sums, agg, grid_embed, chunks):
    grid_rows, width = sums.shape
    outs = pred.shape[0]
    block = (chunks, width // chunks + outs // 2, width // 2)
    per_step = NCOL * chunks // width
    whole = lambda t, c: (0, 0)
    return pl.pallas_call(
        middle_kernel,
        grid_spec=pltpu.PrefetchScalarGridSpec(
            num_scalar_prefetch=1,
            grid=(width // NCOL,),
            in_specs=[
                pl.BlockSpec(everyone.shape, lambda t, c: (0, 0, 0)),
                pl.BlockSpec(pred.shape, whole),
                pl.BlockSpec(truth_t.shape, whole),
                pl.BlockSpec(area.shape, whole),
                pl.BlockSpec(var.shape, whole),
                pl.BlockSpec(wout_t.shape, whole),
                pl.BlockSpec(scale.shape, whole),
                pl.BlockSpec(sums.shape, whole),
                pl.BlockSpec((grid_rows, NCOL), lambda t, c: (0, t)),
                pl.BlockSpec((grid_rows, NCOL), lambda t, c: (0, t)),
            ],
            out_specs=[
                pl.BlockSpec((grid_rows, width), whole),
                pl.BlockSpec((per_step,) + block[1:], lambda t, c: (t, 0, 0)),
                pl.BlockSpec((per_step,) + block[1:], lambda t, c: (t, 0, 0)),
            ],
            scratch_shapes=[
                pltpu.VMEM((outs, grid_rows), bf16),
                pltpu.VMEM((grid_rows, width), bf16),
                pltpu.VMEM((outs, NCOL), f32),
            ],
        ),
        out_shape=[
            jax.ShapeDtypeStruct((grid_rows, width), bf16),
            jax.ShapeDtypeStruct(block, f32),
            jax.ShapeDtypeStruct(block, bf16),
        ],
        compiler_params=pltpu.CompilerParams(vmem_limit_bytes=VMEM_LIMIT),
        cost_estimate=pl.CostEstimate(
            flops=2 * grid_rows * width * width, bytes_accessed=10 * grid_rows * width, transcendentals=0
        ),
        name="middle",
    )(core, everyone, pred, truth_t, area, var, wout_t, scale, sums, agg, grid_embed)


def backward_kernel(slots, col_ref, gp_ref, lead_ref, idx_ref, feats_ref, wide_ref, part_ref, prod, acc):
    step = pl.program_id(0)
    nodes, half = acc.shape
    tile = lead_ref.shape[0]

    @pl.when(step == 0)
    def _():
        acc[...] = jnp.zeros_like(acc)

    node = lax.broadcasted_iota(jnp.int32, (nodes, tile * slots), 0)
    hot = jnp.where(node == idx_ref[0], 1.0, 0.0).astype(bf16)
    for k in range(slots):
        rows = slice(k * tile, (k + 1) * tile)
        prod[rows, :] = gp_ref[rows, :] * lead_ref[...]
    for n in range(half // NCOL):
        cols = slice(n * NCOL, (n + 1) * NCOL)
        acc[:, cols] += jnp.dot(hot, prod[:, cols], preferred_element_type=f32)

    @pl.when(step == pl.num_programs(0) - 1)
    def _():
        wide_ref[...] = acc[...].astype(bf16)
        for n in range(part_ref.shape[0] // NCOL):
            rows = slice(n * NCOL, (n + 1) * NCOL)
            part_ref[rows, :] = lax.dot_general(
                feats_ref[:, rows], wide_ref[...], (((0,), (0,)), ((), ())), preferred_element_type=f32
            ).astype(part_ref.dtype)


def backward(col, gp, lead, idx_rows, feats, part_type):
    grid_rows, width = lead.shape
    slots = gp.shape[0] // grid_rows
    nodes = feats.shape[0]
    half = width // 2
    whole = lambda t, c: (0, 0)
    return pl.pallas_call(
        functools.partial(backward_kernel, slots),
        grid_spec=pltpu.PrefetchScalarGridSpec(
            num_scalar_prefetch=1,
            grid=(grid_rows // TILE,),
            in_specs=[
                pl.BlockSpec((TILE * slots, half), lambda t, c: (t, c[0])),
                pl.BlockSpec((TILE, half), lambda t, c: (t, c[0])),
                pl.BlockSpec((1, 1, TILE * slots), lambda t, c: (t, 0, 0)),
                pl.BlockSpec(feats.shape, whole),
            ],
            out_specs=[
                pl.BlockSpec((nodes, half), whole),
                pl.BlockSpec((width, half), whole),
            ],
            scratch_shapes=[
                pltpu.VMEM((TILE * slots, half), bf16),
                pltpu.VMEM((nodes, half), f32),
            ],
        ),
        out_shape=[
            jax.ShapeDtypeStruct((nodes, half), bf16),
            jax.ShapeDtypeStruct((width, half), part_type),
        ],
        compiler_params=pltpu.CompilerParams(vmem_limit_bytes=VMEM_LIMIT),
        cost_estimate=pl.CostEstimate(
            flops=grid_rows * slots * 256 * width,
            bytes_accessed=grid_rows * slots * width,
            transcendentals=0,
        ),
        name="backward",
    )(col, gp, lead, idx_rows, feats)


def x_pieces(total):
    count = lax.axis_size("x")
    here = lax.axis_index("x")
    total = total.reshape(lax.axis_size("zh"), count, -1, total.shape[-1])
    quarter = lambda d: lax.dynamic_index_in_dim(total, (here + d) % count, 1, keepdims=False)
    return quarter(0), [quarter(d).astype(bf16) for d in (2, 1, 3)]


def x_moved(pieces):
    return [shifted(piece, "x", d) for piece, d in zip(pieces, (2, 1, 3))]


def summed(kept, moved):
    for piece in moved:
        kept = kept + piece.astype(f32)
    return kept


def body(
    mesh_feats,
    grid_embed,
    w_src,
    w_dst,
    w_out,
    truth,
    area_weight,
    var_weight,
    neighbour,
    edge_mask,
):
    own = mesh_feats[0]
    node_rows, width = own.shape
    grid_rows, slots = neighbour.shape
    half = width // 2
    tiles = grid_rows // TILE
    space_count = lax.axis_size(SPACE)
    block_id = lax.axis_index(SPACE)
    members = lax.axis_size(ENS)
    swap = [(0, 1), (1, 0)]
    core = lax.axis_index("c")
    mine = jnp.full((1,), core, jnp.int32)

    below = shifted(own, SPACE, 1)
    above = shifted(own, SPACE, -1)
    feats = jnp.concatenate([below, own, above], axis=0)

    dst = jnp.dot(grid_embed, w_dst, preferred_element_type=f32).astype(bf16)
    local = jnp.mod(neighbour - (block_id - 1) * node_rows, node_rows * space_count)
    idx = jnp.where(edge_mask > 0, local, -1)
    idx_rows = idx.reshape(tiles, TILE, slots).transpose(0, 2, 1).reshape(tiles, 1, slots * TILE)
    scale = 0.5 / jnp.sum(edge_mask.astype(f32), axis=1, keepdims=True)
    wout_t = w_out.T
    truth_t = truth.T
    dst, idx, idx_rows, scale, wout_t, truth_t, below = lax.optimization_barrier(
        (dst, idx, idx_rows, scale, wout_t, truth_t, below)
    )
    feats = jnp.concatenate([below, own, above], axis=0)
    wide = jnp.dot(feats, w_src, preferred_element_type=f32).astype(bf16)

    gp, agg, sums, pred = forward(wide, dst, idx, scale, wout_t)
    everyone = lax.all_to_all(
        jnp.broadcast_to(pred[None], (members,) + pred.shape), ENS, 0, 0, tiled=True
    )
    lead, dst_own, dst_far = middle(
        mine,
        everyone,
        pred,
        truth_t,
        area_weight[None, :],
        var_weight[:, None],
        wout_t,
        scale,
        sums,
        agg,
        grid_embed,
        members,
    )
    dst_far = lax.ppermute(dst_far, "c", swap)
    wide_far, src_far = backward(1 - mine, gp, lead, idx_rows, feats, bf16)
    src_far = lax.ppermute(src_far, "c", swap)
    dst_kept, dst_pieces = x_pieces(dst_own + dst_far.astype(f32))
    lead, *dst_pieces = lax.optimization_barrier((lead, *dst_pieces))
    dst_moved = x_moved(dst_pieces)
    wide_own, src_own = backward(mine, gp, lead, idx_rows, feats, f32)
    src_own, src_far, *dst_moved = lax.optimization_barrier((src_own, src_far, *dst_moved))
    src_kept, src_pieces = x_pieces(src_own + src_far.astype(f32))
    src_moved = x_moved(src_pieces)

    lower = core == 0
    dwide = jnp.concatenate(
        [jnp.where(lower, wide_own, wide_far), jnp.where(lower, wide_far, wide_own)], axis=1
    )
    from_above = shifted(dwide[:node_rows], SPACE, -1)
    from_below = shifted(dwide[2 * node_rows :], SPACE, 1)

    dst_sum = summed(dst_kept, dst_moved)
    late_rows = width // lax.axis_size("x")
    per_chunk = width // members
    total = jnp.concatenate(
        [
            summed(src_kept, src_moved).reshape(late_rows, half),
            dst_sum[:, :per_chunk].reshape(late_rows, half),
            dst_sum[:, per_chunk:, :per_chunk].transpose(0, 2, 1).reshape(late_rows, -1),
        ],
        axis=1,
    )
    total, from_above, from_below = lax.optimization_barrier(
        (total.astype(bf16), from_above, from_below)
    )
    dproj = (
        dwide[node_rows : 2 * node_rows].astype(f32)
        + from_above.astype(f32)
        + from_below.astype(f32)
    ).astype(bf16)
    grad_mesh = lax.dot_general(
        dproj, w_src, (((1,), (1,)), ((), ())), preferred_element_type=f32
    ).astype(bf16)
    columns = total.shape[1]
    pieces = lax.all_to_all(total, LATE, 0, 0, tiled=True)
    pieces = pieces.reshape(-1, 2, pieces.shape[0] // lax.axis_size(LATE), columns)
    total = jnp.sum(pieces.astype(f32), axis=0)
    joined = lambda a, b: jnp.concatenate([total[0, :, a:b], total[1, :, a:b]], axis=1)
    return (
        grad_mesh[None],
        joined(0, half),
        joined(half, 2 * half),
        joined(2 * half, columns),
    )


def solution(mesh):
    fine = Mesh(mesh.devices.reshape(2, 4, 4, 4, 2), ("zh", "x", "y", "zl", "c"))
    everywhere = ENS + SPACE
    in_specs = (
        P(ENS, SPACE, None),
        P(SPACE, None),
        P(),
        P(),
        P(),
        P(SPACE, None),
        P(SPACE),
        P(),
        P(SPACE, None),
        P(SPACE, None),
    )
    out_specs = (
        P(ENS, SPACE, None),
        P(everywhere, None),
        P(everywhere, None),
        P(everywhere, None),
    )
    return jax.shard_map(body, mesh=fine, in_specs=in_specs, out_specs=out_specs, check_vma=False)
```

time: 171 us -> 152 us (0.89)
  local copies, waits for them, and re-layouts: 27 us -> 10.4 us
  matrix products: 19.6 us -> 9.58 us
  starting transfers between devices: 35.1 us -> 38.8 us
  other arithmetic: 8.28 us -> 11.6 us
  Pallas kernels: 39.9 us -> 42.2 us
    ppermute x7 -> x10, waiting for transfers between devices: 38.7 us -> 9.4 us  [shifted(): lax.ppermute(block, axes, [(i, (i + distance) % count) for i in range(cou...]
    all_to_all x1, waiting for transfers between devices: 0.01 us -> 16.9 us  [body(): pieces = lax.all_to_all(total, LATE, 0, 0, tiled=True)]
    dot_general x7 -> x0, matrix products: 13.4 us -> none  [the longest x4 6.13 us: contract_first(): lax.dot_general(left, right, (((0,), (0,)), ((), ())), preferred_element_...]
    all_to_all x1, waiting for transfers between devices: 0.01 us -> 11.2 us  [body(): lax.all_to_all(jnp.broadcast_to(pred[None], (members,) + pred.shape), ENS...]
    unnamed x48 -> x24, local copies, waits for them, and re-layouts: 11 us -> 3.37 us
    slice x5 -> x2, local copies, waits for them, and re-layouts: 4.43 us -> 0.21 us  [body(): dst_sum[:, :per_chunk].reshape(late_rows, half)]
    concatenate x1 -> x6, other arithmetic: 0.34 us -> 4.33 us  [the longest x3 1.87 us: body(): jnp.concatenate([total[0, :, a:b], total[1, :, a:b]], axis=1)]
    convert_element_type x2 -> x0, other arithmetic: 3.76 us -> none  [the longest x1 2.81 us: body(): total_x.reshape(-1, columns).astype(bf16)]
  transfers between devices with their start and end apart: 12 -> 14, of which waited for: 4 -> 5; matrix products, arithmetic and copies ran while one was open for 19% -> 14% of each run, Pallas kernels for 6% -> 12%
where the time goes in v2:
time: 152 us; the launch traced here: 151 us
  Pallas kernels  42.2 us (28%)
  starting transfers between devices  38.8 us (26%)
  waiting for transfers between devices  37.5 us (25%)
  other arithmetic  11.6 us (8%)
  local copies, waits for them, and re-layouts  10.4 us (7%)
  matrix products  9.58 us (6%)
    pallas_call x2, Pallas kernels, backward(): pl.pallas_call(functools.partial(backward_kernel, slots), grid_spec=pltpu...  18.4 us
    pallas_call x1, Pallas kernels, forward(): pl.pallas_call(functools.partial(forward_kernel, slots), grid=(grid_rows...  17.2 us
    all_to_all x1, waiting for transfers between devices, body(): pieces = lax.all_to_all(total, LATE, 0, 0, tiled=True)  16.9 us
    ppermute x10, starting transfers between devices, shifted(): lax.ppermute(block, axes, [(i, (i + distance) % count) for i in range(cou...  13.2 us
    all_to_all x1, waiting for transfers between devices, body(): lax.all_to_all(jnp.broadcast_to(pred[None], (members,) + pred.shape), ENS...  11.2 us
    all_to_all x1, starting transfers between devices, body(): lax.all_to_all(jnp.broadcast_to(pred[None], (members,) + pred.shape), ENS...  9.98 us
    all_to_all x1, starting transfers between devices, body(): pieces = lax.all_to_all(total, LATE, 0, 0, tiled=True)  9.75 us
    ppermute x10, waiting for transfers between devices, shifted(): lax.ppermute(block, axes, [(i, (i + distance) % count) for i in range(cou...  9.4 us
  transfers between devices with their start and end apart: 14, of which 5 were waited for; matrix products, arithmetic and copies ran while one was open for 14% of the time, Pallas kernels for 12%

profile of v2, /device:TPU:1, one launch (start us, length us, event | category | flops | bytes accessed | tf_op | source)
XLA Modules:
  0.0 150.9 jit_solution(9212748415357570821)
XLA Ops:
  0.6 3.3 %collective-permute-start.1 = (bf16[64,1024]{1,0:T(8,128)(2,1)}, bf16[64,1024]{1,0:T(8,128)(2,1)S(1)}, u32[]{:S(2)}, u32[]{:S(2)}) collective-permute-start(bf16[64,1024]{1,0:T(8,128)(2,1)} %bitcast.84), channel_id=1, source_target_pairs={{0,31},{1,0},{2,1},{3,2},{4,3},{5,4},{6,5},{7,6},{8,7},{9,8},{10,9... | collective-permute-start | bytes 393224 | tf_op jit(solution)/shard_map/ppermute | solution.py:25
  4.0 0.8 broadcast_compare_fusion
  4.7 0.8 convert_reduce_fusion.1
  5.7 0.9 copy.24
  7.6 3.5 %convolution_convert_fusion.dst_ref = bf16[512,1024]{1,0:T(8,128)(2,1)} fusion(bf16[512,1024]{1,0:T(8,128)(2,1)} %grid_ref.1, bf16[1024,1024]{1,0:T(8,128)(2,1)S(1)} %copy-done), kind=kOutput, calls=%fused_computation.2 | convolution fusion | flops 1074266112 | bytes 4194304 | tf_op jit(solution)/shard_map/dot_general | solution.py:359
  11.1 0.8 copy.27.scale_ref
  11.9 2.9 %convolution_convert_fusion.1.wide_ref = bf16[192,1024]{1,0:T(8,128)(2,1)} fusion(bf16[1024,1024]{1,0:T(8,128)(2,1)} %param.12, bf16[64,1024]{1,0:T(8,128)(2,1)S(1)} %collective-permute-done.1, bf16[64,1024]{1,0:T(8,128)(2,1)S(1)} %bitcast.86, bf16[64,1024]{1,0:T(8,128)(2,1)S(1)} %collective-permute-done), kind=kOutput, calls=%fused_computation.3 | convolution fusion | flops 404029440 | bytes 2883584 | tf_op jit(solution)/shard_map/dot_general | solution.py:370
  14.9 17.2 %forward.1 = (bf16[8192,1024]{1,0:T(8,128)(2,1)}, bf16[512,1024]{1,0:T(8,128)(2,1)}, bf16[512,1024]{1,0:T(8,128)(2,1)}, f32[32,512]{1,0:T(8,128)}) custom-call(bf16[192,1024]{1,0:T(8,128)(2,1)} %convolution_convert_fusion.1.wide_ref, bf16[512,1024]{1,0:T(8,128)(2,1)} %convolution_convert_fusion.dst_ref, s32[512,16]{1,0:T(8,128)} %copy-done.5, ...), custom_call_target="tpu_custom_call" | custom-call | flops 4294967296 | bytes 16777216 | tf_op jit(solution)/shard_map/forward/pallas_call | solution.py:98
  32.1 1.7 %broadcast_in_dim.25 = f32[8,32,512]{2,1,0:T(8,128)} broadcast(f32[32,512]{1,0:T(8,128)} %get-tuple-element.40.pred_ref), dimensions={1,2} | broadcast | bytes 589824 | tf_op jit(solution)/shard_map/broadcast_in_dim | solution.py:374
  33.8 10.0 %all-to-all-start = ((f32[8,32,512]{2,1,0:T(8,128)}), f32[8,32,512]{2,1,0:T(8,128)S(1)}, u32[]{:S(2)}, u32[]{:S(2)}) async-start(f32[8,32,512]{2,1,0:T(8,128)} %broadcast_in_dim.25), calls=%async_computation | async-start | bytes 1048576 | tf_op jit(solution)/shard_map/all_to_all | solution.py:373
  44.5 11.2 %all-to-all-done.every_ref = f32[8,32,512]{2,1,0:T(8,128)S(1)} async-done(((f32[8,32,512]{2,1,0:T(8,128)}), f32[8,32,512]{2,1,0:T(8,128)S(1)}, u32[]{:S(2)}, u32[]{:S(2)}) %all-to-all-start) | async-done | bytes 524320 | tf_op jit(solution)/shard_map/all_to_all | solution.py:373
  55.6 0.8 copy-done.4
  56.4 6.6 %middle.1 = (bf16[512,1024]{1,0:T(8,128)(2,1)}, f32[8,144,512]{2,1,0:T(8,128)}, bf16[8,144,512]{2,1,0:T(8,128)(2,1)}) custom-call(s32[1]{0:T(128)} %bitcast.core_ref.col_ref, f32[8,32,512]{2,1,0:T(8,128)} %copy-done.4, f32[32,512]{1,0:T(8,128)} %get-tuple-element.40.pred_ref, f32[32,512]{1,0:T(8,128)} %bitcast.90, f32[1,512]{1,0:T(1,128)} %bitcast.92, ...), custom_call_target="tpu_custom_call" | custom-call | flops 1073741824 | bytes 5242880 | tf_op jit(solution)/shard_map/middle/pallas_call | solution.py:204
  63.0 5.8 %collective-permute-start.2 = (bf16[8,144,512]{2,1,0:T(8,128)(2,1)}, bf16[8,144,512]{2,1,0:T(8,128)(2,1)S(1)}, u32[]{:S(2)}, u32[]{:S(2)}) collective-permute-start(bf16[8,144,512]{2,1,0:T(8,128)(2,1)} %get-tuple-element.46), channel_id=1, source_target_pairs={{0,1},{1,0},{2,3},{3,2},{4,5},{5,4},{6,7},{7,6},{8,9},{9,8},{10,11... | collective-permute-start | bytes 3538952 | tf_op jit(solution)/shard_map/ppermute | solution.py:390
  68.8 1.7 %pad_maximum_fusion.1.feats_ref = bf16[192,1024]{1,0:T(8,128)(2,1)} fusion(bf16[64,1024]{1,0:T(8,128)(2,1)S(1)} %collective-permute-done.1, bf16[64,1024]{1,0:T(8,128)(2,1)S(1)} %bitcast.87, bf16[64,1024]{1,0:T(8,128)(2,1)} %copy-done.9), kind=kLoop, calls=%fused_computation.26 | loop fusion | flops 1179648 | bytes 786432 | tf_op jit(solution)/shard_map/concatenate | solution.py:369
  70.5 9.1 %backward.3 = (bf16[192,512]{1,0:T(8,128)(2,1)}, bf16[1024,512]{1,0:T(8,128)(2,1)}) custom-call(s32[1]{0:T(128)S(6)} %sub.15.col_ref, bf16[8192,1024]{1,0:T(8,128)(2,1)} %get-tuple-element.39.gp_ref, bf16[512,1024]{1,0:T(8,128)(2,1)} %get-tuple-element.47.lead_ref, s32[8,1,1024]{2,1,0:T(1,128)} %reshape.56.idx_ref, bf16[192,1024]{1,0:T(8,128)(2,1)} %pad_maximum_fusion.1.feats_ref), custom_call_target="tpu_custom_call" | custom-call | flops 2147483648 | bytes 8388608 | tf_op jit(solution)/shard_map/backward/pallas_call | solution.py:279
  81.7 2.4 %collective-permute-start.6 = (bf16[2,144,512]{2,0,1:T(2,128)(2,1)S(1)}, bf16[2,144,512]{2,0,1:T(2,128)(2,1)S(1)}, u32[]{:S(2)}, u32[]{:S(2)}) collective-permute-start(bf16[2,144,512]{2,0,1:T(2,128)(2,1)S(1)} %get-tuple-element.55), channel_id=1, source_target_pairs={{0,96},{32,0},{64,32},{96,64},{1,97},{33,1},{65,33},{97,65},{2,98}... | collective-permute-start | bytes 884744 | tf_op jit(solution)/shard_map/ppermute | solution.py:25
  84.1 9.3 %backward.2 = (bf16[192,512]{1,0:T(8,128)(2,1)}, f32[1024,512]{1,0:T(8,128)}) custom-call(s32[1]{0:T(128)} %bitcast.core_ref.col_ref, bf16[8192,1024]{1,0:T(8,128)(2,1)} %get-tuple-element.39.gp_ref, bf16[512,1024]{1,0:T(8,128)(2,1)} %get-tuple-element.47.lead_ref, s32[8,1,1024]{2,1,0:T(1,128)} %reshape.56.idx_ref, bf16[192,1024]{1,0:T(8,128)(2,1)} %pad_maximum_fusion.1.feats_ref), custom_call_target="tpu_custom_call" | custom-call | flops 2147483648 | bytes 8388608 | tf_op jit(solution)/shard_map/backward/pallas_call | solution.py:279
  93.4 1.1 broadcast_select_fusion
  95.2 1.3 collective-permute-start.10
  96.6 4.1 %collective-permute-start.11 = (bf16[64,1024]{1,0:T(8,128)(2,1)}, bf16[64,1024]{1,0:T(8,128)(2,1)}, u32[]{:S(2)}, u32[]{:S(2)}) collective-permute-start(bf16[64,1024]{1,0:T(8,128)(2,1)} %get-tuple-element.70), channel_id=1, source_target_pairs={{0,1},{1,2},{2,3},{3,4},{4,5},{5,6},{6,7},{7,8},{8,9},{9,10},{10,1... | collective-permute-start | bytes 393224 | tf_op jit(solution)/shard_map/ppermute | solution.py:25
  100.7 1.5 %convert_add_fusion.1 = f32[1024,512]{1,0:T(8,128)S(1)} fusion(f32[1024,512]{1,0:T(8,128)S(1)} %copy-done.3, bf16[1024,512]{1,0:T(8,128)(2,1)} %collective-permute-done.3), kind=kLoop, calls=%fused_computation.1 | loop fusion | flops 1048576 | bytes 5242880 | tf_op jit(solution)/shard_map/add | solution.py:398
  102.2 1.4 copy-done.1
  103.8 1.5 collective-permute-start.8
  105.2 0.8 fusion.3
  107.0 4.8 %collective-permute-done.9 = bf16[2,128,512]{2,1,0:T(8,128)(2,1)} collective-permute-done((bf16[2,128,512]{2,1,0:T(8,128)(2,1)S(1)}, bf16[2,128,512]{2,1,0:T(8,128)(2,1)}, u32[]{:S(2)}, u32[]{:S(2)}) %collective-permute-start.9) | collective-permute-done | bytes 262176 | tf_op jit(solution)/shard_map/ppermute | solution.py:25
  112.6 3.8 %collective-permute-done.7 = bf16[2,128,512]{2,1,0:T(8,128)(2,1)} collective-permute-done((bf16[2,128,512]{2,1,0:T(8,128)(2,1)S(1)}, bf16[2,128,512]{2,1,0:T(8,128)(2,1)}, u32[]{:S(2)}, u32[]{:S(2)}) %collective-permute-start.7) | collective-permute-done | bytes 262176 | tf_op jit(solution)/shard_map/ppermute | solution.py:25
  116.4 1.4 fusion.6
  117.9 1.0 all_to_all.10
  118.9 9.8 %all-to-all-start.1 = ((bf16[64,4,1040]{2,1,0:T(4,128)(2,1)}), bf16[64,4,1040]{2,1,0:T(4,128)(2,1)S(1)}, u32[]{:S(2)}, u32[]{:S(2)}) async-start(bf16[64,4,1040]{2,1,0:T(4,128)(2,1)} %all_to_all.10), calls=%async_computation.1 | async-start | bytes 1179648 | tf_op jit(solution)/shard_map/all_to_all | solution.py:431
  128.7 3.2 %fusion = bf16[1,64,1024]{2,1,0:T(8,128)(2,1)} fusion(bf16[1024,1024]{1,0:T(8,128)(2,1)} %param.12, bf16[64,1024]{1,0:T(8,128)(2,1)} %collective-permute-done.11, bf16[64,1024]{1,0:T(8,128)(2,1)} %collective-permute-done.10, bf16[192,512]{1,0:T(8,128)(2,1)S(1)} %get-tuple-element.73, bf16[192,512]{1,0:T(8,128)(2,1)S(1)} %get-tuple-element.72), kind=kOutput, calls=%fused_computation.6 | convolution fusion | flops 134873088 | bytes 2883584 | tf_op jit(solution)/shard_map/dot_general | solution.py:427
  131.8 16.9 %all-to-all-done.1 = bf16[64,4,1040]{2,1,0:T(4,128)(2,1)S(1)} async-done(((bf16[64,4,1040]{2,1,0:T(4,128)(2,1)}), bf16[64,4,1040]{2,1,0:T(4,128)(2,1)S(1)}, u32[]{:S(2)}, u32[]{:S(2)}) %all-to-all-start.1) | async-done | bytes 532512 | tf_op jit(solution)/shard_map/all_to_all | solution.py:431
  (60 shorter events, 8.8 us)
Async XLA Ops:
  0.6 6.9 %copy-start = (bf16[1024,1024]{1,0:T(8,128)(2,1)S(1)}, bf16[1024,1024]{1,0:T(8,128)(2,1)}, u32[]{:S(2)}) copy-start(bf16[1024,1024]{1,0:T(8,128)(2,1)} %param.13) | copy-start | bytes 6291460
  0.6 11.3 %collective-permute-start.1 = (bf16[64,1024]{1,0:T(8,128)(2,1)}, bf16[64,1024]{1,0:T(8,128)(2,1)S(1)}, u32[]{:S(2)}, u32[]{:S(2)}) collective-permute-start(bf16[64,1024]{1,0:T(8,128)(2,1)} %bitcast.84), channel_id=1, source_target_pairs={{0,31},{1,0},{2,1},{3,2},{4,3},{5,4},{6,5},{7,6},{8,7},{9,8},{10,9... | collective-permute-start | bytes 393224 | tf_op jit(solution)/shard_map/ppermute | solution.py:25
  4.0 7.1 %collective-permute-start = (bf16[64,1024]{1,0:T(8,128)(2,1)}, bf16[64,1024]{1,0:T(8,128)(2,1)S(1)}, u32[]{:S(2)}, u32[]{:S(2)}) collective-permute-start(bf16[64,1024]{1,0:T(8,128)(2,1)} %bitcast.85), channel_id=1, source_target_pairs={{0,1},{1,2},{2,3},{3,4},{4,5},{5,6},{6,7},{7,8},{8,9},{9,10},{10,1... | collective-permute-start | bytes 393224 | tf_op jit(solution)/shard_map/ppermute | solution.py:25
  6.7 4.3 %copy-start.5 = (s32[512,16]{1,0:T(8,128)}, s32[512,16]{1,0:T(8,128)S(1)}, u32[]{:S(2)}) copy-start(s32[512,16]{1,0:T(8,128)S(1)} %fusion.8.idx_ref) | copy-start | bytes 98308
  7.6 4.4 %copy-start.8 = (bf16[1,64,1024]{2,1,0:T(8,128)(2,1)S(1)}, bf16[1,64,1024]{2,1,0:T(8,128)(2,1)}, u32[]{:S(2)}) copy-start(bf16[1,64,1024]{2,1,0:T(8,128)(2,1)} %param.10) | copy-start | bytes 393220
  11.1 21.0 %copy-start.9 = (bf16[64,1024]{1,0:T(8,128)(2,1)}, bf16[64,1024]{1,0:T(8,128)(2,1)S(1)}, u32[]{:S(2)}) copy-start(bf16[64,1024]{1,0:T(8,128)(2,1)S(1)} %collective-permute-done) | copy-start | bytes 393220
  14.9 28.9 %copy-start.10 = (f32[32]{0:T(128)S(1)}, f32[32]{0:T(128)}, u32[]{:S(2)}) copy-start(f32[32]{0:T(128)} %param.17) | copy-start | bytes 388
  33.8 21.9 %all-to-all-start = ((f32[8,32,512]{2,1,0:T(8,128)}), f32[8,32,512]{2,1,0:T(8,128)S(1)}, u32[]{:S(2)}, u32[]{:S(2)}) async-start(f32[8,32,512]{2,1,0:T(8,128)} %broadcast_in_dim.25), calls=%async_computation | async-start | bytes 1048576 | tf_op jit(solution)/shard_map/all_to_all | solution.py:373
  55.6 0.8 copy-start.4
  63.0 16.6 %collective-permute-start.2 = (bf16[8,144,512]{2,1,0:T(8,128)(2,1)}, bf16[8,144,512]{2,1,0:T(8,128)(2,1)S(1)}, u32[]{:S(2)}, u32[]{:S(2)}) collective-permute-start(bf16[8,144,512]{2,1,0:T(8,128)(2,1)} %get-tuple-element.46), channel_id=1, source_target_pairs={{0,1},{1,0},{2,3},{3,2},{4,5},{5,4},{6,7},{7,6},{8,9},{9,8},{10,11... | collective-permute-start | bytes 3538952 | tf_op jit(solution)/shard_map/ppermute | solution.py:390
  70.5 9.2 %copy-start.2 = (f32[8,144,512]{2,1,0:T(8,128)S(1)}, f32[8,144,512]{2,1,0:T(8,128)}, u32[]{:S(2)}) copy-start(f32[8,144,512]{2,1,0:T(8,128)} %get-tuple-element.45) | copy-start | bytes 7077892
  79.6 17.0 %collective-permute-start.3 = (bf16[1024,512]{1,0:T(8,128)(2,1)}, bf16[1024,512]{1,0:T(8,128)(2,1)}, u32[]{:S(2)}, u32[]{:S(2)}) collective-permute-start(bf16[1024,512]{1,0:T(8,128)(2,1)} %get-tuple-element.52), channel_id=1, source_target_pairs={{0,1},{1,0},{2,3},{3,2},{4,5},{5,4},{6,7},{7,6},{8,9},{9,8},{10,11... | collective-permute-start | bytes 3145736 | tf_op jit(solution)/shard_map/ppermute | solution.py:392
  81.1 12.3 %copy-start.7 = (bf16[192,512]{1,0:T(8,128)(2,1)S(1)}, bf16[192,512]{1,0:T(8,128)(2,1)}, u32[]{:S(2)}) copy-start(bf16[192,512]{1,0:T(8,128)(2,1)} %get-tuple-element.50) | copy-start | bytes 589828
  81.2 19.5 %collective-permute-start.4 = (bf16[2,144,512]{2,0,1:T(2,128)(2,1)S(1)}, bf16[2,144,512]{2,0,1:T(2,128)(2,1)S(1)}, u32[]{:S(2)}, u32[]{:S(2)}) collective-permute-start(bf16[2,144,512]{2,0,1:T(2,128)(2,1)S(1)} %bitcast.81), channel_id=1, source_target_pairs={{0,64},{32,96},{64,0},{96,32},{1,65},{33,97},{65,1},{97,33},{2,66}... | collective-permute-start | bytes 884744 | tf_op jit(solution)/shard_map/ppermute | solution.py:25
  81.4 19.3 %collective-permute-start.5 = (bf16[2,144,512]{2,0,1:T(2,128)(2,1)S(1)}, bf16[2,144,512]{2,0,1:T(2,128)(2,1)S(1)}, u32[]{:S(2)}, u32[]{:S(2)}) collective-permute-start(bf16[2,144,512]{2,0,1:T(2,128)(2,1)S(1)} %get-tuple-element.54), channel_id=1, source_target_pairs={{0,32},{32,64},{64,96},{96,0},{1,33},{33,65},{65,97},{97,1},{2,34}... | collective-permute-start | bytes 884744 | tf_op jit(solution)/shard_map/ppermute | solution.py:25
  81.7 19.0 %collective-permute-start.6 = (bf16[2,144,512]{2,0,1:T(2,128)(2,1)S(1)}, bf16[2,144,512]{2,0,1:T(2,128)(2,1)S(1)}, u32[]{:S(2)}, u32[]{:S(2)}) collective-permute-start(bf16[2,144,512]{2,0,1:T(2,128)(2,1)S(1)} %get-tuple-element.55), channel_id=1, source_target_pairs={{0,96},{32,0},{64,32},{96,64},{1,97},{33,1},{65,33},{97,65},{2,98}... | collective-permute-start | bytes 884744 | tf_op jit(solution)/shard_map/ppermute | solution.py:25
  93.4 7.3 %copy-start.3 = (f32[1024,512]{1,0:T(8,128)S(1)}, f32[1024,512]{1,0:T(8,128)}, u32[]{:S(2)}) copy-start(f32[1024,512]{1,0:T(8,128)} %get-tuple-element.56) | copy-start | bytes 6291460
  95.2 22.7 %collective-permute-start.10 = (bf16[64,1024]{1,0:T(8,128)(2,1)}, bf16[64,1024]{1,0:T(8,128)(2,1)}, u32[]{:S(2)}, u32[]{:S(2)}) collective-permute-start(bf16[64,1024]{1,0:T(8,128)(2,1)} %get-tuple-element.71), channel_id=1, source_target_pairs={{0,31},{1,0},{2,1},{3,2},{4,3},{5,4},{6,5},{7,6},{8,7},{9,8},{10,9... | collective-permute-start | bytes 393224 | tf_op jit(solution)/shard_map/ppermute | solution.py:25
  96.6 21.3 %collective-permute-start.11 = (bf16[64,1024]{1,0:T(8,128)(2,1)}, bf16[64,1024]{1,0:T(8,128)(2,1)}, u32[]{:S(2)}, u32[]{:S(2)}) collective-permute-start(bf16[64,1024]{1,0:T(8,128)(2,1)} %get-tuple-element.70), channel_id=1, source_target_pairs={{0,1},{1,2},{2,3},{3,4},{4,5},{5,6},{6,7},{7,8},{8,9},{9,10},{10,1... | collective-permute-start | bytes 393224 | tf_op jit(solution)/shard_map/ppermute | solution.py:25
  102.2 1.4 copy-start.1
  103.7 8.2 %collective-permute-start.9 = (bf16[2,128,512]{2,1,0:T(8,128)(2,1)S(1)}, bf16[2,128,512]{2,1,0:T(8,128)(2,1)}, u32[]{:S(2)}, u32[]{:S(2)}) collective-permute-start(bf16[2,128,512]{2,1,0:T(8,128)(2,1)S(1)} %get-tuple-element.68), channel_id=1, source_target_pairs={{0,96},{32,0},{64,32},{96,64},{1,97},{33,1},{65,33},{97,65},{2,98}... | collective-permute-start | bytes 786440 | tf_op jit(solution)/shard_map/ppermute | solution.py:25
  103.8 8.8 %collective-permute-start.8 = (bf16[2,128,512]{2,1,0:T(8,128)(2,1)S(1)}, bf16[2,128,512]{2,1,0:T(8,128)(2,1)}, u32[]{:S(2)}, u32[]{:S(2)}) collective-permute-start(bf16[2,128,512]{2,1,0:T(8,128)(2,1)S(1)} %get-tuple-element.69), channel_id=1, source_target_pairs={{0,32},{32,64},{64,96},{96,0},{1,33},{33,65},{65,97},{97,1},{2,34}... | collective-permute-start | bytes 786440 | tf_op jit(solution)/shard_map/ppermute | solution.py:25
  105.2 11.2 %collective-permute-start.7 = (bf16[2,128,512]{2,1,0:T(8,128)(2,1)S(1)}, bf16[2,128,512]{2,1,0:T(8,128)(2,1)}, u32[]{:S(2)}, u32[]{:S(2)}) collective-permute-start(bf16[2,128,512]{2,1,0:T(8,128)(2,1)S(1)} %get-tuple-element.67), channel_id=1, source_target_pairs={{0,64},{32,96},{64,0},{96,32},{1,65},{33,97},{65,1},{97,33},{2,66}... | collective-permute-start | bytes 786440 | tf_op jit(solution)/shard_map/ppermute | solution.py:25
  107.0 10.8 %copy-start.6 = (bf16[2,128,16]{2,1,0:T(8,128)(2,1)S(1)}, bf16[2,128,16]{2,1,0:T(8,128)(2,1)}, u32[]{:S(2)}) copy-start(bf16[2,128,16]{2,1,0:T(8,128)(2,1)} %copy.38) | copy-start | bytes 24580
  118.9 29.8 %all-to-all-start.1 = ((bf16[64,4,1040]{2,1,0:T(4,128)(2,1)}), bf16[64,4,1040]{2,1,0:T(4,128)(2,1)S(1)}, u32[]{:S(2)}, u32[]{:S(2)}) async-start(bf16[64,4,1040]{2,1,0:T(4,128)(2,1)} %all_to_all.10), calls=%async_computation.1 | async-start | bytes 1179648 | tf_op jit(solution)/shard_map/all_to_all | solution.py:431

commit v3 on v2

v3 whole, which is shorter than its diff:
```python
import functools
import jax
import jax.numpy as jnp
from jax import lax
from jax.experimental import pallas as pl
from jax.experimental.pallas import tpu as pltpu
from jax.sharding import Mesh, PartitionSpec as P

loss_scale = 8.0
smooth_sq = 0.01
TILE = 64
NCOL = 256
ROWS = 32
GROUP = 4
VMEM_LIMIT = 12 * 1024 * 1024
BACK = 2
AHEAD = (2, 1, 3)
f32 = jnp.float32
bf16 = jnp.bfloat16
SPACE = ("y", "zl", "c")
ENS = ("zh", "x")
LATE = ("zh", "y", "zl", "c")


def shifted(block, axes, distance):
    count = lax.axis_size(axes)
    return lax.ppermute(block, axes, [(i, (i + distance) % count) for i in range(count)])


def smooth_grad(diff):
    return diff / jnp.sqrt(diff * diff + smooth_sq)


def gelu_parts(v):
    c0 = 0.7978845608
    c1 = c0 * 0.044715
    sq = v * v
    t = jnp.tanh(v * (c0 + c1 * sq))
    u = 1.0 + t
    slope = v * (c0 + (3.0 * c1) * sq)
    return v * u, u * (1.0 + (1.0 - t) * slope)


def resident(shape, dtype):
    return pltpu.VMEM(shape, dtype)


def in_vmem():
    return pl.BlockSpec(memory_space=pltpu.VMEM)


def params():
    return pltpu.CompilerParams(vmem_limit_bytes=VMEM_LIMIT)


def forward_kernel(
    slots,
    members,
    below_ref,
    here_ref,
    above_ref,
    wsrc_ref,
    dst_ref,
    idx_ref,
    scale_ref,
    wout_ref,
    gp_ref,
    agg_ref,
    sum_ref,
    pred_ref,
    sent_ref,
    feats,
    rhs,
    hot,
    pre,
):
    step = pl.program_id(0)
    nodes, width = feats.shape
    depth = rhs.shape[0]
    tile = depth - nodes
    block = below_ref.shape[0]

    @pl.when(step == 0)
    def _():
        for i, ref in enumerate((below_ref, here_ref, above_ref)):
            feats[i * block : (i + 1) * block, :] = ref[...]
        for n in range(width // NCOL):
            cols = slice(n * NCOL, (n + 1) * NCOL)
            rhs[:nodes, cols] = jnp.dot(
                feats[...], wsrc_ref[:, cols], preferred_element_type=f32
            ).astype(bf16)

    base = pl.multiple_of(step * tile, tile)
    rhs[nodes:, :] = dst_ref[pl.ds(base, tile), :]
    lane = lax.broadcasted_iota(jnp.int32, (tile, depth), 1)
    row = lax.broadcasted_iota(jnp.int32, (tile, depth), 0)
    eye = lane == row + nodes
    idx = idx_ref[pl.ds(base, tile), :]
    for k in range(slots):
        col = idx[:, k : k + 1]
        hit = (lane == col) | (eye & (col >= 0))
        hot[k * tile : (k + 1) * tile, :] = jnp.where(hit, 1.0, 0.0).astype(bf16)
    for n in range(width // NCOL):
        cols = slice(n * NCOL, (n + 1) * NCOL)
        pre[n % 2] = jnp.dot(hot[...], rhs[:, cols], preferred_element_type=f32).astype(bf16)
        for r in range(0, tile, ROWS):
            acc_g = jnp.zeros((ROWS, NCOL), f32)
            acc_s = jnp.zeros((ROWS, NCOL), f32)
            for k in range(slots):
                rows = k * tile + r
                value, grad = gelu_parts(pre[n % 2, rows : rows + ROWS, :])
                gp_ref[pl.ds(pl.multiple_of(step * tile * slots + rows, ROWS), ROWS), cols] = grad
                if k % GROUP == 0:
                    some_g, some_s = value, grad
                else:
                    some_g, some_s = some_g + value, some_s + grad
                if k % GROUP == GROUP - 1:
                    acc_g = acc_g + some_g.astype(f32)
                    acc_s = acc_s + some_s.astype(f32)
            at = pl.ds(pl.multiple_of(base + r, ROWS), ROWS)
            scale = scale_ref[at, :]
            agg_ref[at, cols] = (acc_g * scale).astype(bf16)
            sum_ref[at, cols] = (acc_s - (slots - 0.5 / scale)).astype(bf16)

    @pl.when(step == pl.num_programs(0) - 1)
    def _():
        pred = lax.dot_general(
            wout_ref[...], agg_ref[...], (((1,), (1,)), ((), ())), preferred_element_type=f32
        )
        pred_ref[...] = pred
        for e in range(members):
            sent_ref[e] = pred.astype(bf16)


def forward(below, here, above, w_src, dst, idx, scale, wout_t, members):
    grid_rows, width = dst.shape
    nodes = 3 * here.shape[0]
    slots = idx.shape[1]
    outs = wout_t.shape[0]
    return pl.pallas_call(
        functools.partial(forward_kernel, slots, members),
        grid=(grid_rows // TILE,),
        in_specs=[in_vmem() for _ in range(8)],
        out_specs=[in_vmem() for _ in range(5)],
        out_shape=[
            resident((grid_rows * slots, width), bf16),
            resident((grid_rows, width), bf16),
            resident((grid_rows, width), bf16),
            resident((outs, grid_rows), f32),
            resident((members, outs, grid_rows), bf16),
        ],
        scratch_shapes=[
            pltpu.VMEM((nodes, width), bf16),
            pltpu.VMEM((nodes + TILE, width), bf16),
            pltpu.VMEM((TILE * slots, nodes + TILE), bf16),
            pltpu.VMEM((2, TILE * slots, NCOL), bf16),
        ],
        compiler_params=params(),
        cost_estimate=pl.CostEstimate(
            flops=2 * grid_rows * slots * 256 * width,
            bytes_accessed=2 * grid_rows * slots * width,
            transcendentals=grid_rows * slots * width,
        ),
        name="forward",
    )(below, here, above, w_src, dst, idx, scale, wout_t)


def middle_kernel(
    core_ref,
    every_ref,
    pred_ref,
    truth_ref,
    area_ref,
    var_ref,
    wout_ref,
    scale_ref,
    sum_ref,
    agg_ref,
    grid_ref,
    lead_ref,
    own_ref,
    far_ref,
    ddst,
    part,
):
    width = sum_ref.shape[1]
    half = width // 2
    members = every_ref.shape[0]
    outs = pred_ref.shape[0]
    core = core_ref[0]

    pred = pred_ref[...]
    pair = -smooth_grad(pred - pred.astype(bf16).astype(f32))
    for e in range(members):
        pair = pair + smooth_grad(pred - every_ref[e].astype(f32))
    weighting = loss_scale * area_ref[...] * var_ref[...]
    dpred = (
        weighting
        * (smooth_grad(pred - truth_ref[...]) / members - pair / (members * (members - 1)))
    ).astype(bf16)
    for n in range(width // NCOL):
        cols = slice(n * NCOL, (n + 1) * NCOL)
        dagg = lax.dot_general(
            dpred, wout_ref[:, cols], (((0,), (0,)), ((), ())), preferred_element_type=f32
        )
        dagg = dagg * scale_ref[...]
        lead_ref[:, cols] = dagg.astype(bf16)
        ddst[:, cols] = (dagg * sum_ref[:, cols].astype(f32)).astype(bf16)

    mine = pl.ds(pl.multiple_of(core * half, half), half)
    other = pl.ds(pl.multiple_of((1 - core) * half, half), half)
    part[...] = jnp.dot(dpred, agg_ref[...], preferred_element_type=f32)
    few = outs // 2
    chunks = far_ref.shape[0]
    rows = far_ref.shape[1] - few
    for ref, columns, which in ((far_ref, other, 1 - core), (own_ref, mine, core)):
        ref[:, :rows, :] = (
            lax.dot_general(
                grid_ref[...], ddst[:, columns], (((0,), (0,)), ((), ())), preferred_element_type=f32
            )
            .reshape(chunks, rows, half)
            .astype(ref.dtype)
        )
        ref[:, rows:, :] = jnp.zeros((chunks, few, half), ref.dtype)
        for chunk in range(chunks):
            ref[chunk, rows:, :rows] = part[
                pl.ds(pl.multiple_of(which * few, few), few), chunk * rows : (chunk + 1) * rows
            ].astype(ref.dtype)


def prefetched(count, ins, outs, scratch):
    return pltpu.PrefetchScalarGridSpec(
        num_scalar_prefetch=1,
        grid=(count,),
        in_specs=[in_vmem() for _ in range(ins)],
        out_specs=[in_vmem() for _ in range(outs)],
        scratch_shapes=scratch,
    )


def middle(core, everyone, pred, truth_t, area, var, wout_t, scale, sums, agg, grid_embed):
    grid_rows, width = sums.shape
    outs = pred.shape[0]
    chunks = everyone.shape[0]
    block = (chunks, width // chunks + outs // 2, width // 2)
    return pl.pallas_call(
        middle_kernel,
        grid_spec=prefetched(
            1,
            10,
            3,
            [pltpu.VMEM((grid_rows, width), bf16), pltpu.VMEM((outs, width), f32)],
        ),
        out_shape=[
            resident((grid_rows, width), bf16),
            resident(block, f32),
            resident(block, bf16),
        ],
        compiler_params=params(),
        cost_estimate=pl.CostEstimate(
            flops=2 * grid_rows * width * width, bytes_accessed=10 * grid_rows * width, transcendentals=0
        ),
        name="middle",
    )(core, everyone, pred, truth_t, area, var, wout_t, scale, sums, agg, grid_embed)


def quarter(here, zh, d, count):
    return zh * count + (here + d) % count


def combine_kernel(place_ref, own_ref, far_ref, kept_ref, *piece_refs):
    count = own_ref.shape[0] // kept_ref.shape[0]
    for zh in range(kept_ref.shape[0]):
        for d, ref in zip((0,) + AHEAD, (kept_ref,) + piece_refs):
            at = quarter(place_ref[0], zh, d, count)
            ref[zh] = (own_ref[at] + far_ref[at].astype(f32)).astype(ref.dtype)


def combine(place, own, far, groups):
    block = (groups,) + own.shape[1:]
    return pl.pallas_call(
        combine_kernel,
        grid_spec=prefetched(1, 2, 1 + len(AHEAD), []),
        out_shape=[resident(block, f32)] + [resident(block, bf16) for _ in AHEAD],
        compiler_params=params(),
        cost_estimate=pl.CostEstimate(flops=own.size, bytes_accessed=12 * own.size, transcendentals=0),
        name="combine",
    )(place, own, far)


def scatter_step(slots, col, gp_ref, lead_ref, idx_ref, hot, prod, acc):
    step = pl.program_id(0)
    nodes, half = acc.shape
    wide = BACK * TILE

    @pl.when(step == 0)
    def _():
        acc[...] = jnp.zeros_like(acc)

    cols = pl.ds(pl.multiple_of(col * half, half), half)
    node = lax.broadcasted_iota(jnp.int32, (nodes, wide), 0)
    idx = idx_ref[:, pl.ds(pl.multiple_of(step * wide, wide), wide)]
    for k in range(slots):
        hot[:, k * wide : (k + 1) * wide] = jnp.where(node == idx[k : k + 1, :], 1.0, 0.0).astype(bf16)
    for part in range(BACK):
        lead = lead_ref[pl.ds(pl.multiple_of(step * wide + part * TILE, TILE), TILE), cols]
        for k in range(slots):
            start = (step * BACK + part) * slots * TILE + k * TILE
            to = k * wide + part * TILE
            prod[to : to + TILE, :] = gp_ref[pl.ds(pl.multiple_of(start, TILE), TILE), cols] * lead
    for n in range(half // NCOL):
        here = slice(n * NCOL, (n + 1) * NCOL)
        acc[:, here] += jnp.dot(hot[...], prod[:, here], preferred_element_type=f32)


def far_kernel(
    slots, core_ref, gp_ref, lead_ref, idx_ref, below_ref, here_ref, above_ref, wide_ref, part_ref, hot, prod, acc
):
    scatter_step(slots, 1 - core_ref[0], gp_ref, lead_ref, idx_ref, hot, prod, acc)

    @pl.when(pl.program_id(0) == pl.num_programs(0) - 1)
    def _():
        wide_ref[...] = acc[...].astype(bf16)
        feats = jnp.concatenate([below_ref[...], here_ref[...], above_ref[...]], axis=0)
        part_ref[...] = (
            lax.dot_general(feats, wide_ref[...], (((0,), (0,)), ((), ())), preferred_element_type=f32)
            .reshape(part_ref.shape)
            .astype(bf16)
        )


def own_kernel(
    slots,
    place_ref,
    gp_ref,
    lead_ref,
    idx_ref,
    below_ref,
    here_ref,
    above_ref,
    widefar_ref,
    far_ref,
    lower_ref,
    centre_ref,
    upper_ref,
    kept_ref,
    *rest,
):
    pieces, (hot, prod, acc, total) = rest[: len(AHEAD)], rest[len(AHEAD) :]
    core = place_ref[1]
    scatter_step(slots, core, gp_ref, lead_ref, idx_ref, hot, prod, acc)

    @pl.when(pl.program_id(0) == pl.num_programs(0) - 1)
    def _():
        half = acc.shape[1]
        block = lower_ref.shape[0]
        mine = pl.ds(pl.multiple_of(core * half, half), half)
        other = pl.ds(pl.multiple_of((1 - core) * half, half), half)
        wide = acc[...].astype(bf16)
        for i, ref in enumerate((lower_ref, centre_ref, upper_ref)):
            ref[:, mine] = wide[i * block : (i + 1) * block, :]
            ref[:, other] = widefar_ref[i * block : (i + 1) * block, :]
        feats = jnp.concatenate([below_ref[...], here_ref[...], above_ref[...]], axis=0)
        total[...] = lax.dot_general(
            feats, wide, (((0,), (0,)), ((), ())), preferred_element_type=f32
        ).reshape(total.shape)
        count = total.shape[0] // kept_ref.shape[0]
        for zh in range(kept_ref.shape[0]):
            for d, ref in zip((0,) + AHEAD, (kept_ref,) + pieces):
                at = quarter(place_ref[0], zh, d, count)
                ref[zh] = (total[at] + far_ref[at].astype(f32)).astype(ref.dtype)


def scatter_scratch(slots, nodes, half):
    wide = BACK * TILE * slots
    return [
        pltpu.VMEM((nodes, wide), bf16),
        pltpu.VMEM((wide, half), bf16),
        pltpu.VMEM((nodes, half), f32),
    ]


def scatter_cost(gp):
    return pl.CostEstimate(flops=gp.size * 256, bytes_accessed=gp.size, transcendentals=0)


def backward_far(core, gp, lead, idx_t, feats, chunks):
    grid_rows, width = lead.shape
    slots = idx_t.shape[0]
    nodes = 3 * feats[0].shape[0]
    half = width // 2
    return pl.pallas_call(
        functools.partial(far_kernel, slots),
        grid_spec=prefetched(
            grid_rows // (BACK * TILE), 6, 2, scatter_scratch(slots, nodes, half)
        ),
        out_shape=[
            resident((nodes, half), bf16),
            resident((chunks, width // chunks, half), bf16),
        ],
        compiler_params=params(),
        cost_estimate=scatter_cost(gp),
        name="backward_far",
    )(core, gp, lead, idx_t, *feats)


def backward_own(place, gp, lead, idx_t, feats, wide_far, far, groups):
    grid_rows, width = lead.shape
    slots = idx_t.shape[0]
    block = feats[0].shape[0]
    half = width // 2
    quarter_shape = (groups,) + far.shape[1:]
    return pl.pallas_call(
        functools.partial(own_kernel, slots),
        grid_spec=prefetched(
            grid_rows // (BACK * TILE),
            8,
            4 + len(AHEAD),
            scatter_scratch(slots, 3 * block, half) + [pltpu.VMEM(far.shape, f32)],
        ),
        out_shape=[resident((block, width), bf16) for _ in range(3)]
        + [resident(quarter_shape, f32)]
        + [resident(quarter_shape, bf16) for _ in AHEAD],
        compiler_params=params(),
        cost_estimate=scatter_cost(gp),
        name="backward_own",
    )(place, gp, lead, idx_t, *feats, wide_far, far)


def x_moved(pieces):
    return [shifted(piece, "x", d) for piece, d in zip(pieces, AHEAD)]


def summed(kept, moved):
    for piece in moved:
        kept = kept + piece.astype(f32)
    return kept


def body(
    mesh_feats,
    grid_embed,
    w_src,
    w_dst,
    w_out,
    truth,
    area_weight,
    var_weight,
    neighbour,
    edge_mask,
):
    own = mesh_feats[0]
    node_rows, width = own.shape
    grid_rows, slots = neighbour.shape
    half = width // 2
    space_count = lax.axis_size(SPACE)
    block_id = lax.axis_index(SPACE)
    members = lax.axis_size(ENS)
    swap = [(0, 1), (1, 0)]
    core = lax.axis_index("c")
    mine = jnp.full((1,), core, jnp.int32)

    groups = lax.axis_size("zh")
    place = jnp.stack([lax.axis_index("x"), core]).astype(jnp.int32)

    below = shifted(own, SPACE, 1)
    above = shifted(own, SPACE, -1)

    dst = jnp.dot(grid_embed, w_dst, preferred_element_type=f32).astype(bf16)
    local = jnp.mod(neighbour.T - (block_id - 1) * node_rows, node_rows * space_count)
    idx_t = jnp.where(edge_mask.T > 0, local, -1)
    idx = idx_t.T
    scale = 0.5 / jnp.sum(edge_mask.T.astype(f32), axis=0)[:, None]
    wout_t = w_out.T
    truth_t = truth.T
    var = var_weight[:, None]
    area = area_weight[None, :]
    dst, idx, idx_t, scale, wout_t, truth_t, var, area, below = lax.optimization_barrier(
        (dst, idx, idx_t, scale, wout_t, truth_t, var, area, below)
    )
    feats = (below, own, above)
    gp, agg, sums, pred, sent = forward(*feats, w_src, dst, idx, scale, wout_t, members)
    everyone = lax.all_to_all(sent, ENS, 0, 0, tiled=True)
    lead, dst_own, dst_far = middle(
        mine, everyone, pred, truth_t, area, var, wout_t, scale, sums, agg, grid_embed
    )
    dst_far = lax.ppermute(dst_far, "c", swap)
    wide_far, src_far = backward_far(mine, gp, lead, idx_t, feats, members)
    src_far = lax.ppermute(src_far, "c", swap)
    dst_kept, *dst_pieces = combine(place, dst_own, dst_far, groups)
    lead, *dst_pieces = lax.optimization_barrier((lead, *dst_pieces))
    dst_moved = x_moved(dst_pieces)
    lower, centre, upper, src_kept, *src_pieces = backward_own(
        place, gp, lead, idx_t, feats, wide_far, src_far, groups
    )
    dst_moved = lax.optimization_barrier(tuple(dst_moved) + tuple(src_pieces))
    src_pieces = dst_moved[len(AHEAD) :]
    dst_moved = dst_moved[: len(AHEAD)]
    src_moved = x_moved(src_pieces)
    from_above = shifted(lower, SPACE, -1)
    from_below = shifted(upper, SPACE, 1)

    dst_sum = summed(dst_kept, dst_moved)
    late_rows = width // lax.axis_size("x")
    per_chunk = width // members
    dst_total = jnp.concatenate(
        [
            dst_sum[:, :per_chunk].reshape(late_rows, half),
            dst_sum[:, per_chunk:, :per_chunk].transpose(0, 2, 1).reshape(late_rows, -1),
        ],
        axis=1,
    ).astype(bf16)
    dst_parts = lax.all_to_all(dst_total, LATE, 0, 0, tiled=True)

    src_total = summed(src_kept, src_moved).reshape(late_rows, half).astype(bf16)
    src_total, dst_parts, from_above, from_below = lax.optimization_barrier(
        (src_total, dst_parts, from_above, from_below)
    )
    src_parts = lax.all_to_all(src_total, LATE, 0, 0, tiled=True)
    dproj = (centre.astype(f32) + from_above.astype(f32) + from_below.astype(f32)).astype(bf16)
    grad_mesh = lax.dot_general(
        dproj, w_src, (((1,), (1,)), ((), ())), preferred_element_type=f32
    ).astype(bf16)

    def late_sum(parts):
        parts = parts.reshape(-1, 2, parts.shape[0] // lax.axis_size(LATE), parts.shape[1])
        return jnp.sum(parts.astype(f32), axis=0)

    def joined(total, a, b):
        return jnp.concatenate([total[0, :, a:b], total[1, :, a:b]], axis=1)

    dst_final = late_sum(dst_parts)
    return (
        grad_mesh[None],
        joined(late_sum(src_parts), 0, half),
        joined(dst_final, 0, half),
        joined(dst_final, half, dst_final.shape[-1]),
    )


def solution(mesh):
    fine = Mesh(mesh.devices.reshape(2, 4, 4, 4, 2), ("zh", "x", "y", "zl", "c"))
    everywhere = ENS + SPACE
    in_specs = (
        P(ENS, SPACE, None),
        P(SPACE, None),
        P(),
        P(),
        P(),
        P(SPACE, None),
        P(SPACE),
        P(),
        P(SPACE, None),
        P(SPACE, None),
    )
    out_specs = (
        P(ENS, SPACE, None),
        P(everywhere, None),
        P(everywhere, None),
        P(everywhere, None),
    )
    return jax.shard_map(body, mesh=fine, in_specs=in_specs, out_specs=out_specs, check_vma=False)
```

time: 152 us -> 159 us (1.046)
  local copies, waits for them, and re-layouts: 10.4 us -> 37.8 us
  Pallas kernels: 42.2 us -> 30.9 us
  other arithmetic: 11.6 us -> 5.75 us
  waiting for transfers between devices: 37.5 us -> 31.8 us
  starting transfers between devices: 38.8 us -> 44.2 us
  matrix products: 9.58 us -> 6.69 us
    unnamed x24 -> x76, local copies, waits for them, and re-layouts: 3.37 us -> 36.2 us
    pallas_call x4 -> x5, Pallas kernels: 42.2 us -> 30.9 us  [the longest x1 17.1 us: forward(): pl.pallas_call(functools.partial(forward_kernel, slots, members), grid=(g...]
    all_to_all x2 -> x3, waiting for transfers between devices: 28.1 us -> 19.7 us  [the longest x1 10.1 us: body(): everyone = lax.all_to_all(sent, ENS, 0, 0, tiled=True)]
    all_to_all x2 -> x3, starting transfers between devices: 19.7 us -> 25.5 us  [the longest x1 10.5 us: body(): src_parts = lax.all_to_all(src_total, LATE, 0, 0, tiled=True)]
    dot_general x1 -> x0, matrix products: 2.92 us -> none  [body(): wide = jnp.dot(feats, w_src, preferred_element_type=f32).astype(bf16)]
    ppermute x10, waiting for transfers between devices: 9.4 us -> 12.1 us  [shifted(): lax.ppermute(block, axes, [(i, (i + distance) % count) for i in range(cou...]
    broadcast_in_dim x2 -> x0, local copies, waits for them, and re-layouts: 2.4 us -> none  [the longest x1 1.71 us: body(): jnp.broadcast_to(pred[None], (members,) + pred.shape)]
    concatenate x6 -> x3, other arithmetic: 4.33 us -> 2.17 us  [the longest x2 1.27 us: joined(): return jnp.concatenate([total[0, :, a:b], total[1, :, a:b]], axis=1)]
  transfers between devices with their start and end apart: 14 -> 15, of which waited for: 5 -> 5; matrix products, arithmetic and copies ran while one was open for 14% -> 7% of each run, Pallas kernels for 12% -> 7%
where the time goes in v3:
time: 159 us; the launch traced here: 158 us
  starting transfers between devices  44.2 us (28%)
  local copies, waits for them, and re-layouts  37.8 us (24%)
  waiting for transfers between devices  31.8 us (20%)
  Pallas kernels  30.9 us (19%)
  matrix products  6.69 us (4%)
  other arithmetic  5.75 us (4%)
    unnamed x76, local copies, waits for them, and re-layouts  36.2 us
    pallas_call x1, Pallas kernels, forward(): pl.pallas_call(functools.partial(forward_kernel, slots, members), grid=(g...  17.1 us
    ppermute x10, starting transfers between devices, shifted(): lax.ppermute(block, axes, [(i, (i + distance) % count) for i in range(cou...  12.8 us
    ppermute x10, waiting for transfers between devices, shifted(): lax.ppermute(block, axes, [(i, (i + distance) % count) for i in range(cou...  12.1 us
    all_to_all x1, starting transfers between devices, body(): src_parts = lax.all_to_all(src_total, LATE, 0, 0, tiled=True)  10.5 us
    all_to_all x1, waiting for transfers between devices, body(): everyone = lax.all_to_all(sent, ENS, 0, 0, tiled=True)  10.1 us
    all_to_all x1, starting transfers between devices, body(): everyone = lax.all_to_all(sent, ENS, 0, 0, tiled=True)  9.98 us
    all_to_all x1, waiting for transfers between devices, body(): src_parts = lax.all_to_all(src_total, LATE, 0, 0, tiled=True)  9.62 us
  transfers between devices with their start and end apart: 15, of which 5 were waited for; matrix products, arithmetic and copies ran while one was open for 7% of the time, Pallas kernels for 7%

profile of v3, /device:TPU:1, one launch (start us, length us, event | category | flops | bytes accessed | tf_op | source)
XLA Modules:
  0.0 158.2 jit_solution(8094584802300158309)
XLA Ops:
  0.6 3.3 %collective-permute-start.1 = (bf16[64,1024]{1,0:T(8,128)(2,1)}, bf16[64,1024]{1,0:T(8,128)(2,1)S(1)}, u32[]{:S(2)}, u32[]{:S(2)}) collective-permute-start(bf16[64,1024]{1,0:T(8,128)(2,1)} %bitcast.37), channel_id=1, source_target_pairs={{0,31},{1,0},{2,1},{3,2},{4,3},{5,4},{6,5},{7,6},{8,7},{9,8},{10,9... | collective-permute-start | bytes 393224 | tf_op jit(solution)/shard_map/ppermute | solution.py:27
  4.8 1.4 fusion.4
  7.0 3.5 %convolution_convert_fusion.dst_ref = bf16[512,1024]{1,0:T(8,128)(2,1)} fusion(bf16[512,1024]{1,0:T(8,128)(2,1)} %grid_ref.1, bf16[1024,1024]{1,0:T(8,128)(2,1)S(1)} %copy-done), kind=kOutput, calls=%fused_computation | convolution fusion | flops 1074266112 | bytes 4194304 | tf_op jit(solution)/shard_map/dot_general | solution.py:469
  10.9 1.6 copy-done.6
  12.4 1.2 copy-done.36
  13.7 17.1 %forward.1 = (bf16[8192,1024]{1,0:T(8,128)(2,1)S(1)}, bf16[512,1024]{1,0:T(8,128)(2,1)S(1)}, bf16[512,1024]{1,0:T(8,128)(2,1)S(1)}, f32[32,512]{1,0:T(8,128)S(1)}, bf16[8,32,512]{2,1,0:T(8,128)(2,1)}) custom-call(bf16[64,1024]{1,0:T(8,128)(2,1)S(1)} %collective-permute-done.below_ref, bf16[64,1024]{1,0:T(8,128)(2,1)S(1)} %bitcast.39, ...), custom_call_target="tpu_custom_call" | custom-call | flops 4294967296 | bytes 16777216 | tf_op jit(solution)/shard_map/forward/pallas_call | solution.py:140
  30.8 5.8 %copy-done.1 = bf16[8192,1024]{1,0:T(8,128)(2,1)} copy-done((bf16[8192,1024]{1,0:T(8,128)(2,1)}, bf16[8192,1024]{1,0:T(8,128)(2,1)S(1)}, u32[]{:S(2)}) %copy-start.1) | copy-done | bytes 16777240
  38.6 10.0 %all-to-all-start = ((bf16[8,32,512]{2,1,0:T(8,128)(2,1)}), bf16[8,32,512]{2,1,0:T(8,128)(2,1)S(1)}, u32[]{:S(2)}, u32[]{:S(2)}) async-start(bf16[8,32,512]{2,1,0:T(8,128)(2,1)} %get-tuple-element.54), calls=%async_computation | async-start | bytes 524288 | tf_op jit(solution)/shard_map/all_to_all | solution.py:483
  48.7 10.1 %all-to-all-done.every_ref = bf16[8,32,512]{2,1,0:T(8,128)(2,1)S(1)} async-done(((bf16[8,32,512]{2,1,0:T(8,128)(2,1)}), bf16[8,32,512]{2,1,0:T(8,128)(2,1)S(1)}, u32[]{:S(2)}, u32[]{:S(2)}) %all-to-all-start) | async-done | bytes 262176 | tf_op jit(solution)/shard_map/all_to_all | solution.py:483
  61.4 1.2 copy-done.20
  65.0 1.2 copy-done.31
  66.2 1.2 copy-done.33
  68.3 2.7 %middle.1 = (bf16[512,1024]{1,0:T(8,128)(2,1)S(1)}, f32[8,144,512]{2,1,0:T(8,128)S(1)}, bf16[8,144,512]{2,1,0:T(8,128)(2,1)}) custom-call(s32[1]{0:T(128)} %bitcast.1.core_ref, bf16[8,32,512]{2,1,0:T(8,128)(2,1)S(1)} %copy-done.15, f32[32,512]{1,0:T(8,128)S(1)} %copy-done.35, f32[32,512]{1,0:T(8,128)S(1)} %bitcast.44, f32[1,512]{1,0:T(1,128)S(1)} %bitcast.45, ...), custom_call_target="tpu_custom_call" | custom-call | flops 1073741824 | bytes 5242880 | tf_op jit(solution)/shard_map/middle/pallas_call | solution.py:246
  71.0 1.4 copy-done.4
  72.4 5.9 %collective-permute-start.2 = (bf16[8,144,512]{2,1,0:T(8,128)(2,1)}, bf16[8,144,512]{2,1,0:T(8,128)(2,1)}, u32[]{:S(2)}, u32[]{:S(2)}) collective-permute-start(bf16[8,144,512]{2,1,0:T(8,128)(2,1)} %get-tuple-element.63), channel_id=1, source_target_pairs={{0,1},{1,0},{2,3},{3,2},{4,5},{5,4},{6,7},{7,6},{8,9},{9,8},{10,11... | collective-permute-start | bytes 3538952 | tf_op jit(solution)/shard_map/ppermute | solution.py:487
  78.3 5.8 %copy-done.2 = bf16[8192,1024]{1,0:T(8,128)(2,1)S(1)} copy-done((bf16[8192,1024]{1,0:T(8,128)(2,1)S(1)}, bf16[8192,1024]{1,0:T(8,128)(2,1)}, u32[]{:S(2)}) %copy-start.2) | copy-done | bytes 16777240
  84.8 3.9 %backward_far.1 = (bf16[192,512]{1,0:T(8,128)(2,1)S(1)}, bf16[8,128,512]{2,1,0:T(8,128)(2,1)}) custom-call(s32[1]{0:T(128)} %bitcast.1.core_ref, bf16[8192,1024]{1,0:T(8,128)(2,1)S(1)} %copy-done.2, bf16[512,1024]{1,0:T(8,128)(2,1)S(1)} %get-tuple-element.67.lead_ref, s32[16,512]{1,0:T(8,128)S(1)} %copy-done.10, ...), custom_call_target="tpu_custom_call" | custom-call | flops 2147483648 | bytes 8388608 | tf_op jit(solution)/shard_map/backward_far/pallas_call | solution.py:392
  89.6 1.7 %copy-done.5 = f32[8,144,512]{2,1,0:T(8,128)S(1)} copy-done((f32[8,144,512]{2,1,0:T(8,128)S(1)}, f32[8,144,512]{2,1,0:T(8,128)}, u32[]{:S(2)}) %copy-start.5) | copy-done | bytes 2359320
  91.2 2.0 %combine.1 = (f32[2,144,512]{2,1,0:T(8,128)S(1)}, bf16[2,144,512]{2,1,0:T(8,128)(2,1)S(1)}, bf16[2,144,512]{2,1,0:T(8,128)(2,1)S(1)}, bf16[2,144,512]{2,1,0:T(8,128)(2,1)S(1)}) custom-call(s32[2]{0:T(128)S(1)} %pad_add_fusion.place_ref, f32[8,144,512]{2,1,0:T(8,128)S(1)} %copy-done.5, bf16[8,144,512]{2,1,0:T(8,128)(2,1)} %collective-permute-done.2.far_ref), custom_call_target="tpu_custom_call" | custom-call | flops 589824 | bytes 7077888 | tf_op jit(solution)/shard_map/combine/pallas_call | solution.py:281
  94.4 2.2 %collective-permute-start.6 = (bf16[2,144,512]{2,1,0:T(8,128)(2,1)S(1)}, bf16[2,144,512]{2,1,0:T(8,128)(2,1)S(1)}, u32[]{:S(2)}, u32[]{:S(2)}) collective-permute-start(bf16[2,144,512]{2,1,0:T(8,128)(2,1)S(1)} %get-tuple-element.75), channel_id=1, source_target_pairs={{0,96},{32,0},{64,32},{96,64},{1,97},{33,1},{65,33},{97,65},{2,98}... | collective-permute-start | bytes 884744 | tf_op jit(solution)/shard_map/ppermute | solution.py:27
  96.7 5.8 %copy-done.3 = bf16[8192,1024]{1,0:T(8,128)(2,1)S(1)} copy-done((bf16[8192,1024]{1,0:T(8,128)(2,1)S(1)}, bf16[8192,1024]{1,0:T(8,128)(2,1)}, u32[]{:S(2)}) %copy-start.3) | copy-done | bytes 16777240
  102.4 5.0 %backward_own.1 = (bf16[64,1024]{1,0:T(8,128)(2,1)S(1)}, bf16[64,1024]{1,0:T(8,128)(2,1)S(1)}, bf16[64,1024]{1,0:T(8,128)(2,1)S(1)}, f32[2,128,512]{2,1,0:T(8,12...) custom-call(s32[2]{0:T(128)S(1)} %pad_add_fusion.place_ref, ...), custom_call_target="tpu_custom_call" | custom-call | flops 2147483648 | bytes 8388608 | tf_op jit(solution)/shard_map/backward_own/pallas_call | solution.py:413
  107.5 2.5 %collective-permute-done.5 = bf16[2,144,512]{2,1,0:T(8,128)(2,1)S(1)} collective-permute-done((bf16[2,144,512]{2,1,0:T(8,128)(2,1)S(1)}, bf16[2,144,512]{2,1,0:T(8,128)(2,1)S(1)}, u32[]{:S(2)}, u32[]{:S(2)}) %collective-permute-start.5) | collective-permute-done | bytes 294944 | tf_op jit(solution)/shard_map/ppermute | solution.py:27
  111.5 5.0 %all-to-all-start.1 = ((bf16[64,4,528]{2,1,0:T(4,128)(2,1)}), bf16[64,4,528]{2,1,0:T(4,128)(2,1)S(1)}, u32[]{:S(2)}, u32[]{:S(2)}) async-start(bf16[64,4,528]{2,1,0:T(4,128)(2,1)} %pad_maximum_fusion), calls=%async_computation.1 | async-start | bytes 655360 | tf_op jit(solution)/shard_map/all_to_all | solution.py:513
  117.7 2.4 %collective-permute-start.9 = (bf16[2,128,512]{2,1,0:T(8,128)(2,1)}, bf16[2,128,512]{2,1,0:T(8,128)(2,1)S(1)}, u32[]{:S(2)}, u32[]{:S(2)}) collective-permute-start(bf16[2,128,512]{2,1,0:T(8,128)(2,1)} %copy-done.21), channel_id=1, source_target_pairs={{0,96},{32,0},{64,32},{96,64},{1,97},{33,1},{65,33},{97,65},{2,98}... | collective-permute-start | bytes 786440 | tf_op jit(solution)/shard_map/ppermute | solution.py:27
  120.1 1.3 collective-permute-start.10
  121.4 1.2 collective-permute-start.11
  122.5 3.2 %collective-permute-done.7 = bf16[2,128,512]{2,1,0:T(8,128)(2,1)S(1)} collective-permute-done((bf16[2,128,512]{2,1,0:T(8,128)(2,1)}, bf16[2,128,512]{2,1,0:T(8,128)(2,1)S(1)}, u32[]{:S(2)}, u32[]{:S(2)}) %collective-permute-start.7) | collective-permute-done | bytes 262176 | tf_op jit(solution)/shard_map/ppermute | solution.py:27
  125.7 6.4 %collective-permute-done.8 = bf16[2,128,512]{2,1,0:T(8,128)(2,1)S(1)} collective-permute-done((bf16[2,128,512]{2,1,0:T(8,128)(2,1)}, bf16[2,128,512]{2,1,0:T(8,128)(2,1)S(1)}, u32[]{:S(2)}, u32[]{:S(2)}) %collective-permute-start.8) | collective-permute-done | bytes 262176 | tf_op jit(solution)/shard_map/ppermute | solution.py:27
  133.2 10.5 %all-to-all-start.2 = ((bf16[64,4,512]{2,1,0:T(4,128)(2,1)}), bf16[64,4,512]{2,1,0:T(4,128)(2,1)S(1)}, u32[]{:S(2)}, u32[]{:S(2)}) async-start(bf16[64,4,512]{2,1,0:T(4,128)(2,1)} %all_to_all.18), calls=%async_computation.2 | async-start | bytes 524288 | tf_op jit(solution)/shard_map/all_to_all | solution.py:519
  144.7 3.2 %fusion = bf16[1,64,1024]{2,1,0:T(8,128)(2,1)} fusion(bf16[1024,1024]{1,0:T(8,128)(2,1)} %wsrc_ref.1, bf16[64,1024]{1,0:T(8,128)(2,1)} %collective-permute-done.11, bf16[64,1024]{1,0:T(8,128)(2,1)} %collective-permute-done.10, bf16[64,1024]{1,0:T(8,128)(2,1)S(1)} %copy-done.19), kind=kOutput, calls=%fused_computation.2 | convolution fusion | flops 134676480 | bytes 2621440 | tf_op jit(solution)/shard_map/dot_general | solution.py:521
  147.8 9.6 %all-to-all-done.2 = bf16[64,4,512]{2,1,0:T(4,128)(2,1)S(1)} async-done(((bf16[64,4,512]{2,1,0:T(4,128)(2,1)}), bf16[64,4,512]{2,1,0:T(4,128)(2,1)S(1)}, u32[]{:S(2)}, u32[]{:S(2)}) %all-to-all-start.2) | async-done | bytes 262176 | tf_op jit(solution)/shard_map/all_to_all | solution.py:519
  (106 shorter events, 17.8 us)
Async XLA Ops:
  0.6 6.3 %copy-start = (bf16[1024,1024]{1,0:T(8,128)(2,1)S(1)}, bf16[1024,1024]{1,0:T(8,128)(2,1)}, u32[]{:S(2)}) copy-start(bf16[1024,1024]{1,0:T(8,128)(2,1)} %param.13) | copy-start | bytes 6291460
  0.6 10.2 %collective-permute-start.1 = (bf16[64,1024]{1,0:T(8,128)(2,1)}, bf16[64,1024]{1,0:T(8,128)(2,1)S(1)}, u32[]{:S(2)}, u32[]{:S(2)}) collective-permute-start(bf16[64,1024]{1,0:T(8,128)(2,1)} %bitcast.37), channel_id=1, source_target_pairs={{0,31},{1,0},{2,1},{3,2},{4,3},{5,4},{6,5},{7,6},{8,7},{9,8},{10,9... | collective-permute-start | bytes 393224 | tf_op jit(solution)/shard_map/ppermute | solution.py:27
  4.0 6.6 %collective-permute-start = (bf16[64,1024]{1,0:T(8,128)(2,1)}, bf16[64,1024]{1,0:T(8,128)(2,1)S(1)}, u32[]{:S(2)}, u32[]{:S(2)}) collective-permute-start(bf16[64,1024]{1,0:T(8,128)(2,1)} %bitcast.38), channel_id=1, source_target_pairs={{0,1},{1,2},{2,3},{3,4},{4,5},{5,6},{6,7},{7,8},{8,9},{9,10},{10,1... | collective-permute-start | bytes 393224 | tf_op jit(solution)/shard_map/ppermute | solution.py:27
  7.0 3.9 %copy-start.7 = (bf16[1,64,1024]{2,1,0:T(8,128)(2,1)S(1)}, bf16[1,64,1024]{2,1,0:T(8,128)(2,1)}, u32[]{:S(2)}) copy-start(bf16[1,64,1024]{2,1,0:T(8,128)(2,1)} %param.10) | copy-start | bytes 393220
  7.0 3.9 %copy-start.26 = (bf16[1024,32]{0,1:T(8,128)(2,1)S(1)}, bf16[1024,32]{0,1:T(8,128)(2,1)}, u32[]{:S(2)}) copy-start(bf16[1024,32]{0,1:T(8,128)(2,1)} %param.14) | copy-start | bytes 196612
  10.7 20.1 %copy-start.12 = (f32[512,1]{1,0:T(8,128)}, f32[512,1]{1,0:T(8,128)S(1)}, u32[]{:S(2)}) copy-start(f32[512,1]{1,0:T(8,128)S(1)} %copy.17.scale_ref) | copy-start | bytes 6148
  13.7 34.9 %copy-start.37 = (f32[32]{0:T(128)S(1)}, f32[32]{0:T(128)}, u32[]{:S(2)}) copy-start(f32[32]{0:T(128)} %param.17) | copy-start | bytes 388
  30.8 5.8 %copy-start.1 = (bf16[8192,1024]{1,0:T(8,128)(2,1)}, bf16[8192,1024]{1,0:T(8,128)(2,1)S(1)}, u32[]{:S(2)}) copy-start(bf16[8192,1024]{1,0:T(8,128)(2,1)S(1)} %get-tuple-element.53.gp_ref) | copy-start | bytes 50331652
  38.6 20.9 %copy-start.34 = (f32[32,512]{1,0:T(8,128)}, f32[32,512]{1,0:T(8,128)S(1)}, u32[]{:S(2)}) copy-start(f32[32,512]{1,0:T(8,128)S(1)} %get-tuple-element.55.pred_ref) | copy-start | bytes 196612
  38.6 20.2 %all-to-all-start = ((bf16[8,32,512]{2,1,0:T(8,128)(2,1)}), bf16[8,32,512]{2,1,0:T(8,128)(2,1)S(1)}, u32[]{:S(2)}, u32[]{:S(2)}) async-start(bf16[8,32,512]{2,1,0:T(8,128)(2,1)} %get-tuple-element.54), calls=%async_computation | async-start | bytes 524288 | tf_op jit(solution)/shard_map/all_to_all | solution.py:483
  72.4 17.2 %collective-permute-start.2 = (bf16[8,144,512]{2,1,0:T(8,128)(2,1)}, bf16[8,144,512]{2,1,0:T(8,128)(2,1)}, u32[]{:S(2)}, u32[]{:S(2)}) collective-permute-start(bf16[8,144,512]{2,1,0:T(8,128)(2,1)} %get-tuple-element.63), channel_id=1, source_target_pairs={{0,1},{1,0},{2,3},{3,2},{4,5},{5,4},{6,7},{7,6},{8,9},{9,8},{10,11... | collective-permute-start | bytes 3538952 | tf_op jit(solution)/shard_map/ppermute | solution.py:487
  78.3 5.8 %copy-start.2 = (bf16[8192,1024]{1,0:T(8,128)(2,1)S(1)}, bf16[8192,1024]{1,0:T(8,128)(2,1)}, u32[]{:S(2)}) copy-start(bf16[8192,1024]{1,0:T(8,128)(2,1)} %copy-done.1) | copy-start | bytes 50331652
  89.4 7.2 %collective-permute-start.3 = (bf16[8,128,512]{2,1,0:T(8,128)(2,1)}, bf16[8,128,512]{2,1,0:T(8,128)(2,1)}, u32[]{:S(2)}, u32[]{:S(2)}) collective-permute-start(bf16[8,128,512]{2,1,0:T(8,128)(2,1)} %get-tuple-element.70), channel_id=1, source_target_pairs={{0,1},{1,0},{2,3},{3,2},{4,5},{5,4},{6,7},{7,6},{8,9},{9,8},{10,11... | collective-permute-start | bytes 3145736 | tf_op jit(solution)/shard_map/ppermute | solution.py:489
  91.2 5.4 %copy-start.11 = (s32[16,512]{1,0:T(8,128)S(1)}, s32[16,512]{1,0:T(8,128)}, u32[]{:S(2)}) copy-start(s32[16,512]{1,0:T(8,128)} %get-tuple-element.68.idx_ref) | copy-start | bytes 98308
  91.2 5.4 %copy-start.17 = (bf16[192,512]{1,0:T(8,128)(2,1)S(1)}, bf16[192,512]{1,0:T(8,128)(2,1)}, u32[]{:S(2)}) copy-start(bf16[192,512]{1,0:T(8,128)(2,1)} %copy-done.16) | copy-start | bytes 589828
  93.2 14.3 %collective-permute-start.4 = (bf16[2,144,512]{2,1,0:T(8,128)(2,1)S(1)}, bf16[2,144,512]{2,1,0:T(8,128)(2,1)S(1)}, u32[]{:S(2)}, u32[]{:S(2)}) collective-permute-start(bf16[2,144,512]{2,1,0:T(8,128)(2,1)S(1)} %get-tuple-element.73), channel_id=1, source_target_pairs={{0,64},{32,96},{64,0},{96,32},{1,65},{33,97},{65,1},{97,33},{2,66}... | collective-permute-start | bytes 884744 | tf_op jit(solution)/shard_map/ppermute | solution.py:27
  94.0 16.1 %collective-permute-start.5 = (bf16[2,144,512]{2,1,0:T(8,128)(2,1)S(1)}, bf16[2,144,512]{2,1,0:T(8,128)(2,1)S(1)}, u32[]{:S(2)}, u32[]{:S(2)}) collective-permute-start(bf16[2,144,512]{2,1,0:T(8,128)(2,1)S(1)} %get-tuple-element.74), channel_id=1, source_target_pairs={{0,32},{32,64},{64,96},{96,0},{1,33},{33,65},{65,97},{97,1},{2,34}... | collective-permute-start | bytes 884744 | tf_op jit(solution)/shard_map/ppermute | solution.py:27
  94.4 15.6 %collective-permute-start.6 = (bf16[2,144,512]{2,1,0:T(8,128)(2,1)S(1)}, bf16[2,144,512]{2,1,0:T(8,128)(2,1)S(1)}, u32[]{:S(2)}, u32[]{:S(2)}) collective-permute-start(bf16[2,144,512]{2,1,0:T(8,128)(2,1)S(1)} %get-tuple-element.75), channel_id=1, source_target_pairs={{0,96},{32,0},{64,32},{96,64},{1,97},{33,1},{65,33},{97,65},{2,98}... | collective-permute-start | bytes 884744 | tf_op jit(solution)/shard_map/ppermute | solution.py:27
  96.6 5.8 %copy-start.3 = (bf16[8192,1024]{1,0:T(8,128)(2,1)S(1)}, bf16[8192,1024]{1,0:T(8,128)(2,1)}, u32[]{:S(2)}) copy-start(bf16[8192,1024]{1,0:T(8,128)(2,1)} %copy-done.1) | copy-start | bytes 50331652
  107.5 2.8 %copy-start.18 = (bf16[64,1024]{1,0:T(8,128)(2,1)}, bf16[64,1024]{1,0:T(8,128)(2,1)S(1)}, u32[]{:S(2)}) copy-start(bf16[64,1024]{1,0:T(8,128)(2,1)S(1)} %get-tuple-element.71) | copy-start | bytes 393220
  107.5 2.8 %copy-start.21 = (bf16[2,128,512]{2,1,0:T(8,128)(2,1)}, bf16[2,128,512]{2,1,0:T(8,128)(2,1)S(1)}, u32[]{:S(2)}) copy-start(bf16[2,128,512]{2,1,0:T(8,128)(2,1)S(1)} %get-tuple-element.81) | copy-start | bytes 786436
  107.5 2.8 %copy-start.22 = (bf16[2,128,512]{2,1,0:T(8,128)(2,1)}, bf16[2,128,512]{2,1,0:T(8,128)(2,1)S(1)}, u32[]{:S(2)}) copy-start(bf16[2,128,512]{2,1,0:T(8,128)(2,1)S(1)} %get-tuple-element.80) | copy-start | bytes 786436
  107.5 2.8 %copy-start.23 = (bf16[2,128,512]{2,1,0:T(8,128)(2,1)}, bf16[2,128,512]{2,1,0:T(8,128)(2,1)S(1)}, u32[]{:S(2)}) copy-start(bf16[2,128,512]{2,1,0:T(8,128)(2,1)S(1)} %get-tuple-element.79) | copy-start | bytes 786436
  110.3 21.8 %copy-start.9 = (f32[2,128,512]{2,1,0:T(8,128)S(1)}, f32[2,128,512]{2,1,0:T(8,128)}, u32[]{:S(2)}) copy-start(f32[2,128,512]{2,1,0:T(8,128)} %copy-done.8) | copy-start | bytes 1572868
  111.5 20.8 %all-to-all-start.1 = ((bf16[64,4,528]{2,1,0:T(4,128)(2,1)}), bf16[64,4,528]{2,1,0:T(4,128)(2,1)S(1)}, u32[]{:S(2)}, u32[]{:S(2)}) async-start(bf16[64,4,528]{2,1,0:T(4,128)(2,1)} %pad_maximum_fusion), calls=%async_computation.1 | async-start | bytes 655360 | tf_op jit(solution)/shard_map/all_to_all | solution.py:513
  116.4 9.3 %collective-permute-start.7 = (bf16[2,128,512]{2,1,0:T(8,128)(2,1)}, bf16[2,128,512]{2,1,0:T(8,128)(2,1)S(1)}, u32[]{:S(2)}, u32[]{:S(2)}) collective-permute-start(bf16[2,128,512]{2,1,0:T(8,128)(2,1)} %copy-done.23), channel_id=1, source_target_pairs={{0,64},{32,96},{64,0},{96,32},{1,65},{33,97},{65,1},{97,33},{2,66}... | collective-permute-start | bytes 786440 | tf_op jit(solution)/shard_map/ppermute | solution.py:27
  117.4 14.7 %collective-permute-start.8 = (bf16[2,128,512]{2,1,0:T(8,128)(2,1)}, bf16[2,128,512]{2,1,0:T(8,128)(2,1)S(1)}, u32[]{:S(2)}, u32[]{:S(2)}) collective-permute-start(bf16[2,128,512]{2,1,0:T(8,128)(2,1)} %copy-done.22), channel_id=1, source_target_pairs={{0,32},{32,64},{64,96},{96,0},{1,33},{33,65},{65,97},{97,1},{2,34}... | collective-permute-start | bytes 786440 | tf_op jit(solution)/shard_map/ppermute | solution.py:27
  117.7 14.4 %collective-permute-start.9 = (bf16[2,128,512]{2,1,0:T(8,128)(2,1)}, bf16[2,128,512]{2,1,0:T(8,128)(2,1)S(1)}, u32[]{:S(2)}, u32[]{:S(2)}) collective-permute-start(bf16[2,128,512]{2,1,0:T(8,128)(2,1)} %copy-done.21), channel_id=1, source_target_pairs={{0,96},{32,0},{64,32},{96,64},{1,97},{33,1},{65,33},{97,65},{2,98}... | collective-permute-start | bytes 786440 | tf_op jit(solution)/shard_map/ppermute | solution.py:27
  120.1 12.4 %collective-permute-start.10 = (bf16[64,1024]{1,0:T(8,128)(2,1)}, bf16[64,1024]{1,0:T(8,128)(2,1)}, u32[]{:S(2)}, u32[]{:S(2)}) collective-permute-start(bf16[64,1024]{1,0:T(8,128)(2,1)} %copy-done.25), channel_id=1, source_target_pairs={{0,31},{1,0},{2,1},{3,2},{4,3},{5,4},{6,5},{7,6},{8,7},{9,8},{10,9... | collective-permute-start | bytes 393224 | tf_op jit(solution)/shard_map/ppermute | solution.py:27
  121.4 11.1 %collective-permute-start.11 = (bf16[64,1024]{1,0:T(8,128)(2,1)}, bf16[64,1024]{1,0:T(8,128)(2,1)}, u32[]{:S(2)}, u32[]{:S(2)}) collective-permute-start(bf16[64,1024]{1,0:T(8,128)(2,1)} %copy-done.24), channel_id=1, source_target_pairs={{0,1},{1,2},{2,3},{3,4},{4,5},{5,6},{6,7},{7,8},{8,9},{9,10},{10,1... | collective-permute-start | bytes 393224 | tf_op jit(solution)/shard_map/ppermute | solution.py:27
  132.2 12.4 %copy-start.19 = (bf16[64,1024]{1,0:T(8,128)(2,1)S(1)}, bf16[64,1024]{1,0:T(8,128)(2,1)}, u32[]{:S(2)}) copy-start(bf16[64,1024]{1,0:T(8,128)(2,1)} %copy-done.18) | copy-start | bytes 393220
  133.2 24.3 %all-to-all-start.2 = ((bf16[64,4,512]{2,1,0:T(4,128)(2,1)}), bf16[64,4,512]{2,1,0:T(4,128)(2,1)S(1)}, u32[]{:S(2)}, u32[]{:S(2)}) async-start(bf16[64,4,512]{2,1,0:T(4,128)(2,1)} %all_to_all.18), calls=%async_computation.2 | async-start | bytes 524288 | tf_op jit(solution)/shard_map/all_to_all | solution.py:519
  (21 other events, 27.1 us)

commit v4 on v3

v4 whole, which is shorter than its diff:
```python
import functools
import jax
import jax.numpy as jnp
from jax import lax
from jax.experimental import pallas as pl
from jax.experimental.pallas import tpu as pltpu
from jax.sharding import Mesh, PartitionSpec as P

loss_scale = 8.0
smooth_sq = 0.01
TILE = 64
NCOL = 256
ROWS = 32
GROUP = 4
VMEM_LIMIT = 56 * 1024 * 1024
BACK = 2
GROUPS = 2
f32 = jnp.float32
bf16 = jnp.bfloat16
SPACE = ("y", "zl", "c")
ENS = ("zh", "x")
FIRST = ("x", "y")
SECOND = ("zh", "zl", "c")


def shifted(block, axes, distance):
    count = lax.axis_size(axes)
    return lax.ppermute(block, axes, [(i, (i + distance) % count) for i in range(count)])


def smooth_grad(diff):
    return diff / jnp.sqrt(diff * diff + smooth_sq)


def gelu_parts(v):
    c0 = 0.7978845608
    c1 = c0 * 0.044715
    sq = v * v
    t = jnp.tanh(v * (c0 + c1 * sq))
    u = 1.0 + t
    slope = v * (c0 + (3.0 * c1) * sq)
    return v * u, u * (1.0 + (1.0 - t) * slope)


def whole(array):
    zeros = (0,) * len(array.shape)
    return pl.BlockSpec(array.shape, lambda *_: zeros)


def params():
    return pltpu.CompilerParams(vmem_limit_bytes=VMEM_LIMIT)


def forward_kernel(
    slots,
    members,
    below_ref,
    here_ref,
    above_ref,
    wsrc_ref,
    dst_ref,
    idx_ref,
    scale_ref,
    wout_ref,
    gp_ref,
    agg_ref,
    sum_ref,
    pred_ref,
    sent_ref,
    feats,
    rhs,
    hot,
    pre,
):
    step = pl.program_id(0)
    nodes, width = feats.shape
    depth = rhs.shape[0]
    tile = depth - nodes
    block = below_ref.shape[0]

    @pl.when(step == 0)
    def _():
        for i, ref in enumerate((below_ref, here_ref, above_ref)):
            feats[i * block : (i + 1) * block, :] = ref[...]
        for n in range(width // NCOL):
            cols = slice(n * NCOL, (n + 1) * NCOL)
            rhs[:nodes, cols] = jnp.dot(
                feats[...], wsrc_ref[:, cols], preferred_element_type=f32
            ).astype(bf16)

    base = pl.multiple_of(step * tile, tile)
    rhs[nodes:, :] = dst_ref[...]
    lane = lax.broadcasted_iota(jnp.int32, (tile, depth), 1)
    row = lax.broadcasted_iota(jnp.int32, (tile, depth), 0)
    eye = lane == row + nodes
    for k in range(slots):
        col = idx_ref[:, k : k + 1]
        hit = (lane == col) | (eye & (col >= 0))
        hot[k * tile : (k + 1) * tile, :] = jnp.where(hit, 1.0, 0.0).astype(bf16)
    for n in range(width // NCOL):
        cols = slice(n * NCOL, (n + 1) * NCOL)
        pre[n % 2] = jnp.dot(hot[...], rhs[:, cols], preferred_element_type=f32).astype(bf16)
        for r in range(0, tile, ROWS):
            acc_g = jnp.zeros((ROWS, NCOL), f32)
            acc_s = jnp.zeros((ROWS, NCOL), f32)
            for k in range(slots):
                rows = slice(k * tile + r, k * tile + r + ROWS)
                value, grad = gelu_parts(pre[n % 2, rows, :])
                gp_ref[rows, cols] = grad
                if k % GROUP == 0:
                    some_g, some_s = value, grad
                else:
                    some_g, some_s = some_g + value, some_s + grad
                if k % GROUP == GROUP - 1:
                    acc_g = acc_g + some_g.astype(f32)
                    acc_s = acc_s + some_s.astype(f32)
            scale = scale_ref[r : r + ROWS, :]
            agg_ref[pl.ds(pl.multiple_of(base + r, ROWS), ROWS), cols] = (acc_g * scale).astype(bf16)
            sum_ref[r : r + ROWS, cols] = (acc_s - (slots - 0.5 / scale)).astype(bf16)

    @pl.when(step == pl.num_programs(0) - 1)
    def _():
        pred = lax.dot_general(
            wout_ref[...], agg_ref[...], (((1,), (1,)), ((), ())), preferred_element_type=f32
        )
        pred_ref[...] = pred
        for e in range(members):
            sent_ref[e] = pred.astype(bf16)


def forward(below, here, above, w_src, dst, idx, scale, wout_t, members):
    grid_rows, width = dst.shape
    nodes = 3 * here.shape[0]
    slots = idx.shape[1]
    outs = wout_t.shape[0]
    step = lambda t: (t, 0)
    out_shape = [
        jax.ShapeDtypeStruct((grid_rows * slots, width), bf16),
        jax.ShapeDtypeStruct((grid_rows, width), bf16),
        jax.ShapeDtypeStruct((grid_rows, width), bf16),
        jax.ShapeDtypeStruct((outs, grid_rows), f32),
        jax.ShapeDtypeStruct((members, outs, grid_rows), bf16),
    ]
    return pl.pallas_call(
        functools.partial(forward_kernel, slots, members),
        grid=(grid_rows // TILE,),
        in_specs=[whole(below), whole(here), whole(above), whole(w_src)]
        + [
            pl.BlockSpec((TILE, width), step),
            pl.BlockSpec((TILE, slots), step),
            pl.BlockSpec((TILE, 1), step),
            whole(wout_t),
        ],
        out_specs=[
            pl.BlockSpec((TILE * slots, width), step),
            whole(out_shape[1]),
            pl.BlockSpec((TILE, width), step),
            whole(out_shape[3]),
            whole(out_shape[4]),
        ],
        out_shape=out_shape,
        scratch_shapes=[
            pltpu.VMEM((nodes, width), bf16),
            pltpu.VMEM((nodes + TILE, width), bf16),
            pltpu.VMEM((TILE * slots, nodes + TILE), bf16),
            pltpu.VMEM((2, TILE * slots, NCOL), bf16),
        ],
        compiler_params=params(),
        cost_estimate=pl.CostEstimate(
            flops=2 * grid_rows * slots * 256 * width,
            bytes_accessed=2 * grid_rows * slots * width,
            transcendentals=grid_rows * slots * width,
        ),
        name="forward",
    )(below, here, above, w_src, dst, idx, scale, wout_t)


def middle_kernel(
    core_ref,
    every_ref,
    pred_ref,
    truth_ref,
    area_ref,
    var_ref,
    wout_ref,
    scale_ref,
    sum_ref,
    agg_hbm,
    grid_hbm,
    lead_hbm,
    own_hbm,
    far_hbm,
    agg_ref,
    grid_ref,
    lead_ref,
    own_ref,
    far_ref,
    ddst,
    part,
    sems,
):
    loads = [
        pltpu.make_async_copy(agg_hbm, agg_ref, sems.at[0]),
        pltpu.make_async_copy(grid_hbm, grid_ref, sems.at[1]),
    ]
    stores = [
        pltpu.make_async_copy(lead_ref, lead_hbm, sems.at[2]),
        pltpu.make_async_copy(far_ref, far_hbm, sems.at[3]),
        pltpu.make_async_copy(own_ref, own_hbm, sems.at[4]),
    ]
    for copy in loads:
        copy.start()
    width = sum_ref.shape[1]
    half = width // 2
    members = every_ref.shape[0]
    outs = pred_ref.shape[0]
    core = core_ref[0]

    pred = pred_ref[...]
    pair = -smooth_grad(pred - pred.astype(bf16).astype(f32))
    for e in range(members):
        pair = pair + smooth_grad(pred - every_ref[e].astype(f32))
    weighting = loss_scale * area_ref[...] * var_ref[...]
    dpred = (
        weighting
        * (smooth_grad(pred - truth_ref[...]) / members - pair / (members * (members - 1)))
    ).astype(bf16)
    for n in range(width // NCOL):
        cols = slice(n * NCOL, (n + 1) * NCOL)
        dagg = lax.dot_general(
            dpred, wout_ref[:, cols], (((0,), (0,)), ((), ())), preferred_element_type=f32
        )
        dagg = dagg * scale_ref[...]
        lead_ref[:, cols] = dagg.astype(bf16)
        ddst[:, cols] = (dagg * sum_ref[:, cols].astype(f32)).astype(bf16)

    stores[0].start()
    for copy in loads:
        copy.wait()
    mine = pl.ds(pl.multiple_of(core * half, half), half)
    other = pl.ds(pl.multiple_of((1 - core) * half, half), half)
    part[...] = jnp.dot(dpred, agg_ref[...], preferred_element_type=f32)
    few = outs // 2
    for ref, columns, which, store in (
        (far_ref, other, 1 - core, stores[1]),
        (own_ref, mine, core, stores[2]),
    ):
        ref[:width, :] = lax.dot_general(
            grid_ref[...], ddst[:, columns], (((0,), (0,)), ((), ())), preferred_element_type=f32
        ).astype(bf16)
        at = pl.ds(pl.multiple_of(which * few, few), few)
        ref[width : width + few, :] = part[at, :half].astype(bf16)
        ref[width + few :, :] = part[at, half:].astype(bf16)
        store.start()
    for copy in stores:
        copy.wait()


def prefetched(count, ins, outs, scratch):
    return pltpu.PrefetchScalarGridSpec(
        num_scalar_prefetch=1, grid=(count,), in_specs=ins, out_specs=outs, scratch_shapes=scratch
    )


def middle(core, everyone, pred, truth_t, area, var, wout_t, scale, sums, agg, grid_embed):
    grid_rows, width = sums.shape
    outs = pred.shape[0]
    block = (width + outs, width // 2)
    anywhere = pl.BlockSpec(memory_space=pl.ANY)
    small = (everyone, pred, truth_t, area, var, wout_t, scale, sums)
    return pl.pallas_call(
        middle_kernel,
        grid_spec=prefetched(
            1,
            [whole(x) for x in small] + [anywhere] * 2,
            [anywhere] * 3,
            [
                pltpu.VMEM((grid_rows, width), bf16),
                pltpu.VMEM((grid_rows, width), bf16),
                pltpu.VMEM((grid_rows, width), bf16),
                pltpu.VMEM(block, bf16),
                pltpu.VMEM(block, bf16),
                pltpu.VMEM((grid_rows, width), bf16),
                pltpu.VMEM((outs, width), f32),
                pltpu.SemaphoreType.DMA((5,)),
            ],
        ),
        out_shape=[
            jax.ShapeDtypeStruct((grid_rows, width), bf16),
            jax.ShapeDtypeStruct(block, bf16),
            jax.ShapeDtypeStruct(block, bf16),
        ],
        compiler_params=params(),
        cost_estimate=pl.CostEstimate(
            flops=2 * grid_rows * width * width, bytes_accessed=10 * grid_rows * width, transcendentals=0
        ),
        name="middle",
    )(core, everyone, pred, truth_t, area, var, wout_t, scale, sums, agg, grid_embed)


def scatter_step(slots, gp_ref, lead_ref, idx_ref, hot, prod, acc):
    nodes, half = acc.shape
    wide = lead_ref.shape[0]

    @pl.when(pl.program_id(0) == 0)
    def _():
        acc[...] = jnp.zeros_like(acc)

    node = lax.broadcasted_iota(jnp.int32, (nodes, wide), 0)
    for k in range(slots):
        hot[:, k * wide : (k + 1) * wide] = jnp.where(node == idx_ref[k : k + 1, :], 1.0, 0.0).astype(bf16)
    for start in range(0, wide, TILE):
        lead = lead_ref[start : start + TILE, :]
        for k in range(slots):
            at = start * slots + k * TILE
            to = k * wide + start
            prod[to : to + TILE, :] = gp_ref[at : at + TILE, :] * lead
    for n in range(half // NCOL):
        here = slice(n * NCOL, (n + 1) * NCOL)
        acc[:, here] += jnp.dot(hot[...], prod[:, here], preferred_element_type=f32)


def far_kernel(
    slots, core_ref, gp_ref, lead_ref, idx_ref, below_ref, here_ref, above_ref, wide_ref, part_ref, hot, prod, acc
):
    scatter_step(slots, gp_ref, lead_ref, idx_ref, hot, prod, acc)

    @pl.when(pl.program_id(0) == pl.num_programs(0) - 1)
    def _():
        wide_ref[...] = acc[...].astype(bf16)
        feats = jnp.concatenate([below_ref[...], here_ref[...], above_ref[...]], axis=0)
        part_ref[...] = lax.dot_general(
            feats, wide_ref[...], (((0,), (0,)), ((), ())), preferred_element_type=f32
        ).astype(bf16)


def own_kernel(
    slots,
    place_ref,
    gp_ref,
    lead_ref,
    idx_ref,
    below_ref,
    here_ref,
    above_ref,
    widefar_ref,
    srcfar_ref,
    dstown_ref,
    dstfar_ref,
    lower_ref,
    centre_ref,
    upper_ref,
    total_ref,
    hot,
    prod,
    acc,
):
    core = place_ref[0]
    scatter_step(slots, gp_ref, lead_ref, idx_ref, hot, prod, acc)

    @pl.when(pl.program_id(0) == pl.num_programs(0) - 1)
    def _():
        half = acc.shape[1]
        block = lower_ref.shape[0]
        mine = pl.ds(pl.multiple_of(core * half, half), half)
        other = pl.ds(pl.multiple_of((1 - core) * half, half), half)
        wide = acc[...].astype(bf16)
        for i, ref in enumerate((lower_ref, centre_ref, upper_ref)):
            ref[:, mine] = wide[i * block : (i + 1) * block, :]
            ref[:, other] = widefar_ref[i * block : (i + 1) * block, :]
        feats = jnp.concatenate([below_ref[...], here_ref[...], above_ref[...]], axis=0)
        total = lax.dot_general(
            feats, wide, (((0,), (0,)), ((), ())), preferred_element_type=f32
        )
        width = total_ref.shape[0] * total_ref.shape[1]
        few = (dstown_ref.shape[0] - width) // 2

        def give(columns, values):
            chunks, rows = total_ref.shape[0], total_ref.shape[1] // GROUPS
            for zh in range(GROUPS):
                some = values[zh * chunks * rows : (zh + 1) * chunks * rows, :]
                total_ref[:, zh * rows : (zh + 1) * rows, columns] = some.astype(bf16).reshape(
                    chunks, rows, values.shape[1]
                )

        give(slice(0, half), total + srcfar_ref[...].astype(f32))
        give(
            slice(half, 2 * half),
            dstown_ref[:width, :].astype(f32) + dstfar_ref[:width, :].astype(f32),
        )
        out = dstown_ref[width:, :].astype(f32) + dstfar_ref[width:, :].astype(f32)
        out = jnp.concatenate([out[:few, :], out[few:, :]], axis=1)
        give(slice(2 * half, 2 * half + few), out.T)


def scatter_scratch(slots, nodes, half):
    wide = BACK * TILE * slots
    return [
        pltpu.VMEM((nodes, wide), bf16),
        pltpu.VMEM((wide, half), bf16),
        pltpu.VMEM((nodes, half), f32),
    ]


def scatter_cost(gp):
    return pl.CostEstimate(flops=gp.size * 256, bytes_accessed=gp.size, transcendentals=0)


def backward(kernel, name, column, mine, gp, lead, idx_t, feats, extra, out_shape):
    grid_rows, width = lead.shape
    slots = idx_t.shape[0]
    nodes = 3 * feats[0].shape[0]
    half = width // 2
    rows = BACK * TILE
    half_at = lambda t, core: (t, column(core[0]))
    others = list(feats) + extra
    return pl.pallas_call(
        functools.partial(kernel, slots),
        grid_spec=prefetched(
            grid_rows // rows,
            [
                pl.BlockSpec((rows * slots, half), half_at),
                pl.BlockSpec((rows, half), half_at),
                pl.BlockSpec((slots, rows), lambda t, core: (0, t)),
            ]
            + [whole(x) for x in others],
            [whole(x) for x in out_shape],
            scatter_scratch(slots, nodes, half),
        ),
        out_shape=out_shape,
        compiler_params=params(),
        cost_estimate=scatter_cost(gp),
        name=name,
    )(mine, gp, lead, idx_t, *others)


def backward_far(mine, gp, lead, idx_t, feats):
    half = lead.shape[1] // 2
    out_shape = [
        jax.ShapeDtypeStruct((3 * feats[0].shape[0], half), bf16),
        jax.ShapeDtypeStruct((lead.shape[1], half), bf16),
    ]
    column = lambda core: 1 - core
    return backward(far_kernel, "backward_far", column, mine, gp, lead, idx_t, feats, [], out_shape)


def backward_own(mine, gp, lead, idx_t, feats, wide_far, src_far, dst_own, dst_far, chunks):
    width = lead.shape[1]
    columns = width + (dst_own.shape[0] - width) // 2
    out_shape = [jax.ShapeDtypeStruct((feats[0].shape[0], width), bf16)] * 3 + [
        jax.ShapeDtypeStruct((chunks, width // chunks, columns), bf16)
    ]
    column = lambda core: core
    return backward(
        own_kernel,
        "backward_own",
        column,
        mine,
        gp,
        lead,
        idx_t,
        feats,
        [wide_far, src_far, dst_own, dst_far],
        out_shape,
    )


def body(
    mesh_feats,
    grid_embed,
    w_src,
    w_dst,
    w_out,
    truth,
    area_weight,
    var_weight,
    neighbour,
    edge_mask,
):
    own = mesh_feats[0]
    node_rows, width = own.shape
    grid_rows, slots = neighbour.shape
    half = width // 2
    space_count = lax.axis_size(SPACE)
    block_id = lax.axis_index(SPACE)
    members = lax.axis_size(ENS)
    swap = [(0, 1), (1, 0)]
    core = lax.axis_index("c")
    mine = jnp.full((1,), core, jnp.int32)

    below = shifted(own, SPACE, 1)
    above = shifted(own, SPACE, -1)

    dst = jnp.dot(grid_embed, w_dst, preferred_element_type=f32).astype(bf16)
    local = jnp.mod(neighbour.T - (block_id - 1) * node_rows, node_rows * space_count)
    idx_t = jnp.where(edge_mask.T > 0, local, -1)
    idx = idx_t.T
    scale = 0.5 / jnp.sum(edge_mask.T.astype(f32), axis=0)[:, None]
    wout_t = w_out.T
    truth_t = truth.T
    var = var_weight[:, None]
    area = area_weight[None, :]
    dst, idx, idx_t, scale, wout_t, truth_t, var, area, below = lax.optimization_barrier(
        (dst, idx, idx_t, scale, wout_t, truth_t, var, area, below)
    )
    feats = (below, own, above)
    gp, agg, sums, pred, sent = forward(*feats, w_src, dst, idx, scale, wout_t, members)
    everyone = lax.all_to_all(sent, ENS, 0, 0, tiled=True)
    lead, dst_own, dst_far = middle(
        mine, everyone, pred, truth_t, area, var, wout_t, scale, sums, agg, grid_embed
    )
    dst_far = lax.ppermute(dst_far, "c", swap)
    wide_far, src_far = backward_far(mine, gp, lead, idx_t, feats)
    src_far = lax.ppermute(src_far, "c", swap)
    lower, centre, upper, total = backward_own(
        mine, gp, lead, idx_t, feats, wide_far, src_far, dst_own, dst_far, lax.axis_size(FIRST)
    )
    from_above = shifted(lower, SPACE, -1)
    from_below = shifted(upper, SPACE, 1)

    parts = lax.all_to_all(total, FIRST, 0, 0, tiled=True)
    total = jnp.sum(parts.astype(f32), axis=0).astype(bf16)
    total, from_above, from_below = lax.optimization_barrier((total, from_above, from_below))
    parts = lax.all_to_all(total, SECOND, 0, 0, tiled=True)
    dproj = (centre.astype(f32) + from_above.astype(f32) + from_below.astype(f32)).astype(bf16)
    grad_mesh = lax.dot_general(
        dproj, w_src, (((1,), (1,)), ((), ())), preferred_element_type=f32
    ).astype(bf16)
    rows_out = width // lax.axis_size(ENS + SPACE)
    total = jnp.sum(parts.reshape(-1, 2, rows_out, parts.shape[1]).astype(f32), axis=0)
    joined = lambda a, b: jnp.concatenate([total[0, :, a:b], total[1, :, a:b]], axis=1)
    return (
        grad_mesh[None],
        joined(0, half),
        joined(half, 2 * half),
        joined(2 * half, total.shape[-1]),
    )


def solution(mesh):
    fine = Mesh(mesh.devices.reshape(2, 4, 4, 4, 2), ("zh", "x", "y", "zl", "c"))
    everywhere = ENS + SPACE
    in_specs = (
        P(ENS, SPACE, None),
        P(SPACE, None),
        P(),
        P(),
        P(),
        P(SPACE, None),
        P(SPACE),
        P(),
        P(SPACE, None),
        P(SPACE, None),
    )
    out_specs = (
        P(ENS, SPACE, None),
        P(everywhere, None),
        P(everywhere, None),
        P(everywhere, None),
    )
    return jax.shard_map(body, mesh=fine, in_specs=in_specs, out_specs=out_specs, check_vma=False)
```

time: 159 us -> 141 us (0.89)
  local copies, waits for them, and re-layouts: 37.8 us -> 5.81 us
  waiting for transfers between devices: 31.8 us -> 48.6 us
  starting transfers between devices: 44.2 us -> 30.8 us
  Pallas kernels: 30.9 us -> 40.3 us
    unnamed x76 -> x20, local copies, waits for them, and re-layouts: 36.2 us -> 2.7 us
    all_to_all x2, waiting for transfers between devices: 9.62 us -> 36.2 us  [the longest x1 29.9 us: body(): parts = lax.all_to_all(total, FIRST, 0, 0, tiled=True)]
    ppermute x10 -> x4, waiting for transfers between devices: 12.1 us -> 0.01 us  [shifted(): lax.ppermute(block, axes, [(i, (i + distance) % count) for i in range(cou...]
    pallas_call x4 -> x3, Pallas kernels: 13.7 us -> 21.7 us  [the longest x2 16.2 us: backward(): pl.pallas_call(functools.partial(kernel, slots), grid_spec=prefetched(gri...]
    ppermute x10 -> x4, starting transfers between devices: 12.8 us -> 5.14 us  [shifted(): lax.ppermute(block, axes, [(i, (i + distance) % count) for i in range(cou...]
    all_to_all x2, starting transfers between devices: 15.5 us -> 9.47 us  [the longest x1 4.88 us: body(): parts = lax.all_to_all(total, SECOND, 0, 0, tiled=True)]
    ppermute x1, waiting for transfers between devices: 0.01 us -> 2.82 us  [body(): src_far = lax.ppermute(src_far, 'c', swap)]
    optimization_barrier x3, local copies, waits for them, and re-layouts: 0.36 us -> 2.4 us  [body(): lax.optimization_barrier((dst, idx, idx_t, scale, wout_t, truth_t, var, a...]
  transfers between devices with their start and end apart: 15 -> 9, of which waited for: 5 -> 4; matrix products, arithmetic and copies ran while one was open for 7% -> 10% of each run, Pallas kernels for 7% -> 5%
where the time goes in v4:
time: 141 us; the launch traced here: 139 us
  waiting for transfers between devices  48.6 us (34%)
  Pallas kernels  40.3 us (29%)
  starting transfers between devices  30.8 us (22%)
  matrix products  6.48 us (5%)
  other arithmetic  6.32 us (4%)
  local copies, waits for them, and re-layouts  5.81 us (4%)
    all_to_all x1, waiting for transfers between devices, body(): parts = lax.all_to_all(total, FIRST, 0, 0, tiled=True)  29.9 us
    pallas_call x1, Pallas kernels, forward(): pl.pallas_call(functools.partial(forward_kernel, slots, members), grid=(g...  18.6 us
    pallas_call x2, Pallas kernels, backward(): pl.pallas_call(functools.partial(kernel, slots), grid_spec=prefetched(gri...  16.2 us
    all_to_all x1, starting transfers between devices, body(): everyone = lax.all_to_all(sent, ENS, 0, 0, tiled=True)  10.1 us
    all_to_all x1, waiting for transfers between devices, body(): everyone = lax.all_to_all(sent, ENS, 0, 0, tiled=True)  9.5 us
    all_to_all x1, waiting for transfers between devices, body(): parts = lax.all_to_all(total, SECOND, 0, 0, tiled=True)  6.3 us
    ppermute x1, starting transfers between devices, body(): dst_far = lax.ppermute(dst_far, 'c', swap)  6.11 us
    pallas_call x1, Pallas kernels, middle(): pl.pallas_call(middle_kernel, grid_spec=prefetched(1, [whole(x) for x in...  5.56 us
  transfers between devices with their start and end apart: 9, of which 4 were waited for; matrix products, arithmetic and copies ran while one was open for 10% of the time, Pallas kernels for 5%

profile of v4, /device:TPU:1, one launch (start us, length us, event | category | flops | bytes accessed | tf_op | source)
XLA Modules:
  0.0 139.1 jit_solution(11368761175103563761)
XLA Ops:
  0.6 3.3 %collective-permute-start.1 = (bf16[64,1024]{1,0:T(8,128)(2,1)}, bf16[64,1024]{1,0:T(8,128)(2,1)S(1)}, u32[]{:S(2)}, u32[]{:S(2)}) collective-permute-start(bf16[64,1024]{1,0:T(8,128)(2,1)} %bitcast.33), channel_id=1, source_target_pairs={{0,31},{1,0},{2,1},{3,2},{4,3},{5,4},{6,5},{7,6},{8,7},{9,8},{10,9... | collective-permute-start | bytes 393224 | tf_op jit(solution)/shard_map/ppermute | solution.py:28
  4.0 0.8 convert_reduce_fusion.1
  4.8 1.4 %fusion.4 = (s32[16,512]{1,0:T(8,128)}, pred[512,16]{0,1:T(8,128)(4,1)S(1)}) fusion(s32[512,16]{0,1:T(8,128)} %param.18, s32[]{:T(128)S(6)} %mul.11, s32[512,16]{0,1:T(8,128)} %param.19), kind=kLoop, calls=%fused_computation.14 | loop fusion | flops 114688 | bytes 106500 | tf_op jit(solution)/shard_map/jit(_where)/select_n | solution.py:496
  6.2 0.8 fusion.2
  6.9 3.5 %convolution_convert_fusion.dst_ref = bf16[512,1024]{1,0:T(8,128)(2,1)} fusion(bf16[512,1024]{1,0:T(8,128)(2,1)} %grid_hbm.1, bf16[1024,1024]{1,0:T(8,128)(2,1)S(1)} %copy-done), kind=kOutput, calls=%fused_computation | convolution fusion | flops 1074266112 | bytes 4194304 | tf_op jit(solution)/shard_map/dot_general | solution.py:494
  10.4 0.8 copy.25.scale_ref
  11.3 0.9 copy.24.idx_ref
  12.1 0.6 copy-done.3
  12.8 18.6 %forward.1 = (bf16[8192,1024]{1,0:T(8,128)(2,1)}, bf16[512,1024]{1,0:T(8,128)(2,1)}, bf16[512,1024]{1,0:T(8,128)(2,1)}, f32[32,512]{1,0:T(8,128)}, bf16[8,32,512]{2,1,0:T(8,128)(2,1)}) custom-call(bf16[64,1024]{1,0:T(8,128)(2,1)} %copy-done.4, bf16[64,1024]{1,0:T(8,128)(2,1)} %bitcast.35, bf16[64,1024]{1,0:T(8,128)(2,1)} %copy-done.3, ...), custom_call_target="tpu_custom_call" | custom-call | flops 4294967296 | bytes 16777216 | tf_op jit(solution)/shard_map/forward/pallas_call | solution.py:144
  31.4 10.1 %all-to-all-start = ((bf16[8,32,512]{2,1,0:T(8,128)(2,1)}), bf16[8,32,512]{2,1,0:T(8,128)(2,1)S(1)}, u32[]{:S(2)}, u32[]{:S(2)}) async-start(bf16[8,32,512]{2,1,0:T(8,128)(2,1)} %get-tuple-element.36), calls=%async_computation | async-start | bytes 524288 | tf_op jit(solution)/shard_map/all_to_all | solution.py:508
  41.4 0.7 copy.26.var_ref
  42.1 9.5 %all-to-all-done.every_ref = bf16[8,32,512]{2,1,0:T(8,128)(2,1)S(1)} async-done(((bf16[8,32,512]{2,1,0:T(8,128)(2,1)}), bf16[8,32,512]{2,1,0:T(8,128)(2,1)S(1)}, u32[]{:S(2)}, u32[]{:S(2)}) %all-to-all-start) | async-done | bytes 262176 | tf_op jit(solution)/shard_map/all_to_all | solution.py:508
  51.6 0.7 copy-done.5
  52.3 5.6 %middle.1 = (bf16[512,1024]{1,0:T(8,128)(2,1)}, bf16[1056,512]{1,0:T(8,128)(2,1)}, bf16[1056,512]{1,0:T(8,128)(2,1)}) custom-call(s32[1]{0:T(128)} %bitcast.core_ref.place_ref, bf16[8,32,512]{2,1,0:T(8,128)(2,1)} %copy-done.5, f32[32,512]{1,0:T(8,128)} %get-tuple-element.37.pred_ref, f32[32,512]{1,0:T(8,128)} %bitcast.42, f32[1,512]{1,0:T(1,128)} %bitcast.43, ...), custom_call_target="tpu_custom_call" | custom-call | flops 1073741824 | bytes 5242880 | tf_op jit(solution)/shard_map/middle/pallas_call | solution.py:271
  57.9 6.1 %collective-permute-start.3 = (bf16[1056,512]{1,0:T(8,128)(2,1)}, bf16[1056,512]{1,0:T(8,128)(2,1)S(1)}, u32[]{:S(2)}, u32[]{:S(2)}) collective-permute-start(bf16[1056,512]{1,0:T(8,128)(2,1)} %get-tuple-element.48), channel_id=1, source_target_pairs={{0,1},{1,0},{2,3},{3,2},{4,5},{5,4},{6,7},{7,6},{8,9},{9,8},{10,11... | collective-permute-start | bytes 3244040 | tf_op jit(solution)/shard_map/ppermute | solution.py:512
  64.0 7.0 %backward_far.1 = (bf16[192,512]{1,0:T(8,128)(2,1)}, bf16[1024,512]{1,0:T(8,128)(2,1)}) custom-call(s32[1]{0:T(128)} %bitcast.core_ref.place_ref, bf16[8192,1024]{1,0:T(8,128)(2,1)} %get-tuple-element.35.gp_ref, bf16[512,1024]{1,0:T(8,128)(2,1)} %get-tuple-element.43.lead_ref, s32[16,512]{1,0:T(8,128)} %get-tuple-element.44.idx_ref, ...), custom_call_target="tpu_custom_call" | custom-call | flops 2147483648 | bytes 8388608 | tf_op jit(solution)/shard_map/backward_far/pallas_call | solution.py:417
  71.1 2.8 %collective-permute-done.2.srcfar_ref = bf16[1024,512]{1,0:T(8,128)(2,1)S(1)} collective-permute-done((bf16[1024,512]{1,0:T(8,128)(2,1)}, bf16[1024,512]{1,0:T(8,128)(2,1)S(1)}, u32[]{:S(2)}, u32[]{:S(2)}) %collective-permute-start.2) | collective-permute-done | bytes 1048608 | tf_op jit(solution)/shard_map/ppermute | solution.py:514
  73.9 1.0 copy-done.2
  74.9 0.3 copy-done.1
  75.2 9.1 %backward_own.1 = (bf16[64,1024]{1,0:T(8,128)(2,1)}, bf16[64,1024]{1,0:T(8,128)(2,1)}, bf16[64,1024]{1,0:T(8,128)(2,1)}, bf16[16,64,1040]{2,1,0:T(8,128)(2,1)}) custom-call(s32[1]{0:T(128)} %bitcast.core_ref.place_ref, bf16[8192,1024]{1,0:T(8,128)(2,1)} %get-tuple-element.35.gp_ref, bf16[512,1024]{1,0:T(8,128)(2,1)} %get-tuple-element.43.lead_ref, ...), custom_call_target="tpu_custom_call" | custom-call | flops 2147483648 | bytes 8388608 | tf_op jit(solution)/shard_map/backward_own/pallas_call | solution.py:417
  84.4 4.6 %all-to-all-start.1 = ((bf16[16,64,1040]{2,1,0:T(8,128)(2,1)}), bf16[16,64,1040]{2,1,0:T(8,128)(2,1)}, u32[]{:S(2)}, u32[]{:S(2)}) async-start(bf16[16,64,1040]{2,1,0:T(8,128)(2,1)} %get-tuple-element.50), calls=%async_computation.1 | async-start | bytes 4718592 | tf_op jit(solution)/shard_map/all_to_all | solution.py:521
  89.0 0.2 collective-permute-start.4
  89.2 1.6 %collective-permute-start.5 = (bf16[64,1024]{1,0:T(8,128)(2,1)S(1)}, bf16[64,1024]{1,0:T(8,128)(2,1)S(1)}, u32[]{:S(2)}, u32[]{:S(2)}) collective-permute-start(bf16[64,1024]{1,0:T(8,128)(2,1)S(1)} %copy-done.8), channel_id=1, source_target_pairs={{0,1},{1,2},{2,3},{3,4},{4,5},{5,6},{6,7},{7,8},{8,9},{9,10},{10,1... | collective-permute-start | bytes 393224 | tf_op jit(solution)/shard_map/ppermute | solution.py:28
  90.8 29.9 %all-to-all-done.1 = bf16[16,64,1040]{2,1,0:T(8,128)(2,1)} async-done(((bf16[16,64,1040]{2,1,0:T(8,128)(2,1)}), bf16[16,64,1040]{2,1,0:T(8,128)(2,1)}, u32[]{:S(2)}, u32[]{:S(2)}) %all-to-all-start.1) | async-done | bytes 2129952 | tf_op jit(solution)/shard_map/all_to_all | solution.py:521
  120.7 2.0 %reduce_sum.31 = bf16[64,1040]{1,0:T(8,128)(2,1)S(1)} reduce(bf16[16,64,1040]{2,1,0:T(8,128)(2,1)} %all-to-all-done.1, bf16[]{:T(256)} %constant.44.clone.1), dimensions={0}, to_apply=%region_1.2 | reduce | flops 998400 | bytes 2263042 | tf_op jit(solution)/shard_map/reduce_sum | solution.py:522
  122.8 0.7 all_to_all.14
  123.5 4.9 %all-to-all-start.2 = ((bf16[16,4,1040]{2,1,0:T(4,128)(2,1)}), bf16[16,4,1040]{2,1,0:T(4,128)(2,1)S(1)}, u32[]{:S(2)}, u32[]{:S(2)}) async-start(bf16[16,4,1040]{2,1,0:T(4,128)(2,1)} %all_to_all.14), calls=%async_computation.2 | async-start | bytes 294912 | tf_op jit(solution)/shard_map/all_to_all | solution.py:524
  128.4 3.0 %fusion = bf16[1,64,1024]{2,1,0:T(8,128)(2,1)} fusion(bf16[1024,1024]{1,0:T(8,128)(2,1)} %wsrc_ref.1, bf16[64,1024]{1,0:T(8,128)(2,1)S(1)} %collective-permute-done.5, bf16[64,1024]{1,0:T(8,128)(2,1)S(1)} %collective-permute-done.4, bf16[64,1024]{1,0:T(8,128)(2,1)S(1)} %copy-done.6), kind=kOutput, calls=%fused_computation.2 | convolution fusion | flops 134676480 | bytes 2621440 | tf_op jit(solution)/shard_map/dot_general | solution.py:526
  131.4 6.3 %all-to-all-done.2 = bf16[16,4,1040]{2,1,0:T(4,128)(2,1)S(1)} async-done(((bf16[16,4,1040]{2,1,0:T(4,128)(2,1)}), bf16[16,4,1040]{2,1,0:T(4,128)(2,1)S(1)}, u32[]{:S(2)}, u32[]{:S(2)}) %all-to-all-start.2) | async-done | bytes 133152 | tf_op jit(solution)/shard_map/all_to_all | solution.py:524
  137.7 0.1 convert_reduce_fusion
  137.8 0.7 pad_maximum_fusion.2
  138.4 0.6 pad_maximum_fusion
  (26 shorter events, 0.1 us)
Async XLA Ops:
  0.6 6.3 %copy-start = (bf16[1024,1024]{1,0:T(8,128)(2,1)S(1)}, bf16[1024,1024]{1,0:T(8,128)(2,1)}, u32[]{:S(2)}) copy-start(bf16[1024,1024]{1,0:T(8,128)(2,1)} %param.13) | copy-start | bytes 6291460
  0.6 11.5 %collective-permute-start.1 = (bf16[64,1024]{1,0:T(8,128)(2,1)}, bf16[64,1024]{1,0:T(8,128)(2,1)S(1)}, u32[]{:S(2)}, u32[]{:S(2)}) collective-permute-start(bf16[64,1024]{1,0:T(8,128)(2,1)} %bitcast.33), channel_id=1, source_target_pairs={{0,31},{1,0},{2,1},{3,2},{4,3},{5,4},{6,5},{7,6},{8,7},{9,8},{10,9... | collective-permute-start | bytes 393224 | tf_op jit(solution)/shard_map/ppermute | solution.py:28
  4.0 6.5 %collective-permute-start = (bf16[64,1024]{1,0:T(8,128)(2,1)}, bf16[64,1024]{1,0:T(8,128)(2,1)S(1)}, u32[]{:S(2)}, u32[]{:S(2)}) collective-permute-start(bf16[64,1024]{1,0:T(8,128)(2,1)} %bitcast.34), channel_id=1, source_target_pairs={{0,1},{1,2},{2,3},{3,4},{4,5},{5,6},{6,7},{7,8},{8,9},{9,10},{10,1... | collective-permute-start | bytes 393224 | tf_op jit(solution)/shard_map/ppermute | solution.py:28
  10.4 1.7 %copy-start.4 = (bf16[64,1024]{1,0:T(8,128)(2,1)}, bf16[64,1024]{1,0:T(8,128)(2,1)S(1)}, u32[]{:S(2)}) copy-start(bf16[64,1024]{1,0:T(8,128)(2,1)S(1)} %collective-permute-done.below_ref) | copy-start | bytes 393220
  12.1 29.3 %copy-start.7 = (f32[32]{0:T(128)S(1)}, f32[32]{0:T(128)}, u32[]{:S(2)}) copy-start(f32[32]{0:T(128)} %param.17) | copy-start | bytes 388
  12.1 0.7 copy-start.3
  31.4 20.3 %all-to-all-start = ((bf16[8,32,512]{2,1,0:T(8,128)(2,1)}), bf16[8,32,512]{2,1,0:T(8,128)(2,1)S(1)}, u32[]{:S(2)}, u32[]{:S(2)}) async-start(bf16[8,32,512]{2,1,0:T(8,128)(2,1)} %get-tuple-element.36), calls=%async_computation | async-start | bytes 524288 | tf_op jit(solution)/shard_map/all_to_all | solution.py:508
  51.6 0.7 copy-start.5
  57.9 16.0 %collective-permute-start.3 = (bf16[1056,512]{1,0:T(8,128)(2,1)}, bf16[1056,512]{1,0:T(8,128)(2,1)S(1)}, u32[]{:S(2)}, u32[]{:S(2)}) collective-permute-start(bf16[1056,512]{1,0:T(8,128)(2,1)} %get-tuple-element.48), channel_id=1, source_target_pairs={{0,1},{1,0},{2,3},{3,2},{4,5},{5,4},{6,7},{7,6},{8,9},{9,8},{10,11... | collective-permute-start | bytes 3244040 | tf_op jit(solution)/shard_map/ppermute | solution.py:512
  71.0 2.9 %collective-permute-start.2 = (bf16[1024,512]{1,0:T(8,128)(2,1)}, bf16[1024,512]{1,0:T(8,128)(2,1)S(1)}, u32[]{:S(2)}, u32[]{:S(2)}) collective-permute-start(bf16[1024,512]{1,0:T(8,128)(2,1)} %get-tuple-element.46), channel_id=1, source_target_pairs={{0,1},{1,0},{2,3},{3,2},{4,5},{5,4},{6,7},{7,6},{8,9},{9,8},{10,11... | collective-permute-start | bytes 3145736 | tf_op jit(solution)/shard_map/ppermute | solution.py:514
  73.9 1.0 copy-start.2
  73.9 1.3 copy-start.1
  84.4 4.6 %copy-start.9 = (bf16[64,1024]{1,0:T(8,128)(2,1)S(1)}, bf16[64,1024]{1,0:T(8,128)(2,1)}, u32[]{:S(2)}) copy-start(bf16[64,1024]{1,0:T(8,128)(2,1)} %get-tuple-element.51) | copy-start | bytes 393220
  84.4 4.8 %copy-start.8 = (bf16[64,1024]{1,0:T(8,128)(2,1)S(1)}, bf16[64,1024]{1,0:T(8,128)(2,1)}, u32[]{:S(2)}) copy-start(bf16[64,1024]{1,0:T(8,128)(2,1)} %get-tuple-element.52) | copy-start | bytes 393220
  84.4 36.4 %all-to-all-start.1 = ((bf16[16,64,1040]{2,1,0:T(8,128)(2,1)}), bf16[16,64,1040]{2,1,0:T(8,128)(2,1)}, u32[]{:S(2)}, u32[]{:S(2)}) async-start(bf16[16,64,1040]{2,1,0:T(8,128)(2,1)} %get-tuple-element.50), calls=%async_computation.1 | async-start | bytes 4718592 | tf_op jit(solution)/shard_map/all_to_all | solution.py:521
  89.0 39.4 %copy-start.6 = (bf16[64,1024]{1,0:T(8,128)(2,1)S(1)}, bf16[64,1024]{1,0:T(8,128)(2,1)}, u32[]{:S(2)}) copy-start(bf16[64,1024]{1,0:T(8,128)(2,1)} %get-tuple-element.49) | copy-start | bytes 393220
  89.0 33.8 %collective-permute-start.4 = (bf16[64,1024]{1,0:T(8,128)(2,1)S(1)}, bf16[64,1024]{1,0:T(8,128)(2,1)S(1)}, u32[]{:S(2)}, u32[]{:S(2)}) collective-permute-start(bf16[64,1024]{1,0:T(8,128)(2,1)S(1)} %copy-done.9), channel_id=1, source_target_pairs={{0,31},{1,0},{2,1},{3,2},{4,3},{5,4},{6,5},{7,6},{8,7},{9,8},{10,9... | collective-permute-start | bytes 393224 | tf_op jit(solution)/shard_map/ppermute | solution.py:28
  89.2 33.6 %collective-permute-start.5 = (bf16[64,1024]{1,0:T(8,128)(2,1)S(1)}, bf16[64,1024]{1,0:T(8,128)(2,1)S(1)}, u32[]{:S(2)}, u32[]{:S(2)}) collective-permute-start(bf16[64,1024]{1,0:T(8,128)(2,1)S(1)} %copy-done.8), channel_id=1, source_target_pairs={{0,1},{1,2},{2,3},{3,4},{4,5},{5,6},{6,7},{7,8},{8,9},{9,10},{10,1... | collective-permute-start | bytes 393224 | tf_op jit(solution)/shard_map/ppermute | solution.py:28
  123.5 14.2 %all-to-all-start.2 = ((bf16[16,4,1040]{2,1,0:T(4,128)(2,1)}), bf16[16,4,1040]{2,1,0:T(4,128)(2,1)S(1)}, u32[]{:S(2)}, u32[]{:S(2)}) async-start(bf16[16,4,1040]{2,1,0:T(4,128)(2,1)} %all_to_all.14), calls=%async_computation.2 | async-start | bytes 294912 | tf_op jit(solution)/shard_map/all_to_all | solution.py:524

commit v5 on v4

--- a/solution.py
+++ b/solution.py
@@ -51,6 +51,18 @@
     return pltpu.CompilerParams(vmem_limit_bytes=VMEM_LIMIT)
 
 
+def give(ref, columns, values):
+    chunks, rows = ref.shape[0], ref.shape[1] // GROUPS
+    for zh in range(GROUPS):
+        some = values[zh * chunks * rows : (zh + 1) * chunks * rows, :].astype(ref.dtype)
+        ref[:, zh * rows : (zh + 1) * rows, columns] = some.reshape(chunks, rows, some.shape[1])
+
+
+def scale_column(idx_ref):
+    used = jnp.sum(jnp.where(idx_ref[...] >= 0, 1.0, 0.0), axis=0, keepdims=True)
+    return jnp.broadcast_to(0.5 / used, (8, used.shape[1])).T[:, :1]
+
+
 def forward_kernel(
     slots,
     members,
@@ -59,8 +71,7 @@
     above_ref,
     wsrc_ref,
     dst_ref,
-    idx_ref,
-    scale_ref,
+    idxt_ref,
     wout_ref,
     gp_ref,
     agg_ref,
@@ -71,6 +82,8 @@
     rhs,
     hot,
     pre,
+    idx_all,
+    scale_all,
 ):
     step = pl.program_id(0)
     nodes, width = feats.shape
@@ -80,6 +93,8 @@
 
     @pl.when(step == 0)
     def _():
+        idx_all[...] = idxt_ref[...].astype(f32).T.astype(jnp.int32)
+        scale_all[...] = scale_column(idxt_ref)
         for i, ref in enumerate((below_ref, here_ref, above_ref)):
             feats[i * block : (i + 1) * block, :] = ref[...]
         for n in range(width // NCOL):
@@ -93,8 +108,9 @@
     lane = lax.broadcasted_iota(jnp.int32, (tile, depth), 1)
     row = lax.broadcasted_iota(jnp.int32, (tile, depth), 0)
     eye = lane == row + nodes
+    idx = idx_all[pl.ds(base, tile), :]
     for k in range(slots):
-        col = idx_ref[:, k : k + 1]
+        col = idx[:, k : k + 1]
         hit = (lane == col) | (eye & (col >= 0))
         hot[k * tile : (k + 1) * tile, :] = jnp.where(hit, 1.0, 0.0).astype(bf16)
     for n in range(width // NCOL):
@@ -114,7 +130,7 @@
                 if k % GROUP == GROUP - 1:
                     acc_g = acc_g + some_g.astype(f32)
                     acc_s = acc_s + some_s.astype(f32)
-            scale = scale_ref[r : r + ROWS, :]
+            scale = scale_all[pl.ds(pl.multiple_of(base + r, ROWS), ROWS), :]
             agg_ref[pl.ds(pl.multiple_of(base + r, ROWS), ROWS), cols] = (acc_g * scale).astype(bf16)
             sum_ref[r : r + ROWS, cols] = (acc_s - (slots - 0.5 / scale)).astype(bf16)
 
@@ -128,10 +144,10 @@
             sent_ref[e] = pred.astype(bf16)
 
 
-def forward(below, here, above, w_src, dst, idx, scale, wout_t, members):
+def forward(below, here, above, w_src, dst, idx_t, wout_t, members):
     grid_rows, width = dst.shape
     nodes = 3 * here.shape[0]
-    slots = idx.shape[1]
+    slots = idx_t.shape[0]
     outs = wout_t.shape[0]
     step = lambda t: (t, 0)
     out_shape = [
@@ -147,8 +163,7 @@
         in_specs=[whole(below), whole(here), whole(above), whole(w_src)]
         + [
             pl.BlockSpec((TILE, width), step),
-            pl.BlockSpec((TILE, slots), step),
-            pl.BlockSpec((TILE, 1), step),
+            whole(idx_t),
             whole(wout_t),
         ],
         out_specs=[
@@ -164,6 +179,8 @@
             pltpu.VMEM((nodes + TILE, width), bf16),
             pltpu.VMEM((TILE * slots, nodes + TILE), bf16),
             pltpu.VMEM((2, TILE * slots, NCOL), bf16),
+            pltpu.VMEM((grid_rows, slots), jnp.int32),
+            pltpu.VMEM((grid_rows, 1), f32),
         ],
         compiler_params=params(),
         cost_estimate=pl.CostEstimate(
@@ -172,7 +189,7 @@
             transcendentals=grid_rows * slots * width,
         ),
         name="forward",
-    )(below, here, above, w_src, dst, idx, scale, wout_t)
+    )(below, here, above, w_src, dst, idx_t, wout_t)
 
 
 def middle_kernel(
@@ -183,7 +200,7 @@
     area_ref,
     var_ref,
     wout_ref,
-    scale_ref,
+    idxt_ref,
     sum_ref,
     agg_hbm,
     grid_hbm,
@@ -225,12 +242,13 @@
         weighting
         * (smooth_grad(pred - truth_ref[...]) / members - pair / (members * (members - 1)))
     ).astype(bf16)
+    scale = scale_column(idxt_ref)
     for n in range(width // NCOL):
         cols = slice(n * NCOL, (n + 1) * NCOL)
         dagg = lax.dot_general(
             dpred, wout_ref[:, cols], (((0,), (0,)), ((), ())), preferred_element_type=f32
         )
-        dagg = dagg * scale_ref[...]
+        dagg = dagg * scale
         lead_ref[:, cols] = dagg.astype(bf16)
         ddst[:, cols] = (dagg * sum_ref[:, cols].astype(f32)).astype(bf16)
 
@@ -245,12 +263,14 @@
         (far_ref, other, 1 - core, stores[1]),
         (own_ref, mine, core, stores[2]),
     ):
-        ref[:width, :] = lax.dot_general(
-            grid_ref[...], ddst[:, columns], (((0,), (0,)), ((), ())), preferred_element_type=f32
-        ).astype(bf16)
-        at = pl.ds(pl.multiple_of(which * few, few), few)
-        ref[width : width + few, :] = part[at, :half].astype(bf16)
-        ref[width + few :, :] = part[at, half:].astype(bf16)
+        give(
+            ref,
+            slice(0, half),
+            lax.dot_general(
+                grid_ref[...], ddst[:, columns], (((0,), (0,)), ((), ())), preferred_element_type=f32
+            ),
+        )
+        give(ref, slice(half, half + few), part[pl.ds(pl.multiple_of(which * few, few), few), :].T)
         store.start()
     for copy in stores:
         copy.wait()
@@ -262,12 +282,12 @@
     )
 
 
-def middle(core, everyone, pred, truth_t, area, var, wout_t, scale, sums, agg, grid_embed):
+def middle(core, everyone, pred, truth_t, area, var, wout_t, idx_t, sums, agg, grid_embed, chunks):
     grid_rows, width = sums.shape
     outs = pred.shape[0]
-    block = (width + outs, width // 2)
+    block = (chunks, width // chunks, (width + outs) // 2)
     anywhere = pl.BlockSpec(memory_space=pl.ANY)
-    small = (everyone, pred, truth_t, area, var, wout_t, scale, sums)
+    small = (everyone, pred, truth_t, area, var, wout_t, idx_t, sums)
     return pl.pallas_call(
         middle_kernel,
         grid_spec=prefetched(
@@ -295,7 +315,7 @@
             flops=2 * grid_rows * width * width, bytes_accessed=10 * grid_rows * width, transcendentals=0
         ),
         name="middle",
-    )(core, everyone, pred, truth_t, area, var, wout_t, scale, sums, agg, grid_embed)
+    )(core, everyone, pred, truth_t, area, var, wout_t, idx_t, sums, agg, grid_embed)
 
 
 def scatter_step(slots, gp_ref, lead_ref, idx_ref, hot, prod, acc):
@@ -329,9 +349,13 @@
     def _():
         wide_ref[...] = acc[...].astype(bf16)
         feats = jnp.concatenate([below_ref[...], here_ref[...], above_ref[...]], axis=0)
-        part_ref[...] = lax.dot_general(
-            feats, wide_ref[...], (((0,), (0,)), ((), ())), preferred_element_type=f32
-        ).astype(bf16)
+        give(
+            part_ref,
+            slice(None),
+            lax.dot_general(
+                feats, wide_ref[...], (((0,), (0,)), ((), ())), preferred_element_type=f32
+            ),
+        )
 
 
 def own_kernel(
@@ -344,9 +368,6 @@
     here_ref,
     above_ref,
     widefar_ref,
-    srcfar_ref,
-    dstown_ref,
-    dstfar_ref,
     lower_ref,
     centre_ref,
     upper_ref,
@@ -369,28 +390,11 @@
             ref[:, mine] = wide[i * block : (i + 1) * block, :]
             ref[:, other] = widefar_ref[i * block : (i + 1) * block, :]
         feats = jnp.concatenate([below_ref[...], here_ref[...], above_ref[...]], axis=0)
-        total = lax.dot_general(
-            feats, wide, (((0,), (0,)), ((), ())), preferred_element_type=f32
+        give(
+            total_ref,
+            slice(None),
+            lax.dot_general(feats, wide, (((0,), (0,)), ((), ())), preferred_element_type=f32),
         )
-        width = total_ref.shape[0] * total_ref.shape[1]
-        few = (dstown_ref.shape[0] - width) // 2
-
-        def give(columns, values):
-            chunks, rows = total_ref.shape[0], total_ref.shape[1] // GROUPS
-            for zh in range(GROUPS):
-                some = values[zh * chunks * rows : (zh + 1) * chunks * rows, :]
-                total_ref[:, zh * rows : (zh + 1) * rows, columns] = some.astype(bf16).reshape(
-                    chunks, rows, values.shape[1]
-                )
-
-        give(slice(0, half), total + srcfar_ref[...].astype(f32))
-        give(
-            slice(half, 2 * half),
-            dstown_ref[:width, :].astype(f32) + dstfar_ref[:width, :].astype(f32),
-        )
-        out = dstown_ref[width:, :].astype(f32) + dstfar_ref[width:, :].astype(f32)
-        out = jnp.concatenate([out[:few, :], out[few:, :]], axis=1)
-        give(slice(2 * half, 2 * half + few), out.T)
 
 
 def scatter_scratch(slots, nodes, half):
@@ -434,35 +438,37 @@
     )(mine, gp, lead, idx_t, *others)
 
 
-def backward_far(mine, gp, lead, idx_t, feats):
+def product_shape(lead, chunks):
+    width = lead.shape[1]
+    return jax.ShapeDtypeStruct((chunks, width // chunks, width // 2), bf16)
+
+
+def backward_far(mine, gp, lead, idx_t, feats, chunks):
     half = lead.shape[1] // 2
     out_shape = [
         jax.ShapeDtypeStruct((3 * feats[0].shape[0], half), bf16),
-        jax.ShapeDtypeStruct((lead.shape[1], half), bf16),
+        product_shape(lead, chunks),
     ]
     column = lambda core: 1 - core
     return backward(far_kernel, "backward_far", column, mine, gp, lead, idx_t, feats, [], out_shape)
 
 
-def backward_own(mine, gp, lead, idx_t, feats, wide_far, src_far, dst_own, dst_far, chunks):
-    width = lead.shape[1]
-    columns = width + (dst_own.shape[0] - width) // 2
-    out_shape = [jax.ShapeDtypeStruct((feats[0].shape[0], width), bf16)] * 3 + [
-        jax.ShapeDtypeStruct((chunks, width // chunks, columns), bf16)
+def backward_own(mine, gp, lead, idx_t, feats, wide_far, chunks):
+    out_shape = [jax.ShapeDtypeStruct((feats[0].shape[0], lead.shape[1]), bf16)] * 3 + [
+        product_shape(lead, chunks)
     ]
     column = lambda core: core
     return backward(
-        own_kernel,
-        "backward_own",
-        column,
-        mine,
-        gp,
-        lead,
-        idx_t,
-        feats,
-        [wide_far, src_far, dst_own, dst_far],
-        out_shape,
+        own_kernel, "backward_own", column, mine, gp, lead, idx_t, feats, [wide_far], out_shape
     )
+
+
+def added(a, b):
+    return (a.astype(f32) + b.astype(f32)).astype(bf16)
+
+
+def summed(parts):
+    return jnp.sum(parts.astype(f32), axis=0).astype(bf16)
 
 
 def body(
@@ -494,32 +500,31 @@
     dst = jnp.dot(grid_embed, w_dst, preferred_element_type=f32).astype(bf16)
     local = jnp.mod(neighbour.T - (block_id - 1) * node_rows, node_rows * space_count)
     idx_t = jnp.where(edge_mask.T > 0, local, -1)
-    idx = idx_t.T
-    scale = 0.5 / jnp.sum(edge_mask.T.astype(f32), axis=0)[:, None]
     wout_t = w_out.T
     truth_t = truth.T
     var = var_weight[:, None]
     area = area_weight[None, :]
-    dst, idx, idx_t, scale, wout_t, truth_t, var, area, below = lax.optimization_barrier(
-        (dst, idx, idx_t, scale, wout_t, truth_t, var, area, below)
-    )
+    dst, idx_t, below = lax.optimization_barrier((dst, idx_t, below))
     feats = (below, own, above)
-    gp, agg, sums, pred, sent = forward(*feats, w_src, dst, idx, scale, wout_t, members)
+    chunks = lax.axis_size(FIRST)
+    gp, agg, sums, pred, sent = forward(*feats, w_src, dst, idx_t, wout_t, members)
     everyone = lax.all_to_all(sent, ENS, 0, 0, tiled=True)
     lead, dst_own, dst_far = middle(
-        mine, everyone, pred, truth_t, area, var, wout_t, scale, sums, agg, grid_embed
+        mine, everyone, pred, truth_t, area, var, wout_t, idx_t, sums, agg, grid_embed, chunks
     )
     dst_far = lax.ppermute(dst_far, "c", swap)
-    wide_far, src_far = backward_far(mine, gp, lead, idx_t, feats)
+    wide_far, src_far = backward_far(mine, gp, lead, idx_t, feats, chunks)
     src_far = lax.ppermute(src_far, "c", swap)
-    lower, centre, upper, total = backward_own(
-        mine, gp, lead, idx_t, feats, wide_far, src_far, dst_own, dst_far, lax.axis_size(FIRST)
-    )
+
+    dst_total = added(dst_own, dst_far)
+    lead, dst_total = lax.optimization_barrier((lead, dst_total))
+    dst_parts = lax.all_to_all(dst_total, FIRST, 0, 0, tiled=True)
+    lower, centre, upper, src_own = backward_own(mine, gp, lead, idx_t, feats, wide_far, chunks)
+    src_own, src_far, dst_parts = lax.optimization_barrier((src_own, src_far, dst_parts))
+    src_parts = lax.all_to_all(added(src_own, src_far), FIRST, 0, 0, tiled=True)
     from_above = shifted(lower, SPACE, -1)
     from_below = shifted(upper, SPACE, 1)
-
-    parts = lax.all_to_all(total, FIRST, 0, 0, tiled=True)
-    total = jnp.sum(parts.astype(f32), axis=0).astype(bf16)
+    total = jnp.concatenate([summed(src_parts), summed(dst_parts)], axis=1)
     total, from_above, from_below = lax.optimization_barrier((total, from_above, from_below))
     parts = lax.all_to_all(total, SECOND, 0, 0, tiled=True)
     dproj = (centre.astype(f32) + from_above.astype(f32) + from_below.astype(f32)).astype(bf16)

time: 141 us -> 135 us (0.957)
  waiting for transfers between devices: 48.6 us -> 40.9 us
  starting transfers between devices: 30.8 us -> 36.3 us
  local copies, waits for them, and re-layouts: 5.81 us -> 2.76 us
  Pallas kernels: 40.3 us -> 38.7 us
  other arithmetic: 6.32 us -> 7.89 us
    all_to_all x1 -> x2, waiting for transfers between devices: 29.9 us -> 23.2 us  [the longest x1 12.1 us: body(): src_parts = lax.all_to_all(added(src_own, src_far), FIRST, 0, 0, tiled=True)]
    convert_element_type x0 -> x2, other arithmetic: none -> 4.34 us  [added(): return (a.astype(f32) + b.astype(f32)).astype(bf16)]
    all_to_all x1 -> x2, starting transfers between devices: 4.59 us -> 8.67 us  [the longest x1 4.9 us: body(): src_parts = lax.all_to_all(added(src_own, src_far), FIRST, 0, 0, tiled=True)]
    ppermute x1, waiting for transfers between devices: 2.82 us -> 0.01 us  [body(): src_far = lax.ppermute(src_far, 'c', swap)]
    optimization_barrier x3 -> x0, local copies, waits for them, and re-layouts: 2.4 us -> none  [body(): lax.optimization_barrier((dst, idx, idx_t, scale, wout_t, truth_t, var, a...]
    all_to_all x1, starting transfers between devices: 4.88 us -> 7.18 us  [body(): parts = lax.all_to_all(total, SECOND, 0, 0, tiled=True)]
    pallas_call x2, Pallas kernels: 16.2 us -> 14.3 us  [backward(): pl.pallas_call(functools.partial(kernel, slots), grid_spec=prefetched(gri...]
    all_to_all x1, starting transfers between devices: 10.1 us -> 8.43 us  [body(): everyone = lax.all_to_all(sent, ENS, 0, 0, tiled=True)]
  transfers between devices with their start and end apart: 9 -> 10, of which waited for: 4 -> 5; matrix products, arithmetic and copies ran while one was open for 10% -> 8% of each run, Pallas kernels for 5% -> 11%
where the time goes in v5:
time: 135 us; the launch traced here: 134 us
  waiting for transfers between devices  40.9 us (30%)
  Pallas kernels  38.7 us (29%)
  starting transfers between devices  36.3 us (27%)
  other arithmetic  7.89 us (6%)
  matrix products  6.7 us (5%)
  local copies, waits for them, and re-layouts  2.76 us (2%)
    pallas_call x1, Pallas kernels, forward(): pl.pallas_call(functools.partial(forward_kernel, slots, members), grid=(g...  18.5 us
    pallas_call x2, Pallas kernels, backward(): pl.pallas_call(functools.partial(kernel, slots), grid_spec=prefetched(gri...  14.3 us
    all_to_all x1, waiting for transfers between devices, body(): src_parts = lax.all_to_all(added(src_own, src_far), FIRST, 0, 0, tiled=True)  12.1 us
    all_to_all x1, waiting for transfers between devices, body(): dst_parts = lax.all_to_all(dst_total, FIRST, 0, 0, tiled=True)  11.1 us
    all_to_all x1, waiting for transfers between devices, body(): everyone = lax.all_to_all(sent, ENS, 0, 0, tiled=True)  9.93 us
    all_to_all x1, starting transfers between devices, body(): everyone = lax.all_to_all(sent, ENS, 0, 0, tiled=True)  8.43 us
    all_to_all x1, starting transfers between devices, body(): parts = lax.all_to_all(total, SECOND, 0, 0, tiled=True)  7.18 us
    ppermute x4, starting transfers between devices, shifted(): lax.ppermute(block, axes, [(i, (i + distance) % count) for i in range(cou...  6.6 us
  transfers between devices with their start and end apart: 10, of which 5 were waited for; matrix products, arithmetic and copies ran while one was open for 8% of the time, Pallas kernels for 11%

profile of v5, /device:TPU:1, one launch (start us, length us, event | category | flops | bytes accessed | tf_op | source)
XLA Modules:
  0.0 133.9 jit_solution(12356079554172134048)
XLA Ops:
  0.6 3.1 %collective-permute-start = (bf16[64,1024]{1,0:T(8,128)(2,1)}, bf16[64,1024]{1,0:T(8,128)(2,1)S(1)}, u32[]{:S(2)}, u32[]{:S(2)}) collective-permute-start(bf16[64,1024]{1,0:T(8,128)(2,1)} %bitcast.32), channel_id=1, source_target_pairs={{0,1},{1,2},{2,3},{3,4},{4,5},{5,6},{6,7},{7,8},{8,9},{9,10},{10,1... | collective-permute-start | bytes 393224 | tf_op jit(solution)/shard_map/ppermute | solution.py:28
  3.8 0.3 collective-permute-start.1
  4.1 3.5 %convolution_convert_fusion.dst_ref = bf16[512,1024]{1,0:T(8,128)(2,1)} fusion(bf16[512,1024]{1,0:T(8,128)(2,1)} %grid_hbm.1, bf16[1024,1024]{1,0:T(8,128)(2,1)S(1)} %copy-done), kind=kOutput, calls=%fused_computation.2 | convolution fusion | flops 1074266112 | bytes 4194304 | tf_op jit(solution)/shard_map/dot_general | solution.py:500
  7.5 0.6 fusion.2.idxt_ref.idx_ref
  8.2 1.6 %collective-permute-done.1.above_ref = bf16[64,1024]{1,0:T(8,128)(2,1)S(1)} collective-permute-done((bf16[64,1024]{1,0:T(8,128)(2,1)}, bf16[64,1024]{1,0:T(8,128)(2,1)S(1)}, u32[]{:S(2)}, u32[]{:S(2)}) %collective-permute-start.1) | collective-permute-done | bytes 131104 | tf_op jit(solution)/shard_map/ppermute | solution.py:28
  9.8 0.6 copy-done.3
  10.4 18.5 %forward.1 = (bf16[8192,1024]{1,0:T(8,128)(2,1)}, bf16[512,1024]{1,0:T(8,128)(2,1)}, bf16[512,1024]{1,0:T(8,128)(2,1)}, f32[32,512]{1,0:T(8,128)}, bf16[8,32,512]{2,1,0:T(8,128)(2,1)}) custom-call(bf16[64,1024]{1,0:T(8,128)(2,1)} %copy-done.2, bf16[64,1024]{1,0:T(8,128)(2,1)} %bitcast.34, bf16[64,1024]{1,0:T(8,128)(2,1)} %copy-done.3, ...), custom_call_target="tpu_custom_call" | custom-call | flops 4294967296 | bytes 16777216 | tf_op jit(solution)/shard_map/forward/pallas_call | solution.py:160
  28.9 8.4 %all-to-all-start = ((bf16[8,32,512]{2,1,0:T(8,128)(2,1)}), bf16[8,32,512]{2,1,0:T(8,128)(2,1)S(1)}, u32[]{:S(2)}, u32[]{:S(2)}) async-start(bf16[8,32,512]{2,1,0:T(8,128)(2,1)} %get-tuple-element.33), calls=%async_computation | async-start | bytes 524288 | tf_op jit(solution)/shard_map/all_to_all | solution.py:511
  37.4 0.7 copy.16.var_ref
  38.0 9.9 %all-to-all-done.every_ref = bf16[8,32,512]{2,1,0:T(8,128)(2,1)S(1)} async-done(((bf16[8,32,512]{2,1,0:T(8,128)(2,1)}), bf16[8,32,512]{2,1,0:T(8,128)(2,1)S(1)}, u32[]{:S(2)}, u32[]{:S(2)}) %all-to-all-start) | async-done | bytes 262176 | tf_op jit(solution)/shard_map/all_to_all | solution.py:511
  48.0 0.7 copy-done.4
  48.7 5.9 %middle.1 = (bf16[512,1024]{1,0:T(8,128)(2,1)}, bf16[16,64,528]{2,1,0:T(8,128)(2,1)}, bf16[16,64,528]{2,1,0:T(8,128)(2,1)}) custom-call(s32[1]{0:T(128)} %bitcast.core_ref.place_ref, bf16[8,32,512]{2,1,0:T(8,128)(2,1)} %copy-done.4, f32[32,512]{1,0:T(8,128)} %get-tuple-element.34.pred_ref, f32[32,512]{1,0:T(8,128)} %bitcast.40, f32[1,512]{1,0:T(1,128)} %bitcast.41, ...), custom_call_target="tpu_custom_call" | custom-call | flops 1073741824 | bytes 5242880 | tf_op jit(solution)/shard_map/middle/pallas_call | solution.py:291
  54.6 5.4 %collective-permute-start.2 = (bf16[16,64,528]{2,1,0:T(8,128)(2,1)}, bf16[16,64,528]{2,1,0:T(8,128)(2,1)S(1)}, u32[]{:S(2)}, u32[]{:S(2)}) collective-permute-start(bf16[16,64,528]{2,1,0:T(8,128)(2,1)} %get-tuple-element.39), channel_id=1, source_target_pairs={{0,1},{1,0},{2,3},{3,2},{4,5},{5,4},{6,7},{7,6},{8,9},{9,8},{10,11... | collective-permute-start | bytes 3244040 | tf_op jit(solution)/shard_map/ppermute | solution.py:515
  59.9 7.1 %backward_far.1 = (bf16[192,512]{1,0:T(8,128)(2,1)}, bf16[16,64,512]{2,1,0:T(8,128)(2,1)}) custom-call(s32[1]{0:T(128)} %bitcast.core_ref.place_ref, bf16[8192,1024]{1,0:T(8,128)(2,1)} %get-tuple-element.32.gp_ref, bf16[512,1024]{1,0:T(8,128)(2,1)} %get-tuple-element.40.lead_ref, s32[16,512]{1,0:T(8,128)} %fusion.2.idxt_ref.idx_ref, ...), custom_call_target="tpu_custom_call" | custom-call | flops 2147483648 | bytes 8388608 | tf_op jit(solution)/shard_map/backward_far/pallas_call | solution.py:421
  67.0 0.0 collective-permute-start.3
  67.1 1.5 %add_convert_fusion = bf16[16,64,528]{2,1,0:T(8,128)(2,1)} fusion(bf16[16,64,528]{2,1,0:T(8,128)(2,1)S(1)} %collective-permute-done.2, bf16[16,64,528]{2,1,0:T(8,128)(2,1)S(1)} %copy-done.1), kind=kLoop, calls=%fused_computation | loop fusion | flops 2162688 | bytes 3244032 | tf_op jit(solution)/shard_map/convert_element_type | solution.py:467
  68.6 3.8 %all-to-all-start.1 = ((bf16[16,64,528]{2,1,0:T(8,128)(2,1)}), bf16[16,64,528]{2,1,0:T(8,128)(2,1)S(1)}, u32[]{:S(2)}, u32[]{:S(2)}) async-start(bf16[16,64,528]{2,1,0:T(8,128)(2,1)} %add_convert_fusion), calls=%async_computation.1 | async-start | bytes 2621440 | tf_op jit(solution)/shard_map/all_to_all | solution.py:521
  72.4 7.2 %backward_own.1 = (bf16[64,1024]{1,0:T(8,128)(2,1)}, bf16[64,1024]{1,0:T(8,128)(2,1)}, bf16[64,1024]{1,0:T(8,128)(2,1)}, bf16[16,64,512]{2,1,0:T(8,128)(2,1)}) custom-call(s32[1]{0:T(128)} %bitcast.core_ref.place_ref, bf16[8192,1024]{1,0:T(8,128)(2,1)} %get-tuple-element.32.gp_ref, bf16[512,1024]{1,0:T(8,128)(2,1)} %get-tuple-element.40.lead_ref, ...), custom_call_target="tpu_custom_call" | custom-call | flops 2147483648 | bytes 8388608 | tf_op jit(solution)/shard_map/backward_own/pallas_call | solution.py:421
  79.5 11.1 %all-to-all-done.1 = bf16[16,64,528]{2,1,0:T(8,128)(2,1)S(1)} async-done(((bf16[16,64,528]{2,1,0:T(8,128)(2,1)}), bf16[16,64,528]{2,1,0:T(8,128)(2,1)S(1)}, u32[]{:S(2)}, u32[]{:S(2)}) %all-to-all-start.1) | async-done | bytes 1081376 | tf_op jit(solution)/shard_map/all_to_all | solution.py:521
  90.6 2.8 %add_convert_fusion.1 = bf16[16,64,512]{2,1,0:T(8,128)(2,1)} fusion(bf16[16,64,512]{2,1,0:T(8,128)(2,1)} %collective-permute-done.3, bf16[16,64,512]{2,1,0:T(8,128)(2,1)} %get-tuple-element.46), kind=kLoop, calls=%fused_computation.1 | loop fusion | flops 2097152 | bytes 3145728 | tf_op jit(solution)/shard_map/convert_element_type | solution.py:467
  93.5 4.9 %all-to-all-start.2 = ((bf16[16,64,512]{2,1,0:T(8,128)(2,1)}), bf16[16,64,512]{2,1,0:T(8,128)(2,1)}, u32[]{:S(2)}, u32[]{:S(2)}) async-start(bf16[16,64,512]{2,1,0:T(8,128)(2,1)} %add_convert_fusion.1), calls=%async_computation.2 | async-start | bytes 2097152 | tf_op jit(solution)/shard_map/all_to_all | solution.py:524
  98.4 3.2 %collective-permute-start.4 = (bf16[64,1024]{1,0:T(8,128)(2,1)}, bf16[64,1024]{1,0:T(8,128)(2,1)}, u32[]{:S(2)}, u32[]{:S(2)}) collective-permute-start(bf16[64,1024]{1,0:T(8,128)(2,1)} %get-tuple-element.49), channel_id=1, source_target_pairs={{0,31},{1,0},{2,1},{3,2},{4,3},{5,4},{6,5},{7,6},{8,7},{9,8},{10,9... | collective-permute-start | bytes 393224 | tf_op jit(solution)/shard_map/ppermute | solution.py:28
  101.6 0.2 reduce_sum.34
  101.8 12.1 %all-to-all-done.2 = bf16[16,64,512]{2,1,0:T(8,128)(2,1)} async-done(((bf16[16,64,512]{2,1,0:T(8,128)(2,1)}), bf16[16,64,512]{2,1,0:T(8,128)(2,1)}, u32[]{:S(2)}, u32[]{:S(2)}) %all-to-all-start.2) | async-done | bytes 1048608 | tf_op jit(solution)/shard_map/all_to_all | solution.py:524
  113.9 1.4 %reduce_sum.33 = bf16[64,512]{1,0:T(8,128)(2,1)S(1)} reduce(bf16[16,64,512]{2,1,0:T(8,128)(2,1)} %all-to-all-done.2, bf16[]{:T(256)} %constant.40.clone.1), dimensions={0}, to_apply=%region_0.1 | reduce | flops 491520 | bytes 1114114 | tf_op jit(solution)/shard_map/reduce_sum | solution.py:471
  115.3 0.7 all_to_all.18
  116.0 7.2 %all-to-all-start.3 = ((bf16[16,4,1040]{2,1,0:T(4,128)(2,1)}), bf16[16,4,1040]{2,1,0:T(4,128)(2,1)S(1)}, u32[]{:S(2)}, u32[]{:S(2)}) async-start(bf16[16,4,1040]{2,1,0:T(4,128)(2,1)} %all_to_all.18), calls=%async_computation.3 | async-start | bytes 294912 | tf_op jit(solution)/shard_map/all_to_all | solution.py:529
  123.2 3.2 %fusion = bf16[1,64,1024]{2,1,0:T(8,128)(2,1)} fusion(bf16[1024,1024]{1,0:T(8,128)(2,1)} %wsrc_ref.1, bf16[64,1024]{1,0:T(8,128)(2,1)} %collective-permute-done.5, bf16[64,1024]{1,0:T(8,128)(2,1)} %collective-permute-done.4, bf16[64,1024]{1,0:T(8,128)(2,1)} %get-tuple-element.42), kind=kOutput, calls=%fused_computation.4 | convolution fusion | flops 134676480 | bytes 2621440 | tf_op jit(solution)/shard_map/dot_general | solution.py:531
  126.4 6.1 %all-to-all-done.3 = bf16[16,4,1040]{2,1,0:T(4,128)(2,1)S(1)} async-done(((bf16[16,4,1040]{2,1,0:T(4,128)(2,1)}), bf16[16,4,1040]{2,1,0:T(4,128)(2,1)S(1)}, u32[]{:S(2)}, u32[]{:S(2)}) %all-to-all-start.3) | async-done | bytes 133152 | tf_op jit(solution)/shard_map/all_to_all | solution.py:529
  132.5 0.1 convert_reduce_fusion
  132.6 0.7 pad_maximum_fusion.3
  133.3 0.6 pad_maximum_fusion.1
  (23 shorter events, 0.1 us)
Async XLA Ops:
  0.6 3.4 %copy-start = (bf16[1024,1024]{1,0:T(8,128)(2,1)S(1)}, bf16[1024,1024]{1,0:T(8,128)(2,1)}, u32[]{:S(2)}) copy-start(bf16[1024,1024]{1,0:T(8,128)(2,1)} %param.13) | copy-start | bytes 6291460
  0.6 7.5 %collective-permute-start = (bf16[64,1024]{1,0:T(8,128)(2,1)}, bf16[64,1024]{1,0:T(8,128)(2,1)S(1)}, u32[]{:S(2)}, u32[]{:S(2)}) collective-permute-start(bf16[64,1024]{1,0:T(8,128)(2,1)} %bitcast.32), channel_id=1, source_target_pairs={{0,1},{1,2},{2,3},{3,4},{4,5},{5,6},{6,7},{7,8},{8,9},{9,10},{10,1... | collective-permute-start | bytes 393224 | tf_op jit(solution)/shard_map/ppermute | solution.py:28
  3.8 6.0 %collective-permute-start.1 = (bf16[64,1024]{1,0:T(8,128)(2,1)}, bf16[64,1024]{1,0:T(8,128)(2,1)S(1)}, u32[]{:S(2)}, u32[]{:S(2)}) collective-permute-start(bf16[64,1024]{1,0:T(8,128)(2,1)} %bitcast.33), channel_id=1, source_target_pairs={{0,31},{1,0},{2,1},{3,2},{4,3},{5,4},{6,5},{7,6},{8,7},{9,8},{10,9... | collective-permute-start | bytes 393224 | tf_op jit(solution)/shard_map/ppermute | solution.py:28
  4.1 3.5 %copy-start.5 = (s32[512,16]{0,1:T(8,128)S(1)}, s32[512,16]{0,1:T(8,128)}, u32[]{:S(2)}) copy-start(s32[512,16]{0,1:T(8,128)} %param.18) | copy-start | bytes 98308
  4.1 3.5 %copy-start.6 = (s32[512,16]{0,1:T(8,128)S(1)}, s32[512,16]{0,1:T(8,128)}, u32[]{:S(2)}) copy-start(s32[512,16]{0,1:T(8,128)} %param.19) | copy-start | bytes 98308
  8.2 1.6 %copy-start.2 = (bf16[64,1024]{1,0:T(8,128)(2,1)}, bf16[64,1024]{1,0:T(8,128)(2,1)S(1)}, u32[]{:S(2)}) copy-start(bf16[64,1024]{1,0:T(8,128)(2,1)S(1)} %collective-permute-done.below_ref) | copy-start | bytes 393220
  9.8 0.6 copy-start.3
  10.4 26.9 %copy-start.7 = (f32[32]{0:T(128)S(1)}, f32[32]{0:T(128)}, u32[]{:S(2)}) copy-start(f32[32]{0:T(128)} %param.17) | copy-start | bytes 388
  28.9 19.1 %all-to-all-start = ((bf16[8,32,512]{2,1,0:T(8,128)(2,1)}), bf16[8,32,512]{2,1,0:T(8,128)(2,1)S(1)}, u32[]{:S(2)}, u32[]{:S(2)}) async-start(bf16[8,32,512]{2,1,0:T(8,128)(2,1)} %get-tuple-element.33), calls=%async_computation | async-start | bytes 524288 | tf_op jit(solution)/shard_map/all_to_all | solution.py:511
  48.0 0.7 copy-start.4
  54.6 12.5 %collective-permute-start.2 = (bf16[16,64,528]{2,1,0:T(8,128)(2,1)}, bf16[16,64,528]{2,1,0:T(8,128)(2,1)S(1)}, u32[]{:S(2)}, u32[]{:S(2)}) collective-permute-start(bf16[16,64,528]{2,1,0:T(8,128)(2,1)} %get-tuple-element.39), channel_id=1, source_target_pairs={{0,1},{1,0},{2,3},{3,2},{4,5},{5,4},{6,7},{7,6},{8,9},{9,8},{10,11... | collective-permute-start | bytes 3244040 | tf_op jit(solution)/shard_map/ppermute | solution.py:515
  59.9 7.2 %copy-start.1 = (bf16[16,64,528]{2,1,0:T(8,128)(2,1)S(1)}, bf16[16,64,528]{2,1,0:T(8,128)(2,1)}, u32[]{:S(2)}) copy-start(bf16[16,64,528]{2,1,0:T(8,128)(2,1)} %get-tuple-element.38) | copy-start | bytes 3244036
  67.0 12.5 %collective-permute-start.3 = (bf16[16,64,512]{2,1,0:T(8,128)(2,1)}, bf16[16,64,512]{2,1,0:T(8,128)(2,1)}, u32[]{:S(2)}, u32[]{:S(2)}) collective-permute-start(bf16[16,64,512]{2,1,0:T(8,128)(2,1)} %get-tuple-element.44), channel_id=1, source_target_pairs={{0,1},{1,0},{2,3},{3,2},{4,5},{5,4},{6,7},{7,6},{8,9},{9,8},{10,11... | collective-permute-start | bytes 3145736 | tf_op jit(solution)/shard_map/ppermute | solution.py:517
  68.6 22.1 %all-to-all-start.1 = ((bf16[16,64,528]{2,1,0:T(8,128)(2,1)}), bf16[16,64,528]{2,1,0:T(8,128)(2,1)S(1)}, u32[]{:S(2)}, u32[]{:S(2)}) async-start(bf16[16,64,528]{2,1,0:T(8,128)(2,1)} %add_convert_fusion), calls=%async_computation.1 | async-start | bytes 2621440 | tf_op jit(solution)/shard_map/all_to_all | solution.py:521
  93.5 20.4 %all-to-all-start.2 = ((bf16[16,64,512]{2,1,0:T(8,128)(2,1)}), bf16[16,64,512]{2,1,0:T(8,128)(2,1)}, u32[]{:S(2)}, u32[]{:S(2)}) async-start(bf16[16,64,512]{2,1,0:T(8,128)(2,1)} %add_convert_fusion.1), calls=%async_computation.2 | async-start | bytes 2097152 | tf_op jit(solution)/shard_map/all_to_all | solution.py:524
  98.4 16.9 %collective-permute-start.4 = (bf16[64,1024]{1,0:T(8,128)(2,1)}, bf16[64,1024]{1,0:T(8,128)(2,1)}, u32[]{:S(2)}, u32[]{:S(2)}) collective-permute-start(bf16[64,1024]{1,0:T(8,128)(2,1)} %get-tuple-element.49), channel_id=1, source_target_pairs={{0,31},{1,0},{2,1},{3,2},{4,3},{5,4},{6,5},{7,6},{8,7},{9,8},{10,9... | collective-permute-start | bytes 393224 | tf_op jit(solution)/shard_map/ppermute | solution.py:28
  101.6 13.7 %collective-permute-start.5 = (bf16[64,1024]{1,0:T(8,128)(2,1)}, bf16[64,1024]{1,0:T(8,128)(2,1)}, u32[]{:S(2)}, u32[]{:S(2)}) collective-permute-start(bf16[64,1024]{1,0:T(8,128)(2,1)} %get-tuple-element.50), channel_id=1, source_target_pairs={{0,1},{1,2},{2,3},{3,4},{4,5},{5,6},{6,7},{7,8},{8,9},{9,10},{10,1... | collective-permute-start | bytes 393224 | tf_op jit(solution)/shard_map/ppermute | solution.py:28
  116.0 16.5 %all-to-all-start.3 = ((bf16[16,4,1040]{2,1,0:T(4,128)(2,1)}), bf16[16,4,1040]{2,1,0:T(4,128)(2,1)S(1)}, u32[]{:S(2)}, u32[]{:S(2)}) async-start(bf16[16,4,1040]{2,1,0:T(4,128)(2,1)} %all_to_all.18), calls=%async_computation.3 | async-start | bytes 294912 | tf_op jit(solution)/shard_map/all_to_all | solution.py:529

commit v6 on v5

--- a/solution.py
+++ b/solution.py
@@ -132,7 +132,7 @@
                     acc_s = acc_s + some_s.astype(f32)
             scale = scale_all[pl.ds(pl.multiple_of(base + r, ROWS), ROWS), :]
             agg_ref[pl.ds(pl.multiple_of(base + r, ROWS), ROWS), cols] = (acc_g * scale).astype(bf16)
-            sum_ref[r : r + ROWS, cols] = (acc_s - (slots - 0.5 / scale)).astype(bf16)
+            sum_ref[n, r : r + ROWS, :] = (acc_s - (slots - 0.5 / scale)).astype(bf16)
 
     @pl.when(step == pl.num_programs(0) - 1)
     def _():
@@ -153,7 +153,7 @@
     out_shape = [
         jax.ShapeDtypeStruct((grid_rows * slots, width), bf16),
         jax.ShapeDtypeStruct((grid_rows, width), bf16),
-        jax.ShapeDtypeStruct((grid_rows, width), bf16),
+        jax.ShapeDtypeStruct((width // NCOL, grid_rows, NCOL), bf16),
         jax.ShapeDtypeStruct((outs, grid_rows), f32),
         jax.ShapeDtypeStruct((members, outs, grid_rows), bf16),
     ]
@@ -169,7 +169,7 @@
         out_specs=[
             pl.BlockSpec((TILE * slots, width), step),
             whole(out_shape[1]),
-            pl.BlockSpec((TILE, width), step),
+            pl.BlockSpec((width // NCOL, TILE, NCOL), lambda t: (0, t, 0)),
             whole(out_shape[3]),
             whole(out_shape[4]),
         ],
@@ -193,7 +193,7 @@
 
 
 def middle_kernel(
-    core_ref,
+    place_ref,
     every_ref,
     pred_ref,
     truth_ref,
@@ -205,75 +205,64 @@
     agg_hbm,
     grid_hbm,
     lead_hbm,
-    own_hbm,
-    far_hbm,
+    own_ref,
+    far_ref,
+    part_ref,
     agg_ref,
     grid_ref,
     lead_ref,
-    own_ref,
-    far_ref,
     ddst,
-    part,
     sems,
 ):
     loads = [
         pltpu.make_async_copy(agg_hbm, agg_ref, sems.at[0]),
         pltpu.make_async_copy(grid_hbm, grid_ref, sems.at[1]),
     ]
-    stores = [
-        pltpu.make_async_copy(lead_ref, lead_hbm, sems.at[2]),
-        pltpu.make_async_copy(far_ref, far_hbm, sems.at[3]),
-        pltpu.make_async_copy(own_ref, own_hbm, sems.at[4]),
-    ]
+    store = pltpu.make_async_copy(lead_ref, lead_hbm, sems.at[2])
     for copy in loads:
         copy.start()
-    width = sum_ref.shape[1]
-    half = width // 2
+    width = wout_ref.shape[1]
     members = every_ref.shape[0]
-    outs = pred_ref.shape[0]
-    core = core_ref[0]
-
-    pred = pred_ref[...]
-    pair = -smooth_grad(pred - pred.astype(bf16).astype(f32))
-    for e in range(members):
-        pair = pair + smooth_grad(pred - every_ref[e].astype(f32))
+    near, columns = sum_ref.shape[0], sum_ref.shape[2]
+    core, x, zh = place_ref[0], place_ref[1], place_ref[2]
     weighting = loss_scale * area_ref[...] * var_ref[...]
-    dpred = (
-        weighting
-        * (smooth_grad(pred - truth_ref[...]) / members - pair / (members * (members - 1)))
-    ).astype(bf16)
+
+    def dpred_of(pred):
+        pair = -smooth_grad(pred - pred.astype(bf16).astype(f32))
+        for e in range(members):
+            pair = pair + smooth_grad(pred - every_ref[e].astype(f32))
+        against = smooth_grad(pred - truth_ref[...]) / members
+        return (weighting * (against - pair / (members * (members - 1)))).astype(bf16)
+
     scale = scale_column(idxt_ref)
+    first = (((0,), (0,)), ((), ()))
+    dpred = dpred_of(pred_ref[...])
     for n in range(width // NCOL):
         cols = slice(n * NCOL, (n + 1) * NCOL)
-        dagg = lax.dot_general(
-            dpred, wout_ref[:, cols], (((0,), (0,)), ((), ())), preferred_element_type=f32
-        )
-        dagg = dagg * scale
-        lead_ref[:, cols] = dagg.astype(bf16)
-        ddst[:, cols] = (dagg * sum_ref[:, cols].astype(f32)).astype(bf16)
-
-    stores[0].start()
+        dagg = lax.dot_general(dpred, wout_ref[:, cols], first, preferred_element_type=f32)
+        lead_ref[:, cols] = (dagg * scale).astype(bf16)
+    store.start()
+
+    quarter = wout_ref[:, pl.ds(pl.multiple_of(x * columns, columns), columns)]
+    total = jnp.zeros((sum_ref.shape[1], columns), f32)
+    for m in range(near):
+        other = dpred_of(every_ref[zh * near + m].astype(f32))
+        dagg = lax.dot_general(other, quarter, first, preferred_element_type=f32)
+        total = total + dagg * sum_ref[m].astype(f32)
+    ddst[...] = (total * scale).astype(bf16)
+
     for copy in loads:
         copy.wait()
-    mine = pl.ds(pl.multiple_of(core * half, half), half)
-    other = pl.ds(pl.multiple_of((1 - core) * half, half), half)
-    part[...] = jnp.dot(dpred, agg_ref[...], preferred_element_type=f32)
-    few = outs // 2
-    for ref, columns, which, store in (
-        (far_ref, other, 1 - core, stores[1]),
-        (own_ref, mine, core, stores[2]),
-    ):
-        give(
-            ref,
-            slice(0, half),
-            lax.dot_general(
-                grid_ref[...], ddst[:, columns], (((0,), (0,)), ((), ())), preferred_element_type=f32
-            ),
-        )
-        give(ref, slice(half, half + few), part[pl.ds(pl.multiple_of(which * few, few), few), :].T)
-        store.start()
-    for copy in stores:
-        copy.wait()
+    part_ref[...] = jnp.dot(dpred, agg_ref[...], preferred_element_type=f32)
+    few = own_ref.shape[1]
+    for ref, which in ((far_ref, 1 - core), (own_ref, core)):
+        ref[...] = lax.dot_general(
+            grid_ref[...],
+            ddst[:, pl.ds(pl.multiple_of(which * few, few), few)],
+            first,
+            preferred_element_type=f32,
+        ).astype(bf16)
+    store.wait()
 
 
 def prefetched(count, ins, outs, scratch):
@@ -282,40 +271,38 @@
     )
 
 
-def middle(core, everyone, pred, truth_t, area, var, wout_t, idx_t, sums, agg, grid_embed, chunks):
-    grid_rows, width = sums.shape
-    outs = pred.shape[0]
-    block = (chunks, width // chunks, (width + outs) // 2)
+def middle(place, everyone, pred, truth_t, area, var, wout_t, idx_t, sums, agg, grid_embed):
+    grid_rows, width = agg.shape
+    columns = sums.shape[2]
     anywhere = pl.BlockSpec(memory_space=pl.ANY)
     small = (everyone, pred, truth_t, area, var, wout_t, idx_t, sums)
+    out_shape = [
+        jax.ShapeDtypeStruct((grid_rows, width), bf16),
+        jax.ShapeDtypeStruct((width, columns // 2), bf16),
+        jax.ShapeDtypeStruct((width, columns // 2), bf16),
+        jax.ShapeDtypeStruct(wout_t.shape, f32),
+    ]
     return pl.pallas_call(
         middle_kernel,
         grid_spec=prefetched(
             1,
             [whole(x) for x in small] + [anywhere] * 2,
-            [anywhere] * 3,
+            [anywhere] + [whole(x) for x in out_shape[1:]],
             [
                 pltpu.VMEM((grid_rows, width), bf16),
                 pltpu.VMEM((grid_rows, width), bf16),
                 pltpu.VMEM((grid_rows, width), bf16),
-                pltpu.VMEM(block, bf16),
-                pltpu.VMEM(block, bf16),
-                pltpu.VMEM((grid_rows, width), bf16),
-                pltpu.VMEM((outs, width), f32),
-                pltpu.SemaphoreType.DMA((5,)),
+                pltpu.VMEM((grid_rows, columns), bf16),
+                pltpu.SemaphoreType.DMA((3,)),
             ],
         ),
-        out_shape=[
-            jax.ShapeDtypeStruct((grid_rows, width), bf16),
-            jax.ShapeDtypeStruct(block, bf16),
-            jax.ShapeDtypeStruct(block, bf16),
-        ],
+        out_shape=out_shape,
         compiler_params=params(),
         cost_estimate=pl.CostEstimate(
-            flops=2 * grid_rows * width * width, bytes_accessed=10 * grid_rows * width, transcendentals=0
+            flops=grid_rows * width * width, bytes_accessed=10 * grid_rows * width, transcendentals=0
         ),
         name="middle",
-    )(core, everyone, pred, truth_t, area, var, wout_t, idx_t, sums, agg, grid_embed)
+    )(place, everyone, pred, truth_t, area, var, wout_t, idx_t, sums, agg, grid_embed)
 
 
 def scatter_step(slots, gp_ref, lead_ref, idx_ref, hot, prod, acc):
@@ -340,25 +327,16 @@
         acc[:, here] += jnp.dot(hot[...], prod[:, here], preferred_element_type=f32)
 
 
+def joined_feats(below_ref, here_ref, above_ref):
+    return jnp.concatenate([below_ref[...], here_ref[...], above_ref[...]], axis=0)
+
+
+def out_columns(part_ref, which):
+    few = part_ref.shape[0] // 2
+    return part_ref[pl.ds(pl.multiple_of(which * few, few), few), :].T
+
+
 def far_kernel(
-    slots, core_ref, gp_ref, lead_ref, idx_ref, below_ref, here_ref, above_ref, wide_ref, part_ref, hot, prod, acc
-):
-    scatter_step(slots, gp_ref, lead_ref, idx_ref, hot, prod, acc)
-
-    @pl.when(pl.program_id(0) == pl.num_programs(0) - 1)
-    def _():
-        wide_ref[...] = acc[...].astype(bf16)
-        feats = jnp.concatenate([below_ref[...], here_ref[...], above_ref[...]], axis=0)
-        give(
-            part_ref,
-            slice(None),
-            lax.dot_general(
-                feats, wide_ref[...], (((0,), (0,)), ((), ())), preferred_element_type=f32
-            ),
-        )
-
-
-def own_kernel(
     slots,
     place_ref,
     gp_ref,
@@ -367,11 +345,38 @@
     below_ref,
     here_ref,
     above_ref,
+    part_ref,
+    wide_ref,
+    far_ref,
+    hot,
+    prod,
+    acc,
+):
+    scatter_step(slots, gp_ref, lead_ref, idx_ref, hot, prod, acc)
+
+    @pl.when(pl.program_id(0) == pl.num_programs(0) - 1)
+    def _():
+        half = acc.shape[1]
+        wide_ref[...] = acc[...].astype(bf16)
+        feats = joined_feats(below_ref, here_ref, above_ref)
+        product = lax.dot_general(
+            feats, wide_ref[...], (((0,), (0,)), ((), ())), preferred_element_type=f32
+        )
+        give(far_ref, slice(0, half), product)
+        give(far_ref, slice(half, far_ref.shape[2]), out_columns(part_ref, 1 - place_ref[0]))
+
+
+def own_kernel(
+    slots,
+    place_ref,
+    gp_ref,
+    lead_ref,
+    idx_ref,
     widefar_ref,
     lower_ref,
     centre_ref,
     upper_ref,
-    total_ref,
+    wide_ref,
     hot,
     prod,
     acc,
@@ -386,15 +391,43 @@
         mine = pl.ds(pl.multiple_of(core * half, half), half)
         other = pl.ds(pl.multiple_of((1 - core) * half, half), half)
         wide = acc[...].astype(bf16)
+        wide_ref[...] = wide
         for i, ref in enumerate((lower_ref, centre_ref, upper_ref)):
             ref[:, mine] = wide[i * block : (i + 1) * block, :]
             ref[:, other] = widefar_ref[i * block : (i + 1) * block, :]
-        feats = jnp.concatenate([below_ref[...], here_ref[...], above_ref[...]], axis=0)
-        give(
-            total_ref,
-            slice(None),
-            lax.dot_general(feats, wide, (((0,), (0,)), ((), ())), preferred_element_type=f32),
-        )
+
+
+def pack_kernel(place_ref, below_ref, here_ref, above_ref, wide_ref, part_ref, far_ref, total_ref):
+    half = wide_ref.shape[1]
+    feats = joined_feats(below_ref, here_ref, above_ref)
+    product = lax.dot_general(
+        feats, wide_ref[...], (((0,), (0,)), ((), ())), preferred_element_type=f32
+    )
+    chunks, rows = total_ref.shape[0], total_ref.shape[1] // GROUPS
+    columns = out_columns(part_ref, place_ref[0])
+    for zh in range(GROUPS):
+        here = slice(zh * rows, (zh + 1) * rows)
+        for values, at in (
+            (product, slice(0, half)),
+            (columns, slice(half, total_ref.shape[2])),
+        ):
+            some = values[zh * chunks * rows : (zh + 1) * chunks * rows, :]
+            some = some.reshape(chunks, rows, some.shape[1])
+            total_ref[:, here, at] = (some + far_ref[:, here, at].astype(f32)).astype(bf16)
+
+
+def pack(place, feats, wide, part, far):
+    ins = list(feats) + [wide, part, far]
+    return pl.pallas_call(
+        pack_kernel,
+        grid_spec=prefetched(1, [whole(x) for x in ins], whole(far), []),
+        out_shape=jax.ShapeDtypeStruct(far.shape, bf16),
+        compiler_params=params(),
+        cost_estimate=pl.CostEstimate(
+            flops=2 * far.size * wide.shape[0], bytes_accessed=4 * far.size, transcendentals=0
+        ),
+        name="pack",
+    )(place, *ins)
 
 
 def scatter_scratch(slots, nodes, half):
@@ -410,14 +443,13 @@
     return pl.CostEstimate(flops=gp.size * 256, bytes_accessed=gp.size, transcendentals=0)
 
 
-def backward(kernel, name, column, mine, gp, lead, idx_t, feats, extra, out_shape):
+def backward(kernel, name, column, place, gp, lead, idx_t, others, out_shape):
     grid_rows, width = lead.shape
     slots = idx_t.shape[0]
-    nodes = 3 * feats[0].shape[0]
     half = width // 2
+    nodes = out_shape[-1].shape[0] if kernel is own_kernel else out_shape[0].shape[0]
     rows = BACK * TILE
-    half_at = lambda t, core: (t, column(core[0]))
-    others = list(feats) + extra
+    half_at = lambda t, place: (t, column(place[0]))
     return pl.pallas_call(
         functools.partial(kernel, slots),
         grid_spec=prefetched(
@@ -425,7 +457,7 @@
             [
                 pl.BlockSpec((rows * slots, half), half_at),
                 pl.BlockSpec((rows, half), half_at),
-                pl.BlockSpec((slots, rows), lambda t, core: (0, t)),
+                pl.BlockSpec((slots, rows), lambda t, place: (0, t)),
             ]
             + [whole(x) for x in others],
             [whole(x) for x in out_shape],
@@ -435,32 +467,28 @@
         compiler_params=params(),
         cost_estimate=scatter_cost(gp),
         name=name,
-    )(mine, gp, lead, idx_t, *others)
-
-
-def product_shape(lead, chunks):
+    )(place, gp, lead, idx_t, *others)
+
+
+def backward_far(place, gp, lead, idx_t, feats, part, chunks):
     width = lead.shape[1]
-    return jax.ShapeDtypeStruct((chunks, width // chunks, width // 2), bf16)
-
-
-def backward_far(mine, gp, lead, idx_t, feats, chunks):
-    half = lead.shape[1] // 2
+    half = width // 2
     out_shape = [
         jax.ShapeDtypeStruct((3 * feats[0].shape[0], half), bf16),
-        product_shape(lead, chunks),
+        jax.ShapeDtypeStruct((chunks, width // chunks, half + part.shape[0] // 2), bf16),
     ]
     column = lambda core: 1 - core
-    return backward(far_kernel, "backward_far", column, mine, gp, lead, idx_t, feats, [], out_shape)
-
-
-def backward_own(mine, gp, lead, idx_t, feats, wide_far, chunks):
-    out_shape = [jax.ShapeDtypeStruct((feats[0].shape[0], lead.shape[1]), bf16)] * 3 + [
-        product_shape(lead, chunks)
+    others = list(feats) + [part]
+    return backward(far_kernel, "backward_far", column, place, gp, lead, idx_t, others, out_shape)
+
+
+def backward_own(place, gp, lead, idx_t, wide_far):
+    nodes, half = wide_far.shape
+    out_shape = [jax.ShapeDtypeStruct((nodes // 3, 2 * half), bf16)] * 3 + [
+        jax.ShapeDtypeStruct((nodes, half), bf16)
     ]
     column = lambda core: core
-    return backward(
-        own_kernel, "backward_own", column, mine, gp, lead, idx_t, feats, [wide_far], out_shape
-    )
+    return backward(own_kernel, "backward_own", column, place, gp, lead, idx_t, [wide_far], out_shape)
 
 
 def added(a, b):
@@ -491,8 +519,8 @@
     block_id = lax.axis_index(SPACE)
     members = lax.axis_size(ENS)
     swap = [(0, 1), (1, 0)]
-    core = lax.axis_index("c")
-    mine = jnp.full((1,), core, jnp.int32)
+    here = [lax.axis_index(name) for name in ("c", "x", "zh")]
+    place = jnp.stack(here).astype(jnp.int32)
 
     below = shifted(own, SPACE, 1)
     above = shifted(own, SPACE, -1)
@@ -509,23 +537,25 @@
     chunks = lax.axis_size(FIRST)
     gp, agg, sums, pred, sent = forward(*feats, w_src, dst, idx_t, wout_t, members)
     everyone = lax.all_to_all(sent, ENS, 0, 0, tiled=True)
-    lead, dst_own, dst_far = middle(
-        mine, everyone, pred, truth_t, area, var, wout_t, idx_t, sums, agg, grid_embed, chunks
+    sums = lax.all_to_all(sums, "x", 0, 0, tiled=True)
+    lead, dst_own, dst_far, part = middle(
+        place, everyone, pred, truth_t, area, var, wout_t, idx_t, sums, agg, grid_embed
     )
     dst_far = lax.ppermute(dst_far, "c", swap)
-    wide_far, src_far = backward_far(mine, gp, lead, idx_t, feats, chunks)
+    wide_far, src_far = backward_far(place, gp, lead, idx_t, feats, part, chunks)
     src_far = lax.ppermute(src_far, "c", swap)
-
-    dst_total = added(dst_own, dst_far)
-    lead, dst_total = lax.optimization_barrier((lead, dst_total))
-    dst_parts = lax.all_to_all(dst_total, FIRST, 0, 0, tiled=True)
-    lower, centre, upper, src_own = backward_own(mine, gp, lead, idx_t, feats, wide_far, chunks)
-    src_own, src_far, dst_parts = lax.optimization_barrier((src_own, src_far, dst_parts))
-    src_parts = lax.all_to_all(added(src_own, src_far), FIRST, 0, 0, tiled=True)
+    lower, centre, upper, wide_own = backward_own(place, gp, lead, idx_t, wide_far)
     from_above = shifted(lower, SPACE, -1)
     from_below = shifted(upper, SPACE, 1)
-    total = jnp.concatenate([summed(src_parts), summed(dst_parts)], axis=1)
-    total, from_above, from_below = lax.optimization_barrier((total, from_above, from_below))
+
+    src_total = pack(place, feats, wide_own, part, src_far)
+    src_parts = lax.all_to_all(src_total, FIRST, 0, 0, tiled=True)
+    src_total, dst_own, dst_far = lax.optimization_barrier((src_total, dst_own, dst_far))
+    dst_parts = lax.all_to_all(added(dst_own, dst_far), ENS + SPACE, 0, 0, tiled=True)
+    total = summed(src_parts)
+    total, dst_parts, from_above, from_below = lax.optimization_barrier(
+        (total, dst_parts, from_above, from_below)
+    )
     parts = lax.all_to_all(total, SECOND, 0, 0, tiled=True)
     dproj = (centre.astype(f32) + from_above.astype(f32) + from_below.astype(f32)).astype(bf16)
     grad_mesh = lax.dot_general(
@@ -534,11 +564,15 @@
     rows_out = width // lax.axis_size(ENS + SPACE)
     total = jnp.sum(parts.reshape(-1, 2, rows_out, parts.shape[1]).astype(f32), axis=0)
     joined = lambda a, b: jnp.concatenate([total[0, :, a:b], total[1, :, a:b]], axis=1)
+    sizes = [lax.axis_size(name) for name in ENS + SPACE]
+    dst_parts = dst_parts.reshape(*sizes, rows_out, dst_parts.shape[1])
+    dst_final = jnp.sum(dst_parts.astype(f32), axis=(0, 2, 3))
+    dst_final = dst_final.transpose(2, 0, 1, 3).reshape(rows_out, width)
     return (
         grad_mesh[None],
         joined(0, half),
-        joined(half, 2 * half),
-        joined(2 * half, total.shape[-1]),
+        dst_final,
+        joined(half, total.shape[-1]),
     )
 
 

time: 135 us -> 162 us (1.20)
  blocking collectives: 0 us -> 18.4 us
  Pallas kernels: 38.7 us -> 43.4 us
  waiting for transfers between devices: 40.9 us -> 44.6 us
  other arithmetic: 7.89 us -> 6.14 us
    all_to_all x0 -> x1, blocking collectives: none -> 18.4 us  [body(): everyone = lax.all_to_all(sent, ENS, 0, 0, tiled=True)]
    ppermute x1, starting transfers between devices: 0.04 us -> 9.61 us  [body(): src_far = lax.ppermute(src_far, 'c', swap)]
    ppermute x4, waiting for transfers between devices: 1.6 us -> 7.05 us  [shifted(): lax.ppermute(block, axes, [(i, (i + distance) % count) for i in range(cou...]
    ppermute x1, starting transfers between devices: 5.35 us -> 0.09 us  [body(): dst_far = lax.ppermute(dst_far, 'c', swap)]
    pallas_call x0 -> x1, Pallas kernels: none -> 3.89 us  [pack(): pl.pallas_call(pack_kernel, grid_spec=prefetched(1, [whole(x) for x in in...]
    all_to_all x1, waiting for transfers between devices: 6.09 us -> 3.25 us  [body(): parts = lax.all_to_all(total, SECOND, 0, 0, tiled=True)]
    convert_element_type x2 -> x1, other arithmetic: 4.34 us -> 1.74 us  [added(): return (a.astype(f32) + b.astype(f32)).astype(bf16)]
    all_to_all x3, starting transfers between devices: 17.1 us -> 15.3 us  [the longest x1 8.07 us: body(): lax.all_to_all(added(dst_own, dst_far), ENS + SPACE, 0, 0, tiled=True)]
  transfers between devices with their start and end apart: 10 -> 10, of which waited for: 5 -> 8; matrix products, arithmetic and copies ran while one was open for 8% -> 8% of each run, Pallas kernels for 11% -> 4%
where the time goes in v6:
time: 162 us; the launch traced here: 161 us
  waiting for transfers between devices  44.6 us (28%)
  Pallas kernels  43.4 us (27%)
  starting transfers between devices  36.7 us (23%)
  blocking collectives  18.4 us (11%)
  matrix products  6.69 us (4%)
  other arithmetic  6.14 us (4%)
  local copies, waits for them, and re-layouts  4.1 us (3%)
    pallas_call x1, Pallas kernels, forward(): pl.pallas_call(functools.partial(forward_kernel, slots, members), grid=(g...  18.6 us
    all_to_all x1, blocking collectives, body(): everyone = lax.all_to_all(sent, ENS, 0, 0, tiled=True)  18.4 us
    all_to_all x1, waiting for transfers between devices, body(): src_parts = lax.all_to_all(src_total, FIRST, 0, 0, tiled=True)  17.5 us
    pallas_call x2, Pallas kernels, backward(): pl.pallas_call(functools.partial(kernel, slots), grid_spec=prefetched(gri...  14.8 us
    ppermute x1, starting transfers between devices, body(): src_far = lax.ppermute(src_far, 'c', swap)  9.61 us
    all_to_all x1, waiting for transfers between devices, body(): sums = lax.all_to_all(sums, 'x', 0, 0, tiled=True)  8.49 us
    all_to_all x1, starting transfers between devices, body(): lax.all_to_all(added(dst_own, dst_far), ENS + SPACE, 0, 0, tiled=True)  8.07 us
    ppermute x4, waiting for transfers between devices, shifted(): lax.ppermute(block, axes, [(i, (i + distance) % count) for i in range(cou...  7.05 us
  transfers between devices with their start and end apart: 10, of which 8 were waited for; matrix products, arithmetic and copies ran while one was open for 8% of the time, Pallas kernels for 4%

profile of v6, /device:TPU:1, one launch (start us, length us, event | category | flops | bytes accessed | tf_op | source)
XLA Modules:
  0.0 160.7 jit_solution(8079444693564368324)
XLA Ops:
  0.6 3.3 %collective-permute-start.1 = (bf16[64,1024]{1,0:T(8,128)(2,1)}, bf16[64,1024]{1,0:T(8,128)(2,1)S(1)}, u32[]{:S(2)}, u32[]{:S(2)}) collective-permute-start(bf16[64,1024]{1,0:T(8,128)(2,1)} %bitcast.37), channel_id=1, source_target_pairs={{0,31},{1,0},{2,1},{3,2},{4,3},{5,4},{6,5},{7,6},{8,7},{9,8},{10,9... | collective-permute-start | bytes 393224 | tf_op jit(solution)/shard_map/ppermute | solution.py:28
  4.0 3.5 %convolution_convert_fusion.dst_ref = bf16[512,1024]{1,0:T(8,128)(2,1)} fusion(bf16[512,1024]{1,0:T(8,128)(2,1)} %grid_hbm.1, bf16[1024,1024]{1,0:T(8,128)(2,1)S(1)} %copy-done), kind=kOutput, calls=%fused_computation | convolution fusion | flops 1074266112 | bytes 4194304 | tf_op jit(solution)/shard_map/dot_general | solution.py:528
  7.4 0.6 fusion.2.idxt_ref.idx_ref
  8.1 1.7 %collective-permute-done.below_ref = bf16[64,1024]{1,0:T(8,128)(2,1)S(1)} collective-permute-done((bf16[64,1024]{1,0:T(8,128)(2,1)}, bf16[64,1024]{1,0:T(8,128)(2,1)S(1)}, u32[]{:S(2)}, u32[]{:S(2)}) %collective-permute-start) | collective-permute-done | bytes 131104 | tf_op jit(solution)/shard_map/ppermute | solution.py:28
  9.8 0.6 copy-done.4
  10.5 18.6 %forward.1 = (bf16[8192,1024]{1,0:T(8,128)(2,1)}, bf16[512,1024]{1,0:T(8,128)(2,1)}, bf16[4,512,256]{2,1,0:T(8,128)(2,1)}, f32[32,512]{1,0:T(8,128)}, bf16[8,32,512]{2,1,0:T(8,128)(2,1)}) custom-call(bf16[64,1024]{1,0:T(8,128)(2,1)} %copy-done.4, bf16[64,1024]{1,0:T(8,128)(2,1)} %bitcast.39, bf16[64,1024]{1,0:T(8,128)(2,1)} %copy-done.3, ...), custom_call_target="tpu_custom_call" | custom-call | flops 4294967296 | bytes 16777216 | tf_op jit(solution)/shard_map/forward/pallas_call | solution.py:160
  29.1 18.4 %all_to_all.36.every_ref = bf16[8,32,512]{2,1,0:T(8,128)(2,1)} all-to-all(bf16[8,32,512]{2,1,0:T(8,128)(2,1)} %get-tuple-element.32), channel_id=1, replica_groups=mesh['zh'=2,'x'=4,'y'=4,'zl'=4,'c'=2] {'zh','x'}, dimensions={0} | all-to-all | bytes 524288 | tf_op jit(solution)/shard_map/all_to_all | solution.py:539
  47.5 3.5 %all-to-all-start.1 = ((bf16[4,512,256]{2,1,0:T(8,128)(2,1)}), bf16[4,512,256]{2,1,0:T(8,128)(2,1)S(1)}, u32[]{:S(2)}, u32[]{:S(2)}) async-start(bf16[4,512,256]{2,1,0:T(8,128)(2,1)} %get-tuple-element.34), calls=%async_computation.1 | async-start | bytes 2097152 | tf_op jit(solution)/shard_map/all_to_all | solution.py:540
  51.0 0.7 copy.17.var_ref
  52.3 8.5 %all-to-all-done.1.sum_ref = bf16[4,512,256]{2,1,0:T(8,128)(2,1)S(1)} async-done(((bf16[4,512,256]{2,1,0:T(8,128)(2,1)}), bf16[4,512,256]{2,1,0:T(8,128)(2,1)S(1)}, u32[]{:S(2)}, u32[]{:S(2)}) %all-to-all-start.1) | async-done | bytes 1048608 | tf_op jit(solution)/shard_map/all_to_all | solution.py:540
  60.8 1.0 copy-done.1
  61.8 6.2 %middle.1 = (bf16[512,1024]{1,0:T(8,128)(2,1)}, bf16[1024,128]{1,0:T(8,128)(2,1)}, bf16[1024,128]{1,0:T(8,128)(2,1)}, f32[32,1024]{1,0:T(8,128)}) custom-call(s32[3]{0:T(128)} %pad_add_fusion.place_ref, bf16[8,32,512]{2,1,0:T(8,128)(2,1)} %all_to_all.36.every_ref, f32[32,512]{1,0:T(8,128)} %get-tuple-element.33.pred_ref, f32[32,512]{1,0:T(8,128)} %bitcast.45, ...), custom_call_target="tpu_custom_call" | custom-call | flops 536870912 | bytes 5242880 | tf_op jit(solution)/shard_map/middle/pallas_call | solution.py:285
  67.9 7.8 %backward_far.1 = (bf16[192,512]{1,0:T(8,128)(2,1)}, bf16[16,64,528]{2,1,0:T(8,128)(2,1)}) custom-call(s32[3]{0:T(128)} %pad_add_fusion.place_ref, bf16[8192,1024]{1,0:T(8,128)(2,1)} %get-tuple-element.31.gp_ref, bf16[512,1024]{1,0:T(8,128)(2,1)} %get-tuple-element.36.lead_ref, s32[16,512]{1,0:T(8,128)} %fusion.2.idxt_ref.idx_ref, ...), custom_call_target="tpu_custom_call" | custom-call | flops 2147483648 | bytes 8388608 | tf_op jit(solution)/shard_map/backward_far/pallas_call | solution.py:453
  75.8 9.6 %collective-permute-start.2 = (bf16[16,64,528]{2,1,0:T(8,128)(2,1)}, bf16[16,64,528]{2,1,0:T(8,128)(2,1)S(1)}, u32[]{:S(2)}, u32[]{:S(2)}) collective-permute-start(bf16[16,64,528]{2,1,0:T(8,128)(2,1)} %get-tuple-element.41), channel_id=1, source_target_pairs={{0,1},{1,0},{2,3},{3,2},{4,5},{5,4},{6,7},{7,6},{8,9},{9,8},{10,11... | collective-permute-start | bytes 3244040 | tf_op jit(solution)/shard_map/ppermute | solution.py:546
  85.4 7.0 %backward_own.1 = (bf16[64,1024]{1,0:T(8,128)(2,1)}, bf16[64,1024]{1,0:T(8,128)(2,1)}, bf16[64,1024]{1,0:T(8,128)(2,1)}, bf16[192,512]{1,0:T(8,128)(2,1)}) custom-call(s32[3]{0:T(128)} %pad_add_fusion.place_ref, bf16[8192,1024]{1,0:T(8,128)(2,1)} %get-tuple-element.31.gp_ref, bf16[512,1024]{1,0:T(8,128)(2,1)} %get-tuple-element.36.lead_ref, ...), custom_call_target="tpu_custom_call" | custom-call | flops 2147483648 | bytes 8388608 | tf_op jit(solution)/shard_map/backward_own/pallas_call | solution.py:453
  92.4 1.1 copy-done.2
  93.5 3.9 %pack.1 = bf16[16,64,528]{2,1,0:T(8,128)(2,1)} custom-call(s32[3]{0:T(128)} %pad_add_fusion.place_ref, bf16[64,1024]{1,0:T(8,128)(2,1)} %copy-done.4, bf16[64,1024]{1,0:T(8,128)(2,1)} %bitcast.41, bf16[64,1024]{1,0:T(8,128)(2,1)} %copy-done.3, bf16[192,512]{1,0:T(8,128)(2,1)} %get-tuple-element.40.wide_ref, f32[32,1024]{1,0:T(8,128)} %get-tuple-element.37.part_ref, ...), custom_call_target="tpu_custom_call" | custom-call | flops 207618048 | bytes 2162688 | tf_op jit(solution)/shard_map/pack/pallas_call | solution.py:421
  97.3 3.7 %all-to-all-start.2 = ((bf16[16,64,528]{2,1,0:T(8,128)(2,1)}), bf16[16,64,528]{2,1,0:T(8,128)(2,1)S(1)}, u32[]{:S(2)}, u32[]{:S(2)}) async-start(bf16[16,64,528]{2,1,0:T(8,128)(2,1)} %pack.1), calls=%async_computation.2 | async-start | bytes 2621440 | tf_op jit(solution)/shard_map/all_to_all | solution.py:552
  101.1 1.7 %collective-permute-done.3 = bf16[1024,128]{1,0:T(8,128)(2,1)S(1)} collective-permute-done((bf16[1024,128]{1,0:T(8,128)(2,1)}, bf16[1024,128]{1,0:T(8,128)(2,1)S(1)}, u32[]{:S(2)}, u32[]{:S(2)}) %collective-permute-start.3) | collective-permute-done | bytes 262176 | tf_op jit(solution)/shard_map/ppermute | solution.py:544
  102.9 1.7 %add_convert_fusion = bf16[1024,128]{1,0:T(8,128)(2,1)} fusion(bf16[1024,128]{1,0:T(8,128)(2,1)S(1)} %collective-permute-done.3, bf16[1024,128]{1,0:T(8,128)(2,1)} %get-tuple-element.44), kind=kLoop, calls=%fused_computation.4 | loop fusion | flops 524288 | bytes 786432 | tf_op jit(solution)/shard_map/convert_element_type | solution.py:495
  104.6 17.5 %all-to-all-done.2 = bf16[16,64,528]{2,1,0:T(8,128)(2,1)S(1)} async-done(((bf16[16,64,528]{2,1,0:T(8,128)(2,1)}), bf16[16,64,528]{2,1,0:T(8,128)(2,1)S(1)}, u32[]{:S(2)}, u32[]{:S(2)}) %all-to-all-start.2) | async-done | bytes 1081376 | tf_op jit(solution)/shard_map/all_to_all | solution.py:552
  122.1 8.1 %all-to-all-start.3 = ((bf16[256,4,128]{2,1,0:T(4,128)(2,1)}), bf16[256,4,128]{2,1,0:T(4,128)(2,1)}, u32[]{:S(2)}, u32[]{:S(2)}) async-start(bf16[256,4,128]{2,1,0:T(4,128)(2,1)} %bitcast.36), calls=%async_computation.3 | async-start | bytes 524288 | tf_op jit(solution)/shard_map/all_to_all | solution.py:554
  130.2 2.4 %collective-permute-start.4 = (bf16[64,1024]{1,0:T(8,128)(2,1)}, bf16[64,1024]{1,0:T(8,128)(2,1)}, u32[]{:S(2)}, u32[]{:S(2)}) collective-permute-start(bf16[64,1024]{1,0:T(8,128)(2,1)} %get-tuple-element.46), channel_id=1, source_target_pairs={{0,31},{1,0},{2,1},{3,2},{4,3},{5,4},{6,5},{7,6},{8,7},{9,8},{10,9... | collective-permute-start | bytes 393224 | tf_op jit(solution)/shard_map/ppermute | solution.py:28
  132.8 4.9 %collective-permute-done.4 = bf16[64,1024]{1,0:T(8,128)(2,1)} collective-permute-done((bf16[64,1024]{1,0:T(8,128)(2,1)}, bf16[64,1024]{1,0:T(8,128)(2,1)}, u32[]{:S(2)}, u32[]{:S(2)}) %collective-permute-start.4) | collective-permute-done | bytes 131104 | tf_op jit(solution)/shard_map/ppermute | solution.py:28
  138.1 6.6 %all-to-all-done.3 = bf16[256,4,128]{2,1,0:T(4,128)(2,1)} async-done(((bf16[256,4,128]{2,1,0:T(4,128)(2,1)}), bf16[256,4,128]{2,1,0:T(4,128)(2,1)}, u32[]{:S(2)}, u32[]{:S(2)}) %all-to-all-start.3) | async-done | bytes 262176 | tf_op jit(solution)/shard_map/all_to_all | solution.py:554
  144.7 0.7 all_to_all.29
  145.4 5.9 %all-to-all-start.4 = ((bf16[16,4,528]{2,1,0:T(4,128)(2,1)}), bf16[16,4,528]{2,1,0:T(4,128)(2,1)S(1)}, u32[]{:S(2)}, u32[]{:S(2)}) async-start(bf16[16,4,528]{2,1,0:T(4,128)(2,1)} %all_to_all.29), calls=%async_computation.4 | async-start | bytes 163840 | tf_op jit(solution)/shard_map/all_to_all | solution.py:559
  151.3 3.2 %fusion = bf16[1,64,1024]{2,1,0:T(8,128)(2,1)} fusion(bf16[1024,1024]{1,0:T(8,128)(2,1)} %wsrc_ref.1, bf16[64,1024]{1,0:T(8,128)(2,1)} %collective-permute-done.5, bf16[64,1024]{1,0:T(8,128)(2,1)} %collective-permute-done.4, bf16[64,1024]{1,0:T(8,128)(2,1)} %get-tuple-element.39), kind=kOutput, calls=%fused_computation.2 | convolution fusion | flops 134676480 | bytes 2621440 | tf_op jit(solution)/shard_map/dot_general | solution.py:561
  154.5 1.7 %convert_reduce_fusion = f32[4,2,4,128]{3,2,1,0:T(4,128)} fusion(bf16[2,4,4,4,2,4,128]{6,5,4,3,2,1,0:T(4,128)(2,1)} %bitcast.22), kind=kLoop, calls=%fused_computation.3 | loop fusion | flops 258048 | bytes 278528 | tf_op jit(solution)/shard_map/reduce_sum | solution.py:569
  156.2 3.2 %all-to-all-done.4 = bf16[16,4,528]{2,1,0:T(4,128)(2,1)S(1)} async-done(((bf16[16,4,528]{2,1,0:T(4,128)(2,1)}), bf16[16,4,528]{2,1,0:T(4,128)(2,1)S(1)}, u32[]{:S(2)}, u32[]{:S(2)}) %all-to-all-start.4) | async-done | bytes 67616 | tf_op jit(solution)/shard_map/all_to_all | solution.py:559
  159.5 0.6 pad_maximum_fusion
  160.1 0.7 pad_maximum_fusion.1
  (24 shorter events, 1.5 us)
Async XLA Ops:
  0.6 3.3 %copy-start = (bf16[1024,1024]{1,0:T(8,128)(2,1)S(1)}, bf16[1024,1024]{1,0:T(8,128)(2,1)}, u32[]{:S(2)}) copy-start(bf16[1024,1024]{1,0:T(8,128)(2,1)} %param.13) | copy-start | bytes 6291460
  0.6 9.2 %collective-permute-start.1 = (bf16[64,1024]{1,0:T(8,128)(2,1)}, bf16[64,1024]{1,0:T(8,128)(2,1)S(1)}, u32[]{:S(2)}, u32[]{:S(2)}) collective-permute-start(bf16[64,1024]{1,0:T(8,128)(2,1)} %bitcast.37), channel_id=1, source_target_pairs={{0,31},{1,0},{2,1},{3,2},{4,3},{5,4},{6,5},{7,6},{8,7},{9,8},{10,9... | collective-permute-start | bytes 393224 | tf_op jit(solution)/shard_map/ppermute | solution.py:28
  4.0 5.8 %collective-permute-start = (bf16[64,1024]{1,0:T(8,128)(2,1)}, bf16[64,1024]{1,0:T(8,128)(2,1)S(1)}, u32[]{:S(2)}, u32[]{:S(2)}) collective-permute-start(bf16[64,1024]{1,0:T(8,128)(2,1)} %bitcast.38), channel_id=1, source_target_pairs={{0,1},{1,2},{2,3},{3,4},{4,5},{5,6},{6,7},{7,8},{8,9},{9,10},{10,1... | collective-permute-start | bytes 393224 | tf_op jit(solution)/shard_map/ppermute | solution.py:28
  4.0 3.5 %copy-start.5 = (s32[512,16]{0,1:T(8,128)S(1)}, s32[512,16]{0,1:T(8,128)}, u32[]{:S(2)}) copy-start(s32[512,16]{0,1:T(8,128)} %param.18) | copy-start | bytes 98308
  4.0 3.5 %copy-start.6 = (s32[512,16]{0,1:T(8,128)S(1)}, s32[512,16]{0,1:T(8,128)}, u32[]{:S(2)}) copy-start(s32[512,16]{0,1:T(8,128)} %param.19) | copy-start | bytes 98308
  9.8 0.7 copy-start.4
  9.8 0.7 copy-start.3
  29.1 22.0 %copy-start.7 = (f32[32]{0:T(128)S(1)}, f32[32]{0:T(128)}, u32[]{:S(2)}) copy-start(f32[32]{0:T(128)} %param.17) | copy-start | bytes 388
  47.5 13.3 %all-to-all-start.1 = ((bf16[4,512,256]{2,1,0:T(8,128)(2,1)}), bf16[4,512,256]{2,1,0:T(8,128)(2,1)S(1)}, u32[]{:S(2)}, u32[]{:S(2)}) async-start(bf16[4,512,256]{2,1,0:T(8,128)(2,1)} %get-tuple-element.34), calls=%async_computation.1 | async-start | bytes 2097152 | tf_op jit(solution)/shard_map/all_to_all | solution.py:540
  60.8 1.0 copy-start.1
  75.8 16.6 %collective-permute-start.2 = (bf16[16,64,528]{2,1,0:T(8,128)(2,1)}, bf16[16,64,528]{2,1,0:T(8,128)(2,1)S(1)}, u32[]{:S(2)}, u32[]{:S(2)}) collective-permute-start(bf16[16,64,528]{2,1,0:T(8,128)(2,1)} %get-tuple-element.41), channel_id=1, source_target_pairs={{0,1},{1,0},{2,3},{3,2},{4,5},{5,4},{6,7},{7,6},{8,9},{9,8},{10,11... | collective-permute-start | bytes 3244040 | tf_op jit(solution)/shard_map/ppermute | solution.py:546
  92.4 1.1 copy-start.2
  97.3 24.8 %all-to-all-start.2 = ((bf16[16,64,528]{2,1,0:T(8,128)(2,1)}), bf16[16,64,528]{2,1,0:T(8,128)(2,1)S(1)}, u32[]{:S(2)}, u32[]{:S(2)}) async-start(bf16[16,64,528]{2,1,0:T(8,128)(2,1)} %pack.1), calls=%async_computation.2 | async-start | bytes 2621440 | tf_op jit(solution)/shard_map/all_to_all | solution.py:552
  101.0 1.8 %collective-permute-start.3 = (bf16[1024,128]{1,0:T(8,128)(2,1)}, bf16[1024,128]{1,0:T(8,128)(2,1)S(1)}, u32[]{:S(2)}, u32[]{:S(2)}) collective-permute-start(bf16[1024,128]{1,0:T(8,128)(2,1)} %get-tuple-element.43), channel_id=1, source_target_pairs={{0,1},{1,0},{2,3},{3,2},{4,5},{5,4},{6,7},{7,6},{8,9},{9,8},{10,11... | collective-permute-start | bytes 786440 | tf_op jit(solution)/shard_map/ppermute | solution.py:544
  122.1 22.6 %all-to-all-start.3 = ((bf16[256,4,128]{2,1,0:T(4,128)(2,1)}), bf16[256,4,128]{2,1,0:T(4,128)(2,1)}, u32[]{:S(2)}, u32[]{:S(2)}) async-start(bf16[256,4,128]{2,1,0:T(4,128)(2,1)} %bitcast.36), calls=%async_computation.3 | async-start | bytes 524288 | tf_op jit(solution)/shard_map/all_to_all | solution.py:554
  130.2 7.5 %collective-permute-start.4 = (bf16[64,1024]{1,0:T(8,128)(2,1)}, bf16[64,1024]{1,0:T(8,128)(2,1)}, u32[]{:S(2)}, u32[]{:S(2)}) collective-permute-start(bf16[64,1024]{1,0:T(8,128)(2,1)} %get-tuple-element.46), channel_id=1, source_target_pairs={{0,31},{1,0},{2,1},{3,2},{4,3},{5,4},{6,5},{7,6},{8,7},{9,8},{10,9... | collective-permute-start | bytes 393224 | tf_op jit(solution)/shard_map/ppermute | solution.py:28
  132.6 5.5 %collective-permute-start.5 = (bf16[64,1024]{1,0:T(8,128)(2,1)}, bf16[64,1024]{1,0:T(8,128)(2,1)}, u32[]{:S(2)}, u32[]{:S(2)}) collective-permute-start(bf16[64,1024]{1,0:T(8,128)(2,1)} %get-tuple-element.47), channel_id=1, source_target_pairs={{0,1},{1,2},{2,3},{3,4},{4,5},{5,6},{6,7},{7,8},{8,9},{9,10},{10,1... | collective-permute-start | bytes 393224 | tf_op jit(solution)/shard_map/ppermute | solution.py:28
  145.4 14.1 %all-to-all-start.4 = ((bf16[16,4,528]{2,1,0:T(4,128)(2,1)}), bf16[16,4,528]{2,1,0:T(4,128)(2,1)S(1)}, u32[]{:S(2)}, u32[]{:S(2)}) async-start(bf16[16,4,528]{2,1,0:T(4,128)(2,1)} %all_to_all.29), calls=%async_computation.4 | async-start | bytes 163840 | tf_op jit(solution)/shard_map/all_to_all | solution.py:559

commit v7 on v6

--- a/solution.py
+++ b/solution.py
@@ -15,6 +15,7 @@
 VMEM_LIMIT = 56 * 1024 * 1024
 BACK = 2
 GROUPS = 2
+QUARTERS = 4
 f32 = jnp.float32
 bf16 = jnp.bfloat16
 SPACE = ("y", "zl", "c")
@@ -66,6 +67,7 @@
 def forward_kernel(
     slots,
     members,
+    place_ref,
     below_ref,
     here_ref,
     above_ref,
@@ -75,27 +77,62 @@
     wout_ref,
     gp_ref,
     agg_ref,
-    sum_ref,
     pred_ref,
     sent_ref,
+    *rest,
+):
+    piece_refs = rest[:QUARTERS]
+    forward_steps(
+        slots,
+        members,
+        place_ref[1],
+        (below_ref, here_ref, above_ref),
+        wsrc_ref,
+        dst_ref,
+        idxt_ref,
+        wout_ref,
+        gp_ref,
+        agg_ref,
+        pred_ref,
+        sent_ref,
+        piece_refs,
+        *rest[QUARTERS:],
+    )
+
+
+def forward_steps(
+    slots,
+    members,
+    along,
+    feat_refs,
+    wsrc_ref,
+    dst_ref,
+    idxt_ref,
+    wout_ref,
+    gp_ref,
+    agg_ref,
+    pred_ref,
+    sent_ref,
+    piece_refs,
     feats,
     rhs,
     hot,
     pre,
     idx_all,
     scale_all,
+    sums,
 ):
     step = pl.program_id(0)
     nodes, width = feats.shape
     depth = rhs.shape[0]
     tile = depth - nodes
-    block = below_ref.shape[0]
+    block = feat_refs[0].shape[0]
 
     @pl.when(step == 0)
     def _():
         idx_all[...] = idxt_ref[...].astype(f32).T.astype(jnp.int32)
         scale_all[...] = scale_column(idxt_ref)
-        for i, ref in enumerate((below_ref, here_ref, above_ref)):
+        for i, ref in enumerate(feat_refs):
             feats[i * block : (i + 1) * block, :] = ref[...]
         for n in range(width // NCOL):
             cols = slice(n * NCOL, (n + 1) * NCOL)
@@ -132,7 +169,9 @@
                     acc_s = acc_s + some_s.astype(f32)
             scale = scale_all[pl.ds(pl.multiple_of(base + r, ROWS), ROWS), :]
             agg_ref[pl.ds(pl.multiple_of(base + r, ROWS), ROWS), cols] = (acc_g * scale).astype(bf16)
-            sum_ref[n, r : r + ROWS, :] = (acc_s - (slots - 0.5 / scale)).astype(bf16)
+            sums[n, pl.ds(pl.multiple_of(base + r, ROWS), ROWS), :] = (
+                acc_s - (slots - 0.5 / scale)
+            ).astype(bf16)
 
     @pl.when(step == pl.num_programs(0) - 1)
     def _():
@@ -142,46 +181,40 @@
         pred_ref[...] = pred
         for e in range(members):
             sent_ref[e] = pred.astype(bf16)
-
-
-def forward(below, here, above, w_src, dst, idx_t, wout_t, members):
+        for d, ref in enumerate(piece_refs):
+            ref[...] = sums[(along + d) % QUARTERS]
+
+
+def forward(place, below, here, above, w_src, dst, idx_t, wout_t, members):
     grid_rows, width = dst.shape
     nodes = 3 * here.shape[0]
     slots = idx_t.shape[0]
     outs = wout_t.shape[0]
-    step = lambda t: (t, 0)
+    step = lambda t, place: (t, 0)
     out_shape = [
         jax.ShapeDtypeStruct((grid_rows * slots, width), bf16),
         jax.ShapeDtypeStruct((grid_rows, width), bf16),
-        jax.ShapeDtypeStruct((width // NCOL, grid_rows, NCOL), bf16),
         jax.ShapeDtypeStruct((outs, grid_rows), f32),
         jax.ShapeDtypeStruct((members, outs, grid_rows), bf16),
-    ]
+    ] + [jax.ShapeDtypeStruct((grid_rows, NCOL), bf16)] * QUARTERS
     return pl.pallas_call(
         functools.partial(forward_kernel, slots, members),
-        grid=(grid_rows // TILE,),
-        in_specs=[whole(below), whole(here), whole(above), whole(w_src)]
-        + [
-            pl.BlockSpec((TILE, width), step),
-            whole(idx_t),
-            whole(wout_t),
-        ],
-        out_specs=[
-            pl.BlockSpec((TILE * slots, width), step),
-            whole(out_shape[1]),
-            pl.BlockSpec((width // NCOL, TILE, NCOL), lambda t: (0, t, 0)),
-            whole(out_shape[3]),
-            whole(out_shape[4]),
-        ],
+        grid_spec=prefetched(
+            grid_rows // TILE,
+            [whole(below), whole(here), whole(above), whole(w_src)]
+            + [pl.BlockSpec((TILE, width), step), whole(idx_t), whole(wout_t)],
+            [pl.BlockSpec((TILE * slots, width), step)] + [whole(x) for x in out_shape[1:]],
+            [
+                pltpu.VMEM((nodes, width), bf16),
+                pltpu.VMEM((nodes + TILE, width), bf16),
+                pltpu.VMEM((TILE * slots, nodes + TILE), bf16),
+                pltpu.VMEM((2, TILE * slots, NCOL), bf16),
+                pltpu.VMEM((grid_rows, slots), jnp.int32),
+                pltpu.VMEM((grid_rows, 1), f32),
+                pltpu.VMEM((QUARTERS, grid_rows, NCOL), bf16),
+            ],
+        ),
         out_shape=out_shape,
-        scratch_shapes=[
-            pltpu.VMEM((nodes, width), bf16),
-            pltpu.VMEM((nodes + TILE, width), bf16),
-            pltpu.VMEM((TILE * slots, nodes + TILE), bf16),
-            pltpu.VMEM((2, TILE * slots, NCOL), bf16),
-            pltpu.VMEM((grid_rows, slots), jnp.int32),
-            pltpu.VMEM((grid_rows, 1), f32),
-        ],
         compiler_params=params(),
         cost_estimate=pl.CostEstimate(
             flops=2 * grid_rows * slots * 256 * width,
@@ -189,7 +222,7 @@
             transcendentals=grid_rows * slots * width,
         ),
         name="forward",
-    )(below, here, above, w_src, dst, idx_t, wout_t)
+    )(place, below, here, above, w_src, dst, idx_t, wout_t)
 
 
 def middle_kernel(
@@ -201,7 +234,10 @@
     var_ref,
     wout_ref,
     idxt_ref,
-    sum_ref,
+    sum0_ref,
+    sum1_ref,
+    sum2_ref,
+    sum3_ref,
     agg_hbm,
     grid_hbm,
     lead_hbm,
@@ -223,7 +259,7 @@
         copy.start()
     width = wout_ref.shape[1]
     members = every_ref.shape[0]
-    near, columns = sum_ref.shape[0], sum_ref.shape[2]
+    near, columns = QUARTERS, sum0_ref.shape[1]
     core, x, zh = place_ref[0], place_ref[1], place_ref[2]
     weighting = loss_scale * area_ref[...] * var_ref[...]
 
@@ -244,24 +280,25 @@
     store.start()
 
     quarter = wout_ref[:, pl.ds(pl.multiple_of(x * columns, columns), columns)]
-    total = jnp.zeros((sum_ref.shape[1], columns), f32)
-    for m in range(near):
-        other = dpred_of(every_ref[zh * near + m].astype(f32))
+    total = jnp.zeros(sum0_ref.shape, f32)
+    for d, sum_ref in enumerate((sum0_ref, sum1_ref, sum2_ref, sum3_ref)):
+        other = dpred_of(every_ref[zh * near + (x + near - d) % near].astype(f32))
         dagg = lax.dot_general(other, quarter, first, preferred_element_type=f32)
-        total = total + dagg * sum_ref[m].astype(f32)
+        total = total + dagg * sum_ref[...].astype(f32)
     ddst[...] = (total * scale).astype(bf16)
 
     for copy in loads:
         copy.wait()
     part_ref[...] = jnp.dot(dpred, agg_ref[...], preferred_element_type=f32)
-    few = own_ref.shape[1]
+    few = own_ref.shape[-1]
     for ref, which in ((far_ref, 1 - core), (own_ref, core)):
-        ref[...] = lax.dot_general(
+        product = lax.dot_general(
             grid_ref[...],
             ddst[:, pl.ds(pl.multiple_of(which * few, few), few)],
             first,
             preferred_element_type=f32,
-        ).astype(bf16)
+        )
+        ref[...] = product.astype(bf16).reshape(ref.shape)
     store.wait()
 
 
@@ -273,13 +310,15 @@
 
 def middle(place, everyone, pred, truth_t, area, var, wout_t, idx_t, sums, agg, grid_embed):
     grid_rows, width = agg.shape
-    columns = sums.shape[2]
+    columns = sums[0].shape[1]
+    along = lax.axis_size("y")
+    product = (QUARTERS * GROUPS, along, width // (QUARTERS * GROUPS * along), columns // 2)
     anywhere = pl.BlockSpec(memory_space=pl.ANY)
-    small = (everyone, pred, truth_t, area, var, wout_t, idx_t, sums)
+    small = (everyone, pred, truth_t, area, var, wout_t, idx_t, *sums)
     out_shape = [
         jax.ShapeDtypeStruct((grid_rows, width), bf16),
-        jax.ShapeDtypeStruct((width, columns // 2), bf16),
-        jax.ShapeDtypeStruct((width, columns // 2), bf16),
+        jax.ShapeDtypeStruct(product, bf16),
+        jax.ShapeDtypeStruct(product, bf16),
         jax.ShapeDtypeStruct(wout_t.shape, f32),
     ]
     return pl.pallas_call(
@@ -302,7 +341,7 @@
             flops=grid_rows * width * width, bytes_accessed=10 * grid_rows * width, transcendentals=0
         ),
         name="middle",
-    )(place, everyone, pred, truth_t, area, var, wout_t, idx_t, sums, agg, grid_embed)
+    )(place, *small, agg, grid_embed)
 
 
 def scatter_step(slots, gp_ref, lead_ref, idx_ref, hot, prod, acc):
@@ -491,12 +530,58 @@
     return backward(own_kernel, "backward_own", column, place, gp, lead, idx_t, [wide_far], out_shape)
 
 
-def added(a, b):
-    return (a.astype(f32) + b.astype(f32)).astype(bf16)
-
-
-def summed(parts):
-    return jnp.sum(parts.astype(f32), axis=0).astype(bf16)
+def y_kernel(place_ref, own_ref, far_ref, *piece_refs):
+    for d, ref in enumerate(piece_refs):
+        at = (place_ref[3] + d) % own_ref.shape[1]
+        ref[...] = (own_ref[:, at].astype(f32) + far_ref[:, at].astype(f32)).astype(bf16)
+
+
+def x_kernel(place_ref, *refs):
+    ins, outs = refs[: len(refs) // 2], refs[len(refs) // 2 :]
+    for d, ref in enumerate(outs):
+        for zh in range(ref.shape[0]):
+            at = zh * QUARTERS + (place_ref[1] + d) % QUARTERS
+            total = ins[0][at].astype(f32)
+            for other in ins[1:]:
+                total = total + other[at].astype(f32)
+            ref[zh] = total.astype(bf16)
+
+
+def small_kernel(kernel, name, place, ins, out_shape):
+    size = sum(x.size for x in ins)
+    return pl.pallas_call(
+        kernel,
+        grid_spec=prefetched(
+            1, [whole(x) for x in ins], jax.tree.map(whole, out_shape), []
+        ),
+        out_shape=out_shape,
+        compiler_params=params(),
+        cost_estimate=pl.CostEstimate(flops=size, bytes_accessed=4 * size, transcendentals=0),
+        name=name,
+    )(place, *ins)
+
+
+def join_kernel(place_ref, src_ref, *refs):
+    pieces, total_ref = refs[:QUARTERS], refs[QUARTERS]
+    few = pieces[0].shape[2]
+    for d, ref in enumerate(pieces):
+        at = pl.multiple_of(((place_ref[1] + QUARTERS - d) % QUARTERS) * few, few)
+        total_ref[:, pl.ds(at, few)] = ref[...].reshape(total_ref.shape[0], few)
+    total_ref[:, QUARTERS * few :] = jnp.sum(src_ref[...].astype(f32), axis=0).astype(bf16)
+
+
+def last_kernel(place_ref, parts_ref, src_ref, dst_ref, out_ref):
+    few, half = dst_ref.shape[1] // (2 * QUARTERS), dst_ref.shape[1] // 2
+    width = out_ref.shape[1] // 2
+    for core in range(2):
+        total = parts_ref[core].astype(f32)
+        for other in range(core + 2, parts_ref.shape[0], 2):
+            total = total + parts_ref[other].astype(f32)
+        for x in range(QUARTERS):
+            at = (2 * x + core) * few
+            dst_ref[:, at : at + few] = total[:, x * few : (x + 1) * few]
+        src_ref[:, core * half : (core + 1) * half] = total[:, half : 2 * half]
+        out_ref[:, core * width : (core + 1) * width] = total[:, 2 * half :]
 
 
 def body(
@@ -519,7 +604,7 @@
     block_id = lax.axis_index(SPACE)
     members = lax.axis_size(ENS)
     swap = [(0, 1), (1, 0)]
-    here = [lax.axis_index(name) for name in ("c", "x", "zh")]
+    here = [lax.axis_index(name) for name in ("c", "x", "zh", "y")]
     place = jnp.stack(here).astype(jnp.int32)
 
     below = shifted(own, SPACE, 1)
@@ -532,12 +617,14 @@
     truth_t = truth.T
     var = var_weight[:, None]
     area = area_weight[None, :]
-    dst, idx_t, below = lax.optimization_barrier((dst, idx_t, below))
+    dst, idx_t, place, below = lax.optimization_barrier((dst, idx_t, place, below))
     feats = (below, own, above)
     chunks = lax.axis_size(FIRST)
-    gp, agg, sums, pred, sent = forward(*feats, w_src, dst, idx_t, wout_t, members)
+    gp, agg, pred, sent, kept, *pieces = forward(
+        place, *feats, w_src, dst, idx_t, wout_t, members
+    )
+    sums = [kept] + [shifted(piece, "x", d + 1) for d, piece in enumerate(pieces)]
     everyone = lax.all_to_all(sent, ENS, 0, 0, tiled=True)
-    sums = lax.all_to_all(sums, "x", 0, 0, tiled=True)
     lead, dst_own, dst_far, part = middle(
         place, everyone, pred, truth_t, area, var, wout_t, idx_t, sums, agg, grid_embed
     )
@@ -550,30 +637,31 @@
 
     src_total = pack(place, feats, wide_own, part, src_far)
     src_parts = lax.all_to_all(src_total, FIRST, 0, 0, tiled=True)
+
     src_total, dst_own, dst_far = lax.optimization_barrier((src_total, dst_own, dst_far))
-    dst_parts = lax.all_to_all(added(dst_own, dst_far), ENS + SPACE, 0, 0, tiled=True)
-    total = summed(src_parts)
-    total, dst_parts, from_above, from_below = lax.optimization_barrier(
-        (total, dst_parts, from_above, from_below)
-    )
+    block = jax.ShapeDtypeStruct((dst_own.shape[0],) + dst_own.shape[2:], bf16)
+    kept, *pieces = small_kernel(y_kernel, "along_y", place, [dst_own, dst_far], [block] * QUARTERS)
+    moved = [kept] + [shifted(piece, "y", d + 1) for d, piece in enumerate(pieces)]
+    block = jax.ShapeDtypeStruct((GROUPS,) + block.shape[1:], bf16)
+    kept, *pieces = small_kernel(x_kernel, "along_x", place, moved, [block] * QUARTERS)
+    moved = [kept] + [shifted(piece, "x", d + 1) for d, piece in enumerate(pieces)]
+
+    rows = GROUPS * block.shape[1]
+    joint = jax.ShapeDtypeStruct((rows, QUARTERS * block.shape[2] + src_parts.shape[2]), bf16)
+    total = small_kernel(join_kernel, "join", place, [src_parts] + moved, joint)
+    total, from_above, from_below = lax.optimization_barrier((total, from_above, from_below))
     parts = lax.all_to_all(total, SECOND, 0, 0, tiled=True)
     dproj = (centre.astype(f32) + from_above.astype(f32) + from_below.astype(f32)).astype(bf16)
     grad_mesh = lax.dot_general(
         dproj, w_src, (((1,), (1,)), ((), ())), preferred_element_type=f32
     ).astype(bf16)
     rows_out = width // lax.axis_size(ENS + SPACE)
-    total = jnp.sum(parts.reshape(-1, 2, rows_out, parts.shape[1]).astype(f32), axis=0)
-    joined = lambda a, b: jnp.concatenate([total[0, :, a:b], total[1, :, a:b]], axis=1)
-    sizes = [lax.axis_size(name) for name in ENS + SPACE]
-    dst_parts = dst_parts.reshape(*sizes, rows_out, dst_parts.shape[1])
-    dst_final = jnp.sum(dst_parts.astype(f32), axis=(0, 2, 3))
-    dst_final = dst_final.transpose(2, 0, 1, 3).reshape(rows_out, width)
-    return (
-        grad_mesh[None],
-        joined(0, half),
-        dst_final,
-        joined(half, total.shape[-1]),
-    )
+    finals = [
+        jax.ShapeDtypeStruct((rows_out, columns), f32) for columns in (width, width, w_out.shape[1])
+    ]
+    parts = parts.reshape(-1, rows_out, parts.shape[1])
+    src_final, dst_final, out_final = small_kernel(last_kernel, "last", place, [parts], finals)
+    return grad_mesh[None], src_final, dst_final, out_final
 
 
 def solution(mesh):

time: 162 us -> 150 us (0.926)
  blocking collectives: 18.4 us -> 0 us
  waiting for transfers between devices: 44.6 us -> 26.8 us
  starting transfers between devices: 36.7 us -> 50.8 us
  Pallas kernels: 43.4 us -> 54.5 us
  other arithmetic: 6.14 us -> 1.22 us
  local copies, waits for them, and re-layouts: 4.1 us -> 8.63 us
    all_to_all x1 -> x0, blocking collectives: 18.4 us -> none  [body(): everyone = lax.all_to_all(sent, ENS, 0, 0, tiled=True)]
    all_to_all x1, waiting for transfers between devices: 17.5 us -> 0.01 us  [body(): src_parts = lax.all_to_all(src_total, FIRST, 0, 0, tiled=True)]
    all_to_all x2 -> x1, waiting for transfers between devices: 15.1 us -> 0.01 us  [body(): everyone = lax.all_to_all(sent, ENS, 0, 0, tiled=True)]
    ppermute x4 -> x13, starting transfers between devices: 5.76 us -> 19.8 us  [shifted(): lax.ppermute(block, axes, [(i, (i + distance) % count) for i in range(cou...]
    ppermute x4 -> x13, waiting for transfers between devices: 7.05 us -> 20.6 us  [shifted(): lax.ppermute(block, axes, [(i, (i + distance) % count) for i in range(cou...]
    pallas_call x1 -> x5, Pallas kernels: 18.6 us -> 29.2 us  [the longest x1 19.5 us: forward(): pl.pallas_call(functools.partial(forward_kernel, slots, members), grid_sp...]
    unnamed x16 -> x40, local copies, waits for them, and re-layouts: 2.75 us -> 6.32 us
    all_to_all x1, waiting for transfers between devices: 3.25 us -> 6.15 us  [body(): parts = lax.all_to_all(total, SECOND, 0, 0, tiled=True)]
  transfers between devices with their start and end apart: 10 -> 18, of which waited for: 8 -> 9; matrix products, arithmetic and copies ran while one was open for 8% -> 6% of each run, Pallas kernels for 4% -> 10%
where the time goes in v7:
time: 150 us; the launch traced here: 149 us
  Pallas kernels  54.5 us (36%)
  starting transfers between devices  50.8 us (34%)
  waiting for transfers between devices  26.8 us (18%)
  local copies, waits for them, and re-layouts  8.63 us (6%)
  matrix products  6.65 us (4%)
    ppermute x13, waiting for transfers between devices, shifted(): lax.ppermute(block, axes, [(i, (i + distance) % count) for i in range(cou...  20.6 us
    ppermute x13, starting transfers between devices, shifted(): lax.ppermute(block, axes, [(i, (i + distance) % count) for i in range(cou...  19.8 us
    pallas_call x1, Pallas kernels, forward(): pl.pallas_call(functools.partial(forward_kernel, slots, members), grid_sp...  19.5 us
    pallas_call x2, Pallas kernels, backward(): pl.pallas_call(functools.partial(kernel, slots), grid_spec=prefetched(gri...  14.9 us
    pallas_call x4, Pallas kernels, small_kernel(): pl.pallas_call(kernel, grid_spec=prefetched(1, [whole(x) for x in ins], j...  9.73 us
    all_to_all x1, starting transfers between devices, body(): everyone = lax.all_to_all(sent, ENS, 0, 0, tiled=True)  8.86 us
    all_to_all x1, starting transfers between devices, body(): parts = lax.all_to_all(total, SECOND, 0, 0, tiled=True)  8.09 us
    ppermute x1, starting transfers between devices, body(): src_far = lax.ppermute(src_far, 'c', swap)  7.92 us
  transfers between devices with their start and end apart: 18, of which 9 were waited for; matrix products, arithmetic and copies ran while one was open for 6% of the time, Pallas kernels for 10%

profile of v7, /device:TPU:1, one launch (start us, length us, event | category | flops | bytes accessed | tf_op | source)
XLA Modules:
  0.0 149.3 jit_solution(16097324903619741988)
XLA Ops:
  0.6 3.3 %collective-permute-start.1 = (bf16[64,1024]{1,0:T(8,128)(2,1)}, bf16[64,1024]{1,0:T(8,128)(2,1)S(1)}, u32[]{:S(2)}, u32[]{:S(2)}) collective-permute-start(bf16[64,1024]{1,0:T(8,128)(2,1)} %bitcast.20), channel_id=1, source_target_pairs={{0,31},{1,0},{2,1},{3,2},{4,3},{5,4},{6,5},{7,6},{8,7},{9,8},{10,9... | collective-permute-start | bytes 393224 | tf_op jit(solution)/shard_map/ppermute | solution.py:29
  4.0 3.5 %convolution_convert_fusion.dst_ref = bf16[512,1024]{1,0:T(8,128)(2,1)} fusion(bf16[512,1024]{1,0:T(8,128)(2,1)} %grid_hbm.1, bf16[1024,1024]{1,0:T(8,128)(2,1)S(1)} %copy-done), kind=kOutput, calls=%fused_computation | convolution fusion | flops 1074266112 | bytes 4194304 | tf_op jit(solution)/shard_map/dot_general | solution.py:613
  8.7 1.1 collective-permute-done.below_ref
  10.5 19.5 %forward.1 = (bf16[8192,1024]{1,0:T(8,128)(2,1)}, bf16[512,1024]{1,0:T(8,128)(2,1)}, f32[32,512]{1,0:T(8,128)}, bf16[8,32,512]{2,1,0:T(8,128)(2,1)}, bf16[512,25...) custom-call(s32[4]{0:T(128)} %pad_add_fusion.place_ref, ...), custom_call_target="tpu_custom_call" | custom-call | flops 4294967296 | bytes 16777216 | tf_op jit(solution)/shard_map/forward/pallas_call | solution.py:200
  30.0 8.9 %all-to-all-start = ((bf16[8,32,512]{2,1,0:T(8,128)(2,1)}), bf16[8,32,512]{2,1,0:T(8,128)(2,1)S(1)}, u32[]{:S(2)}, u32[]{:S(2)}) async-start(bf16[8,32,512]{2,1,0:T(8,128)(2,1)} %get-tuple-element.47), calls=%async_computation | async-start | bytes 524288 | tf_op jit(solution)/shard_map/all_to_all | solution.py:627
  38.9 1.5 collective-permute-start.2
  40.3 2.4 %collective-permute-start.3 = (bf16[512,256]{1,0:T(8,128)(2,1)}, bf16[512,256]{1,0:T(8,128)(2,1)S(1)}, u32[]{:S(2)}, u32[]{:S(2)}) collective-permute-start(bf16[512,256]{1,0:T(8,128)(2,1)} %get-tuple-element.51), channel_id=1, source_target_pairs={{0,64},{32,96},{64,0},{96,32},{1,65},{33,97},{65,1},{97,33},{2,66}... | collective-permute-start | bytes 786440 | tf_op jit(solution)/shard_map/ppermute | solution.py:29
  42.7 1.2 collective-permute-start.4
  44.6 1.6 %collective-permute-done.2.sum1_ref = bf16[512,256]{1,0:T(8,128)(2,1)S(1)} collective-permute-done((bf16[512,256]{1,0:T(8,128)(2,1)}, bf16[512,256]{1,0:T(8,128)(2,1)S(1)}, u32[]{:S(2)}, u32[]{:S(2)}) %collective-permute-start.2) | collective-permute-done | bytes 262176 | tf_op jit(solution)/shard_map/ppermute | solution.py:29
  46.2 4.0 %collective-permute-done.3.sum2_ref = bf16[512,256]{1,0:T(8,128)(2,1)S(1)} collective-permute-done((bf16[512,256]{1,0:T(8,128)(2,1)}, bf16[512,256]{1,0:T(8,128)(2,1)S(1)}, u32[]{:S(2)}, u32[]{:S(2)}) %collective-permute-start.3) | collective-permute-done | bytes 262176 | tf_op jit(solution)/shard_map/ppermute | solution.py:29
  51.4 6.4 %middle.1 = (bf16[512,1024]{1,0:T(8,128)(2,1)}, bf16[8,4,32,128]{3,2,1,0:T(8,128)(2,1)}, bf16[8,4,32,128]{3,2,1,0:T(8,128)(2,1)}, f32[32,1024]{1,0:T(8,128)}) custom-call(s32[4]{0:T(128)} %pad_add_fusion.place_ref, bf16[8,32,512]{2,1,0:T(8,128)(2,1)} %copy-done.3, f32[32,512]{1,0:T(8,128)} %get-tuple-element.48.pred_ref, f32[32,512]{1,0:T(8,128)} %bitcast.27, ...), custom_call_target="tpu_custom_call" | custom-call | flops 536870912 | bytes 5242880 | tf_op jit(solution)/shard_map/middle/pallas_call | solution.py:324
  57.8 7.9 %backward_far.1 = (bf16[192,512]{1,0:T(8,128)(2,1)}, bf16[16,64,528]{2,1,0:T(8,128)(2,1)}) custom-call(s32[4]{0:T(128)} %pad_add_fusion.place_ref, bf16[8192,1024]{1,0:T(8,128)(2,1)} %get-tuple-element.46.gp_ref, bf16[512,1024]{1,0:T(8,128)(2,1)} %get-tuple-element.54.lead_ref, s32[16,512]{1,0:T(8,128)} %fusion.2.idxt_ref.idx_ref, ...), custom_call_target="tpu_custom_call" | custom-call | flops 2147483648 | bytes 8388608 | tf_op jit(solution)/shard_map/backward_far/pallas_call | solution.py:492
  65.7 7.9 %collective-permute-start.5 = (bf16[16,64,528]{2,1,0:T(8,128)(2,1)}, bf16[16,64,528]{2,1,0:T(8,128)(2,1)S(1)}, u32[]{:S(2)}, u32[]{:S(2)}) collective-permute-start(bf16[16,64,528]{2,1,0:T(8,128)(2,1)} %get-tuple-element.59), channel_id=1, source_target_pairs={{0,1},{1,0},{2,3},{3,2},{4,5},{5,4},{6,7},{7,6},{8,9},{9,8},{10,11... | collective-permute-start | bytes 3244040 | tf_op jit(solution)/shard_map/ppermute | solution.py:633
  73.6 7.0 %backward_own.1 = (bf16[64,1024]{1,0:T(8,128)(2,1)}, bf16[64,1024]{1,0:T(8,128)(2,1)}, bf16[64,1024]{1,0:T(8,128)(2,1)}, bf16[192,512]{1,0:T(8,128)(2,1)}) custom-call(s32[4]{0:T(128)} %pad_add_fusion.place_ref, bf16[8192,1024]{1,0:T(8,128)(2,1)} %get-tuple-element.46.gp_ref, bf16[512,1024]{1,0:T(8,128)(2,1)} %get-tuple-element.54.lead_ref, ...), custom_call_target="tpu_custom_call" | custom-call | flops 2147483648 | bytes 8388608 | tf_op jit(solution)/shard_map/backward_own/pallas_call | solution.py:492
  81.7 3.9 %pack.1 = bf16[16,64,528]{2,1,0:T(8,128)(2,1)} custom-call(s32[4]{0:T(128)} %pad_add_fusion.place_ref, bf16[64,1024]{1,0:T(8,128)(2,1)} %copy-done.6, bf16[64,1024]{1,0:T(8,128)(2,1)} %bitcast.24, bf16[64,1024]{1,0:T(8,128)(2,1)} %copy-done.5, bf16[192,512]{1,0:T(8,128)(2,1)} %get-tuple-element.58.wide_ref, f32[32,1024]{1,0:T(8,128)} %get-tuple-element.55.part_ref, ...), custom_call_target="tpu_custom_call" | custom-call | flops 207618048 | bytes 2162688 | tf_op jit(solution)/shard_map/pack/pallas_call | solution.py:460
  85.6 5.8 %all-to-all-start.1 = ((bf16[16,64,528]{2,1,0:T(8,128)(2,1)}), bf16[16,64,528]{2,1,0:T(8,128)(2,1)S(1)}, u32[]{:S(2)}, u32[]{:S(2)}) async-start(bf16[16,64,528]{2,1,0:T(8,128)(2,1)} %pack.1), calls=%async_computation.1 | async-start | bytes 2621440 | tf_op jit(solution)/shard_map/all_to_all | solution.py:639
  92.0 1.5 %collective-permute-start.14 = (bf16[64,1024]{1,0:T(8,128)(2,1)}, bf16[64,1024]{1,0:T(8,128)(2,1)}, u32[]{:S(2)}, u32[]{:S(2)}) collective-permute-start(bf16[64,1024]{1,0:T(8,128)(2,1)} %get-tuple-element.73), channel_id=1, source_target_pairs={{0,1},{1,2},{2,3},{3,4},{4,5},{5,6},{6,7},{7,8},{8,9},{9,10},{10,1... | collective-permute-start | bytes 393224 | tf_op jit(solution)/shard_map/ppermute | solution.py:29
  94.3 2.4 %along_y.1 = (bf16[8,32,128]{2,1,0:T(8,128)(2,1)}, bf16[8,32,128]{2,1,0:T(8,128)(2,1)}, bf16[8,32,128]{2,1,0:T(8,128)(2,1)}, bf16[8,32,128]{2,1,0:T(8,128)(2,1)}) custom-call(s32[4]{0:T(128)} %pad_add_fusion.place_ref, bf16[8,4,32,128]{3,2,1,0:T(8,128)(2,1)} %get-tuple-element.62.own_ref, bf16[8,4,32,128]{3,2,1,0:T(8,128)(2,1)} %copy-done.10), custom_call_target="tpu_custom_call" | custom-call | flops 262144 | bytes 1048576 | tf_op jit(solution)/shard_map/along_y/pallas_call | solution.py:552
  96.7 1.6 %collective-permute-start.7 = (bf16[8,32,128]{2,1,0:T(8,128)(2,1)}, bf16[8,32,128]{2,1,0:T(8,128)(2,1)S(1)}, u32[]{:S(2)}, u32[]{:S(2)}) collective-permute-start(bf16[8,32,128]{2,1,0:T(8,128)(2,1)} %get-tuple-element.65), channel_id=1, source_target_pairs={{0,8},{8,16},{16,24},{24,0},{1,9},{9,17},{17,25},{25,1},{2,10},{10... | collective-permute-start | bytes 196616 | tf_op jit(solution)/shard_map/ppermute | solution.py:29
  98.3 2.4 %collective-permute-start.8 = (bf16[8,32,128]{2,1,0:T(8,128)(2,1)}, bf16[8,32,128]{2,1,0:T(8,128)(2,1)S(1)}, u32[]{:S(2)}, u32[]{:S(2)}) collective-permute-start(bf16[8,32,128]{2,1,0:T(8,128)(2,1)} %get-tuple-element.66), channel_id=1, source_target_pairs={{0,16},{8,24},{16,0},{24,8},{1,17},{9,25},{17,1},{25,9},{2,18},{10... | collective-permute-start | bytes 196616 | tf_op jit(solution)/shard_map/ppermute | solution.py:29
  100.7 1.2 collective-permute-start.9
  101.9 9.4 %collective-permute-done.7.refs_1_ = bf16[8,32,128]{2,1,0:T(8,128)(2,1)S(1)} collective-permute-done((bf16[8,32,128]{2,1,0:T(8,128)(2,1)}, bf16[8,32,128]{2,1,0:T(8,128)(2,1)S(1)}, u32[]{:S(2)}, u32[]{:S(2)}) %collective-permute-start.7) | collective-permute-done | bytes 65568 | tf_op jit(solution)/shard_map/ppermute | solution.py:29
  111.2 2.6 %collective-permute-done.8.refs_2_ = bf16[8,32,128]{2,1,0:T(8,128)(2,1)S(1)} collective-permute-done((bf16[8,32,128]{2,1,0:T(8,128)(2,1)}, bf16[8,32,128]{2,1,0:T(8,128)(2,1)S(1)}, u32[]{:S(2)}, u32[]{:S(2)}) %collective-permute-start.8) | collective-permute-done | bytes 65568 | tf_op jit(solution)/shard_map/ppermute | solution.py:29
  114.5 2.2 %along_x.1 = (bf16[2,32,128]{2,1,0:T(8,128)(2,1)}, bf16[2,32,128]{2,1,0:T(8,128)(2,1)}, bf16[2,32,128]{2,1,0:T(8,128)(2,1)}, bf16[2,32,128]{2,1,0:T(8,128)(2,1)}) custom-call(s32[4]{0:T(128)} %pad_add_fusion.place_ref, bf16[8,32,128]{2,1,0:T(8,128)(2,1)} %get-tuple-element.64.refs_0_, bf16[8,32,128]{2,1,0:T(8,128)(2,1)} %copy-done.12, ...), custom_call_target="tpu_custom_call" | custom-call | flops 131072 | bytes 524288 | tf_op jit(solution)/shard_map/along_x/pallas_call | solution.py:552
  117.7 2.5 %collective-permute-start.11 = (bf16[2,32,128]{2,1,0:T(8,128)(2,1)}, bf16[2,32,128]{2,1,0:T(8,128)(2,1)S(1)}, u32[]{:S(2)}, u32[]{:S(2)}) collective-permute-start(bf16[2,32,128]{2,1,0:T(8,128)(2,1)} %get-tuple-element.70), channel_id=1, source_target_pairs={{0,64},{32,96},{64,0},{96,32},{1,65},{33,97},{65,1},{97,33},{2,66}... | collective-permute-start | bytes 49160 | tf_op jit(solution)/shard_map/ppermute | solution.py:29
  123.4 1.1 copy-done.1
  124.5 2.9 %join.1 = bf16[64,1040]{1,0:T(8,128)(2,1)} custom-call(s32[4]{0:T(128)} %pad_add_fusion.place_ref, bf16[16,64,528]{2,1,0:T(8,128)(2,1)} %copy-done.1, bf16[2,32,128]{2,1,0:T(8,128)(2,1)} %get-tuple-element.68.refs_0_, bf16[2,32,128]{2,1,0:T(8,128)(2,1)} %copy-done.17, bf16[2,32,128]{2,1,0:T(8,128)(2,1)} %copy-done.18, ...), custom_call_target="tpu_custom_call" | custom-call | flops 573440 | bytes 2293760 | tf_op jit(solution)/shard_map/join/pallas_call | solution.py:552
  127.4 1.6 %all_to_all.14 = bf16[16,4,1040]{2,1,0:T(4,128)(2,1)} reshape(bf16[64,1040]{1,0:T(8,128)(2,1)} %join.1) | data formatting | bytes 266240 | tf_op jit(solution)/shard_map/all_to_all | solution.py:653
  129.0 8.1 %all-to-all-start.2 = ((bf16[16,4,1040]{2,1,0:T(4,128)(2,1)}), bf16[16,4,1040]{2,1,0:T(4,128)(2,1)S(1)}, u32[]{:S(2)}, u32[]{:S(2)}) async-start(bf16[16,4,1040]{2,1,0:T(4,128)(2,1)} %all_to_all.14), calls=%async_computation.2 | async-start | bytes 294912 | tf_op jit(solution)/shard_map/all_to_all | solution.py:653
  137.1 3.2 %fusion = bf16[1,64,1024]{2,1,0:T(8,128)(2,1)} fusion(bf16[1024,1024]{1,0:T(8,128)(2,1)} %wsrc_ref.1, bf16[64,1024]{1,0:T(8,128)(2,1)} %collective-permute-done.14, bf16[64,1024]{1,0:T(8,128)(2,1)} %collective-permute-done.13, bf16[64,1024]{1,0:T(8,128)(2,1)S(1)} %copy-done.11), kind=kOutput, calls=%fused_computation.2 | convolution fusion | flops 134676480 | bytes 2621440 | tf_op jit(solution)/shard_map/dot_general | solution.py:655
  140.3 6.1 %all-to-all-done.2.parts_ref = bf16[16,4,1040]{2,1,0:T(4,128)(2,1)S(1)} async-done(((bf16[16,4,1040]{2,1,0:T(4,128)(2,1)}), bf16[16,4,1040]{2,1,0:T(4,128)(2,1)S(1)}, u32[]{:S(2)}, u32[]{:S(2)}) %all-to-all-start.2) | async-done | bytes 133152 | tf_op jit(solution)/shard_map/all_to_all | solution.py:653
  147.1 2.2 %last.1 = (f32[4,1024]{1,0:T(4,128)}, f32[4,1024]{1,0:T(4,128)}, f32[4,32]{1,0:T(4,128)}) custom-call(s32[4]{0:T(128)} %pad_add_fusion.place_ref, bf16[16,4,1040]{2,1,0:T(4,128)(2,1)} %copy-done.4), custom_call_target="tpu_custom_call" | custom-call | flops 66560 | bytes 266240 | tf_op jit(solution)/shard_map/last/pallas_call | solution.py:552
  (59 shorter events, 11.7 us)
Async XLA Ops:
  0.6 3.3 %copy-start = (bf16[1024,1024]{1,0:T(8,128)(2,1)S(1)}, bf16[1024,1024]{1,0:T(8,128)(2,1)}, u32[]{:S(2)}) copy-start(bf16[1024,1024]{1,0:T(8,128)(2,1)} %param.13) | copy-start | bytes 6291460
  0.6 9.2 %collective-permute-start.1 = (bf16[64,1024]{1,0:T(8,128)(2,1)}, bf16[64,1024]{1,0:T(8,128)(2,1)S(1)}, u32[]{:S(2)}, u32[]{:S(2)}) collective-permute-start(bf16[64,1024]{1,0:T(8,128)(2,1)} %bitcast.20), channel_id=1, source_target_pairs={{0,31},{1,0},{2,1},{3,2},{4,3},{5,4},{6,5},{7,6},{8,7},{9,8},{10,9... | collective-permute-start | bytes 393224 | tf_op jit(solution)/shard_map/ppermute | solution.py:29
  4.0 5.8 %collective-permute-start = (bf16[64,1024]{1,0:T(8,128)(2,1)}, bf16[64,1024]{1,0:T(8,128)(2,1)S(1)}, u32[]{:S(2)}, u32[]{:S(2)}) collective-permute-start(bf16[64,1024]{1,0:T(8,128)(2,1)} %bitcast.21), channel_id=1, source_target_pairs={{0,1},{1,2},{2,3},{3,4},{4,5},{5,6},{6,7},{7,8},{8,9},{9,10},{10,1... | collective-permute-start | bytes 393224 | tf_op jit(solution)/shard_map/ppermute | solution.py:29
  4.0 3.5 %copy-start.15 = (s32[512,16]{0,1:T(8,128)S(1)}, s32[512,16]{0,1:T(8,128)}, u32[]{:S(2)}) copy-start(s32[512,16]{0,1:T(8,128)} %param.18) | copy-start | bytes 98308
  4.0 3.5 %copy-start.16 = (s32[512,16]{0,1:T(8,128)S(1)}, s32[512,16]{0,1:T(8,128)}, u32[]{:S(2)}) copy-start(s32[512,16]{0,1:T(8,128)} %param.19) | copy-start | bytes 98308
  9.8 0.7 copy-start.5
  10.5 33.4 %copy-start.19 = (f32[32]{0:T(128)S(1)}, f32[32]{0:T(128)}, u32[]{:S(2)}) copy-start(f32[32]{0:T(128)} %param.17) | copy-start | bytes 388
  30.0 20.6 %all-to-all-start = ((bf16[8,32,512]{2,1,0:T(8,128)(2,1)}), bf16[8,32,512]{2,1,0:T(8,128)(2,1)S(1)}, u32[]{:S(2)}, u32[]{:S(2)}) async-start(bf16[8,32,512]{2,1,0:T(8,128)(2,1)} %get-tuple-element.47), calls=%async_computation | async-start | bytes 524288 | tf_op jit(solution)/shard_map/all_to_all | solution.py:627
  38.9 7.3 %collective-permute-start.2 = (bf16[512,256]{1,0:T(8,128)(2,1)}, bf16[512,256]{1,0:T(8,128)(2,1)S(1)}, u32[]{:S(2)}, u32[]{:S(2)}) collective-permute-start(bf16[512,256]{1,0:T(8,128)(2,1)} %get-tuple-element.50), channel_id=1, source_target_pairs={{0,32},{32,64},{64,96},{96,0},{1,33},{33,65},{65,97},{97,1},{2,34}... | collective-permute-start | bytes 786440 | tf_op jit(solution)/shard_map/ppermute | solution.py:29
  40.3 9.9 %collective-permute-start.3 = (bf16[512,256]{1,0:T(8,128)(2,1)}, bf16[512,256]{1,0:T(8,128)(2,1)S(1)}, u32[]{:S(2)}, u32[]{:S(2)}) collective-permute-start(bf16[512,256]{1,0:T(8,128)(2,1)} %get-tuple-element.51), channel_id=1, source_target_pairs={{0,64},{32,96},{64,0},{96,32},{1,65},{33,97},{65,1},{97,33},{2,66}... | collective-permute-start | bytes 786440 | tf_op jit(solution)/shard_map/ppermute | solution.py:29
  42.7 7.9 %collective-permute-start.4 = (bf16[512,256]{1,0:T(8,128)(2,1)}, bf16[512,256]{1,0:T(8,128)(2,1)S(1)}, u32[]{:S(2)}, u32[]{:S(2)}) collective-permute-start(bf16[512,256]{1,0:T(8,128)(2,1)} %get-tuple-element.52), channel_id=1, source_target_pairs={{0,96},{32,0},{64,32},{96,64},{1,97},{33,1},{65,33},{97,65},{2,98}... | collective-permute-start | bytes 786440 | tf_op jit(solution)/shard_map/ppermute | solution.py:29
  46.2 4.4 %copy-start.7 = (bf16[512,256]{1,0:T(8,128)(2,1)}, bf16[512,256]{1,0:T(8,128)(2,1)S(1)}, u32[]{:S(2)}) copy-start(bf16[512,256]{1,0:T(8,128)(2,1)S(1)} %collective-permute-done.2.sum1_ref) | copy-start | bytes 786436
  50.2 0.7 copy-start.8
  50.6 0.8 copy-start.3
  65.7 14.9 %collective-permute-start.5 = (bf16[16,64,528]{2,1,0:T(8,128)(2,1)}, bf16[16,64,528]{2,1,0:T(8,128)(2,1)S(1)}, u32[]{:S(2)}, u32[]{:S(2)}) collective-permute-start(bf16[16,64,528]{2,1,0:T(8,128)(2,1)} %get-tuple-element.59), channel_id=1, source_target_pairs={{0,1},{1,0},{2,3},{3,2},{4,5},{5,4},{6,7},{7,6},{8,9},{9,8},{10,11... | collective-permute-start | bytes 3244040 | tf_op jit(solution)/shard_map/ppermute | solution.py:633
  80.6 1.1 copy-start.2
  85.6 37.8 %all-to-all-start.1 = ((bf16[16,64,528]{2,1,0:T(8,128)(2,1)}), bf16[16,64,528]{2,1,0:T(8,128)(2,1)S(1)}, u32[]{:S(2)}, u32[]{:S(2)}) async-start(bf16[16,64,528]{2,1,0:T(8,128)(2,1)} %pack.1), calls=%async_computation.1 | async-start | bytes 2621440 | tf_op jit(solution)/shard_map/all_to_all | solution.py:639
  91.4 45.7 %copy-start.11 = (bf16[64,1024]{1,0:T(8,128)(2,1)S(1)}, bf16[64,1024]{1,0:T(8,128)(2,1)}, u32[]{:S(2)}) copy-start(bf16[64,1024]{1,0:T(8,128)(2,1)} %get-tuple-element.57) | copy-start | bytes 393220
  91.4 2.1 %collective-permute-start.6 = (bf16[8,4,32,128]{3,2,1,0:T(8,128)(2,1)}, bf16[8,4,32,128]{3,2,1,0:T(8,128)(2,1)S(1)}, u32[]{:S(2)}, u32[]{:S(2)}) collective-permute-start(bf16[8,4,32,128]{3,2,1,0:T(8,128)(2,1)} %get-tuple-element.61), channel_id=1, source_target_pairs={{0,1},{1,0},{2,3},{3,2},{4,5},{5,4},{6,7},{7,6},{8,9},{9,8},{10,11... | collective-permute-start | bytes 786440 | tf_op jit(solution)/shard_map/ppermute | solution.py:631
  91.8 35.6 %collective-permute-start.13 = (bf16[64,1024]{1,0:T(8,128)(2,1)}, bf16[64,1024]{1,0:T(8,128)(2,1)}, u32[]{:S(2)}, u32[]{:S(2)}) collective-permute-start(bf16[64,1024]{1,0:T(8,128)(2,1)} %get-tuple-element.72), channel_id=1, source_target_pairs={{0,31},{1,0},{2,1},{3,2},{4,3},{5,4},{6,5},{7,6},{8,7},{9,8},{10,9... | collective-permute-start | bytes 393224 | tf_op jit(solution)/shard_map/ppermute | solution.py:29
  92.0 35.4 %collective-permute-start.14 = (bf16[64,1024]{1,0:T(8,128)(2,1)}, bf16[64,1024]{1,0:T(8,128)(2,1)}, u32[]{:S(2)}, u32[]{:S(2)}) collective-permute-start(bf16[64,1024]{1,0:T(8,128)(2,1)} %get-tuple-element.73), channel_id=1, source_target_pairs={{0,1},{1,2},{2,3},{3,4},{4,5},{5,6},{6,7},{7,8},{8,9},{9,10},{10,1... | collective-permute-start | bytes 393224 | tf_op jit(solution)/shard_map/ppermute | solution.py:29
  93.6 0.7 copy-start.10
  96.7 14.6 %collective-permute-start.7 = (bf16[8,32,128]{2,1,0:T(8,128)(2,1)}, bf16[8,32,128]{2,1,0:T(8,128)(2,1)S(1)}, u32[]{:S(2)}, u32[]{:S(2)}) collective-permute-start(bf16[8,32,128]{2,1,0:T(8,128)(2,1)} %get-tuple-element.65), channel_id=1, source_target_pairs={{0,8},{8,16},{16,24},{24,0},{1,9},{9,17},{17,25},{25,1},{2,10},{10... | collective-permute-start | bytes 196616 | tf_op jit(solution)/shard_map/ppermute | solution.py:29
  98.3 15.5 %collective-permute-start.8 = (bf16[8,32,128]{2,1,0:T(8,128)(2,1)}, bf16[8,32,128]{2,1,0:T(8,128)(2,1)S(1)}, u32[]{:S(2)}, u32[]{:S(2)}) collective-permute-start(bf16[8,32,128]{2,1,0:T(8,128)(2,1)} %get-tuple-element.66), channel_id=1, source_target_pairs={{0,16},{8,24},{16,0},{24,8},{1,17},{9,25},{17,1},{25,9},{2,18},{10... | collective-permute-start | bytes 196616 | tf_op jit(solution)/shard_map/ppermute | solution.py:29
  100.7 13.1 %collective-permute-start.9 = (bf16[8,32,128]{2,1,0:T(8,128)(2,1)}, bf16[8,32,128]{2,1,0:T(8,128)(2,1)S(1)}, u32[]{:S(2)}, u32[]{:S(2)}) collective-permute-start(bf16[8,32,128]{2,1,0:T(8,128)(2,1)} %get-tuple-element.67), channel_id=1, source_target_pairs={{0,24},{8,0},{16,8},{24,16},{1,25},{9,1},{17,9},{25,17},{2,26},{10... | collective-permute-start | bytes 196616 | tf_op jit(solution)/shard_map/ppermute | solution.py:29
  111.2 2.6 %copy-start.12 = (bf16[8,32,128]{2,1,0:T(8,128)(2,1)}, bf16[8,32,128]{2,1,0:T(8,128)(2,1)S(1)}, u32[]{:S(2)}) copy-start(bf16[8,32,128]{2,1,0:T(8,128)(2,1)S(1)} %collective-permute-done.7.refs_1_) | copy-start | bytes 196612
  116.7 4.5 %collective-permute-start.10 = (bf16[2,32,128]{2,1,0:T(8,128)(2,1)}, bf16[2,32,128]{2,1,0:T(8,128)(2,1)S(1)}, u32[]{:S(2)}, u32[]{:S(2)}) collective-permute-start(bf16[2,32,128]{2,1,0:T(8,128)(2,1)} %get-tuple-element.69), channel_id=1, source_target_pairs={{0,32},{32,64},{64,96},{96,0},{1,33},{33,65},{65,97},{97,1},{2,34}... | collective-permute-start | bytes 49160 | tf_op jit(solution)/shard_map/ppermute | solution.py:29
  117.7 4.3 %collective-permute-start.11 = (bf16[2,32,128]{2,1,0:T(8,128)(2,1)}, bf16[2,32,128]{2,1,0:T(8,128)(2,1)S(1)}, u32[]{:S(2)}, u32[]{:S(2)}) collective-permute-start(bf16[2,32,128]{2,1,0:T(8,128)(2,1)} %get-tuple-element.70), channel_id=1, source_target_pairs={{0,64},{32,96},{64,0},{96,32},{1,65},{33,97},{65,1},{97,33},{2,66}... | collective-permute-start | bytes 49160 | tf_op jit(solution)/shard_map/ppermute | solution.py:29
  120.2 3.1 %collective-permute-start.12 = (bf16[2,32,128]{2,1,0:T(8,128)(2,1)}, bf16[2,32,128]{2,1,0:T(8,128)(2,1)}, u32[]{:S(2)}, u32[]{:S(2)}) collective-permute-start(bf16[2,32,128]{2,1,0:T(8,128)(2,1)} %get-tuple-element.71), channel_id=1, source_target_pairs={{0,96},{32,0},{64,32},{96,64},{1,97},{33,1},{65,33},{97,65},{2,98}... | collective-permute-start | bytes 49160 | tf_op jit(solution)/shard_map/ppermute | solution.py:29
  121.2 2.2 %copy-start.17 = (bf16[2,32,128]{2,1,0:T(8,128)(2,1)}, bf16[2,32,128]{2,1,0:T(8,128)(2,1)S(1)}, u32[]{:S(2)}) copy-start(bf16[2,32,128]{2,1,0:T(8,128)(2,1)S(1)} %collective-permute-done.10.refs_1_) | copy-start | bytes 49156
  123.4 1.1 copy-start.1
  129.0 17.4 %all-to-all-start.2 = ((bf16[16,4,1040]{2,1,0:T(4,128)(2,1)}), bf16[16,4,1040]{2,1,0:T(4,128)(2,1)S(1)}, u32[]{:S(2)}, u32[]{:S(2)}) async-start(bf16[16,4,1040]{2,1,0:T(4,128)(2,1)} %all_to_all.14), calls=%async_computation.2 | async-start | bytes 294912 | tf_op jit(solution)/shard_map/all_to_all | solution.py:653
  (6 other events, 3.9 us)

commit v8 on v7

--- a/solution.py
+++ b/solution.py
@@ -30,7 +30,7 @@
 
 
 def smooth_grad(diff):
-    return diff / jnp.sqrt(diff * diff + smooth_sq)
+    return diff * lax.rsqrt(diff * diff + smooth_sq)
 
 
 def gelu_parts(v):
@@ -243,11 +243,11 @@
     lead_hbm,
     own_ref,
     far_ref,
-    part_ref,
     agg_ref,
     grid_ref,
     lead_ref,
     ddst,
+    part_ref,
     sems,
 ):
     loads = [
@@ -290,7 +290,9 @@
     for copy in loads:
         copy.wait()
     part_ref[...] = jnp.dot(dpred, agg_ref[...], preferred_element_type=f32)
-    few = own_ref.shape[-1]
+    chunks, rows, few = own_ref.shape
+    outs = part_ref.shape[0] // 2
+    rows = rows - outs
     for ref, which in ((far_ref, 1 - core), (own_ref, core)):
         product = lax.dot_general(
             grid_ref[...],
@@ -298,7 +300,10 @@
             first,
             preferred_element_type=f32,
         )
-        ref[...] = product.astype(bf16).reshape(ref.shape)
+        ref[:, :rows, :] = product.astype(bf16).reshape(chunks, rows, few)
+        at = pl.ds(pl.multiple_of(which * outs, outs), outs)
+        for chunk in range(chunks):
+            ref[chunk, rows:, :] = part_ref[at, chunk * few : (chunk + 1) * few].astype(bf16)
     store.wait()
 
 
@@ -311,15 +316,14 @@
 def middle(place, everyone, pred, truth_t, area, var, wout_t, idx_t, sums, agg, grid_embed):
     grid_rows, width = agg.shape
     columns = sums[0].shape[1]
-    along = lax.axis_size("y")
-    product = (QUARTERS * GROUPS, along, width // (QUARTERS * GROUPS * along), columns // 2)
+    chunks = GROUPS * QUARTERS
+    product = (chunks, width // chunks + wout_t.shape[0] // 2, columns // 2)
     anywhere = pl.BlockSpec(memory_space=pl.ANY)
     small = (everyone, pred, truth_t, area, var, wout_t, idx_t, *sums)
     out_shape = [
         jax.ShapeDtypeStruct((grid_rows, width), bf16),
         jax.ShapeDtypeStruct(product, bf16),
         jax.ShapeDtypeStruct(product, bf16),
-        jax.ShapeDtypeStruct(wout_t.shape, f32),
     ]
     return pl.pallas_call(
         middle_kernel,
@@ -332,6 +336,7 @@
                 pltpu.VMEM((grid_rows, width), bf16),
                 pltpu.VMEM((grid_rows, width), bf16),
                 pltpu.VMEM((grid_rows, columns), bf16),
+                pltpu.VMEM(wout_t.shape, f32),
                 pltpu.SemaphoreType.DMA((3,)),
             ],
         ),
@@ -366,26 +371,16 @@
         acc[:, here] += jnp.dot(hot[...], prod[:, here], preferred_element_type=f32)
 
 
-def joined_feats(below_ref, here_ref, above_ref):
-    return jnp.concatenate([below_ref[...], here_ref[...], above_ref[...]], axis=0)
-
-
-def out_columns(part_ref, which):
-    few = part_ref.shape[0] // 2
-    return part_ref[pl.ds(pl.multiple_of(which * few, few), few), :].T
-
-
-def far_kernel(
+def backward_kernel(
     slots,
     place_ref,
     gp_ref,
     lead_ref,
     idx_ref,
-    below_ref,
-    here_ref,
-    above_ref,
-    part_ref,
-    wide_ref,
+    lower_ref,
+    centre_ref,
+    upper_ref,
+    own_ref,
     far_ref,
     hot,
     prod,
@@ -395,193 +390,97 @@
 
     @pl.when(pl.program_id(0) == pl.num_programs(0) - 1)
     def _():
-        half = acc.shape[1]
-        wide_ref[...] = acc[...].astype(bf16)
-        feats = joined_feats(below_ref, here_ref, above_ref)
-        product = lax.dot_general(
-            feats, wide_ref[...], (((0,), (0,)), ((), ())), preferred_element_type=f32
-        )
-        give(far_ref, slice(0, half), product)
-        give(far_ref, slice(half, far_ref.shape[2]), out_columns(part_ref, 1 - place_ref[0]))
-
-
-def own_kernel(
-    slots,
-    place_ref,
-    gp_ref,
-    lead_ref,
-    idx_ref,
-    widefar_ref,
-    lower_ref,
-    centre_ref,
-    upper_ref,
-    wide_ref,
-    hot,
-    prod,
-    acc,
+        core = place_ref[0]
+        half = own_ref.shape[1]
+        block = lower_ref.shape[0]
+        for i, ref in enumerate((lower_ref, centre_ref, upper_ref)):
+            ref[...] = acc[i * block : (i + 1) * block, :].astype(bf16)
+        own_ref[...] = acc[:, pl.ds(pl.multiple_of(core * half, half), half)].astype(bf16)
+        far_ref[...] = acc[:, pl.ds(pl.multiple_of((1 - core) * half, half), half)].astype(bf16)
+
+
+def backward(place, gp, lead, idx_t, nodes):
+    grid_rows, width = lead.shape
+    slots = idx_t.shape[0]
+    rows = BACK * TILE
+    out_shape = [jax.ShapeDtypeStruct((nodes // 3, width), bf16)] * 3 + [
+        jax.ShapeDtypeStruct((nodes, width // 2), bf16)
+    ] * 2
+    return pl.pallas_call(
+        functools.partial(backward_kernel, slots),
+        grid_spec=prefetched(
+            grid_rows // rows,
+            [
+                pl.BlockSpec((rows * slots, width), lambda t, place: (t, 0)),
+                pl.BlockSpec((rows, width), lambda t, place: (t, 0)),
+                pl.BlockSpec((slots, rows), lambda t, place: (0, t)),
+            ],
+            [whole(x) for x in out_shape],
+            [
+                pltpu.VMEM((nodes, rows * slots), bf16),
+                pltpu.VMEM((rows * slots, width), bf16),
+                pltpu.VMEM((nodes, width), f32),
+            ],
+        ),
+        out_shape=out_shape,
+        compiler_params=params(),
+        cost_estimate=pl.CostEstimate(flops=gp.size * 512, bytes_accessed=2 * gp.size, transcendentals=0),
+        name="backward",
+    )(place, gp, lead, idx_t)
+
+
+def pack_kernel(
+    place_ref, below_ref, here_ref, above_ref, edge_ref, own_ref, far_ref, dst_ref, dstfar_ref, total_ref
 ):
-    core = place_ref[0]
-    scatter_step(slots, gp_ref, lead_ref, idx_ref, hot, prod, acc)
-
-    @pl.when(pl.program_id(0) == pl.num_programs(0) - 1)
-    def _():
-        half = acc.shape[1]
-        block = lower_ref.shape[0]
-        mine = pl.ds(pl.multiple_of(core * half, half), half)
-        other = pl.ds(pl.multiple_of((1 - core) * half, half), half)
-        wide = acc[...].astype(bf16)
-        wide_ref[...] = wide
-        for i, ref in enumerate((lower_ref, centre_ref, upper_ref)):
-            ref[:, mine] = wide[i * block : (i + 1) * block, :]
-            ref[:, other] = widefar_ref[i * block : (i + 1) * block, :]
-
-
-def pack_kernel(place_ref, below_ref, here_ref, above_ref, wide_ref, part_ref, far_ref, total_ref):
-    half = wide_ref.shape[1]
-    feats = joined_feats(below_ref, here_ref, above_ref)
-    product = lax.dot_general(
-        feats, wide_ref[...], (((0,), (0,)), ((), ())), preferred_element_type=f32
-    )
-    chunks, rows = total_ref.shape[0], total_ref.shape[1] // GROUPS
-    columns = out_columns(part_ref, place_ref[0])
-    for zh in range(GROUPS):
-        here = slice(zh * rows, (zh + 1) * rows)
-        for values, at in (
-            (product, slice(0, half)),
-            (columns, slice(half, total_ref.shape[2])),
-        ):
-            some = values[zh * chunks * rows : (zh + 1) * chunks * rows, :]
-            some = some.reshape(chunks, rows, some.shape[1])
-            total_ref[:, here, at] = (some + far_ref[:, here, at].astype(f32)).astype(bf16)
-
-
-def pack(place, feats, wide, part, far):
-    ins = list(feats) + [wide, part, far]
+    low = place_ref[0] == 0
+    below, here, above, edge = below_ref[...], here_ref[...], above_ref[...], edge_ref[...]
+    first = (((0,), (0,)), ((), ()))
+    half = own_ref.shape[1]
+    mine = jnp.concatenate([below, here, above], axis=0)
+    other = jnp.concatenate(
+        [jnp.where(low, here, edge), jnp.where(low, above, below), jnp.where(low, edge, here)], axis=0
+    )
+    product = lax.dot_general(mine, own_ref[...], first, preferred_element_type=f32)
+    product = product + lax.dot_general(other, far_ref[...], first, preferred_element_type=f32)
+    give(total_ref, slice(0, half), product)
+    outs = total_ref.shape[2] - half
+    chunks, rows = dst_ref.shape[0], dst_ref.shape[1] - outs
+    columns = [
+        dst_ref[chunk, rows:, :].astype(f32) + dstfar_ref[chunk, rows:, :].astype(f32)
+        for chunk in range(chunks)
+    ]
+    give(total_ref, slice(half, half + outs), jnp.concatenate(columns, axis=1).T)
+
+
+def pack(place, feats, edge, own, far, dst_own, dst_far, chunks, outs):
+    width = feats[0].shape[1]
+    ins = list(feats) + [edge, own, far, dst_own, dst_far]
+    out_shape = jax.ShapeDtypeStruct((chunks, width // chunks, (width + outs) // 2), bf16)
     return pl.pallas_call(
         pack_kernel,
-        grid_spec=prefetched(1, [whole(x) for x in ins], whole(far), []),
-        out_shape=jax.ShapeDtypeStruct(far.shape, bf16),
+        grid_spec=prefetched(1, [whole(x) for x in ins], whole(out_shape), []),
+        out_shape=out_shape,
         compiler_params=params(),
         cost_estimate=pl.CostEstimate(
-            flops=2 * far.size * wide.shape[0], bytes_accessed=4 * far.size, transcendentals=0
+            flops=4 * width * own.size, bytes_accessed=4 * width * width, transcendentals=0
         ),
         name="pack",
     )(place, *ins)
 
 
-def scatter_scratch(slots, nodes, half):
-    wide = BACK * TILE * slots
+def quarters(array, axis, name):
+    count = lax.axis_size(name)
+    here = lax.axis_index(name)
     return [
-        pltpu.VMEM((nodes, wide), bf16),
-        pltpu.VMEM((wide, half), bf16),
-        pltpu.VMEM((nodes, half), f32),
+        lax.dynamic_index_in_dim(array, (here + d) % count, axis, keepdims=False) for d in range(count)
     ]
 
 
-def scatter_cost(gp):
-    return pl.CostEstimate(flops=gp.size * 256, bytes_accessed=gp.size, transcendentals=0)
-
-
-def backward(kernel, name, column, place, gp, lead, idx_t, others, out_shape):
-    grid_rows, width = lead.shape
-    slots = idx_t.shape[0]
-    half = width // 2
-    nodes = out_shape[-1].shape[0] if kernel is own_kernel else out_shape[0].shape[0]
-    rows = BACK * TILE
-    half_at = lambda t, place: (t, column(place[0]))
-    return pl.pallas_call(
-        functools.partial(kernel, slots),
-        grid_spec=prefetched(
-            grid_rows // rows,
-            [
-                pl.BlockSpec((rows * slots, half), half_at),
-                pl.BlockSpec((rows, half), half_at),
-                pl.BlockSpec((slots, rows), lambda t, place: (0, t)),
-            ]
-            + [whole(x) for x in others],
-            [whole(x) for x in out_shape],
-            scatter_scratch(slots, nodes, half),
-        ),
-        out_shape=out_shape,
-        compiler_params=params(),
-        cost_estimate=scatter_cost(gp),
-        name=name,
-    )(place, gp, lead, idx_t, *others)
-
-
-def backward_far(place, gp, lead, idx_t, feats, part, chunks):
-    width = lead.shape[1]
-    half = width // 2
-    out_shape = [
-        jax.ShapeDtypeStruct((3 * feats[0].shape[0], half), bf16),
-        jax.ShapeDtypeStruct((chunks, width // chunks, half + part.shape[0] // 2), bf16),
-    ]
-    column = lambda core: 1 - core
-    others = list(feats) + [part]
-    return backward(far_kernel, "backward_far", column, place, gp, lead, idx_t, others, out_shape)
-
-
-def backward_own(place, gp, lead, idx_t, wide_far):
-    nodes, half = wide_far.shape
-    out_shape = [jax.ShapeDtypeStruct((nodes // 3, 2 * half), bf16)] * 3 + [
-        jax.ShapeDtypeStruct((nodes, half), bf16)
-    ]
-    column = lambda core: core
-    return backward(own_kernel, "backward_own", column, place, gp, lead, idx_t, [wide_far], out_shape)
-
-
-def y_kernel(place_ref, own_ref, far_ref, *piece_refs):
-    for d, ref in enumerate(piece_refs):
-        at = (place_ref[3] + d) % own_ref.shape[1]
-        ref[...] = (own_ref[:, at].astype(f32) + far_ref[:, at].astype(f32)).astype(bf16)
-
-
-def x_kernel(place_ref, *refs):
-    ins, outs = refs[: len(refs) // 2], refs[len(refs) // 2 :]
-    for d, ref in enumerate(outs):
-        for zh in range(ref.shape[0]):
-            at = zh * QUARTERS + (place_ref[1] + d) % QUARTERS
-            total = ins[0][at].astype(f32)
-            for other in ins[1:]:
-                total = total + other[at].astype(f32)
-            ref[zh] = total.astype(bf16)
-
-
-def small_kernel(kernel, name, place, ins, out_shape):
-    size = sum(x.size for x in ins)
-    return pl.pallas_call(
-        kernel,
-        grid_spec=prefetched(
-            1, [whole(x) for x in ins], jax.tree.map(whole, out_shape), []
-        ),
-        out_shape=out_shape,
-        compiler_params=params(),
-        cost_estimate=pl.CostEstimate(flops=size, bytes_accessed=4 * size, transcendentals=0),
-        name=name,
-    )(place, *ins)
-
-
-def join_kernel(place_ref, src_ref, *refs):
-    pieces, total_ref = refs[:QUARTERS], refs[QUARTERS]
-    few = pieces[0].shape[2]
-    for d, ref in enumerate(pieces):
-        at = pl.multiple_of(((place_ref[1] + QUARTERS - d) % QUARTERS) * few, few)
-        total_ref[:, pl.ds(at, few)] = ref[...].reshape(total_ref.shape[0], few)
-    total_ref[:, QUARTERS * few :] = jnp.sum(src_ref[...].astype(f32), axis=0).astype(bf16)
-
-
-def last_kernel(place_ref, parts_ref, src_ref, dst_ref, out_ref):
-    few, half = dst_ref.shape[1] // (2 * QUARTERS), dst_ref.shape[1] // 2
-    width = out_ref.shape[1] // 2
-    for core in range(2):
-        total = parts_ref[core].astype(f32)
-        for other in range(core + 2, parts_ref.shape[0], 2):
-            total = total + parts_ref[other].astype(f32)
-        for x in range(QUARTERS):
-            at = (2 * x + core) * few
-            dst_ref[:, at : at + few] = total[:, x * few : (x + 1) * few]
-        src_ref[:, core * half : (core + 1) * half] = total[:, half : 2 * half]
-        out_ref[:, core * width : (core + 1) * width] = total[:, 2 * half :]
+def added(first, *others):
+    total = first.astype(f32)
+    for other in others:
+        total = total + other.astype(f32)
+    return total.astype(bf16)
 
 
 def body(
@@ -625,30 +524,39 @@
     )
     sums = [kept] + [shifted(piece, "x", d + 1) for d, piece in enumerate(pieces)]
     everyone = lax.all_to_all(sent, ENS, 0, 0, tiled=True)
-    lead, dst_own, dst_far, part = middle(
+    low = place[0] == 0
+    edge = lax.ppermute(jnp.where(low, below, above), "c", swap)
+    everyone, edge = lax.optimization_barrier((everyone, edge))
+    lead, dst_own, dst_far = middle(
         place, everyone, pred, truth_t, area, var, wout_t, idx_t, sums, agg, grid_embed
     )
     dst_far = lax.ppermute(dst_far, "c", swap)
-    wide_far, src_far = backward_far(place, gp, lead, idx_t, feats, part, chunks)
-    src_far = lax.ppermute(src_far, "c", swap)
-    lower, centre, upper, wide_own = backward_own(place, gp, lead, idx_t, wide_far)
+
+    outs = w_out.shape[1]
+    split = (members, lax.axis_size("y"), -1, dst_own.shape[2])
+    both = added(dst_own[:, : width // members], dst_far[:, : width // members]).reshape(split)
+    kept, *pieces = quarters(both, 1, "y")
+    lead, *pieces = lax.optimization_barrier((lead, *pieces))
+    moved = [shifted(piece, "y", d + 1) for d, piece in enumerate(pieces)]
+
+    lower, centre, upper, wide_own, wide_far = backward(place, gp, lead, idx_t, 3 * node_rows)
+    lower, upper, wide_far, *moved = lax.optimization_barrier((lower, upper, wide_far, *moved))
+    wide_far = lax.ppermute(wide_far, "c", swap)
     from_above = shifted(lower, SPACE, -1)
     from_below = shifted(upper, SPACE, 1)
 
-    src_total = pack(place, feats, wide_own, part, src_far)
+    src_total = pack(place, feats, edge, wide_own, wide_far, dst_own, dst_far, chunks, outs)
+    src_total, kept, *moved = lax.optimization_barrier((src_total, kept, *moved))
     src_parts = lax.all_to_all(src_total, FIRST, 0, 0, tiled=True)
 
-    src_total, dst_own, dst_far = lax.optimization_barrier((src_total, dst_own, dst_far))
-    block = jax.ShapeDtypeStruct((dst_own.shape[0],) + dst_own.shape[2:], bf16)
-    kept, *pieces = small_kernel(y_kernel, "along_y", place, [dst_own, dst_far], [block] * QUARTERS)
-    moved = [kept] + [shifted(piece, "y", d + 1) for d, piece in enumerate(pieces)]
-    block = jax.ShapeDtypeStruct((GROUPS,) + block.shape[1:], bf16)
-    kept, *pieces = small_kernel(x_kernel, "along_x", place, moved, [block] * QUARTERS)
-    moved = [kept] + [shifted(piece, "x", d + 1) for d, piece in enumerate(pieces)]
-
-    rows = GROUPS * block.shape[1]
-    joint = jax.ShapeDtypeStruct((rows, QUARTERS * block.shape[2] + src_parts.shape[2]), bf16)
-    total = small_kernel(join_kernel, "join", place, [src_parts] + moved, joint)
+    both = added(kept, *moved).reshape((GROUPS, QUARTERS) + kept.shape[1:])
+    kept, *pieces = quarters(both, 1, "x")
+    dst_parts = [kept] + [shifted(piece, "x", d + 1) for d, piece in enumerate(pieces)]
+
+    rows = GROUPS * kept.shape[1]
+    src_sum = jnp.sum(src_parts.astype(f32), axis=0).astype(bf16)
+    dst_sum = jnp.concatenate([x.reshape(rows, -1) for x in dst_parts], axis=1)
+    total = jnp.concatenate([dst_sum, src_sum], axis=1)
     total, from_above, from_below = lax.optimization_barrier((total, from_above, from_below))
     parts = lax.all_to_all(total, SECOND, 0, 0, tiled=True)
     dproj = (centre.astype(f32) + from_above.astype(f32) + from_below.astype(f32)).astype(bf16)
@@ -656,12 +564,20 @@
         dproj, w_src, (((1,), (1,)), ((), ())), preferred_element_type=f32
     ).astype(bf16)
     rows_out = width // lax.axis_size(ENS + SPACE)
-    finals = [
-        jax.ShapeDtypeStruct((rows_out, columns), f32) for columns in (width, width, w_out.shape[1])
-    ]
-    parts = parts.reshape(-1, rows_out, parts.shape[1])
-    src_final, dst_final, out_final = small_kernel(last_kernel, "last", place, [parts], finals)
-    return grad_mesh[None], src_final, dst_final, out_final
+    total = jnp.sum(parts.reshape(-1, 2, rows_out, parts.shape[1]).astype(f32), axis=0)
+    joined = lambda a, b: jnp.concatenate([total[0, :, a:b], total[1, :, a:b]], axis=1)
+    by_distance = total[:, :, :half].reshape(2, rows_out, QUARTERS, -1)
+    along = lax.axis_index("x")
+    x = jnp.arange(QUARTERS)
+    chosen = ((along - x[:, None]) % QUARTERS == x[None, :])[None, :, None, :, None]
+    by_distance = by_distance.transpose(1, 0, 2, 3)[:, None]
+    dst_final = jnp.sum(jnp.where(chosen, by_distance, 0.0), axis=3).reshape(rows_out, width)
+    return (
+        grad_mesh[None],
+        joined(half, 2 * half),
+        dst_final,
+        joined(2 * half, total.shape[-1]),
+    )
 
 
 def solution(mesh):

time: 150 us -> 136 us (0.907)
  Pallas kernels: 54.5 us -> 38.9 us
  waiting for transfers between devices: 26.8 us -> 18.5 us
  other arithmetic: 1.22 us -> 7.11 us
  starting transfers between devices: 50.8 us -> 55.2 us
    pallas_call x6 -> x1, Pallas kernels: 24.6 us -> 9.84 us  [backward(): pl.pallas_call(functools.partial(backward_kernel, slots), grid_spec=prefe...]
    ppermute x13, waiting for transfers between devices: 20.6 us -> 10.2 us  [shifted(): lax.ppermute(block, axes, [(i, (i + distance) % count) for i in range(cou...]
    ppermute x1, starting transfers between devices: 0.36 us -> 5.58 us  [body(): dst_far = lax.ppermute(dst_far, 'c', swap)]
    convert_element_type x0 -> x2, other arithmetic: none -> 2.04 us  [added(): return total.astype(bf16)]
    ppermute x1 -> x2, waiting for transfers between devices: 0.01 us -> 1.57 us  [the longest x1 1.28 us: body(): wide_far = lax.ppermute(wide_far, 'c', swap)]
    unnamed x40 -> x36, local copies, waits for them, and re-layouts: 6.32 us -> 4.76 us
    ppermute x1 -> x2, starting transfers between devices: 7.92 us -> 7.49 us  [the longest x1 6.32 us: body(): edge = lax.ppermute(jnp.where(low, below, above), 'c', swap)]
  transfers between devices with their start and end apart: 18 -> 19, of which waited for: 9 -> 7; matrix products, arithmetic and copies ran while one was open for 6% -> 11% of each run, Pallas kernels for 10% -> 7%
where the time goes in v8:
time: 136 us
  starting transfers between devices  55.2 us (41%)
  Pallas kernels  38.9 us (29%)
  waiting for transfers between devices  18.5 us (14%)
  local copies, waits for them, and re-layouts  8.41 us (6%)
  other arithmetic  7.11 us (5%)
  matrix products  6.69 us (5%)
    ppermute x13, starting transfers between devices, shifted(): lax.ppermute(block, axes, [(i, (i + distance) % count) for i in range(cou...  20.5 us
    pallas_call x1, Pallas kernels, forward(): pl.pallas_call(functools.partial(forward_kernel, slots, members), grid_sp...  19.5 us
    ppermute x13, waiting for transfers between devices, shifted(): lax.ppermute(block, axes, [(i, (i + distance) % count) for i in range(cou...  10.2 us
    pallas_call x1, Pallas kernels, backward(): pl.pallas_call(functools.partial(backward_kernel, slots), grid_spec=prefe...  9.84 us
    all_to_all x1, starting transfers between devices, body(): everyone = lax.all_to_all(sent, ENS, 0, 0, tiled=True)  8.69 us
    all_to_all x1, starting transfers between devices, body(): parts = lax.all_to_all(total, SECOND, 0, 0, tiled=True)  7.93 us
    ppermute x1, starting transfers between devices, body(): edge = lax.ppermute(jnp.where(low, below, above), 'c', swap)  6.32 us
    pallas_call x1, Pallas kernels, middle(): pl.pallas_call(middle_kernel, grid_spec=prefetched(1, [whole(x) for x in...  5.61 us
  transfers between devices with their start and end apart: 19, of which 7 were waited for; matrix products, arithmetic and copies ran while one was open for 11% of the time, Pallas kernels for 7%

profile of v8, /device:TPU:1, one launch (start us, length us, event | category | flops | bytes accessed | tf_op | source)
XLA Modules:
  0.0 135.8 jit_solution(9636704137597393690)
XLA Ops:
  0.6 3.1 %collective-permute-start = (bf16[64,1024]{1,0:T(8,128)(2,1)}, bf16[64,1024]{1,0:T(8,128)(2,1)S(1)}, u32[]{:S(2)}, u32[]{:S(2)}) collective-permute-start(bf16[64,1024]{1,0:T(8,128)(2,1)} %bitcast.59), channel_id=1, source_target_pairs={{0,1},{1,2},{2,3},{3,4},{4,5},{5,6},{6,7},{7,8},{8,9},{9,10},{10,1... | collective-permute-start | bytes 393224 | tf_op jit(solution)/shard_map/ppermute | solution.py:29
  4.1 3.5 %convolution_convert_fusion.dst_ref = bf16[512,1024]{1,0:T(8,128)(2,1)} fusion(bf16[512,1024]{1,0:T(8,128)(2,1)} %grid_hbm.1, bf16[1024,1024]{1,0:T(8,128)(2,1)S(1)} %copy-done), kind=kOutput, calls=%fused_computation | convolution fusion | flops 1074266112 | bytes 4194304 | tf_op jit(solution)/shard_map/dot_general | solution.py:512
  8.8 1.0 collective-permute-done.1.above_ref
  10.4 19.5 %forward.1 = (bf16[8192,1024]{1,0:T(8,128)(2,1)}, bf16[512,1024]{1,0:T(8,128)(2,1)}, f32[32,512]{1,0:T(8,128)}, bf16[8,32,512]{2,1,0:T(8,128)(2,1)}, bf16[512,25...) custom-call(s32[4]{0:T(128)} %pad_add_fusion.place_ref, ...), custom_call_target="tpu_custom_call" | custom-call | flops 4294967296 | bytes 16777216 | tf_op jit(solution)/shard_map/forward/pallas_call | solution.py:200
  30.0 8.7 %all-to-all-start = ((bf16[8,32,512]{2,1,0:T(8,128)(2,1)}), bf16[8,32,512]{2,1,0:T(8,128)(2,1)S(1)}, u32[]{:S(2)}, u32[]{:S(2)}) async-start(bf16[8,32,512]{2,1,0:T(8,128)(2,1)} %get-tuple-element.49), calls=%async_computation | async-start | bytes 524288 | tf_op jit(solution)/shard_map/all_to_all | solution.py:526
  38.6 1.5 %collective-permute-start.3 = (bf16[512,256]{1,0:T(8,128)(2,1)}, bf16[512,256]{1,0:T(8,128)(2,1)S(1)}, u32[]{:S(2)}, u32[]{:S(2)}) collective-permute-start(bf16[512,256]{1,0:T(8,128)(2,1)} %get-tuple-element.53), channel_id=1, source_target_pairs={{0,32},{32,64},{64,96},{96,0},{1,33},{33,65},{65,97},{97,1},{2,34}... | collective-permute-start | bytes 786440 | tf_op jit(solution)/shard_map/ppermute | solution.py:29
  40.1 2.4 %collective-permute-start.4 = (bf16[512,256]{1,0:T(8,128)(2,1)}, bf16[512,256]{1,0:T(8,128)(2,1)S(1)}, u32[]{:S(2)}, u32[]{:S(2)}) collective-permute-start(bf16[512,256]{1,0:T(8,128)(2,1)} %get-tuple-element.54), channel_id=1, source_target_pairs={{0,64},{32,96},{64,0},{96,32},{1,65},{33,97},{65,1},{97,33},{2,66}... | collective-permute-start | bytes 786440 | tf_op jit(solution)/shard_map/ppermute | solution.py:29
  42.5 1.2 collective-permute-start.5
  43.7 0.9 broadcast_select_fusion
  44.7 6.3 %collective-permute-start.2 = (bf16[64,1024]{1,0:T(8,128)(2,1)S(1)}, bf16[64,1024]{1,0:T(8,128)(2,1)S(1)}, u32[]{:S(2)}, u32[]{:S(2)}) collective-permute-start(bf16[64,1024]{1,0:T(8,128)(2,1)S(1)} %broadcast_select_fusion), channel_id=1, source_target_pairs={{0,1},{1,0},{2,3},{3,2},{4,5},{5,4},{6,7},{7,6},{8,9},{9,8},{10,11... | collective-permute-start | bytes 393224 | tf_op jit(solution)/shard_map/ppermute | solution.py:528
  53.0 5.6 %middle.1 = (bf16[512,1024]{1,0:T(8,128)(2,1)}, bf16[8,144,128]{2,1,0:T(8,128)(2,1)}, bf16[8,144,128]{2,1,0:T(8,128)(2,1)}) custom-call(s32[4]{0:T(128)} %pad_add_fusion.place_ref, bf16[8,32,512]{2,1,0:T(8,128)(2,1)} %copy-done.2, f32[32,512]{1,0:T(8,128)} %get-tuple-element.51.pred_ref, f32[32,512]{1,0:T(8,128)} %bitcast.65, f32[1,512]{1,0:T(1,128)} %bitcast.71, ...), custom_call_target="tpu_custom_call" | custom-call | flops 536870912 | bytes 5242880 | tf_op jit(solution)/shard_map/middle/pallas_call | solution.py:328
  58.6 5.6 %collective-permute-start.6 = (bf16[8,144,128]{2,1,0:T(8,128)(2,1)}, bf16[8,144,128]{2,1,0:T(8,128)(2,1)S(1)}, u32[]{:S(2)}, u32[]{:S(2)}) collective-permute-start(bf16[8,144,128]{2,1,0:T(8,128)(2,1)} %get-tuple-element.59), channel_id=1, source_target_pairs={{0,1},{1,0},{2,3},{3,2},{4,5},{5,4},{6,7},{7,6},{8,9},{9,8},{10,11... | collective-permute-start | bytes 884744 | tf_op jit(solution)/shard_map/ppermute | solution.py:533
  64.2 1.4 %collective-permute-done.6.dstfar_ref = bf16[8,144,128]{2,1,0:T(8,128)(2,1)S(1)} collective-permute-done((bf16[8,144,128]{2,1,0:T(8,128)(2,1)}, bf16[8,144,128]{2,1,0:T(8,128)(2,1)S(1)}, u32[]{:S(2)}, u32[]{:S(2)}) %collective-permute-start.6) | collective-permute-done | bytes 294944 | tf_op jit(solution)/shard_map/ppermute | solution.py:533
  65.6 1.1 add_convert_fusion
  66.8 1.4 %collective-permute-start.7 = (bf16[8,32,128]{2,1,0:T(8,128)(2,1)S(1)}, bf16[8,32,128]{2,1,0:T(8,128)(2,1)S(1)}, u32[]{:S(2)}, u32[]{:S(2)}) collective-permute-start(bf16[8,32,128]{2,1,0:T(8,128)(2,1)S(1)} %get-tuple-element.67), channel_id=1, source_target_pairs={{0,8},{8,16},{16,24},{24,0},{1,9},{9,17},{17,25},{25,1},{2,10},{10... | collective-permute-start | bytes 196616 | tf_op jit(solution)/shard_map/ppermute | solution.py:29
  68.2 4.0 %collective-permute-start.8 = (bf16[8,32,128]{2,1,0:T(8,128)(2,1)S(1)}, bf16[8,32,128]{2,1,0:T(8,128)(2,1)S(1)}, u32[]{:S(2)}, u32[]{:S(2)}) collective-permute-start(bf16[8,32,128]{2,1,0:T(8,128)(2,1)S(1)} %get-tuple-element.68), channel_id=1, source_target_pairs={{0,16},{8,24},{16,0},{24,8},{1,17},{9,25},{17,1},{25,9},{2,18},{10... | collective-permute-start | bytes 196616 | tf_op jit(solution)/shard_map/ppermute | solution.py:29
  72.1 9.8 %backward.1 = (bf16[64,1024]{1,0:T(8,128)(2,1)}, bf16[64,1024]{1,0:T(8,128)(2,1)}, bf16[64,1024]{1,0:T(8,128)(2,1)}, bf16[192,512]{1,0:T(8,128)(2,1)}, bf16[192,512]{1,0:T(8,128)(2,1)}) custom-call(s32[4]{0:T(128)} %pad_add_fusion.place_ref, bf16[8192,1024]{1,0:T(8,128)(2,1)} %get-tuple-element.48.gp_ref, bf16[512,1024]{1,0:T(8,128)(2,1)} %get-tuple-element.60.lead_ref, ...), custom_call_target="tpu_custom_call" | custom-call | flops 4294967296 | bytes 16777216 | tf_op jit(solution)/shard_map/backward/pallas_call | solution.py:409
  82.0 1.2 collective-permute-start.10
  83.2 1.3 collective-permute-done.10.far_ref
  85.2 3.9 %pack.1 = bf16[16,64,528]{2,1,0:T(8,128)(2,1)} custom-call(s32[4]{0:T(128)} %pad_add_fusion.place_ref, bf16[64,1024]{1,0:T(8,128)(2,1)} %copy-done.3, bf16[64,1024]{1,0:T(8,128)(2,1)} %bitcast.62, bf16[64,1024]{1,0:T(8,128)(2,1)} %copy-done.4, bf16[64,1024]{1,0:T(8,128)(2,1)} %copy-done.9, bf16[192,512]{1,0:T(8,128)(2,1)} %get-tuple-element.63.own_ref, ...), custom_call_target="tpu_custom_call" | custom-call | flops 402653184 | bytes 4194304 | tf_op jit(solution)/shard_map/pack/pallas_call | solution.py:459
  89.1 5.0 %all-to-all-start.1 = ((bf16[16,64,528]{2,1,0:T(8,128)(2,1)}), bf16[16,64,528]{2,1,0:T(8,128)(2,1)S(1)}, u32[]{:S(2)}, u32[]{:S(2)}) async-start(bf16[16,64,528]{2,1,0:T(8,128)(2,1)} %pack.1), calls=%async_computation.1 | async-start | bytes 2621440 | tf_op jit(solution)/shard_map/all_to_all | solution.py:550
  95.3 1.1 collective-permute-start.15
  96.4 0.9 add_convert_fusion.3
  97.4 1.4 %collective-permute-start.11 = (bf16[2,32,128]{2,1,0:T(8,128)(2,1)S(1)}, bf16[2,32,128]{2,1,0:T(8,128)(2,1)S(1)}, u32[]{:S(2)}, u32[]{:S(2)}) collective-permute-start(bf16[2,32,128]{2,1,0:T(8,128)(2,1)S(1)} %get-tuple-element.90), channel_id=1, source_target_pairs={{0,32},{32,64},{64,96},{96,0},{1,33},{33,65},{65,97},{97,1},{2,34}... | collective-permute-start | bytes 49160 | tf_op jit(solution)/shard_map/ppermute | solution.py:29
  99.3 2.4 %collective-permute-start.12 = (bf16[2,32,128]{2,1,0:T(8,128)(2,1)S(1)}, bf16[2,32,128]{2,1,0:T(8,128)(2,1)S(1)}, u32[]{:S(2)}, u32[]{:S(2)}) collective-permute-start(bf16[2,32,128]{2,1,0:T(8,128)(2,1)S(1)} %get-tuple-element.89), channel_id=1, source_target_pairs={{0,64},{32,96},{64,0},{96,32},{1,65},{33,97},{65,1},{97,33},{2,66}... | collective-permute-start | bytes 49160 | tf_op jit(solution)/shard_map/ppermute | solution.py:29
  101.7 1.2 collective-permute-start.13
  102.9 6.2 %collective-permute-done.11 = bf16[2,32,128]{2,1,0:T(8,128)(2,1)S(1)} collective-permute-done((bf16[2,32,128]{2,1,0:T(8,128)(2,1)S(1)}, bf16[2,32,128]{2,1,0:T(8,128)(2,1)S(1)}, u32[]{:S(2)}, u32[]{:S(2)}) %collective-permute-start.11) | collective-permute-done | bytes 16416 | tf_op jit(solution)/shard_map/ppermute | solution.py:29
  109.8 2.9 %collective-permute-done.12 = bf16[2,32,128]{2,1,0:T(8,128)(2,1)S(1)} collective-permute-done((bf16[2,32,128]{2,1,0:T(8,128)(2,1)S(1)}, bf16[2,32,128]{2,1,0:T(8,128)(2,1)S(1)}, u32[]{:S(2)}, u32[]{:S(2)}) %collective-permute-start.12) | collective-permute-done | bytes 16416 | tf_op jit(solution)/shard_map/ppermute | solution.py:29
  114.8 1.6 %all_to_all.14 = bf16[16,4,1040]{2,1,0:T(4,128)(2,1)} reshape(bf16[64,1040]{1,0:T(8,128)(2,1)} %constant_dynamic-update-slice_fusion) | data formatting | bytes 266240 | tf_op jit(solution)/shard_map/all_to_all | solution.py:561
  116.4 7.9 %all-to-all-start.2 = ((bf16[16,4,1040]{2,1,0:T(4,128)(2,1)}), bf16[16,4,1040]{2,1,0:T(4,128)(2,1)S(1)}, u32[]{:S(2)}, u32[]{:S(2)}) async-start(bf16[16,4,1040]{2,1,0:T(4,128)(2,1)} %all_to_all.14), calls=%async_computation.2 | async-start | bytes 294912 | tf_op jit(solution)/shard_map/all_to_all | solution.py:561
  125.0 3.2 %fusion = bf16[1,64,1024]{2,1,0:T(8,128)(2,1)} fusion(bf16[1024,1024]{1,0:T(8,128)(2,1)} %wsrc_ref.1, bf16[64,1024]{1,0:T(8,128)(2,1)} %collective-permute-done.15, bf16[64,1024]{1,0:T(8,128)(2,1)} %collective-permute-done.14, bf16[64,1024]{1,0:T(8,128)(2,1)} %get-tuple-element.61), kind=kOutput, calls=%fused_computation.2 | convolution fusion | flops 134676480 | bytes 2621440 | tf_op jit(solution)/shard_map/dot_general | solution.py:563
  128.3 5.4 %all-to-all-done.2 = bf16[16,4,1040]{2,1,0:T(4,128)(2,1)S(1)} async-done(((bf16[16,4,1040]{2,1,0:T(4,128)(2,1)}), bf16[16,4,1040]{2,1,0:T(4,128)(2,1)S(1)}, u32[]{:S(2)}, u32[]{:S(2)}) %all-to-all-start.2) | async-done | bytes 133152 | tf_op jit(solution)/shard_map/all_to_all | solution.py:561
  (70 shorter events, 12.2 us)
Async XLA Ops:
  0.6 3.4 %copy-start = (bf16[1024,1024]{1,0:T(8,128)(2,1)S(1)}, bf16[1024,1024]{1,0:T(8,128)(2,1)}, u32[]{:S(2)}) copy-start(bf16[1024,1024]{1,0:T(8,128)(2,1)} %param.13) | copy-start | bytes 6291460
  0.6 8.1 %collective-permute-start = (bf16[64,1024]{1,0:T(8,128)(2,1)}, bf16[64,1024]{1,0:T(8,128)(2,1)S(1)}, u32[]{:S(2)}, u32[]{:S(2)}) collective-permute-start(bf16[64,1024]{1,0:T(8,128)(2,1)} %bitcast.59), channel_id=1, source_target_pairs={{0,1},{1,2},{2,3},{3,4},{4,5},{5,6},{6,7},{7,8},{8,9},{9,10},{10,1... | collective-permute-start | bytes 393224 | tf_op jit(solution)/shard_map/ppermute | solution.py:29
  3.8 6.0 %collective-permute-start.1 = (bf16[64,1024]{1,0:T(8,128)(2,1)}, bf16[64,1024]{1,0:T(8,128)(2,1)S(1)}, u32[]{:S(2)}, u32[]{:S(2)}) collective-permute-start(bf16[64,1024]{1,0:T(8,128)(2,1)} %bitcast.60), channel_id=1, source_target_pairs={{0,31},{1,0},{2,1},{3,2},{4,3},{5,4},{6,5},{7,6},{8,7},{9,8},{10,9... | collective-permute-start | bytes 393224 | tf_op jit(solution)/shard_map/ppermute | solution.py:29
  4.1 3.5 %copy-start.12 = (s32[512,16]{0,1:T(8,128)S(1)}, s32[512,16]{0,1:T(8,128)}, u32[]{:S(2)}) copy-start(s32[512,16]{0,1:T(8,128)} %param.18) | copy-start | bytes 98308
  4.1 3.5 %copy-start.13 = (s32[512,16]{0,1:T(8,128)S(1)}, s32[512,16]{0,1:T(8,128)}, u32[]{:S(2)}) copy-start(s32[512,16]{0,1:T(8,128)} %param.19) | copy-start | bytes 98308
  8.8 1.0 copy-start.3
  10.4 33.3 %copy-start.14 = (s32[4]{0:T(128)S(1)}, s32[4]{0:T(128)}, u32[]{:S(2)}) copy-start(s32[4]{0:T(128)} %pad_add_fusion.place_ref) | copy-start | bytes 52
  10.4 40.6 %copy-start.15 = (f32[32]{0:T(128)S(1)}, f32[32]{0:T(128)}, u32[]{:S(2)}) copy-start(f32[32]{0:T(128)} %param.17) | copy-start | bytes 388
  30.0 22.0 %all-to-all-start = ((bf16[8,32,512]{2,1,0:T(8,128)(2,1)}), bf16[8,32,512]{2,1,0:T(8,128)(2,1)S(1)}, u32[]{:S(2)}, u32[]{:S(2)}) async-start(bf16[8,32,512]{2,1,0:T(8,128)(2,1)} %get-tuple-element.49), calls=%async_computation | async-start | bytes 524288 | tf_op jit(solution)/shard_map/all_to_all | solution.py:526
  38.6 13.3 %collective-permute-start.3 = (bf16[512,256]{1,0:T(8,128)(2,1)}, bf16[512,256]{1,0:T(8,128)(2,1)S(1)}, u32[]{:S(2)}, u32[]{:S(2)}) collective-permute-start(bf16[512,256]{1,0:T(8,128)(2,1)} %get-tuple-element.53), channel_id=1, source_target_pairs={{0,32},{32,64},{64,96},{96,0},{1,33},{33,65},{65,97},{97,1},{2,34}... | collective-permute-start | bytes 786440 | tf_op jit(solution)/shard_map/ppermute | solution.py:29
  40.1 11.9 %collective-permute-start.4 = (bf16[512,256]{1,0:T(8,128)(2,1)}, bf16[512,256]{1,0:T(8,128)(2,1)S(1)}, u32[]{:S(2)}, u32[]{:S(2)}) collective-permute-start(bf16[512,256]{1,0:T(8,128)(2,1)} %get-tuple-element.54), channel_id=1, source_target_pairs={{0,64},{32,96},{64,0},{96,32},{1,65},{33,97},{65,1},{97,33},{2,66}... | collective-permute-start | bytes 786440 | tf_op jit(solution)/shard_map/ppermute | solution.py:29
  42.5 9.5 %collective-permute-start.5 = (bf16[512,256]{1,0:T(8,128)(2,1)}, bf16[512,256]{1,0:T(8,128)(2,1)S(1)}, u32[]{:S(2)}, u32[]{:S(2)}) collective-permute-start(bf16[512,256]{1,0:T(8,128)(2,1)} %get-tuple-element.55), channel_id=1, source_target_pairs={{0,96},{32,0},{64,32},{96,64},{1,97},{33,1},{65,33},{97,65},{2,98}... | collective-permute-start | bytes 786440 | tf_op jit(solution)/shard_map/ppermute | solution.py:29
  44.7 7.3 %collective-permute-start.2 = (bf16[64,1024]{1,0:T(8,128)(2,1)S(1)}, bf16[64,1024]{1,0:T(8,128)(2,1)S(1)}, u32[]{:S(2)}, u32[]{:S(2)}) collective-permute-start(bf16[64,1024]{1,0:T(8,128)(2,1)S(1)} %broadcast_select_fusion), channel_id=1, source_target_pairs={{0,1},{1,0},{2,3},{3,2},{4,5},{5,4},{6,7},{7,6},{8,9},{9,8},{10,11... | collective-permute-start | bytes 393224 | tf_op jit(solution)/shard_map/ppermute | solution.py:528
  52.0 30.0 %copy-start.9 = (bf16[64,1024]{1,0:T(8,128)(2,1)}, bf16[64,1024]{1,0:T(8,128)(2,1)S(1)}, u32[]{:S(2)}) copy-start(bf16[64,1024]{1,0:T(8,128)(2,1)S(1)} %collective-permute-done.2.edge_ref) | copy-start | bytes 393220
  52.0 0.8 copy-start.5
  52.0 0.9 copy-start.6
  52.0 1.0 copy-start.7
  58.6 7.0 %collective-permute-start.6 = (bf16[8,144,128]{2,1,0:T(8,128)(2,1)}, bf16[8,144,128]{2,1,0:T(8,128)(2,1)S(1)}, u32[]{:S(2)}, u32[]{:S(2)}) collective-permute-start(bf16[8,144,128]{2,1,0:T(8,128)(2,1)} %get-tuple-element.59), channel_id=1, source_target_pairs={{0,1},{1,0},{2,3},{3,2},{4,5},{5,4},{6,7},{7,6},{8,9},{9,8},{10,11... | collective-permute-start | bytes 884744 | tf_op jit(solution)/shard_map/ppermute | solution.py:533
  65.6 16.4 %copy-start.1 = (bf16[8,144,128]{2,1,0:T(8,128)(2,1)}, bf16[8,144,128]{2,1,0:T(8,128)(2,1)S(1)}, u32[]{:S(2)}) copy-start(bf16[8,144,128]{2,1,0:T(8,128)(2,1)S(1)} %collective-permute-done.6.dstfar_ref) | copy-start | bytes 884740
  66.8 15.2 %collective-permute-start.7 = (bf16[8,32,128]{2,1,0:T(8,128)(2,1)S(1)}, bf16[8,32,128]{2,1,0:T(8,128)(2,1)S(1)}, u32[]{:S(2)}, u32[]{:S(2)}) collective-permute-start(bf16[8,32,128]{2,1,0:T(8,128)(2,1)S(1)} %get-tuple-element.67), channel_id=1, source_target_pairs={{0,8},{8,16},{16,24},{24,0},{1,9},{9,17},{17,25},{25,1},{2,10},{10... | collective-permute-start | bytes 196616 | tf_op jit(solution)/shard_map/ppermute | solution.py:29
  68.2 13.8 %collective-permute-start.8 = (bf16[8,32,128]{2,1,0:T(8,128)(2,1)S(1)}, bf16[8,32,128]{2,1,0:T(8,128)(2,1)S(1)}, u32[]{:S(2)}, u32[]{:S(2)}) collective-permute-start(bf16[8,32,128]{2,1,0:T(8,128)(2,1)S(1)} %get-tuple-element.68), channel_id=1, source_target_pairs={{0,16},{8,24},{16,0},{24,8},{1,17},{9,25},{17,1},{25,9},{2,18},{10... | collective-permute-start | bytes 196616 | tf_op jit(solution)/shard_map/ppermute | solution.py:29
  72.1 9.9 %collective-permute-start.9 = (bf16[8,32,128]{2,1,0:T(8,128)(2,1)S(1)}, bf16[8,32,128]{2,1,0:T(8,128)(2,1)S(1)}, u32[]{:S(2)}, u32[]{:S(2)}) collective-permute-start(bf16[8,32,128]{2,1,0:T(8,128)(2,1)S(1)} %get-tuple-element.69), channel_id=1, source_target_pairs={{0,24},{8,0},{16,8},{24,16},{1,25},{9,1},{17,9},{25,17},{2,26},{10... | collective-permute-start | bytes 196616 | tf_op jit(solution)/shard_map/ppermute | solution.py:29
  82.0 7.1 %copy-start.10 = (bf16[8,32,128]{2,1,0:T(8,128)(2,1)}, bf16[8,32,128]{2,1,0:T(8,128)(2,1)S(1)}, u32[]{:S(2)}) copy-start(bf16[8,32,128]{2,1,0:T(8,128)(2,1)S(1)} %collective-permute-done.8) | copy-start | bytes 196612
  82.0 7.1 %copy-start.11 = (bf16[8,32,128]{2,1,0:T(8,128)(2,1)}, bf16[8,32,128]{2,1,0:T(8,128)(2,1)S(1)}, u32[]{:S(2)}) copy-start(bf16[8,32,128]{2,1,0:T(8,128)(2,1)S(1)} %collective-permute-done.9) | copy-start | bytes 196612
  82.0 2.5 %collective-permute-start.10 = (bf16[192,512]{1,0:T(8,128)(2,1)}, bf16[192,512]{1,0:T(8,128)(2,1)S(1)}, u32[]{:S(2)}, u32[]{:S(2)}) collective-permute-start(bf16[192,512]{1,0:T(8,128)(2,1)} %get-tuple-element.70), channel_id=1, source_target_pairs={{0,1},{1,0},{2,3},{3,2},{4,5},{5,4},{6,7},{7,6},{8,9},{9,8},{10,11... | collective-permute-start | bytes 589832 | tf_op jit(solution)/shard_map/ppermute | solution.py:544
  89.1 24.8 %all-to-all-start.1 = ((bf16[16,64,528]{2,1,0:T(8,128)(2,1)}), bf16[16,64,528]{2,1,0:T(8,128)(2,1)S(1)}, u32[]{:S(2)}, u32[]{:S(2)}) async-start(bf16[16,64,528]{2,1,0:T(8,128)(2,1)} %pack.1), calls=%async_computation.1 | async-start | bytes 2621440 | tf_op jit(solution)/shard_map/all_to_all | solution.py:550
  94.7 20.1 %collective-permute-start.14 = (bf16[64,1024]{1,0:T(8,128)(2,1)}, bf16[64,1024]{1,0:T(8,128)(2,1)}, u32[]{:S(2)}, u32[]{:S(2)}) collective-permute-start(bf16[64,1024]{1,0:T(8,128)(2,1)} %get-tuple-element.79), channel_id=1, source_target_pairs={{0,31},{1,0},{2,1},{3,2},{4,3},{5,4},{6,5},{7,6},{8,7},{9,8},{10,9... | collective-permute-start | bytes 393224 | tf_op jit(solution)/shard_map/ppermute | solution.py:29
  95.3 19.4 %collective-permute-start.15 = (bf16[64,1024]{1,0:T(8,128)(2,1)}, bf16[64,1024]{1,0:T(8,128)(2,1)}, u32[]{:S(2)}, u32[]{:S(2)}) collective-permute-start(bf16[64,1024]{1,0:T(8,128)(2,1)} %get-tuple-element.80), channel_id=1, source_target_pairs={{0,1},{1,2},{2,3},{3,4},{4,5},{5,6},{6,7},{7,8},{8,9},{9,10},{10,1... | collective-permute-start | bytes 393224 | tf_op jit(solution)/shard_map/ppermute | solution.py:29
  97.4 11.8 %collective-permute-start.11 = (bf16[2,32,128]{2,1,0:T(8,128)(2,1)S(1)}, bf16[2,32,128]{2,1,0:T(8,128)(2,1)S(1)}, u32[]{:S(2)}, u32[]{:S(2)}) collective-permute-start(bf16[2,32,128]{2,1,0:T(8,128)(2,1)S(1)} %get-tuple-element.90), channel_id=1, source_target_pairs={{0,32},{32,64},{64,96},{96,0},{1,33},{33,65},{65,97},{97,1},{2,34}... | collective-permute-start | bytes 49160 | tf_op jit(solution)/shard_map/ppermute | solution.py:29
  99.3 13.3 %collective-permute-start.12 = (bf16[2,32,128]{2,1,0:T(8,128)(2,1)S(1)}, bf16[2,32,128]{2,1,0:T(8,128)(2,1)S(1)}, u32[]{:S(2)}, u32[]{:S(2)}) collective-permute-start(bf16[2,32,128]{2,1,0:T(8,128)(2,1)S(1)} %get-tuple-element.89), channel_id=1, source_target_pairs={{0,64},{32,96},{64,0},{96,32},{1,65},{33,97},{65,1},{97,33},{2,66}... | collective-permute-start | bytes 49160 | tf_op jit(solution)/shard_map/ppermute | solution.py:29
  101.7 11.6 %collective-permute-start.13 = (bf16[2,32,128]{2,1,0:T(8,128)(2,1)S(1)}, bf16[2,32,128]{2,1,0:T(8,128)(2,1)S(1)}, u32[]{:S(2)}, u32[]{:S(2)}) collective-permute-start(bf16[2,32,128]{2,1,0:T(8,128)(2,1)S(1)} %get-tuple-element.88), channel_id=1, source_target_pairs={{0,96},{32,0},{64,32},{96,64},{1,97},{33,1},{65,33},{97,65},{2,98}... | collective-permute-start | bytes 49160 | tf_op jit(solution)/shard_map/ppermute | solution.py:29
  116.4 17.3 %all-to-all-start.2 = ((bf16[16,4,1040]{2,1,0:T(4,128)(2,1)}), bf16[16,4,1040]{2,1,0:T(4,128)(2,1)S(1)}, u32[]{:S(2)}, u32[]{:S(2)}) async-start(bf16[16,4,1040]{2,1,0:T(4,128)(2,1)} %all_to_all.14), calls=%async_computation.2 | async-start | bytes 294912 | tf_op jit(solution)/shard_map/all_to_all | solution.py:561
  (3 other events, 2.1 us)

commit v9 on v8

--- a/solution.py
+++ b/solution.py
@@ -169,9 +169,10 @@
                     acc_s = acc_s + some_s.astype(f32)
             scale = scale_all[pl.ds(pl.multiple_of(base + r, ROWS), ROWS), :]
             agg_ref[pl.ds(pl.multiple_of(base + r, ROWS), ROWS), cols] = (acc_g * scale).astype(bf16)
-            sums[n, pl.ds(pl.multiple_of(base + r, ROWS), ROWS), :] = (
-                acc_s - (slots - 0.5 / scale)
-            ).astype(bf16)
+            sums[n, r : r + ROWS, :] = (acc_s - (slots - 0.5 / scale)).astype(bf16)
+
+    for d, ref in enumerate(piece_refs):
+        ref[...] = sums[(along + d) % QUARTERS]
 
     @pl.when(step == pl.num_programs(0) - 1)
     def _():
@@ -181,8 +182,6 @@
         pred_ref[...] = pred
         for e in range(members):
             sent_ref[e] = pred.astype(bf16)
-        for d, ref in enumerate(piece_refs):
-            ref[...] = sums[(along + d) % QUARTERS]
 
 
 def forward(place, below, here, above, w_src, dst, idx_t, wout_t, members):
@@ -203,7 +202,9 @@
             grid_rows // TILE,
             [whole(below), whole(here), whole(above), whole(w_src)]
             + [pl.BlockSpec((TILE, width), step), whole(idx_t), whole(wout_t)],
-            [pl.BlockSpec((TILE * slots, width), step)] + [whole(x) for x in out_shape[1:]],
+            [pl.BlockSpec((TILE * slots, width), step)]
+            + [whole(x) for x in out_shape[1:4]]
+            + [pl.BlockSpec((TILE, NCOL), step)] * QUARTERS,
             [
                 pltpu.VMEM((nodes, width), bf16),
                 pltpu.VMEM((nodes + TILE, width), bf16),
@@ -211,7 +212,7 @@
                 pltpu.VMEM((2, TILE * slots, NCOL), bf16),
                 pltpu.VMEM((grid_rows, slots), jnp.int32),
                 pltpu.VMEM((grid_rows, 1), f32),
-                pltpu.VMEM((QUARTERS, grid_rows, NCOL), bf16),
+                pltpu.VMEM((QUARTERS, TILE, NCOL), bf16),
             ],
         ),
         out_shape=out_shape,
@@ -442,45 +443,75 @@
     )
     product = lax.dot_general(mine, own_ref[...], first, preferred_element_type=f32)
     product = product + lax.dot_general(other, far_ref[...], first, preferred_element_type=f32)
-    give(total_ref, slice(0, half), product)
-    outs = total_ref.shape[2] - half
-    chunks, rows = dst_ref.shape[0], dst_ref.shape[1] - outs
-    columns = [
-        dst_ref[chunk, rows:, :].astype(f32) + dstfar_ref[chunk, rows:, :].astype(f32)
-        for chunk in range(chunks)
-    ]
-    give(total_ref, slice(half, half + outs), jnp.concatenate(columns, axis=1).T)
-
-
-def pack(place, feats, edge, own, far, dst_own, dst_far, chunks, outs):
-    width = feats[0].shape[1]
-    ins = list(feats) + [edge, own, far, dst_own, dst_far]
-    out_shape = jax.ShapeDtypeStruct((chunks, width // chunks, (width + outs) // 2), bf16)
+    chunks, rows, columns = total_ref.shape
+    total_ref[:, :, :half] = product.astype(bf16).reshape(chunks, rows, half)
+    both = dst_ref[...].astype(f32) + dstfar_ref[...].astype(f32)
+    few = both.shape[2]
+    outs = columns - half - few
+    some = both[:, : both.shape[1] - outs].astype(bf16)
+    total_ref[:, :, half : half + few] = some.reshape(chunks, rows, few)
+    some = jnp.concatenate([both[i, both.shape[1] - outs :] for i in range(both.shape[0])], axis=1)
+    total_ref[:, :, half + few :] = some.T.astype(bf16).reshape(chunks, rows, outs)
+
+
+def pack(place, feats, edge, own, far, dst_own, dst_far, chunks):
+    nodes, width = feats[0].shape
+    per_zh = (dst_own.shape[0] // GROUPS,) + dst_own.shape[1:]
+    outs = dst_own.shape[1] - width // dst_own.shape[0]
+    columns = width // 2 + dst_own.shape[2] + outs
+    rows = width // chunks
+    feat = pl.BlockSpec((nodes, width // GROUPS), lambda t, place: (0, t))
+    dst = pl.BlockSpec(per_zh, lambda t, place: (t, 0, 0))
     return pl.pallas_call(
         pack_kernel,
-        grid_spec=prefetched(1, [whole(x) for x in ins], whole(out_shape), []),
-        out_shape=out_shape,
+        grid_spec=prefetched(
+            GROUPS,
+            [feat] * 4 + [whole(own), whole(far), dst, dst],
+            pl.BlockSpec((chunks, rows // GROUPS, columns), lambda t, place: (0, t, 0)),
+            [],
+        ),
+        out_shape=jax.ShapeDtypeStruct((chunks, rows, columns), bf16),
         compiler_params=params(),
         cost_estimate=pl.CostEstimate(
             flops=4 * width * own.size, bytes_accessed=4 * width * width, transcendentals=0
         ),
         name="pack",
-    )(place, *ins)
-
-
-def quarters(array, axis, name):
-    count = lax.axis_size(name)
-    here = lax.axis_index(name)
-    return [
-        lax.dynamic_index_in_dim(array, (here + d) % count, axis, keepdims=False) for d in range(count)
-    ]
-
-
-def added(first, *others):
-    total = first.astype(f32)
-    for other in others:
-        total = total + other.astype(f32)
-    return total.astype(bf16)
+    )(place, *feats, edge, own, far, dst_own, dst_far)
+
+
+def join_kernel(parts_ref, total_ref):
+    half = total_ref.shape[2] - parts_ref.shape[2]
+    half = half * QUARTERS // (QUARTERS - 1)
+    few = half // QUARTERS
+    each = parts_ref.shape[0] // QUARTERS
+    pieces = []
+    ends = 0.0
+    for x in range(QUARTERS):
+        some = parts_ref[x * each].astype(f32)
+        for y in range(1, each):
+            some = some + parts_ref[x * each + y].astype(f32)
+        pieces.append(some[:, half : half + few])
+        ends = ends + some
+    total = jnp.concatenate([ends[:, :half]] + pieces + [ends[:, half + few :]], axis=1).astype(bf16)
+    for i in range(total_ref.shape[0]):
+        rows = total_ref.shape[1]
+        total_ref[i] = total[i * rows : (i + 1) * rows, :]
+
+
+def join(parts, rows_out, half):
+    sources, rows, columns = parts.shape
+    wide = columns - half // QUARTERS + half
+    count = rows // rows_out
+    return pl.pallas_call(
+        join_kernel,
+        grid=(GROUPS,),
+        in_specs=[pl.BlockSpec((sources, rows // GROUPS, columns), lambda t: (0, t, 0))],
+        out_specs=pl.BlockSpec((count // GROUPS, rows_out, wide), lambda t: (t, 0, 0)),
+        out_shape=jax.ShapeDtypeStruct((count, rows_out, wide), bf16),
+        compiler_params=params(),
+        cost_estimate=pl.CostEstimate(flops=parts.size, bytes_accessed=2 * parts.size, transcendentals=0),
+        name="join",
+    )(parts)
 
 
 def body(
@@ -532,49 +563,30 @@
     )
     dst_far = lax.ppermute(dst_far, "c", swap)
 
-    outs = w_out.shape[1]
-    split = (members, lax.axis_size("y"), -1, dst_own.shape[2])
-    both = added(dst_own[:, : width // members], dst_far[:, : width // members]).reshape(split)
-    kept, *pieces = quarters(both, 1, "y")
-    lead, *pieces = lax.optimization_barrier((lead, *pieces))
-    moved = [shifted(piece, "y", d + 1) for d, piece in enumerate(pieces)]
-
     lower, centre, upper, wide_own, wide_far = backward(place, gp, lead, idx_t, 3 * node_rows)
-    lower, upper, wide_far, *moved = lax.optimization_barrier((lower, upper, wide_far, *moved))
     wide_far = lax.ppermute(wide_far, "c", swap)
     from_above = shifted(lower, SPACE, -1)
     from_below = shifted(upper, SPACE, 1)
 
-    src_total = pack(place, feats, edge, wide_own, wide_far, dst_own, dst_far, chunks, outs)
-    src_total, kept, *moved = lax.optimization_barrier((src_total, kept, *moved))
-    src_parts = lax.all_to_all(src_total, FIRST, 0, 0, tiled=True)
-
-    both = added(kept, *moved).reshape((GROUPS, QUARTERS) + kept.shape[1:])
-    kept, *pieces = quarters(both, 1, "x")
-    dst_parts = [kept] + [shifted(piece, "x", d + 1) for d, piece in enumerate(pieces)]
-
-    rows = GROUPS * kept.shape[1]
-    src_sum = jnp.sum(src_parts.astype(f32), axis=0).astype(bf16)
-    dst_sum = jnp.concatenate([x.reshape(rows, -1) for x in dst_parts], axis=1)
-    total = jnp.concatenate([dst_sum, src_sum], axis=1)
+    total = pack(place, feats, edge, wide_own, wide_far, dst_own, dst_far, chunks)
+    parts = lax.all_to_all(total, FIRST, 0, 0, tiled=True)
+    few = half // QUARTERS
+    rows_out = width // lax.axis_size(ENS + SPACE)
+
+    total = join(parts, rows_out, half)
     total, from_above, from_below = lax.optimization_barrier((total, from_above, from_below))
     parts = lax.all_to_all(total, SECOND, 0, 0, tiled=True)
     dproj = (centre.astype(f32) + from_above.astype(f32) + from_below.astype(f32)).astype(bf16)
     grad_mesh = lax.dot_general(
         dproj, w_src, (((1,), (1,)), ((), ())), preferred_element_type=f32
     ).astype(bf16)
-    rows_out = width // lax.axis_size(ENS + SPACE)
-    total = jnp.sum(parts.reshape(-1, 2, rows_out, parts.shape[1]).astype(f32), axis=0)
+    total = jnp.sum(parts.reshape(-1, 2, rows_out, parts.shape[2]).astype(f32), axis=0)
     joined = lambda a, b: jnp.concatenate([total[0, :, a:b], total[1, :, a:b]], axis=1)
-    by_distance = total[:, :, :half].reshape(2, rows_out, QUARTERS, -1)
-    along = lax.axis_index("x")
-    x = jnp.arange(QUARTERS)
-    chosen = ((along - x[:, None]) % QUARTERS == x[None, :])[None, :, None, :, None]
-    by_distance = by_distance.transpose(1, 0, 2, 3)[:, None]
-    dst_final = jnp.sum(jnp.where(chosen, by_distance, 0.0), axis=3).reshape(rows_out, width)
+    dst_final = total[:, :, half : 2 * half].reshape(2, rows_out, QUARTERS, few)
+    dst_final = dst_final.transpose(1, 2, 0, 3).reshape(rows_out, width)
     return (
         grad_mesh[None],
-        joined(half, 2 * half),
+        joined(0, half),
         dst_final,
         joined(2 * half, total.shape[-1]),
     )

time: 136 us -> 133 us (0.978)
  waiting for transfers between devices: 18.5 us -> 31 us
  starting transfers between devices: 55.2 us -> 45.5 us
  local copies, waits for them, and re-layouts: 8.41 us -> 3.82 us
  other arithmetic: 7.11 us -> 3.54 us
  Pallas kernels: 38.9 us -> 41.1 us
    all_to_all x1, waiting for transfers between devices: 0.01 us -> 21.7 us  [body(): parts = lax.all_to_all(total, FIRST, 0, 0, tiled=True)]
    ppermute x13 -> x7, starting transfers between devices: 20.5 us -> 10.2 us  [shifted(): lax.ppermute(block, axes, [(i, (i + distance) % count) for i in range(cou...]
    ppermute x13 -> x7, waiting for transfers between devices: 10.2 us -> 1.1 us  [shifted(): lax.ppermute(block, axes, [(i, (i + distance) % count) for i in range(cou...]
    unnamed x36 -> x34, local copies, waits for them, and re-layouts: 4.76 us -> 2.46 us
    pallas_call x1 -> x2, Pallas kernels: 3.95 us -> 6.11 us  [the longest x1 4.01 us: pack(): pl.pallas_call(pack_kernel, grid_spec=prefetched(GROUPS, [feat] * 4 + [wh...]
    convert_element_type x2 -> x0, other arithmetic: 2.04 us -> none  [added(): return total.astype(bf16)]
    ppermute x1, starting transfers between devices: 6.32 us -> 8 us  [body(): edge = lax.ppermute(jnp.where(low, below, above), 'c', swap)]
    all_to_all x1 -> x0, local copies, waits for them, and re-layouts: 1.61 us -> none  [body(): parts = lax.all_to_all(total, SECOND, 0, 0, tiled=True)]
  transfers between devices with their start and end apart: 19 -> 13, of which waited for: 7 -> 5; matrix products, arithmetic and copies ran while one was open for 11% -> 7% of each run, Pallas kernels for 7% -> 9%
where the time goes in v9:
time: 133 us; the launch traced here: 132 us
  starting transfers between devices  45.5 us (34%)
  Pallas kernels  41.1 us (31%)
  waiting for transfers between devices  31 us (23%)
  matrix products  6.46 us (5%)
  local copies, waits for them, and re-layouts  3.82 us (3%)
  other arithmetic  3.54 us (3%)
    all_to_all x1, waiting for transfers between devices, body(): parts = lax.all_to_all(total, FIRST, 0, 0, tiled=True)  21.7 us
    pallas_call x1, Pallas kernels, forward(): pl.pallas_call(functools.partial(forward_kernel, slots, members), grid_sp...  19.5 us
    ppermute x7, starting transfers between devices, shifted(): lax.ppermute(block, axes, [(i, (i + distance) % count) for i in range(cou...  10.2 us
    pallas_call x1, Pallas kernels, backward(): pl.pallas_call(functools.partial(backward_kernel, slots), grid_spec=prefe...  9.85 us
    all_to_all x1, starting transfers between devices, body(): everyone = lax.all_to_all(sent, ENS, 0, 0, tiled=True)  8.96 us
    ppermute x1, starting transfers between devices, body(): edge = lax.ppermute(jnp.where(low, below, above), 'c', swap)  8 us
    all_to_all x1, starting transfers between devices, body(): parts = lax.all_to_all(total, SECOND, 0, 0, tiled=True)  7.71 us
    all_to_all x1, waiting for transfers between devices, body(): parts = lax.all_to_all(total, SECOND, 0, 0, tiled=True)  6.3 us
  transfers between devices with their start and end apart: 13, of which 5 were waited for; matrix products, arithmetic and copies ran while one was open for 7% of the time, Pallas kernels for 9%

profile of v9, /device:TPU:1, one launch (start us, length us, event | category | flops | bytes accessed | tf_op | source)
XLA Modules:
  0.0 132.2 jit_solution(18192489541931561056)
XLA Ops:
  0.6 3.3 %collective-permute-start.1 = (bf16[64,1024]{1,0:T(8,128)(2,1)}, bf16[64,1024]{1,0:T(8,128)(2,1)S(1)}, u32[]{:S(2)}, u32[]{:S(2)}) collective-permute-start(bf16[64,1024]{1,0:T(8,128)(2,1)} %bitcast.36), channel_id=1, source_target_pairs={{0,31},{1,0},{2,1},{3,2},{4,3},{5,4},{6,5},{7,6},{8,7},{9,8},{10,9... | collective-permute-start | bytes 393224 | tf_op jit(solution)/shard_map/ppermute | solution.py:29
  4.0 3.5 %convolution_convert_fusion.dst_ref = bf16[512,1024]{1,0:T(8,128)(2,1)} fusion(bf16[512,1024]{1,0:T(8,128)(2,1)} %grid_hbm.1, bf16[1024,1024]{1,0:T(8,128)(2,1)S(1)} %copy-done), kind=kOutput, calls=%fused_computation | convolution fusion | flops 1074266112 | bytes 4194304 | tf_op jit(solution)/shard_map/dot_general | solution.py:543
  7.4 0.6 fusion.2.idxt_ref.idx_ref
  8.1 0.7 pad_add_fusion.place_ref
  8.7 1.1 collective-permute-done.below_ref
  9.8 0.6 copy-done.3
  10.5 19.5 %forward.1 = (bf16[8192,1024]{1,0:T(8,128)(2,1)}, bf16[512,1024]{1,0:T(8,128)(2,1)}, f32[32,512]{1,0:T(8,128)}, bf16[8,32,512]{2,1,0:T(8,128)(2,1)}, bf16[512,25...) custom-call(s32[4]{0:T(128)} %pad_add_fusion.place_ref, ...), custom_call_target="tpu_custom_call" | custom-call | flops 4294967296 | bytes 16777216 | tf_op jit(solution)/shard_map/forward/pallas_call | solution.py:199
  30.0 9.0 %all-to-all-start = ((bf16[8,32,512]{2,1,0:T(8,128)(2,1)}), bf16[8,32,512]{2,1,0:T(8,128)(2,1)S(1)}, u32[]{:S(2)}, u32[]{:S(2)}) async-start(bf16[8,32,512]{2,1,0:T(8,128)(2,1)} %get-tuple-element.34), calls=%async_computation | async-start | bytes 524288 | tf_op jit(solution)/shard_map/all_to_all | solution.py:557
  39.0 1.5 %collective-permute-start.3 = (bf16[512,256]{1,0:T(8,128)(2,1)}, bf16[512,256]{1,0:T(8,128)(2,1)S(1)}, u32[]{:S(2)}, u32[]{:S(2)}) collective-permute-start(bf16[512,256]{1,0:T(8,128)(2,1)} %get-tuple-element.38), channel_id=1, source_target_pairs={{0,32},{32,64},{64,96},{96,0},{1,33},{33,65},{65,97},{97,1},{2,34}... | collective-permute-start | bytes 786440 | tf_op jit(solution)/shard_map/ppermute | solution.py:29
  40.4 2.4 %collective-permute-start.4 = (bf16[512,256]{1,0:T(8,128)(2,1)}, bf16[512,256]{1,0:T(8,128)(2,1)S(1)}, u32[]{:S(2)}, u32[]{:S(2)}) collective-permute-start(bf16[512,256]{1,0:T(8,128)(2,1)} %get-tuple-element.39), channel_id=1, source_target_pairs={{0,64},{32,96},{64,0},{96,32},{1,65},{33,97},{65,1},{97,33},{2,66}... | collective-permute-start | bytes 786440 | tf_op jit(solution)/shard_map/ppermute | solution.py:29
  42.8 1.2 collective-permute-start.5
  44.1 0.9 broadcast_select_fusion
  45.0 8.0 %collective-permute-start.2 = (bf16[64,1024]{1,0:T(8,128)(2,1)S(1)}, bf16[64,1024]{1,0:T(8,128)(2,1)S(1)}, u32[]{:S(2)}, u32[]{:S(2)}) collective-permute-start(bf16[64,1024]{1,0:T(8,128)(2,1)S(1)} %broadcast_select_fusion), channel_id=1, source_target_pairs={{0,1},{1,0},{2,3},{3,2},{4,5},{5,4},{6,7},{7,6},{8,9},{9,8},{10,11... | collective-permute-start | bytes 393224 | tf_op jit(solution)/shard_map/ppermute | solution.py:559
  53.0 0.7 copy.14.var_ref
  54.1 0.7 copy-done.1
  55.0 5.6 %middle.1 = (bf16[512,1024]{1,0:T(8,128)(2,1)}, bf16[8,144,128]{2,1,0:T(8,128)(2,1)}, bf16[8,144,128]{2,1,0:T(8,128)(2,1)}) custom-call(s32[4]{0:T(128)} %pad_add_fusion.place_ref, bf16[8,32,512]{2,1,0:T(8,128)(2,1)} %copy-done.1, f32[32,512]{1,0:T(8,128)} %get-tuple-element.36.pred_ref, f32[32,512]{1,0:T(8,128)} %bitcast.42, f32[1,512]{1,0:T(1,128)} %bitcast.45, ...), custom_call_target="tpu_custom_call" | custom-call | flops 536870912 | bytes 5242880 | tf_op jit(solution)/shard_map/middle/pallas_call | solution.py:329
  60.6 4.4 %collective-permute-start.7 = (bf16[8,144,128]{2,1,0:T(8,128)(2,1)}, bf16[8,144,128]{2,1,0:T(8,128)(2,1)S(1)}, u32[]{:S(2)}, u32[]{:S(2)}) collective-permute-start(bf16[8,144,128]{2,1,0:T(8,128)(2,1)} %get-tuple-element.48), channel_id=1, source_target_pairs={{0,1},{1,0},{2,3},{3,2},{4,5},{5,4},{6,7},{7,6},{8,9},{9,8},{10,11... | collective-permute-start | bytes 884744 | tf_op jit(solution)/shard_map/ppermute | solution.py:564
  65.0 9.9 %backward.1 = (bf16[64,1024]{1,0:T(8,128)(2,1)}, bf16[64,1024]{1,0:T(8,128)(2,1)}, bf16[64,1024]{1,0:T(8,128)(2,1)}, bf16[192,512]{1,0:T(8,128)(2,1)}, bf16[192,512]{1,0:T(8,128)(2,1)}) custom-call(s32[4]{0:T(128)} %pad_add_fusion.place_ref, bf16[8192,1024]{1,0:T(8,128)(2,1)} %get-tuple-element.33.gp_ref, bf16[512,1024]{1,0:T(8,128)(2,1)} %get-tuple-element.42.lead_ref, ...), custom_call_target="tpu_custom_call" | custom-call | flops 4294967296 | bytes 16777216 | tf_op jit(solution)/shard_map/backward/pallas_call | solution.py:410
  75.1 1.6 %collective-permute-done.6.far_ref = bf16[192,512]{1,0:T(8,128)(2,1)S(1)} collective-permute-done((bf16[192,512]{1,0:T(8,128)(2,1)}, bf16[192,512]{1,0:T(8,128)(2,1)S(1)}, u32[]{:S(2)}, u32[]{:S(2)}) %collective-permute-start.6) | collective-permute-done | bytes 196640 | tf_op jit(solution)/shard_map/ppermute | solution.py:567
  76.7 0.7 copy-done.8
  77.5 4.0 %pack.1 = bf16[16,64,656]{2,1,0:T(8,128)(2,1)} custom-call(s32[4]{0:T(128)} %pad_add_fusion.place_ref, bf16[64,1024]{1,0:T(8,128)(2,1)} %copy-done.3, bf16[64,1024]{1,0:T(8,128)(2,1)} %bitcast.39, bf16[64,1024]{1,0:T(8,128)(2,1)} %copy-done.2, bf16[64,1024]{1,0:T(8,128)(2,1)} %copy-done.9, bf16[192,512]{1,0:T(8,128)(2,1)} %get-tuple-element.45.own_ref, ...), custom_call_target="tpu_custom_call" | custom-call | flops 402653184 | bytes 4194304 | tf_op jit(solution)/shard_map/pack/pallas_call | solution.py:465
  81.6 6.0 %all-to-all-start.1 = ((bf16[16,64,656]{2,1,0:T(8,128)(2,1)}), bf16[16,64,656]{2,1,0:T(8,128)(2,1)}, u32[]{:S(2)}, u32[]{:S(2)}) async-start(bf16[16,64,656]{2,1,0:T(8,128)(2,1)} %pack.1), calls=%async_computation.1 | async-start | bytes 3145728 | tf_op jit(solution)/shard_map/all_to_all | solution.py:572
  87.6 0.5 collective-permute-start.8
  88.1 1.3 collective-permute-start.9
  89.4 21.7 %all-to-all-done.1.parts_ref = bf16[16,64,656]{2,1,0:T(8,128)(2,1)} async-done(((bf16[16,64,656]{2,1,0:T(8,128)(2,1)}), bf16[16,64,656]{2,1,0:T(8,128)(2,1)}, u32[]{:S(2)}, u32[]{:S(2)}) %all-to-all-start.1) | async-done | bytes 1343520 | tf_op jit(solution)/shard_map/all_to_all | solution.py:572
  111.1 2.1 %join.1 = bf16[16,4,1040]{2,1,0:T(4,128)(2,1)} custom-call(bf16[16,64,656]{2,1,0:T(8,128)(2,1)} %all-to-all-done.1.parts_ref), custom_call_target="tpu_custom_call" | custom-call | flops 671744 | bytes 1343488 | tf_op jit(solution)/shard_map/join/pallas_call | solution.py:505
  113.2 7.7 %all-to-all-start.2 = ((bf16[16,4,1040]{2,1,0:T(4,128)(2,1)}), bf16[16,4,1040]{2,1,0:T(4,128)(2,1)S(1)}, u32[]{:S(2)}, u32[]{:S(2)}) async-start(bf16[16,4,1040]{2,1,0:T(4,128)(2,1)} %join.1), calls=%async_computation.2 | async-start | bytes 294912 | tf_op jit(solution)/shard_map/all_to_all | solution.py:578
  120.9 3.0 %fusion = bf16[1,64,1024]{2,1,0:T(8,128)(2,1)} fusion(bf16[1024,1024]{1,0:T(8,128)(2,1)} %wsrc_ref.1, bf16[64,1024]{1,0:T(8,128)(2,1)S(1)} %collective-permute-done.9, bf16[64,1024]{1,0:T(8,128)(2,1)S(1)} %collective-permute-done.8, bf16[64,1024]{1,0:T(8,128)(2,1)S(1)} %copy-done.10), kind=kOutput, calls=%fused_computation.2 | convolution fusion | flops 134676480 | bytes 2621440 | tf_op jit(solution)/shard_map/dot_general | solution.py:580
  123.9 6.3 %all-to-all-done.2 = bf16[16,4,1040]{2,1,0:T(4,128)(2,1)S(1)} async-done(((bf16[16,4,1040]{2,1,0:T(4,128)(2,1)}), bf16[16,4,1040]{2,1,0:T(4,128)(2,1)S(1)}, u32[]{:S(2)}, u32[]{:S(2)}) %all-to-all-start.2) | async-done | bytes 133152 | tf_op jit(solution)/shard_map/all_to_all | solution.py:578
  130.4 0.6 reshape.20
  131.0 0.7 pad_maximum_fusion.1
  131.6 0.6 pad_maximum_fusion
  (48 shorter events, 1.1 us)
Async XLA Ops:
  0.6 3.3 %copy-start = (bf16[1024,1024]{1,0:T(8,128)(2,1)S(1)}, bf16[1024,1024]{1,0:T(8,128)(2,1)}, u32[]{:S(2)}) copy-start(bf16[1024,1024]{1,0:T(8,128)(2,1)} %param.13) | copy-start | bytes 6291460
  0.6 9.2 %collective-permute-start.1 = (bf16[64,1024]{1,0:T(8,128)(2,1)}, bf16[64,1024]{1,0:T(8,128)(2,1)S(1)}, u32[]{:S(2)}, u32[]{:S(2)}) collective-permute-start(bf16[64,1024]{1,0:T(8,128)(2,1)} %bitcast.36), channel_id=1, source_target_pairs={{0,31},{1,0},{2,1},{3,2},{4,3},{5,4},{6,5},{7,6},{8,7},{9,8},{10,9... | collective-permute-start | bytes 393224 | tf_op jit(solution)/shard_map/ppermute | solution.py:29
  4.0 5.8 %collective-permute-start = (bf16[64,1024]{1,0:T(8,128)(2,1)}, bf16[64,1024]{1,0:T(8,128)(2,1)S(1)}, u32[]{:S(2)}, u32[]{:S(2)}) collective-permute-start(bf16[64,1024]{1,0:T(8,128)(2,1)} %bitcast.37), channel_id=1, source_target_pairs={{0,1},{1,2},{2,3},{3,4},{4,5},{5,6},{6,7},{7,8},{8,9},{9,10},{10,1... | collective-permute-start | bytes 393224 | tf_op jit(solution)/shard_map/ppermute | solution.py:29
  4.0 3.5 %copy-start.11 = (s32[512,16]{0,1:T(8,128)S(1)}, s32[512,16]{0,1:T(8,128)}, u32[]{:S(2)}) copy-start(s32[512,16]{0,1:T(8,128)} %param.18) | copy-start | bytes 98308
  4.0 3.5 %copy-start.12 = (s32[512,16]{0,1:T(8,128)S(1)}, s32[512,16]{0,1:T(8,128)}, u32[]{:S(2)}) copy-start(s32[512,16]{0,1:T(8,128)} %param.19) | copy-start | bytes 98308
  9.8 0.7 copy-start.3
  9.8 0.7 copy-start.2
  10.5 33.5 %copy-start.13 = (s32[4]{0:T(128)S(1)}, s32[4]{0:T(128)}, u32[]{:S(2)}) copy-start(s32[4]{0:T(128)} %pad_add_fusion.place_ref) | copy-start | bytes 52
  10.5 42.5 %copy-start.14 = (f32[32]{0:T(128)S(1)}, f32[32]{0:T(128)}, u32[]{:S(2)}) copy-start(f32[32]{0:T(128)} %param.17) | copy-start | bytes 388
  30.0 24.0 %all-to-all-start = ((bf16[8,32,512]{2,1,0:T(8,128)(2,1)}), bf16[8,32,512]{2,1,0:T(8,128)(2,1)S(1)}, u32[]{:S(2)}, u32[]{:S(2)}) async-start(bf16[8,32,512]{2,1,0:T(8,128)(2,1)} %get-tuple-element.34), calls=%async_computation | async-start | bytes 524288 | tf_op jit(solution)/shard_map/all_to_all | solution.py:557
  39.0 15.0 %collective-permute-start.3 = (bf16[512,256]{1,0:T(8,128)(2,1)}, bf16[512,256]{1,0:T(8,128)(2,1)S(1)}, u32[]{:S(2)}, u32[]{:S(2)}) collective-permute-start(bf16[512,256]{1,0:T(8,128)(2,1)} %get-tuple-element.38), channel_id=1, source_target_pairs={{0,32},{32,64},{64,96},{96,0},{1,33},{33,65},{65,97},{97,1},{2,34}... | collective-permute-start | bytes 786440 | tf_op jit(solution)/shard_map/ppermute | solution.py:29
  40.4 13.6 %collective-permute-start.4 = (bf16[512,256]{1,0:T(8,128)(2,1)}, bf16[512,256]{1,0:T(8,128)(2,1)S(1)}, u32[]{:S(2)}, u32[]{:S(2)}) collective-permute-start(bf16[512,256]{1,0:T(8,128)(2,1)} %get-tuple-element.39), channel_id=1, source_target_pairs={{0,64},{32,96},{64,0},{96,32},{1,65},{33,97},{65,1},{97,33},{2,66}... | collective-permute-start | bytes 786440 | tf_op jit(solution)/shard_map/ppermute | solution.py:29
  42.8 11.2 %collective-permute-start.5 = (bf16[512,256]{1,0:T(8,128)(2,1)}, bf16[512,256]{1,0:T(8,128)(2,1)S(1)}, u32[]{:S(2)}, u32[]{:S(2)}) collective-permute-start(bf16[512,256]{1,0:T(8,128)(2,1)} %get-tuple-element.40), channel_id=1, source_target_pairs={{0,96},{32,0},{64,32},{96,64},{1,97},{33,1},{65,33},{97,65},{2,98}... | collective-permute-start | bytes 786440 | tf_op jit(solution)/shard_map/ppermute | solution.py:29
  45.0 9.0 %collective-permute-start.2 = (bf16[64,1024]{1,0:T(8,128)(2,1)S(1)}, bf16[64,1024]{1,0:T(8,128)(2,1)S(1)}, u32[]{:S(2)}, u32[]{:S(2)}) collective-permute-start(bf16[64,1024]{1,0:T(8,128)(2,1)S(1)} %broadcast_select_fusion), channel_id=1, source_target_pairs={{0,1},{1,0},{2,3},{3,2},{4,5},{5,4},{6,7},{7,6},{8,9},{9,8},{10,11... | collective-permute-start | bytes 393224 | tf_op jit(solution)/shard_map/ppermute | solution.py:559
  54.0 20.9 %copy-start.9 = (bf16[64,1024]{1,0:T(8,128)(2,1)}, bf16[64,1024]{1,0:T(8,128)(2,1)S(1)}, u32[]{:S(2)}) copy-start(bf16[64,1024]{1,0:T(8,128)(2,1)S(1)} %collective-permute-done.2.edge_ref) | copy-start | bytes 393220
  54.0 0.7 copy-start.1
  54.0 0.8 copy-start.5
  54.0 0.9 copy-start.6
  54.0 1.0 copy-start.7
  60.6 16.1 %collective-permute-start.7 = (bf16[8,144,128]{2,1,0:T(8,128)(2,1)}, bf16[8,144,128]{2,1,0:T(8,128)(2,1)S(1)}, u32[]{:S(2)}, u32[]{:S(2)}) collective-permute-start(bf16[8,144,128]{2,1,0:T(8,128)(2,1)} %get-tuple-element.48), channel_id=1, source_target_pairs={{0,1},{1,0},{2,3},{3,2},{4,5},{5,4},{6,7},{7,6},{8,9},{9,8},{10,11... | collective-permute-start | bytes 884744 | tf_op jit(solution)/shard_map/ppermute | solution.py:564
  74.9 1.8 %collective-permute-start.6 = (bf16[192,512]{1,0:T(8,128)(2,1)}, bf16[192,512]{1,0:T(8,128)(2,1)S(1)}, u32[]{:S(2)}, u32[]{:S(2)}) collective-permute-start(bf16[192,512]{1,0:T(8,128)(2,1)} %get-tuple-element.46), channel_id=1, source_target_pairs={{0,1},{1,0},{2,3},{3,2},{4,5},{5,4},{6,7},{7,6},{8,9},{9,8},{10,11... | collective-permute-start | bytes 589832 | tf_op jit(solution)/shard_map/ppermute | solution.py:567
  76.7 0.7 copy-start.8
  76.7 0.8 copy-start.4
  81.5 6.0 %copy-start.16 = (bf16[64,1024]{1,0:T(8,128)(2,1)S(1)}, bf16[64,1024]{1,0:T(8,128)(2,1)}, u32[]{:S(2)}) copy-start(bf16[64,1024]{1,0:T(8,128)(2,1)} %get-tuple-element.49) | copy-start | bytes 393220
  81.5 6.5 %copy-start.15 = (bf16[64,1024]{1,0:T(8,128)(2,1)S(1)}, bf16[64,1024]{1,0:T(8,128)(2,1)}, u32[]{:S(2)}) copy-start(bf16[64,1024]{1,0:T(8,128)(2,1)} %get-tuple-element.50) | copy-start | bytes 393220
  81.5 39.4 %copy-start.10 = (bf16[64,1024]{1,0:T(8,128)(2,1)S(1)}, bf16[64,1024]{1,0:T(8,128)(2,1)}, u32[]{:S(2)}) copy-start(bf16[64,1024]{1,0:T(8,128)(2,1)} %get-tuple-element.43) | copy-start | bytes 393220
  81.6 29.5 %all-to-all-start.1 = ((bf16[16,64,656]{2,1,0:T(8,128)(2,1)}), bf16[16,64,656]{2,1,0:T(8,128)(2,1)}, u32[]{:S(2)}, u32[]{:S(2)}) async-start(bf16[16,64,656]{2,1,0:T(8,128)(2,1)} %pack.1), calls=%async_computation.1 | async-start | bytes 3145728 | tf_op jit(solution)/shard_map/all_to_all | solution.py:572
  87.6 25.6 %collective-permute-start.8 = (bf16[64,1024]{1,0:T(8,128)(2,1)S(1)}, bf16[64,1024]{1,0:T(8,128)(2,1)S(1)}, u32[]{:S(2)}, u32[]{:S(2)}) collective-permute-start(bf16[64,1024]{1,0:T(8,128)(2,1)S(1)} %copy-done.16), channel_id=1, source_target_pairs={{0,31},{1,0},{2,1},{3,2},{4,3},{5,4},{6,5},{7,6},{8,7},{9,8},{10,9... | collective-permute-start | bytes 393224 | tf_op jit(solution)/shard_map/ppermute | solution.py:29
  88.1 25.1 %collective-permute-start.9 = (bf16[64,1024]{1,0:T(8,128)(2,1)S(1)}, bf16[64,1024]{1,0:T(8,128)(2,1)S(1)}, u32[]{:S(2)}, u32[]{:S(2)}) collective-permute-start(bf16[64,1024]{1,0:T(8,128)(2,1)S(1)} %copy-done.15), channel_id=1, source_target_pairs={{0,1},{1,2},{2,3},{3,4},{4,5},{5,6},{6,7},{7,8},{8,9},{9,10},{10,1... | collective-permute-start | bytes 393224 | tf_op jit(solution)/shard_map/ppermute | solution.py:29
  113.2 17.0 %all-to-all-start.2 = ((bf16[16,4,1040]{2,1,0:T(4,128)(2,1)}), bf16[16,4,1040]{2,1,0:T(4,128)(2,1)S(1)}, u32[]{:S(2)}, u32[]{:S(2)}) async-start(bf16[16,4,1040]{2,1,0:T(4,128)(2,1)} %join.1), calls=%async_computation.2 | async-start | bytes 294912 | tf_op jit(solution)/shard_map/all_to_all | solution.py:578

commit v10 on v9

--- a/solution.py
+++ b/solution.py
@@ -46,6 +46,14 @@
 def whole(array):
     zeros = (0,) * len(array.shape)
     return pl.BlockSpec(array.shape, lambda *_: zeros)
+
+
+def landed():
+    return pl.BlockSpec(memory_space=pltpu.VMEM)
+
+
+def kept_near(array):
+    return pltpu.with_memory_space_constraint(array, pltpu.VMEM)
 
 
 def params():
@@ -200,7 +208,7 @@
         functools.partial(forward_kernel, slots, members),
         grid_spec=prefetched(
             grid_rows // TILE,
-            [whole(below), whole(here), whole(above), whole(w_src)]
+            [landed(), whole(here), landed(), whole(w_src)]
             + [pl.BlockSpec((TILE, width), step), whole(idx_t), whole(wout_t)],
             [pl.BlockSpec((TILE * slots, width), step)]
             + [whole(x) for x in out_shape[1:4]]
@@ -223,7 +231,7 @@
             transcendentals=grid_rows * slots * width,
         ),
         name="forward",
-    )(place, below, here, above, w_src, dst, idx_t, wout_t)
+    )(place, kept_near(below), here, kept_near(above), w_src, dst, idx_t, wout_t)
 
 
 def middle_kernel(
@@ -330,7 +338,11 @@
         middle_kernel,
         grid_spec=prefetched(
             1,
-            [whole(x) for x in small] + [anywhere] * 2,
+            [landed()]
+            + [whole(x) for x in small[1 : -len(sums)]]
+            + [whole(sums[0])]
+            + [landed()] * (len(sums) - 1)
+            + [anywhere] * 2,
             [anywhere] + [whole(x) for x in out_shape[1:]],
             [
                 pltpu.VMEM((grid_rows, width), bf16),
@@ -347,7 +359,7 @@
             flops=grid_rows * width * width, bytes_accessed=10 * grid_rows * width, transcendentals=0
         ),
         name="middle",
-    )(place, *small, agg, grid_embed)
+    )(place, kept_near(everyone), *small[1:-3], *map(kept_near, sums[1:]), agg, grid_embed)
 
 
 def scatter_step(slots, gp_ref, lead_ref, idx_ref, hot, prod, acc):
@@ -405,7 +417,7 @@
     slots = idx_t.shape[0]
     rows = BACK * TILE
     out_shape = [jax.ShapeDtypeStruct((nodes // 3, width), bf16)] * 3 + [
-        jax.ShapeDtypeStruct((nodes, width // 2), bf16)
+        pltpu.VMEM((nodes, width // 2), bf16)
     ] * 2
     return pl.pallas_call(
         functools.partial(backward_kernel, slots),
@@ -416,7 +428,7 @@
                 pl.BlockSpec((rows, width), lambda t, place: (t, 0)),
                 pl.BlockSpec((slots, rows), lambda t, place: (0, t)),
             ],
-            [whole(x) for x in out_shape],
+            [whole(x) for x in out_shape[:3]] + [landed()] * 2,
             [
                 pltpu.VMEM((nodes, rows * slots), bf16),
                 pltpu.VMEM((rows * slots, width), bf16),
@@ -445,7 +457,9 @@
     product = product + lax.dot_general(other, far_ref[...], first, preferred_element_type=f32)
     chunks, rows, columns = total_ref.shape
     total_ref[:, :, :half] = product.astype(bf16).reshape(chunks, rows, half)
-    both = dst_ref[...].astype(f32) + dstfar_ref[...].astype(f32)
+    per_zh = dst_ref.shape[0]
+    at = pl.ds(pl.program_id(0) * per_zh, per_zh)
+    both = dst_ref[...].astype(f32) + dstfar_ref[at].astype(f32)
     few = both.shape[2]
     outs = columns - half - few
     some = both[:, : both.shape[1] - outs].astype(bf16)
@@ -466,7 +480,7 @@
         pack_kernel,
         grid_spec=prefetched(
             GROUPS,
-            [feat] * 4 + [whole(own), whole(far), dst, dst],
+            [feat] * 4 + [landed(), landed(), dst, landed()],
             pl.BlockSpec((chunks, rows // GROUPS, columns), lambda t, place: (0, t, 0)),
             [],
         ),
@@ -476,7 +490,7 @@
             flops=4 * width * own.size, bytes_accessed=4 * width * width, transcendentals=0
         ),
         name="pack",
-    )(place, *feats, edge, own, far, dst_own, dst_far)
+    )(place, *feats, edge, kept_near(own), kept_near(far), dst_own, kept_near(dst_far))
 
 
 def join_kernel(parts_ref, total_ref):

time: 133 us -> 130 us (0.977)
  local copies, waits for them, and re-layouts: 3.82 us -> 1.41 us
    unnamed x34 -> x22, local copies, waits for them, and re-layouts: 2.46 us -> 0.05 us
where the time goes in v10:
time: 130 us; the launch traced here: 129 us
  starting transfers between devices  46.5 us (36%)
  Pallas kernels  40.5 us (31%)
  waiting for transfers between devices  30.8 us (24%)
  matrix products  6.5 us (5%)
  other arithmetic  2.64 us (2%)
  local copies, waits for them, and re-layouts  1.41 us (1%)
    all_to_all x1, waiting for transfers between devices, body(): parts = lax.all_to_all(total, FIRST, 0, 0, tiled=True)  21.7 us
    pallas_call x1, Pallas kernels, forward(): pl.pallas_call(functools.partial(forward_kernel, slots, members), grid_sp...  19.4 us
    ppermute x7, starting transfers between devices, shifted(): lax.ppermute(block, axes, [(i, (i + distance) % count) for i in range(cou...  10.2 us
    pallas_call x1, Pallas kernels, backward(): pl.pallas_call(functools.partial(backward_kernel, slots), grid_spec=prefe...  9.68 us
    all_to_all x1, starting transfers between devices, body(): everyone = lax.all_to_all(sent, ENS, 0, 0, tiled=True)  9.03 us
    ppermute x1, starting transfers between devices, body(): edge = lax.ppermute(jnp.where(low, below, above), 'c', swap)  7.95 us
    all_to_all x1, starting transfers between devices, body(): parts = lax.all_to_all(total, SECOND, 0, 0, tiled=True)  7.69 us
    all_to_all x1, waiting for transfers between devices, body(): parts = lax.all_to_all(total, SECOND, 0, 0, tiled=True)  6.3 us
  transfers between devices with their start and end apart: 13, of which 5 were waited for; matrix products, arithmetic and copies ran while one was open for 7% of the time, Pallas kernels for 9%

profile of v10, /device:TPU:1, one launch (start us, length us, event | category | flops | bytes accessed | tf_op | source)
XLA Modules:
  0.0 129.1 jit_solution(16205357272627316371)
XLA Ops:
  0.6 0.0 copy-start
  0.6 3.3 %collective-permute-start.1 = (bf16[64,1024]{1,0:T(8,128)(2,1)}, bf16[64,1024]{1,0:T(8,128)(2,1)S(1)}, u32[]{:S(2)}, u32[]{:S(2)}) collective-permute-start(bf16[64,1024]{1,0:T(8,128)(2,1)} %bitcast.36), channel_id=1, source_target_pairs={{0,31},{1,0},{2,1},{3,2},{4,3},{5,4},{6,5},{7,6},{8,7},{9,8},{10,9... | collective-permute-start | bytes 393224 | tf_op jit(solution)/shard_map/ppermute | solution.py:29
  4.0 3.5 %convolution_convert_fusion.dst_ref = bf16[512,1024]{1,0:T(8,128)(2,1)} fusion(bf16[512,1024]{1,0:T(8,128)(2,1)} %grid_hbm.1, bf16[1024,1024]{1,0:T(8,128)(2,1)S(1)} %copy-done), kind=kOutput, calls=%fused_computation | convolution fusion | flops 1074266112 | bytes 4194304 | tf_op jit(solution)/shard_map/dot_general | solution.py:557
  7.5 0.6 fusion.2.idxt_ref.idx_ref
  8.1 0.7 pad_add_fusion.place_ref
  8.8 1.0 collective-permute-done.below_ref
  9.8 19.4 %forward.1 = (bf16[8192,1024]{1,0:T(8,128)(2,1)}, bf16[512,1024]{1,0:T(8,128)(2,1)}, f32[32,512]{1,0:T(8,128)}, bf16[8,32,512]{2,1,0:T(8,128)(2,1)}, bf16[512,25...) custom-call(s32[4]{0:T(128)} %pad_add_fusion.place_ref, ...), custom_call_target="tpu_custom_call" | custom-call | flops 4294967296 | bytes 16777216 | tf_op jit(solution)/shard_map/forward/pallas_call | solution.py:207
  29.2 9.0 %all-to-all-start = ((bf16[8,32,512]{2,1,0:T(8,128)(2,1)}), bf16[8,32,512]{2,1,0:T(8,128)(2,1)S(1)}, u32[]{:S(2)}, u32[]{:S(2)}) async-start(bf16[8,32,512]{2,1,0:T(8,128)(2,1)} %get-tuple-element.34), calls=%async_computation | async-start | bytes 524288 | tf_op jit(solution)/shard_map/all_to_all | solution.py:571
  38.3 1.5 %collective-permute-start.3 = (bf16[512,256]{1,0:T(8,128)(2,1)}, bf16[512,256]{1,0:T(8,128)(2,1)S(1)}, u32[]{:S(2)}, u32[]{:S(2)}) collective-permute-start(bf16[512,256]{1,0:T(8,128)(2,1)} %get-tuple-element.38), channel_id=1, source_target_pairs={{0,32},{32,64},{64,96},{96,0},{1,33},{33,65},{65,97},{97,1},{2,34}... | collective-permute-start | bytes 786440 | tf_op jit(solution)/shard_map/ppermute | solution.py:29
  39.7 2.4 %collective-permute-start.4 = (bf16[512,256]{1,0:T(8,128)(2,1)}, bf16[512,256]{1,0:T(8,128)(2,1)S(1)}, u32[]{:S(2)}, u32[]{:S(2)}) collective-permute-start(bf16[512,256]{1,0:T(8,128)(2,1)} %get-tuple-element.39), channel_id=1, source_target_pairs={{0,64},{32,96},{64,0},{96,32},{1,65},{33,97},{65,1},{97,33},{2,66}... | collective-permute-start | bytes 786440 | tf_op jit(solution)/shard_map/ppermute | solution.py:29
  42.1 1.2 collective-permute-start.5
  43.4 7.9 %collective-permute-start.2 = (bf16[64,1024]{1,0:T(8,128)(2,1)S(1)}, bf16[64,1024]{1,0:T(8,128)(2,1)S(1)}, u32[]{:S(2)}, u32[]{:S(2)}) collective-permute-start(bf16[64,1024]{1,0:T(8,128)(2,1)S(1)} %broadcast_select_fusion), channel_id=1, source_target_pairs={{0,1},{1,0},{2,3},{3,2},{4,5},{5,4},{6,7},{7,6},{8,9},{9,8},{10,11... | collective-permute-start | bytes 393224 | tf_op jit(solution)/shard_map/ppermute | solution.py:573
  51.3 0.7 copy.14.var_ref
  52.0 0.3 collective-permute-done.2.edge_ref
  52.4 5.6 %middle.1 = (bf16[512,1024]{1,0:T(8,128)(2,1)}, bf16[8,144,128]{2,1,0:T(8,128)(2,1)}, bf16[8,144,128]{2,1,0:T(8,128)(2,1)}) custom-call(s32[4]{0:T(128)} %pad_add_fusion.place_ref, bf16[8,32,512]{2,1,0:T(8,128)(2,1)S(1)} %all-to-all-done.every_ref, f32[32,512]{1,0:T(8,128)} %get-tuple-element.36.pred_ref, f32[32,512]{1,0:T(8,128)} %bitcast.42, ...), custom_call_target="tpu_custom_call" | custom-call | flops 536870912 | bytes 5242880 | tf_op jit(solution)/shard_map/middle/pallas_call | solution.py:337
  58.0 5.5 %collective-permute-start.7 = (bf16[8,144,128]{2,1,0:T(8,128)(2,1)}, bf16[8,144,128]{2,1,0:T(8,128)(2,1)S(1)}, u32[]{:S(2)}, u32[]{:S(2)}) collective-permute-start(bf16[8,144,128]{2,1,0:T(8,128)(2,1)} %get-tuple-element.48), channel_id=1, source_target_pairs={{0,1},{1,0},{2,3},{3,2},{4,5},{5,4},{6,7},{7,6},{8,9},{9,8},{10,11... | collective-permute-start | bytes 884744 | tf_op jit(solution)/shard_map/ppermute | solution.py:578
  63.5 9.7 %backward.1 = (bf16[64,1024]{1,0:T(8,128)(2,1)}, bf16[64,1024]{1,0:T(8,128)(2,1)}, bf16[64,1024]{1,0:T(8,128)(2,1)}, bf16[192,512]{1,0:T(8,128)(2,1)S(1)}, bf16[192,512]{1,0:T(8,128)(2,1)S(1)}) custom-call(s32[4]{0:T(128)} %pad_add_fusion.place_ref, bf16[8192,1024]{1,0:T(8,128)(2,1)} %get-tuple-element.33.gp_ref, ...), custom_call_target="tpu_custom_call" | custom-call | flops 4294967296 | bytes 16777216 | tf_op jit(solution)/shard_map/backward/pallas_call | solution.py:422
  73.2 0.1 collective-permute-start.6
  73.2 1.4 %collective-permute-done.6.far_ref = bf16[192,512]{1,0:T(8,128)(2,1)S(1)} collective-permute-done((bf16[192,512]{1,0:T(8,128)(2,1)S(1)}, bf16[192,512]{1,0:T(8,128)(2,1)S(1)}, u32[]{:S(2)}, u32[]{:S(2)}) %collective-permute-start.6) | collective-permute-done | bytes 196640 | tf_op jit(solution)/shard_map/ppermute | solution.py:581
  74.7 3.6 %pack.1 = bf16[16,64,656]{2,1,0:T(8,128)(2,1)} custom-call(s32[4]{0:T(128)} %pad_add_fusion.place_ref, bf16[64,1024]{1,0:T(8,128)(2,1)} %copy-done.2, bf16[64,1024]{1,0:T(8,128)(2,1)} %bitcast.39, bf16[64,1024]{1,0:T(8,128)(2,1)} %copy-done.1, bf16[64,1024]{1,0:T(8,128)(2,1)} %copy-done.3, bf16[192,512]{1,0:T(8,128)(2,1)S(1)} %get-tuple-element.45.own_ref, ...), custom_call_target="tpu_custom_call" | custom-call | flops 402653184 | bytes 4194304 | tf_op jit(solution)/shard_map/pack/pallas_call | solution.py:479
  78.3 6.1 %all-to-all-start.1 = ((bf16[16,64,656]{2,1,0:T(8,128)(2,1)}), bf16[16,64,656]{2,1,0:T(8,128)(2,1)}, u32[]{:S(2)}, u32[]{:S(2)}) async-start(bf16[16,64,656]{2,1,0:T(8,128)(2,1)} %pack.1), calls=%async_computation.1 | async-start | bytes 3145728 | tf_op jit(solution)/shard_map/all_to_all | solution.py:586
  84.4 0.5 collective-permute-start.8
  85.0 1.3 %collective-permute-start.9 = (bf16[64,1024]{1,0:T(8,128)(2,1)S(1)}, bf16[64,1024]{1,0:T(8,128)(2,1)S(1)}, u32[]{:S(2)}, u32[]{:S(2)}) collective-permute-start(bf16[64,1024]{1,0:T(8,128)(2,1)S(1)} %copy-done.9), channel_id=1, source_target_pairs={{0,1},{1,2},{2,3},{3,4},{4,5},{5,6},{6,7},{7,8},{8,9},{9,10},{10,1... | collective-permute-start | bytes 393224 | tf_op jit(solution)/shard_map/ppermute | solution.py:29
  86.3 21.7 %all-to-all-done.1.parts_ref = bf16[16,64,656]{2,1,0:T(8,128)(2,1)} async-done(((bf16[16,64,656]{2,1,0:T(8,128)(2,1)}), bf16[16,64,656]{2,1,0:T(8,128)(2,1)}, u32[]{:S(2)}, u32[]{:S(2)}) %all-to-all-start.1) | async-done | bytes 1343520 | tf_op jit(solution)/shard_map/all_to_all | solution.py:586
  108.0 2.1 %join.1 = bf16[16,4,1040]{2,1,0:T(4,128)(2,1)} custom-call(bf16[16,64,656]{2,1,0:T(8,128)(2,1)} %all-to-all-done.1.parts_ref), custom_call_target="tpu_custom_call" | custom-call | flops 671744 | bytes 1343488 | tf_op jit(solution)/shard_map/join/pallas_call | solution.py:519
  110.1 7.7 %all-to-all-start.2 = ((bf16[16,4,1040]{2,1,0:T(4,128)(2,1)}), bf16[16,4,1040]{2,1,0:T(4,128)(2,1)S(1)}, u32[]{:S(2)}, u32[]{:S(2)}) async-start(bf16[16,4,1040]{2,1,0:T(4,128)(2,1)} %join.1), calls=%async_computation.2 | async-start | bytes 294912 | tf_op jit(solution)/shard_map/all_to_all | solution.py:592
  117.8 3.0 %fusion = bf16[1,64,1024]{2,1,0:T(8,128)(2,1)} fusion(bf16[1024,1024]{1,0:T(8,128)(2,1)} %wsrc_ref.1, bf16[64,1024]{1,0:T(8,128)(2,1)S(1)} %collective-permute-done.9, bf16[64,1024]{1,0:T(8,128)(2,1)S(1)} %collective-permute-done.8, bf16[64,1024]{1,0:T(8,128)(2,1)S(1)} %copy-done.4), kind=kOutput, calls=%fused_computation.2 | convolution fusion | flops 134676480 | bytes 2621440 | tf_op jit(solution)/shard_map/dot_general | solution.py:594
  120.8 6.3 %all-to-all-done.2 = bf16[16,4,1040]{2,1,0:T(4,128)(2,1)S(1)} async-done(((bf16[16,4,1040]{2,1,0:T(4,128)(2,1)}), bf16[16,4,1040]{2,1,0:T(4,128)(2,1)S(1)}, u32[]{:S(2)}, u32[]{:S(2)}) %all-to-all-start.2) | async-done | bytes 133152 | tf_op jit(solution)/shard_map/all_to_all | solution.py:592
  127.1 0.1 convert_reduce_fusion
  127.2 0.6 reshape.20
  127.9 0.7 pad_maximum_fusion.1
  128.5 0.6 pad_maximum_fusion
  (36 shorter events, 0.1 us)
Async XLA Ops:
  0.6 3.3 %copy-start = (bf16[1024,1024]{1,0:T(8,128)(2,1)S(1)}, bf16[1024,1024]{1,0:T(8,128)(2,1)}, u32[]{:S(2)}) copy-start(bf16[1024,1024]{1,0:T(8,128)(2,1)} %param.13) | copy-start | bytes 6291460
  0.6 9.2 %collective-permute-start.1 = (bf16[64,1024]{1,0:T(8,128)(2,1)}, bf16[64,1024]{1,0:T(8,128)(2,1)S(1)}, u32[]{:S(2)}, u32[]{:S(2)}) collective-permute-start(bf16[64,1024]{1,0:T(8,128)(2,1)} %bitcast.36), channel_id=1, source_target_pairs={{0,31},{1,0},{2,1},{3,2},{4,3},{5,4},{6,5},{7,6},{8,7},{9,8},{10,9... | collective-permute-start | bytes 393224 | tf_op jit(solution)/shard_map/ppermute | solution.py:29
  4.0 5.8 %collective-permute-start = (bf16[64,1024]{1,0:T(8,128)(2,1)}, bf16[64,1024]{1,0:T(8,128)(2,1)S(1)}, u32[]{:S(2)}, u32[]{:S(2)}) collective-permute-start(bf16[64,1024]{1,0:T(8,128)(2,1)} %bitcast.37), channel_id=1, source_target_pairs={{0,1},{1,2},{2,3},{3,4},{4,5},{5,6},{6,7},{7,8},{8,9},{9,10},{10,1... | collective-permute-start | bytes 393224 | tf_op jit(solution)/shard_map/ppermute | solution.py:29
  4.0 3.5 %copy-start.5 = (s32[512,16]{0,1:T(8,128)S(1)}, s32[512,16]{0,1:T(8,128)}, u32[]{:S(2)}) copy-start(s32[512,16]{0,1:T(8,128)} %param.18) | copy-start | bytes 98308
  4.0 3.5 %copy-start.6 = (s32[512,16]{0,1:T(8,128)S(1)}, s32[512,16]{0,1:T(8,128)}, u32[]{:S(2)}) copy-start(s32[512,16]{0,1:T(8,128)} %param.19) | copy-start | bytes 98308
  9.8 33.6 %copy-start.2 = (bf16[64,1024]{1,0:T(8,128)(2,1)}, bf16[64,1024]{1,0:T(8,128)(2,1)S(1)}, u32[]{:S(2)}) copy-start(bf16[64,1024]{1,0:T(8,128)(2,1)S(1)} %collective-permute-done.below_ref) | copy-start | bytes 393220
  9.8 33.6 %copy-start.1 = (bf16[64,1024]{1,0:T(8,128)(2,1)}, bf16[64,1024]{1,0:T(8,128)(2,1)S(1)}, u32[]{:S(2)}) copy-start(bf16[64,1024]{1,0:T(8,128)(2,1)S(1)} %collective-permute-done.1.above_ref) | copy-start | bytes 393220
  9.8 33.5 %copy-start.7 = (s32[4]{0:T(128)S(1)}, s32[4]{0:T(128)}, u32[]{:S(2)}) copy-start(s32[4]{0:T(128)} %pad_add_fusion.place_ref) | copy-start | bytes 52
  9.8 41.5 %copy-start.8 = (f32[32]{0:T(128)S(1)}, f32[32]{0:T(128)}, u32[]{:S(2)}) copy-start(f32[32]{0:T(128)} %param.17) | copy-start | bytes 388
  29.2 23.1 %all-to-all-start = ((bf16[8,32,512]{2,1,0:T(8,128)(2,1)}), bf16[8,32,512]{2,1,0:T(8,128)(2,1)S(1)}, u32[]{:S(2)}, u32[]{:S(2)}) async-start(bf16[8,32,512]{2,1,0:T(8,128)(2,1)} %get-tuple-element.34), calls=%async_computation | async-start | bytes 524288 | tf_op jit(solution)/shard_map/all_to_all | solution.py:571
  38.3 14.1 %collective-permute-start.3 = (bf16[512,256]{1,0:T(8,128)(2,1)}, bf16[512,256]{1,0:T(8,128)(2,1)S(1)}, u32[]{:S(2)}, u32[]{:S(2)}) collective-permute-start(bf16[512,256]{1,0:T(8,128)(2,1)} %get-tuple-element.38), channel_id=1, source_target_pairs={{0,32},{32,64},{64,96},{96,0},{1,33},{33,65},{65,97},{97,1},{2,34}... | collective-permute-start | bytes 786440 | tf_op jit(solution)/shard_map/ppermute | solution.py:29
  39.7 12.6 %collective-permute-start.4 = (bf16[512,256]{1,0:T(8,128)(2,1)}, bf16[512,256]{1,0:T(8,128)(2,1)S(1)}, u32[]{:S(2)}, u32[]{:S(2)}) collective-permute-start(bf16[512,256]{1,0:T(8,128)(2,1)} %get-tuple-element.39), channel_id=1, source_target_pairs={{0,64},{32,96},{64,0},{96,32},{1,65},{33,97},{65,1},{97,33},{2,66}... | collective-permute-start | bytes 786440 | tf_op jit(solution)/shard_map/ppermute | solution.py:29
  42.1 10.2 %collective-permute-start.5 = (bf16[512,256]{1,0:T(8,128)(2,1)}, bf16[512,256]{1,0:T(8,128)(2,1)S(1)}, u32[]{:S(2)}, u32[]{:S(2)}) collective-permute-start(bf16[512,256]{1,0:T(8,128)(2,1)} %get-tuple-element.40), channel_id=1, source_target_pairs={{0,96},{32,0},{64,32},{96,64},{1,97},{33,1},{65,33},{97,65},{2,98}... | collective-permute-start | bytes 786440 | tf_op jit(solution)/shard_map/ppermute | solution.py:29
  43.4 8.9 %collective-permute-start.2 = (bf16[64,1024]{1,0:T(8,128)(2,1)S(1)}, bf16[64,1024]{1,0:T(8,128)(2,1)S(1)}, u32[]{:S(2)}, u32[]{:S(2)}) collective-permute-start(bf16[64,1024]{1,0:T(8,128)(2,1)S(1)} %broadcast_select_fusion), channel_id=1, source_target_pairs={{0,1},{1,0},{2,3},{3,2},{4,5},{5,4},{6,7},{7,6},{8,9},{9,8},{10,11... | collective-permute-start | bytes 393224 | tf_op jit(solution)/shard_map/ppermute | solution.py:573
  52.3 20.8 %copy-start.3 = (bf16[64,1024]{1,0:T(8,128)(2,1)}, bf16[64,1024]{1,0:T(8,128)(2,1)S(1)}, u32[]{:S(2)}) copy-start(bf16[64,1024]{1,0:T(8,128)(2,1)S(1)} %collective-permute-done.2.edge_ref) | copy-start | bytes 393220
  58.0 16.7 %collective-permute-start.7 = (bf16[8,144,128]{2,1,0:T(8,128)(2,1)}, bf16[8,144,128]{2,1,0:T(8,128)(2,1)S(1)}, u32[]{:S(2)}, u32[]{:S(2)}) collective-permute-start(bf16[8,144,128]{2,1,0:T(8,128)(2,1)} %get-tuple-element.48), channel_id=1, source_target_pairs={{0,1},{1,0},{2,3},{3,2},{4,5},{5,4},{6,7},{7,6},{8,9},{9,8},{10,11... | collective-permute-start | bytes 884744 | tf_op jit(solution)/shard_map/ppermute | solution.py:578
  73.2 1.5 %collective-permute-start.6 = (bf16[192,512]{1,0:T(8,128)(2,1)S(1)}, bf16[192,512]{1,0:T(8,128)(2,1)S(1)}, u32[]{:S(2)}, u32[]{:S(2)}) collective-permute-start(bf16[192,512]{1,0:T(8,128)(2,1)S(1)} %get-tuple-element.46), channel_id=1, source_target_pairs={{0,1},{1,0},{2,3},{3,2},{4,5},{5,4},{6,7},{7,6},{8,9},{9,8},{10,11... | collective-permute-start | bytes 589832 | tf_op jit(solution)/shard_map/ppermute | solution.py:581
  78.3 6.1 %copy-start.10 = (bf16[64,1024]{1,0:T(8,128)(2,1)S(1)}, bf16[64,1024]{1,0:T(8,128)(2,1)}, u32[]{:S(2)}) copy-start(bf16[64,1024]{1,0:T(8,128)(2,1)} %get-tuple-element.49) | copy-start | bytes 393220
  78.3 6.7 %copy-start.9 = (bf16[64,1024]{1,0:T(8,128)(2,1)S(1)}, bf16[64,1024]{1,0:T(8,128)(2,1)}, u32[]{:S(2)}) copy-start(bf16[64,1024]{1,0:T(8,128)(2,1)} %get-tuple-element.50) | copy-start | bytes 393220
  78.3 39.5 %copy-start.4 = (bf16[64,1024]{1,0:T(8,128)(2,1)S(1)}, bf16[64,1024]{1,0:T(8,128)(2,1)}, u32[]{:S(2)}) copy-start(bf16[64,1024]{1,0:T(8,128)(2,1)} %get-tuple-element.43) | copy-start | bytes 393220
  78.3 29.7 %all-to-all-start.1 = ((bf16[16,64,656]{2,1,0:T(8,128)(2,1)}), bf16[16,64,656]{2,1,0:T(8,128)(2,1)}, u32[]{:S(2)}, u32[]{:S(2)}) async-start(bf16[16,64,656]{2,1,0:T(8,128)(2,1)} %pack.1), calls=%async_computation.1 | async-start | bytes 3145728 | tf_op jit(solution)/shard_map/all_to_all | solution.py:586
  84.4 25.6 %collective-permute-start.8 = (bf16[64,1024]{1,0:T(8,128)(2,1)S(1)}, bf16[64,1024]{1,0:T(8,128)(2,1)S(1)}, u32[]{:S(2)}, u32[]{:S(2)}) collective-permute-start(bf16[64,1024]{1,0:T(8,128)(2,1)S(1)} %copy-done.10), channel_id=1, source_target_pairs={{0,31},{1,0},{2,1},{3,2},{4,3},{5,4},{6,5},{7,6},{8,7},{9,8},{10,9... | collective-permute-start | bytes 393224 | tf_op jit(solution)/shard_map/ppermute | solution.py:29
  85.0 25.1 %collective-permute-start.9 = (bf16[64,1024]{1,0:T(8,128)(2,1)S(1)}, bf16[64,1024]{1,0:T(8,128)(2,1)S(1)}, u32[]{:S(2)}, u32[]{:S(2)}) collective-permute-start(bf16[64,1024]{1,0:T(8,128)(2,1)S(1)} %copy-done.9), channel_id=1, source_target_pairs={{0,1},{1,2},{2,3},{3,4},{4,5},{5,6},{6,7},{7,8},{8,9},{9,10},{10,1... | collective-permute-start | bytes 393224 | tf_op jit(solution)/shard_map/ppermute | solution.py:29
  110.1 17.0 %all-to-all-start.2 = ((bf16[16,4,1040]{2,1,0:T(4,128)(2,1)}), bf16[16,4,1040]{2,1,0:T(4,128)(2,1)S(1)}, u32[]{:S(2)}, u32[]{:S(2)}) async-start(bf16[16,4,1040]{2,1,0:T(4,128)(2,1)} %join.1), calls=%async_computation.2 | async-start | bytes 294912 | tf_op jit(solution)/shard_map/all_to_all | solution.py:592

commit v11 on v10

--- a/solution.py
+++ b/solution.py
@@ -303,10 +303,9 @@
     outs = part_ref.shape[0] // 2
     rows = rows - outs
     for ref, which in ((far_ref, 1 - core), (own_ref, core)):
-        product = lax.dot_general(
+        product = jnp.dot(
             grid_ref[...],
             ddst[:, pl.ds(pl.multiple_of(which * few, few), few)],
-            first,
             preferred_element_type=f32,
         )
         ref[:, :rows, :] = product.astype(bf16).reshape(chunks, rows, few)
@@ -322,7 +321,7 @@
     )
 
 
-def middle(place, everyone, pred, truth_t, area, var, wout_t, idx_t, sums, agg, grid_embed):
+def middle(place, everyone, pred, truth_t, area, var, wout_t, idx_t, sums, agg, grid_t):
     grid_rows, width = agg.shape
     columns = sums[0].shape[1]
     chunks = GROUPS * QUARTERS
@@ -346,7 +345,7 @@
             [anywhere] + [whole(x) for x in out_shape[1:]],
             [
                 pltpu.VMEM((grid_rows, width), bf16),
-                pltpu.VMEM((grid_rows, width), bf16),
+                pltpu.VMEM((width, grid_rows), bf16),
                 pltpu.VMEM((grid_rows, width), bf16),
                 pltpu.VMEM((grid_rows, columns), bf16),
                 pltpu.VMEM(wout_t.shape, f32),
@@ -359,7 +358,7 @@
             flops=grid_rows * width * width, bytes_accessed=10 * grid_rows * width, transcendentals=0
         ),
         name="middle",
-    )(place, kept_near(everyone), *small[1:-3], *map(kept_near, sums[1:]), agg, grid_embed)
+    )(place, kept_near(everyone), *small[1:-3], *map(kept_near, sums[1:]), agg, grid_t)
 
 
 def scatter_step(slots, gp_ref, lead_ref, idx_ref, hot, prod, acc):
@@ -561,7 +560,10 @@
     truth_t = truth.T
     var = var_weight[:, None]
     area = area_weight[None, :]
-    dst, idx_t, place, below = lax.optimization_barrier((dst, idx_t, place, below))
+    grid_t = grid_embed.T
+    dst, idx_t, place, grid_t, var, below = lax.optimization_barrier(
+        (dst, idx_t, place, grid_t, var, below)
+    )
     feats = (below, own, above)
     chunks = lax.axis_size(FIRST)
     gp, agg, pred, sent, kept, *pieces = forward(
@@ -573,22 +575,22 @@
     edge = lax.ppermute(jnp.where(low, below, above), "c", swap)
     everyone, edge = lax.optimization_barrier((everyone, edge))
     lead, dst_own, dst_far = middle(
-        place, everyone, pred, truth_t, area, var, wout_t, idx_t, sums, agg, grid_embed
+        place, everyone, pred, truth_t, area, var, wout_t, idx_t, sums, agg, grid_t
     )
     dst_far = lax.ppermute(dst_far, "c", swap)
 
     lower, centre, upper, wide_own, wide_far = backward(place, gp, lead, idx_t, 3 * node_rows)
     wide_far = lax.ppermute(wide_far, "c", swap)
+    total = pack(place, feats, edge, wide_own, wide_far, dst_own, dst_far, chunks)
+    parts = lax.all_to_all(total, FIRST, 0, 0, tiled=True)
+
+    parts, lower, upper = lax.optimization_barrier((parts, lower, upper))
     from_above = shifted(lower, SPACE, -1)
     from_below = shifted(upper, SPACE, 1)
-
-    total = pack(place, feats, edge, wide_own, wide_far, dst_own, dst_far, chunks)
-    parts = lax.all_to_all(total, FIRST, 0, 0, tiled=True)
     few = half // QUARTERS
     rows_out = width // lax.axis_size(ENS + SPACE)
 
     total = join(parts, rows_out, half)
-    total, from_above, from_below = lax.optimization_barrier((total, from_above, from_below))
     parts = lax.all_to_all(total, SECOND, 0, 0, tiled=True)
     dproj = (centre.astype(f32) + from_above.astype(f32) + from_below.astype(f32)).astype(bf16)
     grad_mesh = lax.dot_general(

time: 130 us -> 131 us (level)
  blocking collectives: 0 us -> 27.9 us
  waiting for transfers between devices: 30.8 us -> 8.02 us
  starting transfers between devices: 46.5 us -> 41.8 us
  local copies, waits for them, and re-layouts: 1.41 us -> 2.74 us
    all_to_all x0 -> x1, blocking collectives: none -> 27.9 us  [body(): parts = lax.all_to_all(total, FIRST, 0, 0, tiled=True)]
    all_to_all x1 -> x0, waiting for transfers between devices: 21.7 us -> none  [body(): parts = lax.all_to_all(total, FIRST, 0, 0, tiled=True)]
    all_to_all x1 -> x0, starting transfers between devices: 6.12 us -> none  [body(): parts = lax.all_to_all(total, FIRST, 0, 0, tiled=True)]
    unnamed x22 -> x25, local copies, waits for them, and re-layouts: 0.05 us -> 1.38 us
    ppermute x1, starting transfers between devices: 7.95 us -> 6.62 us  [body(): edge = lax.ppermute(jnp.where(low, below, above), 'c', swap)]
  transfers between devices with their start and end apart: 13 -> 12, of which waited for: 5 -> 3; matrix products, arithmetic and copies ran while one was open for 7% -> 7% of each run, Pallas kernels for 9% -> 9%
where the time goes in v11:
time: 131 us
  starting transfers between devices  41.8 us (32%)
  Pallas kernels  40.4 us (31%)
  blocking collectives  27.9 us (21%)
  waiting for transfers between devices  8.02 us (6%)
  matrix products  6.55 us (5%)
  local copies, waits for them, and re-layouts  2.74 us (2%)
  other arithmetic  2.57 us (2%)
    all_to_all x1, blocking collectives, body(): parts = lax.all_to_all(total, FIRST, 0, 0, tiled=True)  27.9 us
    pallas_call x1, Pallas kernels, forward(): pl.pallas_call(functools.partial(forward_kernel, slots, members), grid_sp...  19.4 us
    ppermute x7, starting transfers between devices, shifted(): lax.ppermute(block, axes, [(i, (i + distance) % count) for i in range(cou...  10.8 us
    all_to_all x1, starting transfers between devices, body(): everyone = lax.all_to_all(sent, ENS, 0, 0, tiled=True)  10 us
    pallas_call x1, Pallas kernels, backward(): pl.pallas_call(functools.partial(backward_kernel, slots), grid_spec=prefe...  9.67 us
    all_to_all x1, starting transfers between devices, body(): parts = lax.all_to_all(total, SECOND, 0, 0, tiled=True)  7.95 us
    ppermute x1, starting transfers between devices, body(): edge = lax.ppermute(jnp.where(low, below, above), 'c', swap)  6.62 us
    ppermute x1, starting transfers between devices, body(): dst_far = lax.ppermute(dst_far, 'c', swap)  6.36 us
  transfers between devices with their start and end apart: 12, of which 3 were waited for; matrix products, arithmetic and copies ran while one was open for 7% of the time, Pallas kernels for 9%

profile of v11, /device:TPU:1, one launch (start us, length us, event | category | flops | bytes accessed | tf_op | source)
XLA Modules:
  0.0 130.8 jit_solution(16819541316147549580)
XLA Ops:
  0.6 0.0 copy-start
  0.6 3.3 %collective-permute-start.1 = (bf16[64,1024]{1,0:T(8,128)(2,1)}, bf16[64,1024]{1,0:T(8,128)(2,1)S(1)}, u32[]{:S(2)}, u32[]{:S(2)}) collective-permute-start(bf16[64,1024]{1,0:T(8,128)(2,1)} %bitcast.38), channel_id=1, source_target_pairs={{0,31},{1,0},{2,1},{3,2},{4,3},{5,4},{6,5},{7,6},{8,7},{9,8},{10,9... | collective-permute-start | bytes 393224 | tf_op jit(solution)/shard_map/ppermute | solution.py:29
  4.0 3.5 %convolution_convert_fusion.dst_ref = bf16[512,1024]{1,0:T(8,128)(2,1)} fusion(bf16[512,1024]{1,0:T(8,128)(2,1)} %param.11, bf16[1024,1024]{1,0:T(8,128)(2,1)S(1)} %copy-done), kind=kOutput, calls=%fused_computation | convolution fusion | flops 1074266112 | bytes 4194304 | tf_op jit(solution)/shard_map/dot_general | solution.py:556
  7.5 0.6 fusion.2.idxt_ref.idx_ref
  8.2 1.3 %copy.14 = bf16[512,1024]{0,1:T(8,128)(2,1)} copy(bf16[512,1024]{1,0:T(8,128)(2,1)S(1)} %copy-done.3) | data formatting | bytes 2097152 | tf_op args[1]
  9.5 0.6 pad_add_fusion.place_ref
  10.1 0.0 copy-start.9
  10.1 19.4 %forward.1 = (bf16[8192,1024]{1,0:T(8,128)(2,1)}, bf16[512,1024]{1,0:T(8,128)(2,1)}, f32[32,512]{1,0:T(8,128)}, bf16[8,32,512]{2,1,0:T(8,128)(2,1)}, bf16[512,25...) custom-call(s32[4]{0:T(128)} %pad_add_fusion.place_ref, ...), custom_call_target="tpu_custom_call" | custom-call | flops 4294967296 | bytes 16777216 | tf_op jit(solution)/shard_map/forward/pallas_call | solution.py:207
  29.5 10.0 %all-to-all-start = ((bf16[8,32,512]{2,1,0:T(8,128)(2,1)}), bf16[8,32,512]{2,1,0:T(8,128)(2,1)S(1)}, u32[]{:S(2)}, u32[]{:S(2)}) async-start(bf16[8,32,512]{2,1,0:T(8,128)(2,1)} %get-tuple-element.36), calls=%async_computation | async-start | bytes 524288 | tf_op jit(solution)/shard_map/all_to_all | solution.py:573
  39.6 1.5 %collective-permute-start.3 = (bf16[512,256]{1,0:T(8,128)(2,1)}, bf16[512,256]{1,0:T(8,128)(2,1)S(1)}, u32[]{:S(2)}, u32[]{:S(2)}) collective-permute-start(bf16[512,256]{1,0:T(8,128)(2,1)} %get-tuple-element.41), channel_id=1, source_target_pairs={{0,32},{32,64},{64,96},{96,0},{1,33},{33,65},{65,97},{97,1},{2,34}... | collective-permute-start | bytes 786440 | tf_op jit(solution)/shard_map/ppermute | solution.py:29
  41.0 2.4 %collective-permute-start.4 = (bf16[512,256]{1,0:T(8,128)(2,1)}, bf16[512,256]{1,0:T(8,128)(2,1)S(1)}, u32[]{:S(2)}, u32[]{:S(2)}) collective-permute-start(bf16[512,256]{1,0:T(8,128)(2,1)} %get-tuple-element.42), channel_id=1, source_target_pairs={{0,64},{32,96},{64,0},{96,32},{1,65},{33,97},{65,1},{97,33},{2,66}... | collective-permute-start | bytes 786440 | tf_op jit(solution)/shard_map/ppermute | solution.py:29
  43.4 1.2 collective-permute-start.5
  44.7 6.6 %collective-permute-start.2 = (bf16[64,1024]{1,0:T(8,128)(2,1)S(1)}, bf16[64,1024]{1,0:T(8,128)(2,1)S(1)}, u32[]{:S(2)}, u32[]{:S(2)}) collective-permute-start(bf16[64,1024]{1,0:T(8,128)(2,1)S(1)} %broadcast_select_fusion), channel_id=1, source_target_pairs={{0,1},{1,0},{2,3},{3,2},{4,5},{5,4},{6,7},{7,6},{8,9},{9,8},{10,11... | collective-permute-start | bytes 393224 | tf_op jit(solution)/shard_map/ppermute | solution.py:575
  51.3 0.7 copy.15.var_ref
  52.0 0.3 collective-permute-done.2.edge_ref
  52.3 5.6 %middle.1 = (bf16[512,1024]{1,0:T(8,128)(2,1)}, bf16[8,144,128]{2,1,0:T(8,128)(2,1)}, bf16[8,144,128]{2,1,0:T(8,128)(2,1)}) custom-call(s32[4]{0:T(128)} %pad_add_fusion.place_ref, bf16[8,32,512]{2,1,0:T(8,128)(2,1)S(1)} %all-to-all-done.every_ref, f32[32,512]{1,0:T(8,128)} %get-tuple-element.38.pred_ref, f32[32,512]{1,0:T(8,128)} %bitcast.44, ...), custom_call_target="tpu_custom_call" | custom-call | flops 536870912 | bytes 5242880 | tf_op jit(solution)/shard_map/middle/pallas_call | solution.py:336
  57.9 6.4 %collective-permute-start.7 = (bf16[8,144,128]{2,1,0:T(8,128)(2,1)}, bf16[8,144,128]{2,1,0:T(8,128)(2,1)S(1)}, u32[]{:S(2)}, u32[]{:S(2)}) collective-permute-start(bf16[8,144,128]{2,1,0:T(8,128)(2,1)} %get-tuple-element.52), channel_id=1, source_target_pairs={{0,1},{1,0},{2,3},{3,2},{4,5},{5,4},{6,7},{7,6},{8,9},{9,8},{10,11... | collective-permute-start | bytes 884744 | tf_op jit(solution)/shard_map/ppermute | solution.py:580
  64.3 9.7 %backward.1 = (bf16[64,1024]{1,0:T(8,128)(2,1)}, bf16[64,1024]{1,0:T(8,128)(2,1)}, bf16[64,1024]{1,0:T(8,128)(2,1)}, bf16[192,512]{1,0:T(8,128)(2,1)S(1)}, bf16[192,512]{1,0:T(8,128)(2,1)S(1)}) custom-call(s32[4]{0:T(128)} %pad_add_fusion.place_ref, bf16[8192,1024]{1,0:T(8,128)(2,1)} %get-tuple-element.35.gp_ref, ...), custom_call_target="tpu_custom_call" | custom-call | flops 4294967296 | bytes 16777216 | tf_op jit(solution)/shard_map/backward/pallas_call | solution.py:421
  74.0 0.1 collective-permute-start.6
  74.0 1.4 %collective-permute-done.6.far_ref = bf16[192,512]{1,0:T(8,128)(2,1)S(1)} collective-permute-done((bf16[192,512]{1,0:T(8,128)(2,1)S(1)}, bf16[192,512]{1,0:T(8,128)(2,1)S(1)}, u32[]{:S(2)}, u32[]{:S(2)}) %collective-permute-start.6) | collective-permute-done | bytes 196640 | tf_op jit(solution)/shard_map/ppermute | solution.py:583
  75.5 3.6 %pack.1 = bf16[16,64,656]{2,1,0:T(8,128)(2,1)} custom-call(s32[4]{0:T(128)} %pad_add_fusion.place_ref, bf16[64,1024]{1,0:T(8,128)(2,1)} %copy-done.2, bf16[64,1024]{1,0:T(8,128)(2,1)} %bitcast.41, bf16[64,1024]{1,0:T(8,128)(2,1)} %copy-done.1, bf16[64,1024]{1,0:T(8,128)(2,1)} %copy-done.4, bf16[192,512]{1,0:T(8,128)(2,1)S(1)} %get-tuple-element.49.own_ref, ...), custom_call_target="tpu_custom_call" | custom-call | flops 402653184 | bytes 4194304 | tf_op jit(solution)/shard_map/pack/pallas_call | solution.py:478
  79.1 27.9 %all_to_all.15.parts_ref = bf16[16,64,656]{2,1,0:T(8,128)(2,1)} all-to-all(bf16[16,64,656]{2,1,0:T(8,128)(2,1)} %pack.1), channel_id=1, replica_groups=mesh['zh'=2,'x'=4,'y'=4,'zl'=4,'c'=2] {'x','y'}, dimensions={0} | all-to-all | bytes 2686976 | tf_op jit(solution)/shard_map/all_to_all | solution.py:585
  107.0 2.3 %collective-permute-start.8 = (bf16[64,1024]{1,0:T(8,128)(2,1)S(1)}, bf16[64,1024]{1,0:T(8,128)(2,1)S(1)}, u32[]{:S(2)}, u32[]{:S(2)}) collective-permute-start(bf16[64,1024]{1,0:T(8,128)(2,1)S(1)} %copy-done.11), channel_id=1, source_target_pairs={{0,31},{1,0},{2,1},{3,2},{4,3},{5,4},{6,5},{7,6},{8,7},{9,8},{10,9... | collective-permute-start | bytes 393224 | tf_op jit(solution)/shard_map/ppermute | solution.py:29
  109.2 0.2 collective-permute-start.9
  109.4 2.1 %join.1 = bf16[16,4,1040]{2,1,0:T(4,128)(2,1)} custom-call(bf16[16,64,656]{2,1,0:T(8,128)(2,1)} %all_to_all.15.parts_ref), custom_call_target="tpu_custom_call" | custom-call | flops 671744 | bytes 1343488 | tf_op jit(solution)/shard_map/join/pallas_call | solution.py:518
  111.5 7.9 %all-to-all-start.2 = ((bf16[16,4,1040]{2,1,0:T(4,128)(2,1)}), bf16[16,4,1040]{2,1,0:T(4,128)(2,1)S(1)}, u32[]{:S(2)}, u32[]{:S(2)}) async-start(bf16[16,4,1040]{2,1,0:T(4,128)(2,1)} %join.1), calls=%async_computation.2 | async-start | bytes 294912 | tf_op jit(solution)/shard_map/all_to_all | solution.py:594
  119.5 3.0 %fusion = bf16[1,64,1024]{2,1,0:T(8,128)(2,1)} fusion(bf16[1024,1024]{1,0:T(8,128)(2,1)} %wsrc_ref.1, bf16[64,1024]{1,0:T(8,128)(2,1)S(1)} %collective-permute-done.9, bf16[64,1024]{1,0:T(8,128)(2,1)S(1)} %collective-permute-done.8, bf16[64,1024]{1,0:T(8,128)(2,1)S(1)} %copy-done.5), kind=kOutput, calls=%fused_computation.2 | convolution fusion | flops 134676480 | bytes 2621440 | tf_op jit(solution)/shard_map/dot_general | solution.py:596
  122.5 6.3 %all-to-all-done.2 = bf16[16,4,1040]{2,1,0:T(4,128)(2,1)S(1)} async-done(((bf16[16,4,1040]{2,1,0:T(4,128)(2,1)}), bf16[16,4,1040]{2,1,0:T(4,128)(2,1)S(1)}, u32[]{:S(2)}, u32[]{:S(2)}) %all-to-all-start.2) | async-done | bytes 133152 | tf_op jit(solution)/shard_map/all_to_all | solution.py:594
  128.8 0.1 convert_reduce_fusion
  128.9 0.6 reshape.20
  129.6 0.7 pad_maximum_fusion.1
  130.2 0.6 pad_maximum_fusion
  (38 shorter events, 0.1 us)
Async XLA Ops:
  0.6 3.3 %copy-start = (bf16[1024,1024]{1,0:T(8,128)(2,1)S(1)}, bf16[1024,1024]{1,0:T(8,128)(2,1)}, u32[]{:S(2)}) copy-start(bf16[1024,1024]{1,0:T(8,128)(2,1)} %param.13) | copy-start | bytes 6291460
  0.6 9.4 %collective-permute-start.1 = (bf16[64,1024]{1,0:T(8,128)(2,1)}, bf16[64,1024]{1,0:T(8,128)(2,1)S(1)}, u32[]{:S(2)}, u32[]{:S(2)}) collective-permute-start(bf16[64,1024]{1,0:T(8,128)(2,1)} %bitcast.38), channel_id=1, source_target_pairs={{0,31},{1,0},{2,1},{3,2},{4,3},{5,4},{6,5},{7,6},{8,7},{9,8},{10,9... | collective-permute-start | bytes 393224 | tf_op jit(solution)/shard_map/ppermute | solution.py:29
  4.0 6.1 %collective-permute-start = (bf16[64,1024]{1,0:T(8,128)(2,1)}, bf16[64,1024]{1,0:T(8,128)(2,1)S(1)}, u32[]{:S(2)}, u32[]{:S(2)}) collective-permute-start(bf16[64,1024]{1,0:T(8,128)(2,1)} %bitcast.39), channel_id=1, source_target_pairs={{0,1},{1,2},{2,3},{3,4},{4,5},{5,6},{6,7},{7,8},{8,9},{9,10},{10,1... | collective-permute-start | bytes 393224 | tf_op jit(solution)/shard_map/ppermute | solution.py:29
  4.0 3.6 %copy-start.6 = (s32[512,16]{0,1:T(8,128)S(1)}, s32[512,16]{0,1:T(8,128)}, u32[]{:S(2)}) copy-start(s32[512,16]{0,1:T(8,128)} %param.18) | copy-start | bytes 98308
  4.0 3.6 %copy-start.7 = (s32[512,16]{0,1:T(8,128)S(1)}, s32[512,16]{0,1:T(8,128)}, u32[]{:S(2)}) copy-start(s32[512,16]{0,1:T(8,128)} %param.19) | copy-start | bytes 98308
  4.0 4.2 %copy-start.3 = (bf16[512,1024]{1,0:T(8,128)(2,1)S(1)}, bf16[512,1024]{1,0:T(8,128)(2,1)}, u32[]{:S(2)}) copy-start(bf16[512,1024]{1,0:T(8,128)(2,1)} %param.11) | copy-start | bytes 3145732
  10.1 34.6 %copy-start.2 = (bf16[64,1024]{1,0:T(8,128)(2,1)}, bf16[64,1024]{1,0:T(8,128)(2,1)S(1)}, u32[]{:S(2)}) copy-start(bf16[64,1024]{1,0:T(8,128)(2,1)S(1)} %collective-permute-done.below_ref) | copy-start | bytes 393220
  10.1 34.6 %copy-start.1 = (bf16[64,1024]{1,0:T(8,128)(2,1)}, bf16[64,1024]{1,0:T(8,128)(2,1)S(1)}, u32[]{:S(2)}) copy-start(bf16[64,1024]{1,0:T(8,128)(2,1)S(1)} %collective-permute-done.1.above_ref) | copy-start | bytes 393220
  10.1 34.5 %copy-start.8 = (s32[4]{0:T(128)S(1)}, s32[4]{0:T(128)}, u32[]{:S(2)}) copy-start(s32[4]{0:T(128)} %pad_add_fusion.place_ref) | copy-start | bytes 52
  10.1 41.2 %copy-start.9 = (f32[32]{0:T(128)S(1)}, f32[32]{0:T(128)}, u32[]{:S(2)}) copy-start(f32[32]{0:T(128)} %param.17) | copy-start | bytes 388
  29.5 22.8 %all-to-all-start = ((bf16[8,32,512]{2,1,0:T(8,128)(2,1)}), bf16[8,32,512]{2,1,0:T(8,128)(2,1)S(1)}, u32[]{:S(2)}, u32[]{:S(2)}) async-start(bf16[8,32,512]{2,1,0:T(8,128)(2,1)} %get-tuple-element.36), calls=%async_computation | async-start | bytes 524288 | tf_op jit(solution)/shard_map/all_to_all | solution.py:573
  39.6 12.7 %collective-permute-start.3 = (bf16[512,256]{1,0:T(8,128)(2,1)}, bf16[512,256]{1,0:T(8,128)(2,1)S(1)}, u32[]{:S(2)}, u32[]{:S(2)}) collective-permute-start(bf16[512,256]{1,0:T(8,128)(2,1)} %get-tuple-element.41), channel_id=1, source_target_pairs={{0,32},{32,64},{64,96},{96,0},{1,33},{33,65},{65,97},{97,1},{2,34}... | collective-permute-start | bytes 786440 | tf_op jit(solution)/shard_map/ppermute | solution.py:29
  41.0 11.3 %collective-permute-start.4 = (bf16[512,256]{1,0:T(8,128)(2,1)}, bf16[512,256]{1,0:T(8,128)(2,1)S(1)}, u32[]{:S(2)}, u32[]{:S(2)}) collective-permute-start(bf16[512,256]{1,0:T(8,128)(2,1)} %get-tuple-element.42), channel_id=1, source_target_pairs={{0,64},{32,96},{64,0},{96,32},{1,65},{33,97},{65,1},{97,33},{2,66}... | collective-permute-start | bytes 786440 | tf_op jit(solution)/shard_map/ppermute | solution.py:29
  43.4 8.9 %collective-permute-start.5 = (bf16[512,256]{1,0:T(8,128)(2,1)}, bf16[512,256]{1,0:T(8,128)(2,1)S(1)}, u32[]{:S(2)}, u32[]{:S(2)}) collective-permute-start(bf16[512,256]{1,0:T(8,128)(2,1)} %get-tuple-element.43), channel_id=1, source_target_pairs={{0,96},{32,0},{64,32},{96,64},{1,97},{33,1},{65,33},{97,65},{2,98}... | collective-permute-start | bytes 786440 | tf_op jit(solution)/shard_map/ppermute | solution.py:29
  44.7 7.6 %collective-permute-start.2 = (bf16[64,1024]{1,0:T(8,128)(2,1)S(1)}, bf16[64,1024]{1,0:T(8,128)(2,1)S(1)}, u32[]{:S(2)}, u32[]{:S(2)}) collective-permute-start(bf16[64,1024]{1,0:T(8,128)(2,1)S(1)} %broadcast_select_fusion), channel_id=1, source_target_pairs={{0,1},{1,0},{2,3},{3,2},{4,5},{5,4},{6,7},{7,6},{8,9},{9,8},{10,11... | collective-permute-start | bytes 393224 | tf_op jit(solution)/shard_map/ppermute | solution.py:575
  52.3 21.7 %copy-start.4 = (bf16[64,1024]{1,0:T(8,128)(2,1)}, bf16[64,1024]{1,0:T(8,128)(2,1)S(1)}, u32[]{:S(2)}) copy-start(bf16[64,1024]{1,0:T(8,128)(2,1)S(1)} %collective-permute-done.2.edge_ref) | copy-start | bytes 393220
  57.9 17.5 %collective-permute-start.7 = (bf16[8,144,128]{2,1,0:T(8,128)(2,1)}, bf16[8,144,128]{2,1,0:T(8,128)(2,1)S(1)}, u32[]{:S(2)}, u32[]{:S(2)}) collective-permute-start(bf16[8,144,128]{2,1,0:T(8,128)(2,1)} %get-tuple-element.52), channel_id=1, source_target_pairs={{0,1},{1,0},{2,3},{3,2},{4,5},{5,4},{6,7},{7,6},{8,9},{9,8},{10,11... | collective-permute-start | bytes 884744 | tf_op jit(solution)/shard_map/ppermute | solution.py:580
  74.0 1.5 %collective-permute-start.6 = (bf16[192,512]{1,0:T(8,128)(2,1)S(1)}, bf16[192,512]{1,0:T(8,128)(2,1)S(1)}, u32[]{:S(2)}, u32[]{:S(2)}) collective-permute-start(bf16[192,512]{1,0:T(8,128)(2,1)S(1)} %get-tuple-element.50), channel_id=1, source_target_pairs={{0,1},{1,0},{2,3},{3,2},{4,5},{5,4},{6,7},{7,6},{8,9},{9,8},{10,11... | collective-permute-start | bytes 589832 | tf_op jit(solution)/shard_map/ppermute | solution.py:583
  79.1 27.9 %copy-start.11 = (bf16[64,1024]{1,0:T(8,128)(2,1)S(1)}, bf16[64,1024]{1,0:T(8,128)(2,1)}, u32[]{:S(2)}) copy-start(bf16[64,1024]{1,0:T(8,128)(2,1)} %get-tuple-element.55) | copy-start | bytes 393220
  79.1 30.1 %copy-start.10 = (bf16[64,1024]{1,0:T(8,128)(2,1)S(1)}, bf16[64,1024]{1,0:T(8,128)(2,1)}, u32[]{:S(2)}) copy-start(bf16[64,1024]{1,0:T(8,128)(2,1)} %get-tuple-element.56) | copy-start | bytes 393220
  79.1 40.4 %copy-start.5 = (bf16[64,1024]{1,0:T(8,128)(2,1)S(1)}, bf16[64,1024]{1,0:T(8,128)(2,1)}, u32[]{:S(2)}) copy-start(bf16[64,1024]{1,0:T(8,128)(2,1)} %get-tuple-element.47) | copy-start | bytes 393220
  107.0 12.5 %collective-permute-start.8 = (bf16[64,1024]{1,0:T(8,128)(2,1)S(1)}, bf16[64,1024]{1,0:T(8,128)(2,1)S(1)}, u32[]{:S(2)}, u32[]{:S(2)}) collective-permute-start(bf16[64,1024]{1,0:T(8,128)(2,1)S(1)} %copy-done.11), channel_id=1, source_target_pairs={{0,31},{1,0},{2,1},{3,2},{4,3},{5,4},{6,5},{7,6},{8,7},{9,8},{10,9... | collective-permute-start | bytes 393224 | tf_op jit(solution)/shard_map/ppermute | solution.py:29
  109.2 10.2 %collective-permute-start.9 = (bf16[64,1024]{1,0:T(8,128)(2,1)S(1)}, bf16[64,1024]{1,0:T(8,128)(2,1)S(1)}, u32[]{:S(2)}, u32[]{:S(2)}) collective-permute-start(bf16[64,1024]{1,0:T(8,128)(2,1)S(1)} %copy-done.10), channel_id=1, source_target_pairs={{0,1},{1,2},{2,3},{3,4},{4,5},{5,6},{6,7},{7,8},{8,9},{9,10},{10,1... | collective-permute-start | bytes 393224 | tf_op jit(solution)/shard_map/ppermute | solution.py:29
  111.5 17.3 %all-to-all-start.2 = ((bf16[16,4,1040]{2,1,0:T(4,128)(2,1)}), bf16[16,4,1040]{2,1,0:T(4,128)(2,1)S(1)}, u32[]{:S(2)}, u32[]{:S(2)}) async-start(bf16[16,4,1040]{2,1,0:T(4,128)(2,1)} %join.1), calls=%async_computation.2 | async-start | bytes 294912 | tf_op jit(solution)/shard_map/all_to_all | solution.py:594

commit v12 on v10

--- a/solution.py
+++ b/solution.py
@@ -234,7 +234,7 @@
     )(place, kept_near(below), here, kept_near(above), w_src, dst, idx_t, wout_t)
 
 
-def middle_kernel(
+def middle_step(
     place_ref,
     every_ref,
     pred_ref,
@@ -243,18 +243,14 @@
     var_ref,
     wout_ref,
     idxt_ref,
-    sum0_ref,
-    sum1_ref,
-    sum2_ref,
-    sum3_ref,
+    sum_refs,
     agg_hbm,
     grid_hbm,
-    lead_hbm,
+    lead_ref,
     own_ref,
     far_ref,
     agg_ref,
     grid_ref,
-    lead_ref,
     ddst,
     part_ref,
     sems,
@@ -263,12 +259,11 @@
         pltpu.make_async_copy(agg_hbm, agg_ref, sems.at[0]),
         pltpu.make_async_copy(grid_hbm, grid_ref, sems.at[1]),
     ]
-    store = pltpu.make_async_copy(lead_ref, lead_hbm, sems.at[2])
     for copy in loads:
         copy.start()
     width = wout_ref.shape[1]
     members = every_ref.shape[0]
-    near, columns = QUARTERS, sum0_ref.shape[1]
+    near, columns = QUARTERS, sum_refs[0].shape[1]
     core, x, zh = place_ref[0], place_ref[1], place_ref[2]
     weighting = loss_scale * area_ref[...] * var_ref[...]
 
@@ -286,11 +281,10 @@
         cols = slice(n * NCOL, (n + 1) * NCOL)
         dagg = lax.dot_general(dpred, wout_ref[:, cols], first, preferred_element_type=f32)
         lead_ref[:, cols] = (dagg * scale).astype(bf16)
-    store.start()
 
     quarter = wout_ref[:, pl.ds(pl.multiple_of(x * columns, columns), columns)]
-    total = jnp.zeros(sum0_ref.shape, f32)
-    for d, sum_ref in enumerate((sum0_ref, sum1_ref, sum2_ref, sum3_ref)):
+    total = jnp.zeros(sum_refs[0].shape, f32)
+    for d, sum_ref in enumerate(sum_refs):
         other = dpred_of(every_ref[zh * near + (x + near - d) % near].astype(f32))
         dagg = lax.dot_general(other, quarter, first, preferred_element_type=f32)
         total = total + dagg * sum_ref[...].astype(f32)
@@ -313,7 +307,6 @@
         at = pl.ds(pl.multiple_of(which * outs, outs), outs)
         for chunk in range(chunks):
             ref[chunk, rows:, :] = part_ref[at, chunk * few : (chunk + 1) * few].astype(bf16)
-    store.wait()
 
 
 def prefetched(count, ins, outs, scratch):
@@ -322,86 +315,85 @@
     )
 
 
-def middle(place, everyone, pred, truth_t, area, var, wout_t, idx_t, sums, agg, grid_embed):
-    grid_rows, width = agg.shape
-    columns = sums[0].shape[1]
-    chunks = GROUPS * QUARTERS
-    product = (chunks, width // chunks + wout_t.shape[0] // 2, columns // 2)
-    anywhere = pl.BlockSpec(memory_space=pl.ANY)
-    small = (everyone, pred, truth_t, area, var, wout_t, idx_t, *sums)
-    out_shape = [
-        jax.ShapeDtypeStruct((grid_rows, width), bf16),
-        jax.ShapeDtypeStruct(product, bf16),
-        jax.ShapeDtypeStruct(product, bf16),
-    ]
-    return pl.pallas_call(
-        middle_kernel,
-        grid_spec=prefetched(
-            1,
-            [landed()]
-            + [whole(x) for x in small[1 : -len(sums)]]
-            + [whole(sums[0])]
-            + [landed()] * (len(sums) - 1)
-            + [anywhere] * 2,
-            [anywhere] + [whole(x) for x in out_shape[1:]],
-            [
-                pltpu.VMEM((grid_rows, width), bf16),
-                pltpu.VMEM((grid_rows, width), bf16),
-                pltpu.VMEM((grid_rows, width), bf16),
-                pltpu.VMEM((grid_rows, columns), bf16),
-                pltpu.VMEM(wout_t.shape, f32),
-                pltpu.SemaphoreType.DMA((3,)),
-            ],
-        ),
-        out_shape=out_shape,
-        compiler_params=params(),
-        cost_estimate=pl.CostEstimate(
-            flops=grid_rows * width * width, bytes_accessed=10 * grid_rows * width, transcendentals=0
-        ),
-        name="middle",
-    )(place, kept_near(everyone), *small[1:-3], *map(kept_near, sums[1:]), agg, grid_embed)
-
-
-def scatter_step(slots, gp_ref, lead_ref, idx_ref, hot, prod, acc):
-    nodes, half = acc.shape
-    wide = lead_ref.shape[0]
-
-    @pl.when(pl.program_id(0) == 0)
-    def _():
-        acc[...] = jnp.zeros_like(acc)
-
-    node = lax.broadcasted_iota(jnp.int32, (nodes, wide), 0)
-    for k in range(slots):
-        hot[:, k * wide : (k + 1) * wide] = jnp.where(node == idx_ref[k : k + 1, :], 1.0, 0.0).astype(bf16)
-    for start in range(0, wide, TILE):
-        lead = lead_ref[start : start + TILE, :]
-        for k in range(slots):
-            at = start * slots + k * TILE
-            to = k * wide + start
-            prod[to : to + TILE, :] = gp_ref[at : at + TILE, :] * lead
-    for n in range(half // NCOL):
-        here = slice(n * NCOL, (n + 1) * NCOL)
-        acc[:, here] += jnp.dot(hot[...], prod[:, here], preferred_element_type=f32)
-
-
 def backward_kernel(
     slots,
     place_ref,
+    every_ref,
+    pred_ref,
+    truth_ref,
+    area_ref,
+    var_ref,
+    wout_ref,
+    idxt_ref,
+    sum0_ref,
+    sum1_ref,
+    sum2_ref,
+    sum3_ref,
+    agg_hbm,
+    grid_hbm,
     gp_ref,
-    lead_ref,
-    idx_ref,
     lower_ref,
     centre_ref,
     upper_ref,
     own_ref,
     far_ref,
+    dst_ref,
+    dstfar_ref,
+    lead,
+    agg_ref,
+    grid_ref,
+    ddst,
+    part_ref,
+    sems,
     hot,
     prod,
     acc,
 ):
-    scatter_step(slots, gp_ref, lead_ref, idx_ref, hot, prod, acc)
-
-    @pl.when(pl.program_id(0) == pl.num_programs(0) - 1)
+    step = pl.program_id(0)
+    nodes, width = acc.shape
+
+    @pl.when(step == 0)
+    def _():
+        middle_step(
+            place_ref,
+            every_ref,
+            pred_ref,
+            truth_ref,
+            area_ref,
+            var_ref,
+            wout_ref,
+            idxt_ref,
+            (sum0_ref, sum1_ref, sum2_ref, sum3_ref),
+            agg_hbm,
+            grid_hbm,
+            lead,
+            dst_ref,
+            dstfar_ref,
+            agg_ref,
+            grid_ref,
+            ddst,
+            part_ref,
+            sems,
+        )
+        acc[...] = jnp.zeros_like(acc)
+
+    wide = gp_ref.shape[0] // slots
+    base = pl.multiple_of(step * wide, wide)
+    node = lax.broadcasted_iota(jnp.int32, (nodes, wide), 0)
+    idx = idxt_ref[:, pl.ds(base, wide)]
+    for k in range(slots):
+        hot[:, k * wide : (k + 1) * wide] = jnp.where(node == idx[k : k + 1, :], 1.0, 0.0).astype(bf16)
+    for start in range(0, wide, TILE):
+        some = lead[pl.ds(pl.multiple_of(base + start, TILE), TILE), :]
+        for k in range(slots):
+            at = start * slots + k * TILE
+            to = k * wide + start
+            prod[to : to + TILE, :] = gp_ref[at : at + TILE, :] * some
+    for n in range(width // NCOL):
+        here = slice(n * NCOL, (n + 1) * NCOL)
+        acc[:, here] += jnp.dot(hot[...], prod[:, here], preferred_element_type=f32)
+
+    @pl.when(step == pl.num_programs(0) - 1)
     def _():
         core = place_ref[0]
         half = own_ref.shape[1]
@@ -412,24 +404,39 @@
         far_ref[...] = acc[:, pl.ds(pl.multiple_of((1 - core) * half, half), half)].astype(bf16)
 
 
-def backward(place, gp, lead, idx_t, nodes):
-    grid_rows, width = lead.shape
+def backward(
+    place, everyone, pred, truth_t, area, var, wout_t, idx_t, sums, agg, grid_embed, gp, nodes
+):
+    grid_rows, width = agg.shape
     slots = idx_t.shape[0]
     rows = BACK * TILE
-    out_shape = [jax.ShapeDtypeStruct((nodes // 3, width), bf16)] * 3 + [
-        pltpu.VMEM((nodes, width // 2), bf16)
-    ] * 2
+    columns = sums[0].shape[1]
+    chunks = GROUPS * QUARTERS
+    product = (chunks, width // chunks + wout_t.shape[0] // 2, columns // 2)
+    anywhere = pl.BlockSpec(memory_space=pl.ANY)
+    out_shape = (
+        [jax.ShapeDtypeStruct((nodes // 3, width), bf16)] * 3
+        + [pltpu.VMEM((nodes, width // 2), bf16)] * 2
+        + [pltpu.VMEM(product, bf16)] * 2
+    )
+    small = (pred, truth_t, area, var, wout_t, idx_t, sums[0])
     return pl.pallas_call(
         functools.partial(backward_kernel, slots),
         grid_spec=prefetched(
             grid_rows // rows,
+            [landed()]
+            + [whole(x) for x in small]
+            + [landed()] * (len(sums) - 1)
+            + [anywhere] * 2
+            + [pl.BlockSpec((rows * slots, width), lambda t, place: (t, 0))],
+            [whole(x) for x in out_shape[:3]] + [landed()] * 4,
             [
-                pl.BlockSpec((rows * slots, width), lambda t, place: (t, 0)),
-                pl.BlockSpec((rows, width), lambda t, place: (t, 0)),
-                pl.BlockSpec((slots, rows), lambda t, place: (0, t)),
-            ],
-            [whole(x) for x in out_shape[:3]] + [landed()] * 2,
-            [
+                pltpu.VMEM((grid_rows, width), bf16),
+                pltpu.VMEM((grid_rows, width), bf16),
+                pltpu.VMEM((grid_rows, width), bf16),
+                pltpu.VMEM((grid_rows, columns), bf16),
+                pltpu.VMEM(wout_t.shape, f32),
+                pltpu.SemaphoreType.DMA((2,)),
                 pltpu.VMEM((nodes, rows * slots), bf16),
                 pltpu.VMEM((rows * slots, width), bf16),
                 pltpu.VMEM((nodes, width), f32),
@@ -439,7 +446,7 @@
         compiler_params=params(),
         cost_estimate=pl.CostEstimate(flops=gp.size * 512, bytes_accessed=2 * gp.size, transcendentals=0),
         name="backward",
-    )(place, gp, lead, idx_t)
+    )(place, kept_near(everyone), *small, *map(kept_near, sums[1:]), agg, grid_embed, gp)
 
 
 def pack_kernel(
@@ -457,9 +464,9 @@
     product = product + lax.dot_general(other, far_ref[...], first, preferred_element_type=f32)
     chunks, rows, columns = total_ref.shape
     total_ref[:, :, :half] = product.astype(bf16).reshape(chunks, rows, half)
-    per_zh = dst_ref.shape[0]
+    per_zh = dst_ref.shape[0] // GROUPS
     at = pl.ds(pl.program_id(0) * per_zh, per_zh)
-    both = dst_ref[...].astype(f32) + dstfar_ref[at].astype(f32)
+    both = dst_ref[at].astype(f32) + dstfar_ref[at].astype(f32)
     few = both.shape[2]
     outs = columns - half - few
     some = both[:, : both.shape[1] - outs].astype(bf16)
@@ -470,17 +477,15 @@
 
 def pack(place, feats, edge, own, far, dst_own, dst_far, chunks):
     nodes, width = feats[0].shape
-    per_zh = (dst_own.shape[0] // GROUPS,) + dst_own.shape[1:]
     outs = dst_own.shape[1] - width // dst_own.shape[0]
     columns = width // 2 + dst_own.shape[2] + outs
     rows = width // chunks
     feat = pl.BlockSpec((nodes, width // GROUPS), lambda t, place: (0, t))
-    dst = pl.BlockSpec(per_zh, lambda t, place: (t, 0, 0))
     return pl.pallas_call(
         pack_kernel,
         grid_spec=prefetched(
             GROUPS,
-            [feat] * 4 + [landed(), landed(), dst, landed()],
+            [feat] * 4 + [landed()] * 4,
             pl.BlockSpec((chunks, rows // GROUPS, columns), lambda t, place: (0, t, 0)),
             [],
         ),
@@ -490,7 +495,7 @@
             flops=4 * width * own.size, bytes_accessed=4 * width * width, transcendentals=0
         ),
         name="pack",
-    )(place, *feats, edge, kept_near(own), kept_near(far), dst_own, kept_near(dst_far))
+    )(place, *feats, edge, kept_near(own), kept_near(far), kept_near(dst_own), kept_near(dst_far))
 
 
 def join_kernel(parts_ref, total_ref):
@@ -572,12 +577,22 @@
     low = place[0] == 0
     edge = lax.ppermute(jnp.where(low, below, above), "c", swap)
     everyone, edge = lax.optimization_barrier((everyone, edge))
-    lead, dst_own, dst_far = middle(
-        place, everyone, pred, truth_t, area, var, wout_t, idx_t, sums, agg, grid_embed
+    lower, centre, upper, wide_own, wide_far, dst_own, dst_far = backward(
+        place,
+        everyone,
+        pred,
+        truth_t,
+        area,
+        var,
+        wout_t,
+        idx_t,
+        sums,
+        agg,
+        grid_embed,
+        gp,
+        3 * node_rows,
     )
     dst_far = lax.ppermute(dst_far, "c", swap)
-
-    lower, centre, upper, wide_own, wide_far = backward(place, gp, lead, idx_t, 3 * node_rows)
     wide_far = lax.ppermute(wide_far, "c", swap)
     from_above = shifted(lower, SPACE, -1)
     from_below = shifted(upper, SPACE, 1)

time: 130 us -> 127 us (0.977)
  Pallas kernels: 40.5 us -> 37.8 us
  starting transfers between devices: 46.5 us -> 48.1 us
  waiting for transfers between devices: 30.8 us -> 29.2 us
    pallas_call x1 -> x0, Pallas kernels: 5.62 us -> none  [middle(): pl.pallas_call(middle_kernel, grid_spec=prefetched(1, [landed()] + [whole...]
    pallas_call x1, Pallas kernels: 9.68 us -> 12.7 us  [backward(): pl.pallas_call(functools.partial(backward_kernel, slots), grid_spec=prefe...]
    all_to_all x1, waiting for transfers between devices: 21.7 us -> 20.4 us  [body(): parts = lax.all_to_all(total, FIRST, 0, 0, tiled=True)]
  transfers between devices with their start and end apart: 13 -> 13, of which waited for: 5 -> 5; matrix products, arithmetic and copies ran while one was open for 7% -> 7% of each run, Pallas kernels for 9% -> 2%
where the time goes in v12:
time: 127 us; the launch traced here: 126 us
  starting transfers between devices  48.1 us (38%)
  Pallas kernels  37.8 us (30%)
  waiting for transfers between devices  29.2 us (23%)
  matrix products  6.51 us (5%)
  other arithmetic  2.67 us (2%)
  local copies, waits for them, and re-layouts  1.41 us (1%)
    all_to_all x1, waiting for transfers between devices, body(): parts = lax.all_to_all(total, FIRST, 0, 0, tiled=True)  20.4 us
    pallas_call x1, Pallas kernels, forward(): pl.pallas_call(functools.partial(forward_kernel, slots, members), grid_sp...  19.4 us
    pallas_call x1, Pallas kernels, backward(): pl.pallas_call(functools.partial(backward_kernel, slots), grid_spec=prefe...  12.7 us
    ppermute x7, starting transfers between devices, shifted(): lax.ppermute(block, axes, [(i, (i + distance) % count) for i in range(cou...  10.2 us
    all_to_all x1, starting transfers between devices, body(): everyone = lax.all_to_all(sent, ENS, 0, 0, tiled=True)  9.06 us
    all_to_all x1, starting transfers between devices, body(): parts = lax.all_to_all(total, SECOND, 0, 0, tiled=True)  8.98 us
    ppermute x1, starting transfers between devices, body(): edge = lax.ppermute(jnp.where(low, below, above), 'c', swap)  7.9 us
    all_to_all x1, waiting for transfers between devices, body(): parts = lax.all_to_all(total, SECOND, 0, 0, tiled=True)  6.3 us
  transfers between devices with their start and end apart: 13, of which 5 were waited for; matrix products, arithmetic and copies ran while one was open for 7% of the time, Pallas kernels for 2%

profile of v12, /device:TPU:1, one launch (start us, length us, event | category | flops | bytes accessed | tf_op | source)
XLA Modules:
  0.0 126.5 jit_solution(625528376080481376)
XLA Ops:
  0.6 0.0 copy-start
  0.6 3.3 %collective-permute-start.1 = (bf16[64,1024]{1,0:T(8,128)(2,1)}, bf16[64,1024]{1,0:T(8,128)(2,1)S(1)}, u32[]{:S(2)}, u32[]{:S(2)}) collective-permute-start(bf16[64,1024]{1,0:T(8,128)(2,1)} %bitcast.36), channel_id=1, source_target_pairs={{0,31},{1,0},{2,1},{3,2},{4,3},{5,4},{6,5},{7,6},{8,7},{9,8},{10,9... | collective-permute-start | bytes 393224 | tf_op jit(solution)/shard_map/ppermute | solution.py:29
  4.0 3.5 %convolution_convert_fusion.dst_ref = bf16[512,1024]{1,0:T(8,128)(2,1)} fusion(bf16[512,1024]{1,0:T(8,128)(2,1)} %grid_hbm.1, bf16[1024,1024]{1,0:T(8,128)(2,1)S(1)} %copy-done), kind=kOutput, calls=%fused_computation | convolution fusion | flops 1074266112 | bytes 4194304 | tf_op jit(solution)/shard_map/dot_general | solution.py:562
  7.5 0.7 fusion.2.idxt_ref
  8.1 0.7 pad_add_fusion.place_ref
  8.8 1.0 collective-permute-done.below_ref
  9.8 0.0 copy-start.8
  9.8 19.4 %forward.1 = (bf16[8192,1024]{1,0:T(8,128)(2,1)}, bf16[512,1024]{1,0:T(8,128)(2,1)}, f32[32,512]{1,0:T(8,128)}, bf16[8,32,512]{2,1,0:T(8,128)(2,1)}, bf16[512,25...) custom-call(s32[4]{0:T(128)} %pad_add_fusion.place_ref, ...), custom_call_target="tpu_custom_call" | custom-call | flops 4294967296 | bytes 16777216 | tf_op jit(solution)/shard_map/forward/pallas_call | solution.py:207
  29.3 9.1 %all-to-all-start = ((bf16[8,32,512]{2,1,0:T(8,128)(2,1)}), bf16[8,32,512]{2,1,0:T(8,128)(2,1)S(1)}, u32[]{:S(2)}, u32[]{:S(2)}) async-start(bf16[8,32,512]{2,1,0:T(8,128)(2,1)} %get-tuple-element.32), calls=%async_computation | async-start | bytes 524288 | tf_op jit(solution)/shard_map/all_to_all | solution.py:576
  38.3 1.5 %collective-permute-start.3 = (bf16[512,256]{1,0:T(8,128)(2,1)}, bf16[512,256]{1,0:T(8,128)(2,1)S(1)}, u32[]{:S(2)}, u32[]{:S(2)}) collective-permute-start(bf16[512,256]{1,0:T(8,128)(2,1)} %get-tuple-element.36), channel_id=1, source_target_pairs={{0,32},{32,64},{64,96},{96,0},{1,33},{33,65},{65,97},{97,1},{2,34}... | collective-permute-start | bytes 786440 | tf_op jit(solution)/shard_map/ppermute | solution.py:29
  39.8 2.4 %collective-permute-start.4 = (bf16[512,256]{1,0:T(8,128)(2,1)}, bf16[512,256]{1,0:T(8,128)(2,1)S(1)}, u32[]{:S(2)}, u32[]{:S(2)}) collective-permute-start(bf16[512,256]{1,0:T(8,128)(2,1)} %get-tuple-element.37), channel_id=1, source_target_pairs={{0,64},{32,96},{64,0},{96,32},{1,65},{33,97},{65,1},{97,33},{2,66}... | collective-permute-start | bytes 786440 | tf_op jit(solution)/shard_map/ppermute | solution.py:29
  42.2 1.2 collective-permute-start.5
  43.4 7.9 %collective-permute-start.2 = (bf16[64,1024]{1,0:T(8,128)(2,1)S(1)}, bf16[64,1024]{1,0:T(8,128)(2,1)S(1)}, u32[]{:S(2)}, u32[]{:S(2)}) collective-permute-start(bf16[64,1024]{1,0:T(8,128)(2,1)S(1)} %broadcast_select_fusion), channel_id=1, source_target_pairs={{0,1},{1,0},{2,3},{3,2},{4,5},{5,4},{6,7},{7,6},{8,9},{9,8},{10,11... | collective-permute-start | bytes 393224 | tf_op jit(solution)/shard_map/ppermute | solution.py:578
  51.4 0.7 copy.14.var_ref
  52.0 0.3 collective-permute-done.2.edge_ref
  52.4 12.7 %backward.1 = (bf16[64,1024]{1,0:T(8,128)(2,1)}, bf16[64,1024]{1,0:T(8,128)(2,1)}, bf16[64,1024]{1,0:T(8,128)(2,1)}, bf16[192,512]{1,0:T(8,128)(2,1)S(1)}, bf16[...) custom-call(s32[4]{0:T(128)} %pad_add_fusion.place_ref, ...), custom_call_target="tpu_custom_call" | custom-call | flops 4294967296 | bytes 16777216 | tf_op jit(solution)/shard_map/backward/pallas_call | solution.py:423
  65.1 5.5 %collective-permute-start.7 = (bf16[8,144,128]{2,1,0:T(8,128)(2,1)S(1)}, bf16[8,144,128]{2,1,0:T(8,128)(2,1)S(1)}, u32[]{:S(2)}, u32[]{:S(2)}) collective-permute-start(bf16[8,144,128]{2,1,0:T(8,128)(2,1)S(1)} %get-tuple-element.46), channel_id=1, source_target_pairs={{0,1},{1,0},{2,3},{3,2},{4,5},{5,4},{6,7},{7,6},{8,9},{9,8},{10,11... | collective-permute-start | bytes 884744 | tf_op jit(solution)/shard_map/ppermute | solution.py:595
  70.6 0.3 collective-permute-start.6
  70.9 1.2 collective-permute-done.6.far_ref
  72.1 3.5 %pack.1 = bf16[16,64,656]{2,1,0:T(8,128)(2,1)} custom-call(s32[4]{0:T(128)} %pad_add_fusion.place_ref, bf16[64,1024]{1,0:T(8,128)(2,1)} %copy-done.2, bf16[64,1024]{1,0:T(8,128)(2,1)} %bitcast.39, bf16[64,1024]{1,0:T(8,128)(2,1)} %copy-done.1, bf16[64,1024]{1,0:T(8,128)(2,1)} %copy-done.4, bf16[192,512]{1,0:T(8,128)(2,1)S(1)} %get-tuple-element.43.own_ref, ...), custom_call_target="tpu_custom_call" | custom-call | flops 402653184 | bytes 4194304 | tf_op jit(solution)/shard_map/pack/pallas_call | solution.py:484
  75.6 6.2 %all-to-all-start.1 = ((bf16[16,64,656]{2,1,0:T(8,128)(2,1)}), bf16[16,64,656]{2,1,0:T(8,128)(2,1)}, u32[]{:S(2)}, u32[]{:S(2)}) async-start(bf16[16,64,656]{2,1,0:T(8,128)(2,1)} %pack.1), calls=%async_computation.1 | async-start | bytes 3145728 | tf_op jit(solution)/shard_map/all_to_all | solution.py:601
  81.8 0.7 collective-permute-start.8
  82.6 1.1 collective-permute-start.9
  83.7 20.4 %all-to-all-done.1.parts_ref = bf16[16,64,656]{2,1,0:T(8,128)(2,1)} async-done(((bf16[16,64,656]{2,1,0:T(8,128)(2,1)}), bf16[16,64,656]{2,1,0:T(8,128)(2,1)}, u32[]{:S(2)}, u32[]{:S(2)}) %all-to-all-start.1) | async-done | bytes 1343520 | tf_op jit(solution)/shard_map/all_to_all | solution.py:601
  104.0 2.1 %join.1 = bf16[16,4,1040]{2,1,0:T(4,128)(2,1)} custom-call(bf16[16,64,656]{2,1,0:T(8,128)(2,1)} %all-to-all-done.1.parts_ref), custom_call_target="tpu_custom_call" | custom-call | flops 671744 | bytes 1343488 | tf_op jit(solution)/shard_map/join/pallas_call | solution.py:524
  106.1 9.0 %all-to-all-start.2 = ((bf16[16,4,1040]{2,1,0:T(4,128)(2,1)}), bf16[16,4,1040]{2,1,0:T(4,128)(2,1)S(1)}, u32[]{:S(2)}, u32[]{:S(2)}) async-start(bf16[16,4,1040]{2,1,0:T(4,128)(2,1)} %join.1), calls=%async_computation.2 | async-start | bytes 294912 | tf_op jit(solution)/shard_map/all_to_all | solution.py:607
  115.1 3.0 %fusion = bf16[1,64,1024]{2,1,0:T(8,128)(2,1)} fusion(bf16[1024,1024]{1,0:T(8,128)(2,1)} %wsrc_ref.1, bf16[64,1024]{1,0:T(8,128)(2,1)S(1)} %collective-permute-done.9, bf16[64,1024]{1,0:T(8,128)(2,1)S(1)} %collective-permute-done.8, bf16[64,1024]{1,0:T(8,128)(2,1)S(1)} %copy-done.3), kind=kOutput, calls=%fused_computation.2 | convolution fusion | flops 134676480 | bytes 2621440 | tf_op jit(solution)/shard_map/dot_general | solution.py:609
  118.1 6.3 %all-to-all-done.2 = bf16[16,4,1040]{2,1,0:T(4,128)(2,1)S(1)} async-done(((bf16[16,4,1040]{2,1,0:T(4,128)(2,1)}), bf16[16,4,1040]{2,1,0:T(4,128)(2,1)S(1)}, u32[]{:S(2)}, u32[]{:S(2)}) %all-to-all-start.2) | async-done | bytes 133152 | tf_op jit(solution)/shard_map/all_to_all | solution.py:607
  124.5 0.1 convert_reduce_fusion
  124.6 0.6 reshape.20
  125.2 0.7 pad_maximum_fusion.1
  125.9 0.6 pad_maximum_fusion
  (35 shorter events, 0.1 us)
Async XLA Ops:
  0.6 3.3 %copy-start = (bf16[1024,1024]{1,0:T(8,128)(2,1)S(1)}, bf16[1024,1024]{1,0:T(8,128)(2,1)}, u32[]{:S(2)}) copy-start(bf16[1024,1024]{1,0:T(8,128)(2,1)} %param.13) | copy-start | bytes 6291460
  0.6 9.2 %collective-permute-start.1 = (bf16[64,1024]{1,0:T(8,128)(2,1)}, bf16[64,1024]{1,0:T(8,128)(2,1)S(1)}, u32[]{:S(2)}, u32[]{:S(2)}) collective-permute-start(bf16[64,1024]{1,0:T(8,128)(2,1)} %bitcast.36), channel_id=1, source_target_pairs={{0,31},{1,0},{2,1},{3,2},{4,3},{5,4},{6,5},{7,6},{8,7},{9,8},{10,9... | collective-permute-start | bytes 393224 | tf_op jit(solution)/shard_map/ppermute | solution.py:29
  4.0 5.8 %collective-permute-start = (bf16[64,1024]{1,0:T(8,128)(2,1)}, bf16[64,1024]{1,0:T(8,128)(2,1)S(1)}, u32[]{:S(2)}, u32[]{:S(2)}) collective-permute-start(bf16[64,1024]{1,0:T(8,128)(2,1)} %bitcast.37), channel_id=1, source_target_pairs={{0,1},{1,2},{2,3},{3,4},{4,5},{5,6},{6,7},{7,8},{8,9},{9,10},{10,1... | collective-permute-start | bytes 393224 | tf_op jit(solution)/shard_map/ppermute | solution.py:29
  4.0 3.5 %copy-start.5 = (s32[512,16]{0,1:T(8,128)S(1)}, s32[512,16]{0,1:T(8,128)}, u32[]{:S(2)}) copy-start(s32[512,16]{0,1:T(8,128)} %param.18) | copy-start | bytes 98308
  4.0 3.5 %copy-start.6 = (s32[512,16]{0,1:T(8,128)S(1)}, s32[512,16]{0,1:T(8,128)}, u32[]{:S(2)}) copy-start(s32[512,16]{0,1:T(8,128)} %param.19) | copy-start | bytes 98308
  9.8 33.6 %copy-start.2 = (bf16[64,1024]{1,0:T(8,128)(2,1)}, bf16[64,1024]{1,0:T(8,128)(2,1)S(1)}, u32[]{:S(2)}) copy-start(bf16[64,1024]{1,0:T(8,128)(2,1)S(1)} %collective-permute-done.below_ref) | copy-start | bytes 393220
  9.8 33.6 %copy-start.1 = (bf16[64,1024]{1,0:T(8,128)(2,1)}, bf16[64,1024]{1,0:T(8,128)(2,1)S(1)}, u32[]{:S(2)}) copy-start(bf16[64,1024]{1,0:T(8,128)(2,1)S(1)} %collective-permute-done.1.above_ref) | copy-start | bytes 393220
  9.8 33.6 %copy-start.7 = (s32[4]{0:T(128)S(1)}, s32[4]{0:T(128)}, u32[]{:S(2)}) copy-start(s32[4]{0:T(128)} %pad_add_fusion.place_ref) | copy-start | bytes 52
  9.8 41.5 %copy-start.8 = (f32[32]{0:T(128)S(1)}, f32[32]{0:T(128)}, u32[]{:S(2)}) copy-start(f32[32]{0:T(128)} %param.17) | copy-start | bytes 388
  29.3 23.1 %all-to-all-start = ((bf16[8,32,512]{2,1,0:T(8,128)(2,1)}), bf16[8,32,512]{2,1,0:T(8,128)(2,1)S(1)}, u32[]{:S(2)}, u32[]{:S(2)}) async-start(bf16[8,32,512]{2,1,0:T(8,128)(2,1)} %get-tuple-element.32), calls=%async_computation | async-start | bytes 524288 | tf_op jit(solution)/shard_map/all_to_all | solution.py:576
  38.3 14.0 %collective-permute-start.3 = (bf16[512,256]{1,0:T(8,128)(2,1)}, bf16[512,256]{1,0:T(8,128)(2,1)S(1)}, u32[]{:S(2)}, u32[]{:S(2)}) collective-permute-start(bf16[512,256]{1,0:T(8,128)(2,1)} %get-tuple-element.36), channel_id=1, source_target_pairs={{0,32},{32,64},{64,96},{96,0},{1,33},{33,65},{65,97},{97,1},{2,34}... | collective-permute-start | bytes 786440 | tf_op jit(solution)/shard_map/ppermute | solution.py:29
  39.8 12.6 %collective-permute-start.4 = (bf16[512,256]{1,0:T(8,128)(2,1)}, bf16[512,256]{1,0:T(8,128)(2,1)S(1)}, u32[]{:S(2)}, u32[]{:S(2)}) collective-permute-start(bf16[512,256]{1,0:T(8,128)(2,1)} %get-tuple-element.37), channel_id=1, source_target_pairs={{0,64},{32,96},{64,0},{96,32},{1,65},{33,97},{65,1},{97,33},{2,66}... | collective-permute-start | bytes 786440 | tf_op jit(solution)/shard_map/ppermute | solution.py:29
  42.2 10.2 %collective-permute-start.5 = (bf16[512,256]{1,0:T(8,128)(2,1)}, bf16[512,256]{1,0:T(8,128)(2,1)S(1)}, u32[]{:S(2)}, u32[]{:S(2)}) collective-permute-start(bf16[512,256]{1,0:T(8,128)(2,1)} %get-tuple-element.38), channel_id=1, source_target_pairs={{0,96},{32,0},{64,32},{96,64},{1,97},{33,1},{65,33},{97,65},{2,98}... | collective-permute-start | bytes 786440 | tf_op jit(solution)/shard_map/ppermute | solution.py:29
  43.4 8.9 %collective-permute-start.2 = (bf16[64,1024]{1,0:T(8,128)(2,1)S(1)}, bf16[64,1024]{1,0:T(8,128)(2,1)S(1)}, u32[]{:S(2)}, u32[]{:S(2)}) collective-permute-start(bf16[64,1024]{1,0:T(8,128)(2,1)S(1)} %broadcast_select_fusion), channel_id=1, source_target_pairs={{0,1},{1,0},{2,3},{3,2},{4,5},{5,4},{6,7},{7,6},{8,9},{9,8},{10,11... | collective-permute-start | bytes 393224 | tf_op jit(solution)/shard_map/ppermute | solution.py:578
  52.3 12.8 %copy-start.4 = (bf16[64,1024]{1,0:T(8,128)(2,1)}, bf16[64,1024]{1,0:T(8,128)(2,1)S(1)}, u32[]{:S(2)}) copy-start(bf16[64,1024]{1,0:T(8,128)(2,1)S(1)} %collective-permute-done.2.edge_ref) | copy-start | bytes 393220
  65.1 7.0 %collective-permute-start.7 = (bf16[8,144,128]{2,1,0:T(8,128)(2,1)S(1)}, bf16[8,144,128]{2,1,0:T(8,128)(2,1)S(1)}, u32[]{:S(2)}, u32[]{:S(2)}) collective-permute-start(bf16[8,144,128]{2,1,0:T(8,128)(2,1)S(1)} %get-tuple-element.46), channel_id=1, source_target_pairs={{0,1},{1,0},{2,3},{3,2},{4,5},{5,4},{6,7},{7,6},{8,9},{9,8},{10,11... | collective-permute-start | bytes 884744 | tf_op jit(solution)/shard_map/ppermute | solution.py:595
  70.6 1.5 %collective-permute-start.6 = (bf16[192,512]{1,0:T(8,128)(2,1)S(1)}, bf16[192,512]{1,0:T(8,128)(2,1)S(1)}, u32[]{:S(2)}, u32[]{:S(2)}) collective-permute-start(bf16[192,512]{1,0:T(8,128)(2,1)S(1)} %get-tuple-element.44), channel_id=1, source_target_pairs={{0,1},{1,0},{2,3},{3,2},{4,5},{5,4},{6,7},{7,6},{8,9},{9,8},{10,11... | collective-permute-start | bytes 589832 | tf_op jit(solution)/shard_map/ppermute | solution.py:596
  75.6 6.2 %copy-start.10 = (bf16[64,1024]{1,0:T(8,128)(2,1)S(1)}, bf16[64,1024]{1,0:T(8,128)(2,1)}, u32[]{:S(2)}) copy-start(bf16[64,1024]{1,0:T(8,128)(2,1)} %get-tuple-element.47) | copy-start | bytes 393220
  75.6 6.9 %copy-start.9 = (bf16[64,1024]{1,0:T(8,128)(2,1)S(1)}, bf16[64,1024]{1,0:T(8,128)(2,1)}, u32[]{:S(2)}) copy-start(bf16[64,1024]{1,0:T(8,128)(2,1)} %get-tuple-element.48) | copy-start | bytes 393220
  75.6 39.5 %copy-start.3 = (bf16[64,1024]{1,0:T(8,128)(2,1)S(1)}, bf16[64,1024]{1,0:T(8,128)(2,1)}, u32[]{:S(2)}) copy-start(bf16[64,1024]{1,0:T(8,128)(2,1)} %get-tuple-element.41) | copy-start | bytes 393220
  75.6 28.4 %all-to-all-start.1 = ((bf16[16,64,656]{2,1,0:T(8,128)(2,1)}), bf16[16,64,656]{2,1,0:T(8,128)(2,1)}, u32[]{:S(2)}, u32[]{:S(2)}) async-start(bf16[16,64,656]{2,1,0:T(8,128)(2,1)} %pack.1), calls=%async_computation.1 | async-start | bytes 3145728 | tf_op jit(solution)/shard_map/all_to_all | solution.py:601
  81.8 24.3 %collective-permute-start.8 = (bf16[64,1024]{1,0:T(8,128)(2,1)S(1)}, bf16[64,1024]{1,0:T(8,128)(2,1)S(1)}, u32[]{:S(2)}, u32[]{:S(2)}) collective-permute-start(bf16[64,1024]{1,0:T(8,128)(2,1)S(1)} %copy-done.10), channel_id=1, source_target_pairs={{0,31},{1,0},{2,1},{3,2},{4,3},{5,4},{6,5},{7,6},{8,7},{9,8},{10,9... | collective-permute-start | bytes 393224 | tf_op jit(solution)/shard_map/ppermute | solution.py:29
  82.6 23.6 %collective-permute-start.9 = (bf16[64,1024]{1,0:T(8,128)(2,1)S(1)}, bf16[64,1024]{1,0:T(8,128)(2,1)S(1)}, u32[]{:S(2)}, u32[]{:S(2)}) collective-permute-start(bf16[64,1024]{1,0:T(8,128)(2,1)S(1)} %copy-done.9), channel_id=1, source_target_pairs={{0,1},{1,2},{2,3},{3,4},{4,5},{5,6},{6,7},{7,8},{8,9},{9,10},{10,1... | collective-permute-start | bytes 393224 | tf_op jit(solution)/shard_map/ppermute | solution.py:29
  106.1 18.3 %all-to-all-start.2 = ((bf16[16,4,1040]{2,1,0:T(4,128)(2,1)}), bf16[16,4,1040]{2,1,0:T(4,128)(2,1)S(1)}, u32[]{:S(2)}, u32[]{:S(2)}) async-start(bf16[16,4,1040]{2,1,0:T(4,128)(2,1)} %join.1), calls=%async_computation.2 | async-start | bytes 294912 | tf_op jit(solution)/shard_map/all_to_all | solution.py:607

commit v13 on v12

--- a/solution.py
+++ b/solution.py
@@ -177,7 +177,11 @@
                     acc_s = acc_s + some_s.astype(f32)
             scale = scale_all[pl.ds(pl.multiple_of(base + r, ROWS), ROWS), :]
             agg_ref[pl.ds(pl.multiple_of(base + r, ROWS), ROWS), cols] = (acc_g * scale).astype(bf16)
-            sums[n, r : r + ROWS, :] = (acc_s - (slots - 0.5 / scale)).astype(bf16)
+            part = (acc_s - (slots - 0.5 / scale)).astype(bf16)
+            few = NCOL // 2
+            for j in range(2):
+                half, x = divmod(2 * n + j, QUARTERS)
+                sums[x, r : r + ROWS, half * few : (half + 1) * few] = part[:, j * few : (j + 1) * few]
 
     for d, ref in enumerate(piece_refs):
         ref[...] = sums[(along + d) % QUARTERS]
@@ -208,7 +212,7 @@
         functools.partial(forward_kernel, slots, members),
         grid_spec=prefetched(
             grid_rows // TILE,
-            [landed(), whole(here), landed(), whole(w_src)]
+            [landed(), whole(here), landed(), landed()]
             + [pl.BlockSpec((TILE, width), step), whole(idx_t), whole(wout_t)],
             [pl.BlockSpec((TILE * slots, width), step)]
             + [whole(x) for x in out_shape[1:4]]
@@ -231,7 +235,7 @@
             transcendentals=grid_rows * slots * width,
         ),
         name="forward",
-    )(place, kept_near(below), here, kept_near(above), w_src, dst, idx_t, wout_t)
+    )(place, kept_near(below), here, kept_near(above), kept_near(w_src), dst, idx_t, wout_t)
 
 
 def middle_step(
@@ -282,7 +286,14 @@
         dagg = lax.dot_general(dpred, wout_ref[:, cols], first, preferred_element_type=f32)
         lead_ref[:, cols] = (dagg * scale).astype(bf16)
 
-    quarter = wout_ref[:, pl.ds(pl.multiple_of(x * columns, columns), columns)]
+    few = columns // 2
+    quarter = jnp.concatenate(
+        [
+            wout_ref[:, pl.ds(pl.multiple_of(x * few + at, few), few)]
+            for at in range(0, width, width // 2)
+        ],
+        axis=1,
+    )
     total = jnp.zeros(sum_refs[0].shape, f32)
     for d, sum_ref in enumerate(sum_refs):
         other = dpred_of(every_ref[zh * near + (x + near - d) % near].astype(f32))
@@ -331,7 +342,7 @@
     sum3_ref,
     agg_hbm,
     grid_hbm,
-    gp_ref,
+    gp_hbm,
     lower_ref,
     centre_ref,
     upper_ref,
@@ -348,12 +359,21 @@
     hot,
     prod,
     acc,
+    blocks,
+    arrived,
 ):
     step = pl.program_id(0)
     nodes, width = acc.shape
+    count, size, _ = blocks.shape
+
+    def block_copy(t):
+        rows = pl.ds(pl.multiple_of(t * size, size), size)
+        return pltpu.make_async_copy(gp_hbm.at[rows], blocks.at[t], arrived.at[t])
 
     @pl.when(step == 0)
     def _():
+        for t in range(count):
+            block_copy(t).start()
         middle_step(
             place_ref,
             every_ref,
@@ -377,7 +397,8 @@
         )
         acc[...] = jnp.zeros_like(acc)
 
-    wide = gp_ref.shape[0] // slots
+    block_copy(step).wait()
+    wide = size // slots
     base = pl.multiple_of(step * wide, wide)
     node = lax.broadcasted_iota(jnp.int32, (nodes, wide), 0)
     idx = idxt_ref[:, pl.ds(base, wide)]
@@ -388,7 +409,7 @@
         for k in range(slots):
             at = start * slots + k * TILE
             to = k * wide + start
-            prod[to : to + TILE, :] = gp_ref[at : at + TILE, :] * some
+            prod[to : to + TILE, :] = blocks[step, at : at + TILE, :] * some
     for n in range(width // NCOL):
         here = slice(n * NCOL, (n + 1) * NCOL)
         acc[:, here] += jnp.dot(hot[...], prod[:, here], preferred_element_type=f32)
@@ -427,8 +448,7 @@
             [landed()]
             + [whole(x) for x in small]
             + [landed()] * (len(sums) - 1)
-            + [anywhere] * 2
-            + [pl.BlockSpec((rows * slots, width), lambda t, place: (t, 0))],
+            + [anywhere] * 3,
             [whole(x) for x in out_shape[:3]] + [landed()] * 4,
             [
                 pltpu.VMEM((grid_rows, width), bf16),
@@ -440,6 +460,8 @@
                 pltpu.VMEM((nodes, rows * slots), bf16),
                 pltpu.VMEM((rows * slots, width), bf16),
                 pltpu.VMEM((nodes, width), f32),
+                pltpu.VMEM((grid_rows // rows, rows * slots, width), bf16),
+                pltpu.SemaphoreType.DMA((grid_rows // rows,)),
             ],
         ),
         out_shape=out_shape,
@@ -599,7 +621,6 @@
 
     total = pack(place, feats, edge, wide_own, wide_far, dst_own, dst_far, chunks)
     parts = lax.all_to_all(total, FIRST, 0, 0, tiled=True)
-    few = half // QUARTERS
     rows_out = width // lax.axis_size(ENS + SPACE)
 
     total = join(parts, rows_out, half)
@@ -611,12 +632,10 @@
     ).astype(bf16)
     total = jnp.sum(parts.reshape(-1, 2, rows_out, parts.shape[2]).astype(f32), axis=0)
     joined = lambda a, b: jnp.concatenate([total[0, :, a:b], total[1, :, a:b]], axis=1)
-    dst_final = total[:, :, half : 2 * half].reshape(2, rows_out, QUARTERS, few)
-    dst_final = dst_final.transpose(1, 2, 0, 3).reshape(rows_out, width)
     return (
         grad_mesh[None],
         joined(0, half),
-        dst_final,
+        joined(half, 2 * half),
         joined(2 * half, total.shape[-1]),
     )
 

time: 127 us -> 128 us (level)
    unnamed x22 -> x24, local copies, waits for them, and re-layouts: 0.05 us -> 1.73 us
where the time goes in v13:
time: 128 us; the launch traced here: 127 us
  starting transfers between devices  47.8 us (37%)
  Pallas kernels  37.5 us (29%)
  waiting for transfers between devices  29.4 us (23%)
  matrix products  6.5 us (5%)
  other arithmetic  2.55 us (2%)
  local copies, waits for them, and re-layouts  2.43 us (2%)
    all_to_all x1, waiting for transfers between devices, body(): parts = lax.all_to_all(total, FIRST, 0, 0, tiled=True)  20.5 us
    pallas_call x1, Pallas kernels, forward(): pl.pallas_call(functools.partial(forward_kernel, slots, members), grid_sp...  18.7 us
    pallas_call x1, Pallas kernels, backward(): pl.pallas_call(functools.partial(backward_kernel, slots), grid_spec=prefe...  13.1 us
    ppermute x7, starting transfers between devices, shifted(): lax.ppermute(block, axes, [(i, (i + distance) % count) for i in range(cou...  10.2 us
    all_to_all x1, starting transfers between devices, body(): everyone = lax.all_to_all(sent, ENS, 0, 0, tiled=True)  8.92 us
    all_to_all x1, starting transfers between devices, body(): parts = lax.all_to_all(total, SECOND, 0, 0, tiled=True)  8.84 us
    ppermute x1, starting transfers between devices, body(): edge = lax.ppermute(jnp.where(low, below, above), 'c', swap)  8.05 us
    all_to_all x1, waiting for transfers between devices, body(): parts = lax.all_to_all(total, SECOND, 0, 0, tiled=True)  6.3 us
  transfers between devices with their start and end apart: 13, of which 5 were waited for; matrix products, arithmetic and copies ran while one was open for 7% of the time, Pallas kernels for 2%

profile of v13, /device:TPU:1, one launch (start us, length us, event | category | flops | bytes accessed | tf_op | source)
XLA Modules:
  0.0 127.0 jit_solution(9718052307303122623)
XLA Ops:
  0.6 0.0 copy-start
  0.6 3.3 %collective-permute-start.1 = (bf16[64,1024]{1,0:T(8,128)(2,1)}, bf16[64,1024]{1,0:T(8,128)(2,1)S(1)}, u32[]{:S(2)}, u32[]{:S(2)}) collective-permute-start(bf16[64,1024]{1,0:T(8,128)(2,1)} %bitcast.37), channel_id=1, source_target_pairs={{0,31},{1,0},{2,1},{3,2},{4,3},{5,4},{6,5},{7,6},{8,7},{9,8},{10,9... | collective-permute-start | bytes 393224 | tf_op jit(solution)/shard_map/ppermute | solution.py:29
  4.0 0.0 collective-permute-start
  4.0 3.5 %convolution_convert_fusion.dst_ref = bf16[512,1024]{1,0:T(8,128)(2,1)} fusion(bf16[512,1024]{1,0:T(8,128)(2,1)} %grid_hbm.1, bf16[1024,1024]{1,0:T(8,128)(2,1)S(1)} %copy-done), kind=kOutput, calls=%fused_computation | convolution fusion | flops 1074266112 | bytes 4194304 | tf_op jit(solution)/shard_map/dot_general | solution.py:584
  7.5 0.6 fusion.2.idxt_ref
  8.1 0.6 pad_add_fusion.place_ref
  8.7 1.1 collective-permute-done.below_ref
  9.8 1.7 %copy-done.1 = bf16[1024,1024]{1,0:T(8,128)(2,1)S(1)} copy-done((bf16[1024,1024]{1,0:T(8,128)(2,1)S(1)}, bf16[1024,1024]{1,0:T(8,128)(2,1)}, u32[]{:S(2)}) %copy-start.1) | copy-done | bytes 2097176
  11.5 18.7 %forward.1 = (bf16[8192,1024]{1,0:T(8,128)(2,1)}, bf16[512,1024]{1,0:T(8,128)(2,1)}, f32[32,512]{1,0:T(8,128)}, bf16[8,32,512]{2,1,0:T(8,128)(2,1)}, bf16[512,25...) custom-call(s32[4]{0:T(128)} %pad_add_fusion.place_ref, ...), custom_call_target="tpu_custom_call" | custom-call | flops 4294967296 | bytes 16777216 | tf_op jit(solution)/shard_map/forward/pallas_call | solution.py:211
  30.2 8.9 %all-to-all-start = ((bf16[8,32,512]{2,1,0:T(8,128)(2,1)}), bf16[8,32,512]{2,1,0:T(8,128)(2,1)S(1)}, u32[]{:S(2)}, u32[]{:S(2)}) async-start(bf16[8,32,512]{2,1,0:T(8,128)(2,1)} %get-tuple-element.32), calls=%async_computation | async-start | bytes 524288 | tf_op jit(solution)/shard_map/all_to_all | solution.py:598
  39.1 1.5 %collective-permute-start.3 = (bf16[512,256]{1,0:T(8,128)(2,1)}, bf16[512,256]{1,0:T(8,128)(2,1)S(1)}, u32[]{:S(2)}, u32[]{:S(2)}) collective-permute-start(bf16[512,256]{1,0:T(8,128)(2,1)} %get-tuple-element.36), channel_id=1, source_target_pairs={{0,32},{32,64},{64,96},{96,0},{1,33},{33,65},{65,97},{97,1},{2,34}... | collective-permute-start | bytes 786440 | tf_op jit(solution)/shard_map/ppermute | solution.py:29
  40.6 2.4 %collective-permute-start.4 = (bf16[512,256]{1,0:T(8,128)(2,1)}, bf16[512,256]{1,0:T(8,128)(2,1)S(1)}, u32[]{:S(2)}, u32[]{:S(2)}) collective-permute-start(bf16[512,256]{1,0:T(8,128)(2,1)} %get-tuple-element.37), channel_id=1, source_target_pairs={{0,64},{32,96},{64,0},{96,32},{1,65},{33,97},{65,1},{97,33},{2,66}... | collective-permute-start | bytes 786440 | tf_op jit(solution)/shard_map/ppermute | solution.py:29
  43.0 1.2 collective-permute-start.5
  44.3 8.0 %collective-permute-start.2 = (bf16[64,1024]{1,0:T(8,128)(2,1)S(1)}, bf16[64,1024]{1,0:T(8,128)(2,1)S(1)}, u32[]{:S(2)}, u32[]{:S(2)}) collective-permute-start(bf16[64,1024]{1,0:T(8,128)(2,1)S(1)} %broadcast_select_fusion), channel_id=1, source_target_pairs={{0,1},{1,0},{2,3},{3,2},{4,5},{5,4},{6,7},{7,6},{8,9},{9,8},{10,11... | collective-permute-start | bytes 393224 | tf_op jit(solution)/shard_map/ppermute | solution.py:600
  52.3 0.7 copy.14.var_ref
  53.0 0.3 collective-permute-done.2.edge_ref
  53.3 13.1 %backward.1 = (bf16[64,1024]{1,0:T(8,128)(2,1)}, bf16[64,1024]{1,0:T(8,128)(2,1)}, bf16[64,1024]{1,0:T(8,128)(2,1)}, bf16[192,512]{1,0:T(8,128)(2,1)S(1)}, bf16[...) custom-call(s32[4]{0:T(128)} %pad_add_fusion.place_ref, ...), custom_call_target="tpu_custom_call" | custom-call | flops 4294967296 | bytes 16777216 | tf_op jit(solution)/shard_map/backward/pallas_call | solution.py:444
  66.5 5.5 %collective-permute-start.7 = (bf16[8,144,128]{2,1,0:T(8,128)(2,1)S(1)}, bf16[8,144,128]{2,1,0:T(8,128)(2,1)S(1)}, u32[]{:S(2)}, u32[]{:S(2)}) collective-permute-start(bf16[8,144,128]{2,1,0:T(8,128)(2,1)S(1)} %get-tuple-element.46), channel_id=1, source_target_pairs={{0,1},{1,0},{2,3},{3,2},{4,5},{5,4},{6,7},{7,6},{8,9},{9,8},{10,11... | collective-permute-start | bytes 884744 | tf_op jit(solution)/shard_map/ppermute | solution.py:617
  72.0 0.3 collective-permute-start.6
  72.2 1.2 collective-permute-done.6.far_ref
  73.4 3.5 %pack.1 = bf16[16,64,656]{2,1,0:T(8,128)(2,1)} custom-call(s32[4]{0:T(128)} %pad_add_fusion.place_ref, bf16[64,1024]{1,0:T(8,128)(2,1)} %copy-done.3, bf16[64,1024]{1,0:T(8,128)(2,1)} %bitcast.40, bf16[64,1024]{1,0:T(8,128)(2,1)} %copy-done.2, bf16[64,1024]{1,0:T(8,128)(2,1)} %copy-done.5, bf16[192,512]{1,0:T(8,128)(2,1)S(1)} %get-tuple-element.43.own_ref, ...), custom_call_target="tpu_custom_call" | custom-call | flops 402653184 | bytes 4194304 | tf_op jit(solution)/shard_map/pack/pallas_call | solution.py:506
  77.0 6.0 %all-to-all-start.1 = ((bf16[16,64,656]{2,1,0:T(8,128)(2,1)}), bf16[16,64,656]{2,1,0:T(8,128)(2,1)}, u32[]{:S(2)}, u32[]{:S(2)}) async-start(bf16[16,64,656]{2,1,0:T(8,128)(2,1)} %pack.1), calls=%async_computation.1 | async-start | bytes 3145728 | tf_op jit(solution)/shard_map/all_to_all | solution.py:623
  83.1 0.7 collective-permute-start.8
  83.8 1.1 collective-permute-start.9
  84.9 20.5 %all-to-all-done.1.parts_ref = bf16[16,64,656]{2,1,0:T(8,128)(2,1)} async-done(((bf16[16,64,656]{2,1,0:T(8,128)(2,1)}), bf16[16,64,656]{2,1,0:T(8,128)(2,1)}, u32[]{:S(2)}, u32[]{:S(2)}) %all-to-all-start.1) | async-done | bytes 1343520 | tf_op jit(solution)/shard_map/all_to_all | solution.py:623
  105.3 2.1 %join.1 = bf16[16,4,1040]{2,1,0:T(4,128)(2,1)} custom-call(bf16[16,64,656]{2,1,0:T(8,128)(2,1)} %all-to-all-done.1.parts_ref), custom_call_target="tpu_custom_call" | custom-call | flops 671744 | bytes 1343488 | tf_op jit(solution)/shard_map/join/pallas_call | solution.py:546
  107.4 8.8 %all-to-all-start.2 = ((bf16[16,4,1040]{2,1,0:T(4,128)(2,1)}), bf16[16,4,1040]{2,1,0:T(4,128)(2,1)S(1)}, u32[]{:S(2)}, u32[]{:S(2)}) async-start(bf16[16,4,1040]{2,1,0:T(4,128)(2,1)} %join.1), calls=%async_computation.2 | async-start | bytes 294912 | tf_op jit(solution)/shard_map/all_to_all | solution.py:628
  116.3 3.0 %fusion = bf16[1,64,1024]{2,1,0:T(8,128)(2,1)} fusion(bf16[1024,1024]{1,0:T(8,128)(2,1)} %wsrc_ref.1, bf16[64,1024]{1,0:T(8,128)(2,1)S(1)} %collective-permute-done.9, bf16[64,1024]{1,0:T(8,128)(2,1)S(1)} %collective-permute-done.8, bf16[64,1024]{1,0:T(8,128)(2,1)S(1)} %copy-done.4), kind=kOutput, calls=%fused_computation.2 | convolution fusion | flops 134676480 | bytes 2621440 | tf_op jit(solution)/shard_map/dot_general | solution.py:630
  119.3 6.3 %all-to-all-done.2 = bf16[16,4,1040]{2,1,0:T(4,128)(2,1)S(1)} async-done(((bf16[16,4,1040]{2,1,0:T(4,128)(2,1)}), bf16[16,4,1040]{2,1,0:T(4,128)(2,1)S(1)}, u32[]{:S(2)}, u32[]{:S(2)}) %all-to-all-start.2) | async-done | bytes 133152 | tf_op jit(solution)/shard_map/all_to_all | solution.py:628
  125.6 0.1 convert_reduce_fusion
  125.7 0.7 pad_maximum_fusion.2
  126.4 0.6 pad_maximum_fusion
  (33 shorter events, 0.1 us)
Async XLA Ops:
  0.6 3.3 %copy-start = (bf16[1024,1024]{1,0:T(8,128)(2,1)S(1)}, bf16[1024,1024]{1,0:T(8,128)(2,1)}, u32[]{:S(2)}) copy-start(bf16[1024,1024]{1,0:T(8,128)(2,1)} %param.13) | copy-start | bytes 6291460
  0.6 9.2 %collective-permute-start.1 = (bf16[64,1024]{1,0:T(8,128)(2,1)}, bf16[64,1024]{1,0:T(8,128)(2,1)S(1)}, u32[]{:S(2)}, u32[]{:S(2)}) collective-permute-start(bf16[64,1024]{1,0:T(8,128)(2,1)} %bitcast.37), channel_id=1, source_target_pairs={{0,31},{1,0},{2,1},{3,2},{4,3},{5,4},{6,5},{7,6},{8,7},{9,8},{10,9... | collective-permute-start | bytes 393224 | tf_op jit(solution)/shard_map/ppermute | solution.py:29
  4.0 5.8 %collective-permute-start = (bf16[64,1024]{1,0:T(8,128)(2,1)}, bf16[64,1024]{1,0:T(8,128)(2,1)S(1)}, u32[]{:S(2)}, u32[]{:S(2)}) collective-permute-start(bf16[64,1024]{1,0:T(8,128)(2,1)} %bitcast.38), channel_id=1, source_target_pairs={{0,1},{1,2},{2,3},{3,4},{4,5},{5,6},{6,7},{7,8},{8,9},{9,10},{10,1... | collective-permute-start | bytes 393224 | tf_op jit(solution)/shard_map/ppermute | solution.py:29
  4.0 3.5 %copy-start.6 = (s32[512,16]{0,1:T(8,128)S(1)}, s32[512,16]{0,1:T(8,128)}, u32[]{:S(2)}) copy-start(s32[512,16]{0,1:T(8,128)} %param.18) | copy-start | bytes 98308
  4.0 3.5 %copy-start.7 = (s32[512,16]{0,1:T(8,128)S(1)}, s32[512,16]{0,1:T(8,128)}, u32[]{:S(2)}) copy-start(s32[512,16]{0,1:T(8,128)} %param.19) | copy-start | bytes 98308
  9.8 34.4 %copy-start.3 = (bf16[64,1024]{1,0:T(8,128)(2,1)}, bf16[64,1024]{1,0:T(8,128)(2,1)S(1)}, u32[]{:S(2)}) copy-start(bf16[64,1024]{1,0:T(8,128)(2,1)S(1)} %collective-permute-done.below_ref) | copy-start | bytes 393220
  9.8 34.4 %copy-start.2 = (bf16[64,1024]{1,0:T(8,128)(2,1)}, bf16[64,1024]{1,0:T(8,128)(2,1)S(1)}, u32[]{:S(2)}) copy-start(bf16[64,1024]{1,0:T(8,128)(2,1)S(1)} %collective-permute-done.1.above_ref) | copy-start | bytes 393220
  9.8 1.7 %copy-start.1 = (bf16[1024,1024]{1,0:T(8,128)(2,1)S(1)}, bf16[1024,1024]{1,0:T(8,128)(2,1)}, u32[]{:S(2)}) copy-start(bf16[1024,1024]{1,0:T(8,128)(2,1)} %wsrc_ref.1) | copy-start | bytes 6291460
  11.5 32.7 %copy-start.8 = (s32[4]{0:T(128)S(1)}, s32[4]{0:T(128)}, u32[]{:S(2)}) copy-start(s32[4]{0:T(128)} %pad_add_fusion.place_ref) | copy-start | bytes 52
  11.5 40.8 %copy-start.9 = (f32[32]{0:T(128)S(1)}, f32[32]{0:T(128)}, u32[]{:S(2)}) copy-start(f32[32]{0:T(128)} %param.17) | copy-start | bytes 388
  30.2 23.1 %all-to-all-start = ((bf16[8,32,512]{2,1,0:T(8,128)(2,1)}), bf16[8,32,512]{2,1,0:T(8,128)(2,1)S(1)}, u32[]{:S(2)}, u32[]{:S(2)}) async-start(bf16[8,32,512]{2,1,0:T(8,128)(2,1)} %get-tuple-element.32), calls=%async_computation | async-start | bytes 524288 | tf_op jit(solution)/shard_map/all_to_all | solution.py:598
  39.1 14.2 %collective-permute-start.3 = (bf16[512,256]{1,0:T(8,128)(2,1)}, bf16[512,256]{1,0:T(8,128)(2,1)S(1)}, u32[]{:S(2)}, u32[]{:S(2)}) collective-permute-start(bf16[512,256]{1,0:T(8,128)(2,1)} %get-tuple-element.36), channel_id=1, source_target_pairs={{0,32},{32,64},{64,96},{96,0},{1,33},{33,65},{65,97},{97,1},{2,34}... | collective-permute-start | bytes 786440 | tf_op jit(solution)/shard_map/ppermute | solution.py:29
  40.6 12.7 %collective-permute-start.4 = (bf16[512,256]{1,0:T(8,128)(2,1)}, bf16[512,256]{1,0:T(8,128)(2,1)S(1)}, u32[]{:S(2)}, u32[]{:S(2)}) collective-permute-start(bf16[512,256]{1,0:T(8,128)(2,1)} %get-tuple-element.37), channel_id=1, source_target_pairs={{0,64},{32,96},{64,0},{96,32},{1,65},{33,97},{65,1},{97,33},{2,66}... | collective-permute-start | bytes 786440 | tf_op jit(solution)/shard_map/ppermute | solution.py:29
  43.0 10.3 %collective-permute-start.5 = (bf16[512,256]{1,0:T(8,128)(2,1)}, bf16[512,256]{1,0:T(8,128)(2,1)S(1)}, u32[]{:S(2)}, u32[]{:S(2)}) collective-permute-start(bf16[512,256]{1,0:T(8,128)(2,1)} %get-tuple-element.38), channel_id=1, source_target_pairs={{0,96},{32,0},{64,32},{96,64},{1,97},{33,1},{65,33},{97,65},{2,98}... | collective-permute-start | bytes 786440 | tf_op jit(solution)/shard_map/ppermute | solution.py:29
  44.3 9.0 %collective-permute-start.2 = (bf16[64,1024]{1,0:T(8,128)(2,1)S(1)}, bf16[64,1024]{1,0:T(8,128)(2,1)S(1)}, u32[]{:S(2)}, u32[]{:S(2)}) collective-permute-start(bf16[64,1024]{1,0:T(8,128)(2,1)S(1)} %broadcast_select_fusion), channel_id=1, source_target_pairs={{0,1},{1,0},{2,3},{3,2},{4,5},{5,4},{6,7},{7,6},{8,9},{9,8},{10,11... | collective-permute-start | bytes 393224 | tf_op jit(solution)/shard_map/ppermute | solution.py:600
  53.3 13.1 %copy-start.5 = (bf16[64,1024]{1,0:T(8,128)(2,1)}, bf16[64,1024]{1,0:T(8,128)(2,1)S(1)}, u32[]{:S(2)}) copy-start(bf16[64,1024]{1,0:T(8,128)(2,1)S(1)} %collective-permute-done.2.edge_ref) | copy-start | bytes 393220
  66.5 7.0 %collective-permute-start.7 = (bf16[8,144,128]{2,1,0:T(8,128)(2,1)S(1)}, bf16[8,144,128]{2,1,0:T(8,128)(2,1)S(1)}, u32[]{:S(2)}, u32[]{:S(2)}) collective-permute-start(bf16[8,144,128]{2,1,0:T(8,128)(2,1)S(1)} %get-tuple-element.46), channel_id=1, source_target_pairs={{0,1},{1,0},{2,3},{3,2},{4,5},{5,4},{6,7},{7,6},{8,9},{9,8},{10,11... | collective-permute-start | bytes 884744 | tf_op jit(solution)/shard_map/ppermute | solution.py:617
  72.0 1.5 %collective-permute-start.6 = (bf16[192,512]{1,0:T(8,128)(2,1)S(1)}, bf16[192,512]{1,0:T(8,128)(2,1)S(1)}, u32[]{:S(2)}, u32[]{:S(2)}) collective-permute-start(bf16[192,512]{1,0:T(8,128)(2,1)S(1)} %get-tuple-element.44), channel_id=1, source_target_pairs={{0,1},{1,0},{2,3},{3,2},{4,5},{5,4},{6,7},{7,6},{8,9},{9,8},{10,11... | collective-permute-start | bytes 589832 | tf_op jit(solution)/shard_map/ppermute | solution.py:618
  77.0 6.1 %copy-start.11 = (bf16[64,1024]{1,0:T(8,128)(2,1)S(1)}, bf16[64,1024]{1,0:T(8,128)(2,1)}, u32[]{:S(2)}) copy-start(bf16[64,1024]{1,0:T(8,128)(2,1)} %get-tuple-element.47) | copy-start | bytes 393220
  77.0 6.8 %copy-start.10 = (bf16[64,1024]{1,0:T(8,128)(2,1)S(1)}, bf16[64,1024]{1,0:T(8,128)(2,1)}, u32[]{:S(2)}) copy-start(bf16[64,1024]{1,0:T(8,128)(2,1)} %get-tuple-element.48) | copy-start | bytes 393220
  77.0 39.3 %copy-start.4 = (bf16[64,1024]{1,0:T(8,128)(2,1)S(1)}, bf16[64,1024]{1,0:T(8,128)(2,1)}, u32[]{:S(2)}) copy-start(bf16[64,1024]{1,0:T(8,128)(2,1)} %get-tuple-element.41) | copy-start | bytes 393220
  77.0 28.3 %all-to-all-start.1 = ((bf16[16,64,656]{2,1,0:T(8,128)(2,1)}), bf16[16,64,656]{2,1,0:T(8,128)(2,1)}, u32[]{:S(2)}, u32[]{:S(2)}) async-start(bf16[16,64,656]{2,1,0:T(8,128)(2,1)} %pack.1), calls=%async_computation.1 | async-start | bytes 3145728 | tf_op jit(solution)/shard_map/all_to_all | solution.py:623
  83.1 24.4 %collective-permute-start.8 = (bf16[64,1024]{1,0:T(8,128)(2,1)S(1)}, bf16[64,1024]{1,0:T(8,128)(2,1)S(1)}, u32[]{:S(2)}, u32[]{:S(2)}) collective-permute-start(bf16[64,1024]{1,0:T(8,128)(2,1)S(1)} %copy-done.11), channel_id=1, source_target_pairs={{0,31},{1,0},{2,1},{3,2},{4,3},{5,4},{6,5},{7,6},{8,7},{9,8},{10,9... | collective-permute-start | bytes 393224 | tf_op jit(solution)/shard_map/ppermute | solution.py:29
  83.8 23.7 %collective-permute-start.9 = (bf16[64,1024]{1,0:T(8,128)(2,1)S(1)}, bf16[64,1024]{1,0:T(8,128)(2,1)S(1)}, u32[]{:S(2)}, u32[]{:S(2)}) collective-permute-start(bf16[64,1024]{1,0:T(8,128)(2,1)S(1)} %copy-done.10), channel_id=1, source_target_pairs={{0,1},{1,2},{2,3},{3,4},{4,5},{5,6},{6,7},{7,8},{8,9},{9,10},{10,1... | collective-permute-start | bytes 393224 | tf_op jit(solution)/shard_map/ppermute | solution.py:29
  107.4 18.2 %all-to-all-start.2 = ((bf16[16,4,1040]{2,1,0:T(4,128)(2,1)}), bf16[16,4,1040]{2,1,0:T(4,128)(2,1)S(1)}, u32[]{:S(2)}, u32[]{:S(2)}) async-start(bf16[16,4,1040]{2,1,0:T(4,128)(2,1)} %join.1), calls=%async_computation.2 | async-start | bytes 294912 | tf_op jit(solution)/shard_map/all_to_all | solution.py:628

commit v14 on v13

--- a/solution.py
+++ b/solution.py
@@ -129,6 +129,8 @@
     idx_all,
     scale_all,
     sums,
+    wsrc,
+    sems,
 ):
     step = pl.program_id(0)
     nodes, width = feats.shape
@@ -138,14 +140,21 @@
 
     @pl.when(step == 0)
     def _():
+        parts = [slice(n * NCOL, (n + 1) * NCOL) for n in range(width // NCOL)]
+        copies = [
+            pltpu.make_async_copy(wsrc_ref.at[:, cols], wsrc.at[:, cols], sems.at[n])
+            for n, cols in enumerate(parts)
+        ]
+        for copy in copies:
+            copy.start()
         idx_all[...] = idxt_ref[...].astype(f32).T.astype(jnp.int32)
         scale_all[...] = scale_column(idxt_ref)
         for i, ref in enumerate(feat_refs):
             feats[i * block : (i + 1) * block, :] = ref[...]
-        for n in range(width // NCOL):
-            cols = slice(n * NCOL, (n + 1) * NCOL)
+        for copy, cols in zip(copies, parts):
+            copy.wait()
             rhs[:nodes, cols] = jnp.dot(
-                feats[...], wsrc_ref[:, cols], preferred_element_type=f32
+                feats[...], wsrc[:, cols], preferred_element_type=f32
             ).astype(bf16)
 
     base = pl.multiple_of(step * tile, tile)
@@ -212,7 +221,7 @@
         functools.partial(forward_kernel, slots, members),
         grid_spec=prefetched(
             grid_rows // TILE,
-            [landed(), whole(here), landed(), landed()]
+            [landed(), whole(here), landed(), pl.BlockSpec(memory_space=pl.ANY)]
             + [pl.BlockSpec((TILE, width), step), whole(idx_t), whole(wout_t)],
             [pl.BlockSpec((TILE * slots, width), step)]
             + [whole(x) for x in out_shape[1:4]]
@@ -225,6 +234,8 @@
                 pltpu.VMEM((grid_rows, slots), jnp.int32),
                 pltpu.VMEM((grid_rows, 1), f32),
                 pltpu.VMEM((QUARTERS, TILE, NCOL), bf16),
+                pltpu.VMEM(w_src.shape, bf16),
+                pltpu.SemaphoreType.DMA((width // NCOL,)),
             ],
         ),
         out_shape=out_shape,
@@ -235,10 +246,11 @@
             transcendentals=grid_rows * slots * width,
         ),
         name="forward",
-    )(place, kept_near(below), here, kept_near(above), kept_near(w_src), dst, idx_t, wout_t)
+    )(place, kept_near(below), here, kept_near(above), w_src, dst, idx_t, wout_t)
 
 
 def middle_step(
+    later,
     place_ref,
     every_ref,
     pred_ref,
@@ -263,7 +275,7 @@
         pltpu.make_async_copy(agg_hbm, agg_ref, sems.at[0]),
         pltpu.make_async_copy(grid_hbm, grid_ref, sems.at[1]),
     ]
-    for copy in loads:
+    for copy in loads + later:
         copy.start()
     width = wout_ref.shape[1]
     members = every_ref.shape[0]
@@ -372,9 +384,8 @@
 
     @pl.when(step == 0)
     def _():
-        for t in range(count):
-            block_copy(t).start()
         middle_step(
+            [block_copy(t) for t in range(count)],
             place_ref,
             every_ref,
             pred_ref,

time: 128 us -> 126 us (0.984)
  local copies, waits for them, and re-layouts: 2.43 us -> 0.75 us
    pallas_call x1, Pallas kernels: 13.1 us -> 10.7 us  [backward(): pl.pallas_call(functools.partial(backward_kernel, slots), grid_spec=prefe...]
    pallas_call x1, Pallas kernels: 18.7 us -> 20.7 us  [forward(): pl.pallas_call(functools.partial(forward_kernel, slots, members), grid_sp...]
    unnamed x24 -> x22, local copies, waits for them, and re-layouts: 1.73 us -> 0.05 us
where the time goes in v14:
time: 126 us; the launch traced here: 125 us
  starting transfers between devices  47.9 us (38%)
  Pallas kernels  37.1 us (29%)
  waiting for transfers between devices  29.5 us (23%)
  matrix products  6.5 us (5%)
  other arithmetic  2.66 us (2%)
    pallas_call x1, Pallas kernels, forward(): pl.pallas_call(functools.partial(forward_kernel, slots, members), grid_sp...  20.7 us
    all_to_all x1, waiting for transfers between devices, body(): parts = lax.all_to_all(total, FIRST, 0, 0, tiled=True)  20.5 us
    pallas_call x1, Pallas kernels, backward(): pl.pallas_call(functools.partial(backward_kernel, slots), grid_spec=prefe...  10.7 us
    ppermute x7, starting transfers between devices, shifted(): lax.ppermute(block, axes, [(i, (i + distance) % count) for i in range(cou...  10.2 us
    all_to_all x1, starting transfers between devices, body(): everyone = lax.all_to_all(sent, ENS, 0, 0, tiled=True)  8.99 us
    all_to_all x1, starting transfers between devices, body(): parts = lax.all_to_all(total, SECOND, 0, 0, tiled=True)  8.84 us
    ppermute x1, starting transfers between devices, body(): edge = lax.ppermute(jnp.where(low, below, above), 'c', swap)  7.94 us
    all_to_all x1, waiting for transfers between devices, body(): parts = lax.all_to_all(total, SECOND, 0, 0, tiled=True)  6.3 us
  transfers between devices with their start and end apart: 13, of which 5 were waited for; matrix products, arithmetic and copies ran while one was open for 7% of the time, Pallas kernels for 2%

profile of v14, /device:TPU:1, one launch (start us, length us, event | category | flops | bytes accessed | tf_op | source)
XLA Modules:
  0.0 125.1 jit_solution(817539887826535169)
XLA Ops:
  0.6 0.0 copy-start
  0.6 3.3 %collective-permute-start.1 = (bf16[64,1024]{1,0:T(8,128)(2,1)}, bf16[64,1024]{1,0:T(8,128)(2,1)S(1)}, u32[]{:S(2)}, u32[]{:S(2)}) collective-permute-start(bf16[64,1024]{1,0:T(8,128)(2,1)} %bitcast.37), channel_id=1, source_target_pairs={{0,31},{1,0},{2,1},{3,2},{4,3},{5,4},{6,5},{7,6},{8,7},{9,8},{10,9... | collective-permute-start | bytes 393224 | tf_op jit(solution)/shard_map/ppermute | solution.py:29
  4.0 3.5 %convolution_convert_fusion.dst_ref = bf16[512,1024]{1,0:T(8,128)(2,1)} fusion(bf16[512,1024]{1,0:T(8,128)(2,1)} %grid_hbm.1, bf16[1024,1024]{1,0:T(8,128)(2,1)S(1)} %copy-done), kind=kOutput, calls=%fused_computation | convolution fusion | flops 1074266112 | bytes 4194304 | tf_op jit(solution)/shard_map/dot_general | solution.py:595
  7.5 0.6 fusion.2.idxt_ref
  8.1 0.7 pad_add_fusion.place_ref
  8.8 1.0 collective-permute-done.below_ref
  9.8 0.0 collective-permute-done.1.above_ref
  9.8 0.0 copy-start.8
  9.8 20.7 %forward.1 = (bf16[8192,1024]{1,0:T(8,128)(2,1)}, bf16[512,1024]{1,0:T(8,128)(2,1)}, f32[32,512]{1,0:T(8,128)}, bf16[8,32,512]{2,1,0:T(8,128)(2,1)}, bf16[512,25...) custom-call(s32[4]{0:T(128)} %pad_add_fusion.place_ref, ...), custom_call_target="tpu_custom_call" | custom-call | flops 4294967296 | bytes 16777216 | tf_op jit(solution)/shard_map/forward/pallas_call | solution.py:220
  30.5 9.0 %all-to-all-start = ((bf16[8,32,512]{2,1,0:T(8,128)(2,1)}), bf16[8,32,512]{2,1,0:T(8,128)(2,1)S(1)}, u32[]{:S(2)}, u32[]{:S(2)}) async-start(bf16[8,32,512]{2,1,0:T(8,128)(2,1)} %get-tuple-element.32), calls=%async_computation | async-start | bytes 524288 | tf_op jit(solution)/shard_map/all_to_all | solution.py:609
  39.5 1.5 %collective-permute-start.3 = (bf16[512,256]{1,0:T(8,128)(2,1)}, bf16[512,256]{1,0:T(8,128)(2,1)S(1)}, u32[]{:S(2)}, u32[]{:S(2)}) collective-permute-start(bf16[512,256]{1,0:T(8,128)(2,1)} %get-tuple-element.36), channel_id=1, source_target_pairs={{0,32},{32,64},{64,96},{96,0},{1,33},{33,65},{65,97},{97,1},{2,34}... | collective-permute-start | bytes 786440 | tf_op jit(solution)/shard_map/ppermute | solution.py:29
  41.0 2.4 %collective-permute-start.4 = (bf16[512,256]{1,0:T(8,128)(2,1)}, bf16[512,256]{1,0:T(8,128)(2,1)S(1)}, u32[]{:S(2)}, u32[]{:S(2)}) collective-permute-start(bf16[512,256]{1,0:T(8,128)(2,1)} %get-tuple-element.37), channel_id=1, source_target_pairs={{0,64},{32,96},{64,0},{96,32},{1,65},{33,97},{65,1},{97,33},{2,66}... | collective-permute-start | bytes 786440 | tf_op jit(solution)/shard_map/ppermute | solution.py:29
  43.4 1.2 collective-permute-start.5
  44.7 7.9 %collective-permute-start.2 = (bf16[64,1024]{1,0:T(8,128)(2,1)S(1)}, bf16[64,1024]{1,0:T(8,128)(2,1)S(1)}, u32[]{:S(2)}, u32[]{:S(2)}) collective-permute-start(bf16[64,1024]{1,0:T(8,128)(2,1)S(1)} %broadcast_select_fusion), channel_id=1, source_target_pairs={{0,1},{1,0},{2,3},{3,2},{4,5},{5,4},{6,7},{7,6},{8,9},{9,8},{10,11... | collective-permute-start | bytes 393224 | tf_op jit(solution)/shard_map/ppermute | solution.py:611
  52.6 0.7 copy.14.var_ref
  53.3 0.3 collective-permute-done.2.edge_ref
  53.6 10.7 %backward.1 = (bf16[64,1024]{1,0:T(8,128)(2,1)}, bf16[64,1024]{1,0:T(8,128)(2,1)}, bf16[64,1024]{1,0:T(8,128)(2,1)}, bf16[192,512]{1,0:T(8,128)(2,1)S(1)}, bf16[...) custom-call(s32[4]{0:T(128)} %pad_add_fusion.place_ref, ...), custom_call_target="tpu_custom_call" | custom-call | flops 4294967296 | bytes 16777216 | tf_op jit(solution)/shard_map/backward/pallas_call | solution.py:455
  64.3 5.7 %collective-permute-start.7 = (bf16[8,144,128]{2,1,0:T(8,128)(2,1)S(1)}, bf16[8,144,128]{2,1,0:T(8,128)(2,1)S(1)}, u32[]{:S(2)}, u32[]{:S(2)}) collective-permute-start(bf16[8,144,128]{2,1,0:T(8,128)(2,1)S(1)} %get-tuple-element.46), channel_id=1, source_target_pairs={{0,1},{1,0},{2,3},{3,2},{4,5},{5,4},{6,7},{7,6},{8,9},{9,8},{10,11... | collective-permute-start | bytes 884744 | tf_op jit(solution)/shard_map/ppermute | solution.py:628
  70.0 0.1 collective-permute-start.6
  70.1 1.4 %collective-permute-done.6.far_ref = bf16[192,512]{1,0:T(8,128)(2,1)S(1)} collective-permute-done((bf16[192,512]{1,0:T(8,128)(2,1)S(1)}, bf16[192,512]{1,0:T(8,128)(2,1)S(1)}, u32[]{:S(2)}, u32[]{:S(2)}) %collective-permute-start.6) | collective-permute-done | bytes 196640 | tf_op jit(solution)/shard_map/ppermute | solution.py:629
  71.5 3.5 %pack.1 = bf16[16,64,656]{2,1,0:T(8,128)(2,1)} custom-call(s32[4]{0:T(128)} %pad_add_fusion.place_ref, bf16[64,1024]{1,0:T(8,128)(2,1)} %copy-done.2, bf16[64,1024]{1,0:T(8,128)(2,1)} %bitcast.40, bf16[64,1024]{1,0:T(8,128)(2,1)} %copy-done.1, bf16[64,1024]{1,0:T(8,128)(2,1)} %copy-done.4, bf16[192,512]{1,0:T(8,128)(2,1)S(1)} %get-tuple-element.43.own_ref, ...), custom_call_target="tpu_custom_call" | custom-call | flops 402653184 | bytes 4194304 | tf_op jit(solution)/shard_map/pack/pallas_call | solution.py:517
  75.0 6.2 %all-to-all-start.1 = ((bf16[16,64,656]{2,1,0:T(8,128)(2,1)}), bf16[16,64,656]{2,1,0:T(8,128)(2,1)}, u32[]{:S(2)}, u32[]{:S(2)}) async-start(bf16[16,64,656]{2,1,0:T(8,128)(2,1)} %pack.1), calls=%async_computation.1 | async-start | bytes 3145728 | tf_op jit(solution)/shard_map/all_to_all | solution.py:634
  81.2 0.7 collective-permute-start.8
  81.9 1.1 collective-permute-start.9
  83.0 20.5 %all-to-all-done.1.parts_ref = bf16[16,64,656]{2,1,0:T(8,128)(2,1)} async-done(((bf16[16,64,656]{2,1,0:T(8,128)(2,1)}), bf16[16,64,656]{2,1,0:T(8,128)(2,1)}, u32[]{:S(2)}, u32[]{:S(2)}) %all-to-all-start.1) | async-done | bytes 1343520 | tf_op jit(solution)/shard_map/all_to_all | solution.py:634
  103.5 2.1 %join.1 = bf16[16,4,1040]{2,1,0:T(4,128)(2,1)} custom-call(bf16[16,64,656]{2,1,0:T(8,128)(2,1)} %all-to-all-done.1.parts_ref), custom_call_target="tpu_custom_call" | custom-call | flops 671744 | bytes 1343488 | tf_op jit(solution)/shard_map/join/pallas_call | solution.py:557
  105.6 8.8 %all-to-all-start.2 = ((bf16[16,4,1040]{2,1,0:T(4,128)(2,1)}), bf16[16,4,1040]{2,1,0:T(4,128)(2,1)S(1)}, u32[]{:S(2)}, u32[]{:S(2)}) async-start(bf16[16,4,1040]{2,1,0:T(4,128)(2,1)} %join.1), calls=%async_computation.2 | async-start | bytes 294912 | tf_op jit(solution)/shard_map/all_to_all | solution.py:639
  114.5 3.0 %fusion = bf16[1,64,1024]{2,1,0:T(8,128)(2,1)} fusion(bf16[1024,1024]{1,0:T(8,128)(2,1)} %wsrc_ref.1, bf16[64,1024]{1,0:T(8,128)(2,1)S(1)} %collective-permute-done.9, bf16[64,1024]{1,0:T(8,128)(2,1)S(1)} %collective-permute-done.8, bf16[64,1024]{1,0:T(8,128)(2,1)S(1)} %copy-done.3), kind=kOutput, calls=%fused_computation.2 | convolution fusion | flops 134676480 | bytes 2621440 | tf_op jit(solution)/shard_map/dot_general | solution.py:641
  117.5 6.3 %all-to-all-done.2 = bf16[16,4,1040]{2,1,0:T(4,128)(2,1)S(1)} async-done(((bf16[16,4,1040]{2,1,0:T(4,128)(2,1)}), bf16[16,4,1040]{2,1,0:T(4,128)(2,1)S(1)}, u32[]{:S(2)}, u32[]{:S(2)}) %all-to-all-start.2) | async-done | bytes 133152 | tf_op jit(solution)/shard_map/all_to_all | solution.py:639
  123.8 0.1 convert_reduce_fusion
  123.9 0.7 pad_maximum_fusion.2
  124.5 0.6 pad_maximum_fusion
  (31 shorter events, 0.1 us)
Async XLA Ops:
  0.6 3.3 %copy-start = (bf16[1024,1024]{1,0:T(8,128)(2,1)S(1)}, bf16[1024,1024]{1,0:T(8,128)(2,1)}, u32[]{:S(2)}) copy-start(bf16[1024,1024]{1,0:T(8,128)(2,1)} %param.13) | copy-start | bytes 6291460
  0.6 9.2 %collective-permute-start.1 = (bf16[64,1024]{1,0:T(8,128)(2,1)}, bf16[64,1024]{1,0:T(8,128)(2,1)S(1)}, u32[]{:S(2)}, u32[]{:S(2)}) collective-permute-start(bf16[64,1024]{1,0:T(8,128)(2,1)} %bitcast.37), channel_id=1, source_target_pairs={{0,31},{1,0},{2,1},{3,2},{4,3},{5,4},{6,5},{7,6},{8,7},{9,8},{10,9... | collective-permute-start | bytes 393224 | tf_op jit(solution)/shard_map/ppermute | solution.py:29
  4.0 5.8 %collective-permute-start = (bf16[64,1024]{1,0:T(8,128)(2,1)}, bf16[64,1024]{1,0:T(8,128)(2,1)S(1)}, u32[]{:S(2)}, u32[]{:S(2)}) collective-permute-start(bf16[64,1024]{1,0:T(8,128)(2,1)} %bitcast.38), channel_id=1, source_target_pairs={{0,1},{1,2},{2,3},{3,4},{4,5},{5,6},{6,7},{7,8},{8,9},{9,10},{10,1... | collective-permute-start | bytes 393224 | tf_op jit(solution)/shard_map/ppermute | solution.py:29
  4.0 3.5 %copy-start.5 = (s32[512,16]{0,1:T(8,128)S(1)}, s32[512,16]{0,1:T(8,128)}, u32[]{:S(2)}) copy-start(s32[512,16]{0,1:T(8,128)} %param.18) | copy-start | bytes 98308
  4.0 3.5 %copy-start.6 = (s32[512,16]{0,1:T(8,128)S(1)}, s32[512,16]{0,1:T(8,128)}, u32[]{:S(2)}) copy-start(s32[512,16]{0,1:T(8,128)} %param.19) | copy-start | bytes 98308
  9.8 34.8 %copy-start.2 = (bf16[64,1024]{1,0:T(8,128)(2,1)}, bf16[64,1024]{1,0:T(8,128)(2,1)S(1)}, u32[]{:S(2)}) copy-start(bf16[64,1024]{1,0:T(8,128)(2,1)S(1)} %collective-permute-done.below_ref) | copy-start | bytes 393220
  9.8 34.8 %copy-start.1 = (bf16[64,1024]{1,0:T(8,128)(2,1)}, bf16[64,1024]{1,0:T(8,128)(2,1)S(1)}, u32[]{:S(2)}) copy-start(bf16[64,1024]{1,0:T(8,128)(2,1)S(1)} %collective-permute-done.1.above_ref) | copy-start | bytes 393220
  9.8 34.8 %copy-start.7 = (s32[4]{0:T(128)S(1)}, s32[4]{0:T(128)}, u32[]{:S(2)}) copy-start(s32[4]{0:T(128)} %pad_add_fusion.place_ref) | copy-start | bytes 52
  9.8 42.8 %copy-start.8 = (f32[32]{0:T(128)S(1)}, f32[32]{0:T(128)}, u32[]{:S(2)}) copy-start(f32[32]{0:T(128)} %param.17) | copy-start | bytes 388
  30.5 23.1 %all-to-all-start = ((bf16[8,32,512]{2,1,0:T(8,128)(2,1)}), bf16[8,32,512]{2,1,0:T(8,128)(2,1)S(1)}, u32[]{:S(2)}, u32[]{:S(2)}) async-start(bf16[8,32,512]{2,1,0:T(8,128)(2,1)} %get-tuple-element.32), calls=%async_computation | async-start | bytes 524288 | tf_op jit(solution)/shard_map/all_to_all | solution.py:609
  39.5 14.1 %collective-permute-start.3 = (bf16[512,256]{1,0:T(8,128)(2,1)}, bf16[512,256]{1,0:T(8,128)(2,1)S(1)}, u32[]{:S(2)}, u32[]{:S(2)}) collective-permute-start(bf16[512,256]{1,0:T(8,128)(2,1)} %get-tuple-element.36), channel_id=1, source_target_pairs={{0,32},{32,64},{64,96},{96,0},{1,33},{33,65},{65,97},{97,1},{2,34}... | collective-permute-start | bytes 786440 | tf_op jit(solution)/shard_map/ppermute | solution.py:29
  41.0 12.6 %collective-permute-start.4 = (bf16[512,256]{1,0:T(8,128)(2,1)}, bf16[512,256]{1,0:T(8,128)(2,1)S(1)}, u32[]{:S(2)}, u32[]{:S(2)}) collective-permute-start(bf16[512,256]{1,0:T(8,128)(2,1)} %get-tuple-element.37), channel_id=1, source_target_pairs={{0,64},{32,96},{64,0},{96,32},{1,65},{33,97},{65,1},{97,33},{2,66}... | collective-permute-start | bytes 786440 | tf_op jit(solution)/shard_map/ppermute | solution.py:29
  43.4 10.2 %collective-permute-start.5 = (bf16[512,256]{1,0:T(8,128)(2,1)}, bf16[512,256]{1,0:T(8,128)(2,1)S(1)}, u32[]{:S(2)}, u32[]{:S(2)}) collective-permute-start(bf16[512,256]{1,0:T(8,128)(2,1)} %get-tuple-element.38), channel_id=1, source_target_pairs={{0,96},{32,0},{64,32},{96,64},{1,97},{33,1},{65,33},{97,65},{2,98}... | collective-permute-start | bytes 786440 | tf_op jit(solution)/shard_map/ppermute | solution.py:29
  44.7 8.9 %collective-permute-start.2 = (bf16[64,1024]{1,0:T(8,128)(2,1)S(1)}, bf16[64,1024]{1,0:T(8,128)(2,1)S(1)}, u32[]{:S(2)}, u32[]{:S(2)}) collective-permute-start(bf16[64,1024]{1,0:T(8,128)(2,1)S(1)} %broadcast_select_fusion), channel_id=1, source_target_pairs={{0,1},{1,0},{2,3},{3,2},{4,5},{5,4},{6,7},{7,6},{8,9},{9,8},{10,11... | collective-permute-start | bytes 393224 | tf_op jit(solution)/shard_map/ppermute | solution.py:611
  53.6 10.7 %copy-start.4 = (bf16[64,1024]{1,0:T(8,128)(2,1)}, bf16[64,1024]{1,0:T(8,128)(2,1)S(1)}, u32[]{:S(2)}) copy-start(bf16[64,1024]{1,0:T(8,128)(2,1)S(1)} %collective-permute-done.2.edge_ref) | copy-start | bytes 393220
  64.3 7.2 %collective-permute-start.7 = (bf16[8,144,128]{2,1,0:T(8,128)(2,1)S(1)}, bf16[8,144,128]{2,1,0:T(8,128)(2,1)S(1)}, u32[]{:S(2)}, u32[]{:S(2)}) collective-permute-start(bf16[8,144,128]{2,1,0:T(8,128)(2,1)S(1)} %get-tuple-element.46), channel_id=1, source_target_pairs={{0,1},{1,0},{2,3},{3,2},{4,5},{5,4},{6,7},{7,6},{8,9},{9,8},{10,11... | collective-permute-start | bytes 884744 | tf_op jit(solution)/shard_map/ppermute | solution.py:628
  70.0 1.5 %collective-permute-start.6 = (bf16[192,512]{1,0:T(8,128)(2,1)S(1)}, bf16[192,512]{1,0:T(8,128)(2,1)S(1)}, u32[]{:S(2)}, u32[]{:S(2)}) collective-permute-start(bf16[192,512]{1,0:T(8,128)(2,1)S(1)} %get-tuple-element.44), channel_id=1, source_target_pairs={{0,1},{1,0},{2,3},{3,2},{4,5},{5,4},{6,7},{7,6},{8,9},{9,8},{10,11... | collective-permute-start | bytes 589832 | tf_op jit(solution)/shard_map/ppermute | solution.py:629
  75.0 6.2 %copy-start.10 = (bf16[64,1024]{1,0:T(8,128)(2,1)S(1)}, bf16[64,1024]{1,0:T(8,128)(2,1)}, u32[]{:S(2)}) copy-start(bf16[64,1024]{1,0:T(8,128)(2,1)} %get-tuple-element.47) | copy-start | bytes 393220
  75.0 6.9 %copy-start.9 = (bf16[64,1024]{1,0:T(8,128)(2,1)S(1)}, bf16[64,1024]{1,0:T(8,128)(2,1)}, u32[]{:S(2)}) copy-start(bf16[64,1024]{1,0:T(8,128)(2,1)} %get-tuple-element.48) | copy-start | bytes 393220
  75.0 39.4 %copy-start.3 = (bf16[64,1024]{1,0:T(8,128)(2,1)S(1)}, bf16[64,1024]{1,0:T(8,128)(2,1)}, u32[]{:S(2)}) copy-start(bf16[64,1024]{1,0:T(8,128)(2,1)} %get-tuple-element.41) | copy-start | bytes 393220
  75.0 28.5 %all-to-all-start.1 = ((bf16[16,64,656]{2,1,0:T(8,128)(2,1)}), bf16[16,64,656]{2,1,0:T(8,128)(2,1)}, u32[]{:S(2)}, u32[]{:S(2)}) async-start(bf16[16,64,656]{2,1,0:T(8,128)(2,1)} %pack.1), calls=%async_computation.1 | async-start | bytes 3145728 | tf_op jit(solution)/shard_map/all_to_all | solution.py:634
  81.2 24.4 %collective-permute-start.8 = (bf16[64,1024]{1,0:T(8,128)(2,1)S(1)}, bf16[64,1024]{1,0:T(8,128)(2,1)S(1)}, u32[]{:S(2)}, u32[]{:S(2)}) collective-permute-start(bf16[64,1024]{1,0:T(8,128)(2,1)S(1)} %copy-done.10), channel_id=1, source_target_pairs={{0,31},{1,0},{2,1},{3,2},{4,3},{5,4},{6,5},{7,6},{8,7},{9,8},{10,9... | collective-permute-start | bytes 393224 | tf_op jit(solution)/shard_map/ppermute | solution.py:29
  81.9 23.7 %collective-permute-start.9 = (bf16[64,1024]{1,0:T(8,128)(2,1)S(1)}, bf16[64,1024]{1,0:T(8,128)(2,1)S(1)}, u32[]{:S(2)}, u32[]{:S(2)}) collective-permute-start(bf16[64,1024]{1,0:T(8,128)(2,1)S(1)} %copy-done.9), channel_id=1, source_target_pairs={{0,1},{1,2},{2,3},{3,4},{4,5},{5,6},{6,7},{7,8},{8,9},{9,10},{10,1... | collective-permute-start | bytes 393224 | tf_op jit(solution)/shard_map/ppermute | solution.py:29
  105.6 18.2 %all-to-all-start.2 = ((bf16[16,4,1040]{2,1,0:T(4,128)(2,1)}), bf16[16,4,1040]{2,1,0:T(4,128)(2,1)S(1)}, u32[]{:S(2)}, u32[]{:S(2)}) async-start(bf16[16,4,1040]{2,1,0:T(4,128)(2,1)} %join.1), calls=%async_computation.2 | async-start | bytes 294912 | tf_op jit(solution)/shard_map/all_to_all | solution.py:639

commit v15 on v13

--- a/solution.py
+++ b/solution.py
@@ -138,7 +138,7 @@
 
     @pl.when(step == 0)
     def _():
-        idx_all[...] = idxt_ref[...].astype(f32).T.astype(jnp.int32)
+        idx_all[...] = idxt_ref[...].astype(f32).T.astype(bf16)
         scale_all[...] = scale_column(idxt_ref)
         for i, ref in enumerate(feat_refs):
             feats[i * block : (i + 1) * block, :] = ref[...]
@@ -152,12 +152,13 @@
     rhs[nodes:, :] = dst_ref[...]
     lane = lax.broadcasted_iota(jnp.int32, (tile, depth), 1)
     row = lax.broadcasted_iota(jnp.int32, (tile, depth), 0)
-    eye = lane == row + nodes
+    eye = jnp.where(lane == row + nodes, 1.0, 0.0).astype(bf16)
+    lane = lane.astype(f32).astype(bf16)
     idx = idx_all[pl.ds(base, tile), :]
     for k in range(slots):
         col = idx[:, k : k + 1]
-        hit = (lane == col) | (eye & (col >= 0))
-        hot[k * tile : (k + 1) * tile, :] = jnp.where(hit, 1.0, 0.0).astype(bf16)
+        used = eye * jnp.where(col >= 0, 1.0, 0.0).astype(bf16)
+        hot[k * tile : (k + 1) * tile, :] = jnp.where(lane == col, jnp.ones_like(used), used)
     for n in range(width // NCOL):
         cols = slice(n * NCOL, (n + 1) * NCOL)
         pre[n % 2] = jnp.dot(hot[...], rhs[:, cols], preferred_element_type=f32).astype(bf16)
@@ -212,7 +213,7 @@
         functools.partial(forward_kernel, slots, members),
         grid_spec=prefetched(
             grid_rows // TILE,
-            [landed(), whole(here), landed(), landed()]
+            [landed(), whole(here), landed(), whole(w_src)]
             + [pl.BlockSpec((TILE, width), step), whole(idx_t), whole(wout_t)],
             [pl.BlockSpec((TILE * slots, width), step)]
             + [whole(x) for x in out_shape[1:4]]
@@ -222,7 +223,7 @@
                 pltpu.VMEM((nodes + TILE, width), bf16),
                 pltpu.VMEM((TILE * slots, nodes + TILE), bf16),
                 pltpu.VMEM((2, TILE * slots, NCOL), bf16),
-                pltpu.VMEM((grid_rows, slots), jnp.int32),
+                pltpu.VMEM((grid_rows, slots), bf16),
                 pltpu.VMEM((grid_rows, 1), f32),
                 pltpu.VMEM((QUARTERS, TILE, NCOL), bf16),
             ],
@@ -235,10 +236,11 @@
             transcendentals=grid_rows * slots * width,
         ),
         name="forward",
-    )(place, kept_near(below), here, kept_near(above), kept_near(w_src), dst, idx_t, wout_t)
+    )(place, kept_near(below), here, kept_near(above), w_src, dst, idx_t, wout_t)
 
 
 def middle_step(
+    later,
     place_ref,
     every_ref,
     pred_ref,
@@ -263,7 +265,7 @@
         pltpu.make_async_copy(agg_hbm, agg_ref, sems.at[0]),
         pltpu.make_async_copy(grid_hbm, grid_ref, sems.at[1]),
     ]
-    for copy in loads:
+    for copy in loads + later:
         copy.start()
     width = wout_ref.shape[1]
     members = every_ref.shape[0]
@@ -372,9 +374,8 @@
 
     @pl.when(step == 0)
     def _():
-        for t in range(count):
-            block_copy(t).start()
         middle_step(
+            [block_copy(t) for t in range(count)],
             place_ref,
             every_ref,
             pred_ref,

time: 128 us -> 124 us (0.969)
  Pallas kernels: 37.5 us -> 35.6 us
  local copies, waits for them, and re-layouts: 2.43 us -> 0.75 us
    pallas_call x1, Pallas kernels: 13.1 us -> 10.7 us  [backward(): pl.pallas_call(functools.partial(backward_kernel, slots), grid_spec=prefe...]
    unnamed x24 -> x22, local copies, waits for them, and re-layouts: 1.73 us -> 0.05 us
where the time goes in v15:
time: 124 us
  starting transfers between devices  47.9 us (39%)
  Pallas kernels  35.6 us (29%)
  waiting for transfers between devices  29.3 us (24%)
  matrix products  6.5 us (5%)
  other arithmetic  2.66 us (2%)
    all_to_all x1, waiting for transfers between devices, body(): parts = lax.all_to_all(total, FIRST, 0, 0, tiled=True)  20.5 us
    pallas_call x1, Pallas kernels, forward(): pl.pallas_call(functools.partial(forward_kernel, slots, members), grid_sp...  19.3 us
    pallas_call x1, Pallas kernels, backward(): pl.pallas_call(functools.partial(backward_kernel, slots), grid_spec=prefe...  10.7 us
    ppermute x7, starting transfers between devices, shifted(): lax.ppermute(block, axes, [(i, (i + distance) % count) for i in range(cou...  10.2 us
    all_to_all x1, starting transfers between devices, body(): everyone = lax.all_to_all(sent, ENS, 0, 0, tiled=True)  8.96 us
    all_to_all x1, starting transfers between devices, body(): parts = lax.all_to_all(total, SECOND, 0, 0, tiled=True)  8.85 us
    ppermute x1, starting transfers between devices, body(): edge = lax.ppermute(jnp.where(low, below, above), 'c', swap)  7.95 us
    all_to_all x1, waiting for transfers between devices, body(): parts = lax.all_to_all(total, SECOND, 0, 0, tiled=True)  6.3 us
  transfers between devices with their start and end apart: 13, of which 5 were waited for; matrix products, arithmetic and copies ran while one was open for 7% of the time, Pallas kernels for 2%

profile of v15, /device:TPU:1, one launch (start us, length us, event | category | flops | bytes accessed | tf_op | source)
XLA Modules:
  0.0 123.5 jit_solution(10860021085942515811)
XLA Ops:
  0.6 0.0 copy-start
  0.6 3.3 %collective-permute-start.1 = (bf16[64,1024]{1,0:T(8,128)(2,1)}, bf16[64,1024]{1,0:T(8,128)(2,1)S(1)}, u32[]{:S(2)}, u32[]{:S(2)}) collective-permute-start(bf16[64,1024]{1,0:T(8,128)(2,1)} %bitcast.37), channel_id=1, source_target_pairs={{0,31},{1,0},{2,1},{3,2},{4,3},{5,4},{6,5},{7,6},{8,7},{9,8},{10,9... | collective-permute-start | bytes 393224 | tf_op jit(solution)/shard_map/ppermute | solution.py:29
  4.0 3.5 %convolution_convert_fusion.dst_ref = bf16[512,1024]{1,0:T(8,128)(2,1)} fusion(bf16[512,1024]{1,0:T(8,128)(2,1)} %grid_hbm.1, bf16[1024,1024]{1,0:T(8,128)(2,1)S(1)} %copy-done), kind=kOutput, calls=%fused_computation | convolution fusion | flops 1074266112 | bytes 4194304 | tf_op jit(solution)/shard_map/dot_general | solution.py:585
  7.5 0.6 fusion.2.idxt_ref
  8.1 0.7 pad_add_fusion.place_ref
  8.8 1.0 collective-permute-done.below_ref
  9.8 0.0 copy-start.8
  9.8 19.3 %forward.1 = (bf16[8192,1024]{1,0:T(8,128)(2,1)}, bf16[512,1024]{1,0:T(8,128)(2,1)}, f32[32,512]{1,0:T(8,128)}, bf16[8,32,512]{2,1,0:T(8,128)(2,1)}, bf16[512,25...) custom-call(s32[4]{0:T(128)} %pad_add_fusion.place_ref, ...), custom_call_target="tpu_custom_call" | custom-call | flops 4294967296 | bytes 16777216 | tf_op jit(solution)/shard_map/forward/pallas_call | solution.py:212
  29.1 9.0 %all-to-all-start = ((bf16[8,32,512]{2,1,0:T(8,128)(2,1)}), bf16[8,32,512]{2,1,0:T(8,128)(2,1)S(1)}, u32[]{:S(2)}, u32[]{:S(2)}) async-start(bf16[8,32,512]{2,1,0:T(8,128)(2,1)} %get-tuple-element.32), calls=%async_computation | async-start | bytes 524288 | tf_op jit(solution)/shard_map/all_to_all | solution.py:599
  38.1 1.5 %collective-permute-start.3 = (bf16[512,256]{1,0:T(8,128)(2,1)}, bf16[512,256]{1,0:T(8,128)(2,1)S(1)}, u32[]{:S(2)}, u32[]{:S(2)}) collective-permute-start(bf16[512,256]{1,0:T(8,128)(2,1)} %get-tuple-element.36), channel_id=1, source_target_pairs={{0,32},{32,64},{64,96},{96,0},{1,33},{33,65},{65,97},{97,1},{2,34}... | collective-permute-start | bytes 786440 | tf_op jit(solution)/shard_map/ppermute | solution.py:29
  39.5 2.4 %collective-permute-start.4 = (bf16[512,256]{1,0:T(8,128)(2,1)}, bf16[512,256]{1,0:T(8,128)(2,1)S(1)}, u32[]{:S(2)}, u32[]{:S(2)}) collective-permute-start(bf16[512,256]{1,0:T(8,128)(2,1)} %get-tuple-element.37), channel_id=1, source_target_pairs={{0,64},{32,96},{64,0},{96,32},{1,65},{33,97},{65,1},{97,33},{2,66}... | collective-permute-start | bytes 786440 | tf_op jit(solution)/shard_map/ppermute | solution.py:29
  41.9 1.2 collective-permute-start.5
  43.2 8.0 %collective-permute-start.2 = (bf16[64,1024]{1,0:T(8,128)(2,1)S(1)}, bf16[64,1024]{1,0:T(8,128)(2,1)S(1)}, u32[]{:S(2)}, u32[]{:S(2)}) collective-permute-start(bf16[64,1024]{1,0:T(8,128)(2,1)S(1)} %broadcast_select_fusion), channel_id=1, source_target_pairs={{0,1},{1,0},{2,3},{3,2},{4,5},{5,4},{6,7},{7,6},{8,9},{9,8},{10,11... | collective-permute-start | bytes 393224 | tf_op jit(solution)/shard_map/ppermute | solution.py:601
  51.2 0.7 copy.14.var_ref
  51.9 0.3 collective-permute-done.2.edge_ref
  52.2 0.0 all-to-all-done.every_ref
  52.2 10.7 %backward.1 = (bf16[64,1024]{1,0:T(8,128)(2,1)}, bf16[64,1024]{1,0:T(8,128)(2,1)}, bf16[64,1024]{1,0:T(8,128)(2,1)}, bf16[192,512]{1,0:T(8,128)(2,1)S(1)}, bf16[...) custom-call(s32[4]{0:T(128)} %pad_add_fusion.place_ref, ...), custom_call_target="tpu_custom_call" | custom-call | flops 4294967296 | bytes 16777216 | tf_op jit(solution)/shard_map/backward/pallas_call | solution.py:445
  62.9 5.5 %collective-permute-start.7 = (bf16[8,144,128]{2,1,0:T(8,128)(2,1)S(1)}, bf16[8,144,128]{2,1,0:T(8,128)(2,1)S(1)}, u32[]{:S(2)}, u32[]{:S(2)}) collective-permute-start(bf16[8,144,128]{2,1,0:T(8,128)(2,1)S(1)} %get-tuple-element.46), channel_id=1, source_target_pairs={{0,1},{1,0},{2,3},{3,2},{4,5},{5,4},{6,7},{7,6},{8,9},{9,8},{10,11... | collective-permute-start | bytes 884744 | tf_op jit(solution)/shard_map/ppermute | solution.py:618
  68.4 0.3 collective-permute-start.6
  68.7 1.2 collective-permute-done.6.far_ref
  69.9 3.5 %pack.1 = bf16[16,64,656]{2,1,0:T(8,128)(2,1)} custom-call(s32[4]{0:T(128)} %pad_add_fusion.place_ref, bf16[64,1024]{1,0:T(8,128)(2,1)} %copy-done.2, bf16[64,1024]{1,0:T(8,128)(2,1)} %bitcast.40, bf16[64,1024]{1,0:T(8,128)(2,1)} %copy-done.1, bf16[64,1024]{1,0:T(8,128)(2,1)} %copy-done.4, bf16[192,512]{1,0:T(8,128)(2,1)S(1)} %get-tuple-element.43.own_ref, ...), custom_call_target="tpu_custom_call" | custom-call | flops 402653184 | bytes 4194304 | tf_op jit(solution)/shard_map/pack/pallas_call | solution.py:507
  73.4 6.1 %all-to-all-start.1 = ((bf16[16,64,656]{2,1,0:T(8,128)(2,1)}), bf16[16,64,656]{2,1,0:T(8,128)(2,1)}, u32[]{:S(2)}, u32[]{:S(2)}) async-start(bf16[16,64,656]{2,1,0:T(8,128)(2,1)} %pack.1), calls=%async_computation.1 | async-start | bytes 3145728 | tf_op jit(solution)/shard_map/all_to_all | solution.py:624
  79.6 0.7 collective-permute-start.8
  80.3 1.1 collective-permute-start.9
  81.4 20.5 %all-to-all-done.1.parts_ref = bf16[16,64,656]{2,1,0:T(8,128)(2,1)} async-done(((bf16[16,64,656]{2,1,0:T(8,128)(2,1)}), bf16[16,64,656]{2,1,0:T(8,128)(2,1)}, u32[]{:S(2)}, u32[]{:S(2)}) %all-to-all-start.1) | async-done | bytes 1343520 | tf_op jit(solution)/shard_map/all_to_all | solution.py:624
  101.9 2.1 %join.1 = bf16[16,4,1040]{2,1,0:T(4,128)(2,1)} custom-call(bf16[16,64,656]{2,1,0:T(8,128)(2,1)} %all-to-all-done.1.parts_ref), custom_call_target="tpu_custom_call" | custom-call | flops 671744 | bytes 1343488 | tf_op jit(solution)/shard_map/join/pallas_call | solution.py:547
  104.0 8.9 %all-to-all-start.2 = ((bf16[16,4,1040]{2,1,0:T(4,128)(2,1)}), bf16[16,4,1040]{2,1,0:T(4,128)(2,1)S(1)}, u32[]{:S(2)}, u32[]{:S(2)}) async-start(bf16[16,4,1040]{2,1,0:T(4,128)(2,1)} %join.1), calls=%async_computation.2 | async-start | bytes 294912 | tf_op jit(solution)/shard_map/all_to_all | solution.py:629
  112.8 3.0 %fusion = bf16[1,64,1024]{2,1,0:T(8,128)(2,1)} fusion(bf16[1024,1024]{1,0:T(8,128)(2,1)} %wsrc_ref.1, bf16[64,1024]{1,0:T(8,128)(2,1)S(1)} %collective-permute-done.9, bf16[64,1024]{1,0:T(8,128)(2,1)S(1)} %collective-permute-done.8, bf16[64,1024]{1,0:T(8,128)(2,1)S(1)} %copy-done.3), kind=kOutput, calls=%fused_computation.2 | convolution fusion | flops 134676480 | bytes 2621440 | tf_op jit(solution)/shard_map/dot_general | solution.py:631
  115.8 6.3 %all-to-all-done.2 = bf16[16,4,1040]{2,1,0:T(4,128)(2,1)S(1)} async-done(((bf16[16,4,1040]{2,1,0:T(4,128)(2,1)}), bf16[16,4,1040]{2,1,0:T(4,128)(2,1)S(1)}, u32[]{:S(2)}, u32[]{:S(2)}) %all-to-all-start.2) | async-done | bytes 133152 | tf_op jit(solution)/shard_map/all_to_all | solution.py:629
  122.2 0.1 convert_reduce_fusion
  122.2 0.7 pad_maximum_fusion.2
  122.9 0.6 pad_maximum_fusion
  (31 shorter events, 0.1 us)
Async XLA Ops:
  0.6 3.3 %copy-start = (bf16[1024,1024]{1,0:T(8,128)(2,1)S(1)}, bf16[1024,1024]{1,0:T(8,128)(2,1)}, u32[]{:S(2)}) copy-start(bf16[1024,1024]{1,0:T(8,128)(2,1)} %param.13) | copy-start | bytes 6291460
  0.6 9.2 %collective-permute-start.1 = (bf16[64,1024]{1,0:T(8,128)(2,1)}, bf16[64,1024]{1,0:T(8,128)(2,1)S(1)}, u32[]{:S(2)}, u32[]{:S(2)}) collective-permute-start(bf16[64,1024]{1,0:T(8,128)(2,1)} %bitcast.37), channel_id=1, source_target_pairs={{0,31},{1,0},{2,1},{3,2},{4,3},{5,4},{6,5},{7,6},{8,7},{9,8},{10,9... | collective-permute-start | bytes 393224 | tf_op jit(solution)/shard_map/ppermute | solution.py:29
  4.0 5.8 %collective-permute-start = (bf16[64,1024]{1,0:T(8,128)(2,1)}, bf16[64,1024]{1,0:T(8,128)(2,1)S(1)}, u32[]{:S(2)}, u32[]{:S(2)}) collective-permute-start(bf16[64,1024]{1,0:T(8,128)(2,1)} %bitcast.38), channel_id=1, source_target_pairs={{0,1},{1,2},{2,3},{3,4},{4,5},{5,6},{6,7},{7,8},{8,9},{9,10},{10,1... | collective-permute-start | bytes 393224 | tf_op jit(solution)/shard_map/ppermute | solution.py:29
  4.0 3.5 %copy-start.5 = (s32[512,16]{0,1:T(8,128)S(1)}, s32[512,16]{0,1:T(8,128)}, u32[]{:S(2)}) copy-start(s32[512,16]{0,1:T(8,128)} %param.18) | copy-start | bytes 98308
  4.0 3.5 %copy-start.6 = (s32[512,16]{0,1:T(8,128)S(1)}, s32[512,16]{0,1:T(8,128)}, u32[]{:S(2)}) copy-start(s32[512,16]{0,1:T(8,128)} %param.19) | copy-start | bytes 98308
  9.8 33.4 %copy-start.2 = (bf16[64,1024]{1,0:T(8,128)(2,1)}, bf16[64,1024]{1,0:T(8,128)(2,1)S(1)}, u32[]{:S(2)}) copy-start(bf16[64,1024]{1,0:T(8,128)(2,1)S(1)} %collective-permute-done.below_ref) | copy-start | bytes 393220
  9.8 33.4 %copy-start.1 = (bf16[64,1024]{1,0:T(8,128)(2,1)}, bf16[64,1024]{1,0:T(8,128)(2,1)S(1)}, u32[]{:S(2)}) copy-start(bf16[64,1024]{1,0:T(8,128)(2,1)S(1)} %collective-permute-done.1.above_ref) | copy-start | bytes 393220
  9.8 33.3 %copy-start.7 = (s32[4]{0:T(128)S(1)}, s32[4]{0:T(128)}, u32[]{:S(2)}) copy-start(s32[4]{0:T(128)} %pad_add_fusion.place_ref) | copy-start | bytes 52
  9.8 41.4 %copy-start.8 = (f32[32]{0:T(128)S(1)}, f32[32]{0:T(128)}, u32[]{:S(2)}) copy-start(f32[32]{0:T(128)} %param.17) | copy-start | bytes 388
  29.1 23.0 %all-to-all-start = ((bf16[8,32,512]{2,1,0:T(8,128)(2,1)}), bf16[8,32,512]{2,1,0:T(8,128)(2,1)S(1)}, u32[]{:S(2)}, u32[]{:S(2)}) async-start(bf16[8,32,512]{2,1,0:T(8,128)(2,1)} %get-tuple-element.32), calls=%async_computation | async-start | bytes 524288 | tf_op jit(solution)/shard_map/all_to_all | solution.py:599
  38.1 14.1 %collective-permute-start.3 = (bf16[512,256]{1,0:T(8,128)(2,1)}, bf16[512,256]{1,0:T(8,128)(2,1)S(1)}, u32[]{:S(2)}, u32[]{:S(2)}) collective-permute-start(bf16[512,256]{1,0:T(8,128)(2,1)} %get-tuple-element.36), channel_id=1, source_target_pairs={{0,32},{32,64},{64,96},{96,0},{1,33},{33,65},{65,97},{97,1},{2,34}... | collective-permute-start | bytes 786440 | tf_op jit(solution)/shard_map/ppermute | solution.py:29
  39.5 12.6 %collective-permute-start.4 = (bf16[512,256]{1,0:T(8,128)(2,1)}, bf16[512,256]{1,0:T(8,128)(2,1)S(1)}, u32[]{:S(2)}, u32[]{:S(2)}) collective-permute-start(bf16[512,256]{1,0:T(8,128)(2,1)} %get-tuple-element.37), channel_id=1, source_target_pairs={{0,64},{32,96},{64,0},{96,32},{1,65},{33,97},{65,1},{97,33},{2,66}... | collective-permute-start | bytes 786440 | tf_op jit(solution)/shard_map/ppermute | solution.py:29
  41.9 10.2 %collective-permute-start.5 = (bf16[512,256]{1,0:T(8,128)(2,1)}, bf16[512,256]{1,0:T(8,128)(2,1)S(1)}, u32[]{:S(2)}, u32[]{:S(2)}) collective-permute-start(bf16[512,256]{1,0:T(8,128)(2,1)} %get-tuple-element.38), channel_id=1, source_target_pairs={{0,96},{32,0},{64,32},{96,64},{1,97},{33,1},{65,33},{97,65},{2,98}... | collective-permute-start | bytes 786440 | tf_op jit(solution)/shard_map/ppermute | solution.py:29
  43.2 8.9 %collective-permute-start.2 = (bf16[64,1024]{1,0:T(8,128)(2,1)S(1)}, bf16[64,1024]{1,0:T(8,128)(2,1)S(1)}, u32[]{:S(2)}, u32[]{:S(2)}) collective-permute-start(bf16[64,1024]{1,0:T(8,128)(2,1)S(1)} %broadcast_select_fusion), channel_id=1, source_target_pairs={{0,1},{1,0},{2,3},{3,2},{4,5},{5,4},{6,7},{7,6},{8,9},{9,8},{10,11... | collective-permute-start | bytes 393224 | tf_op jit(solution)/shard_map/ppermute | solution.py:601
  52.1 10.7 %copy-start.4 = (bf16[64,1024]{1,0:T(8,128)(2,1)}, bf16[64,1024]{1,0:T(8,128)(2,1)S(1)}, u32[]{:S(2)}) copy-start(bf16[64,1024]{1,0:T(8,128)(2,1)S(1)} %collective-permute-done.2.edge_ref) | copy-start | bytes 393220
  62.9 7.0 %collective-permute-start.7 = (bf16[8,144,128]{2,1,0:T(8,128)(2,1)S(1)}, bf16[8,144,128]{2,1,0:T(8,128)(2,1)S(1)}, u32[]{:S(2)}, u32[]{:S(2)}) collective-permute-start(bf16[8,144,128]{2,1,0:T(8,128)(2,1)S(1)} %get-tuple-element.46), channel_id=1, source_target_pairs={{0,1},{1,0},{2,3},{3,2},{4,5},{5,4},{6,7},{7,6},{8,9},{9,8},{10,11... | collective-permute-start | bytes 884744 | tf_op jit(solution)/shard_map/ppermute | solution.py:618
  68.4 1.5 %collective-permute-start.6 = (bf16[192,512]{1,0:T(8,128)(2,1)S(1)}, bf16[192,512]{1,0:T(8,128)(2,1)S(1)}, u32[]{:S(2)}, u32[]{:S(2)}) collective-permute-start(bf16[192,512]{1,0:T(8,128)(2,1)S(1)} %get-tuple-element.44), channel_id=1, source_target_pairs={{0,1},{1,0},{2,3},{3,2},{4,5},{5,4},{6,7},{7,6},{8,9},{9,8},{10,11... | collective-permute-start | bytes 589832 | tf_op jit(solution)/shard_map/ppermute | solution.py:619
  73.4 6.2 %copy-start.10 = (bf16[64,1024]{1,0:T(8,128)(2,1)S(1)}, bf16[64,1024]{1,0:T(8,128)(2,1)}, u32[]{:S(2)}) copy-start(bf16[64,1024]{1,0:T(8,128)(2,1)} %get-tuple-element.47) | copy-start | bytes 393220
  73.4 6.9 %copy-start.9 = (bf16[64,1024]{1,0:T(8,128)(2,1)S(1)}, bf16[64,1024]{1,0:T(8,128)(2,1)}, u32[]{:S(2)}) copy-start(bf16[64,1024]{1,0:T(8,128)(2,1)} %get-tuple-element.48) | copy-start | bytes 393220
  73.4 39.4 %copy-start.3 = (bf16[64,1024]{1,0:T(8,128)(2,1)S(1)}, bf16[64,1024]{1,0:T(8,128)(2,1)}, u32[]{:S(2)}) copy-start(bf16[64,1024]{1,0:T(8,128)(2,1)} %get-tuple-element.41) | copy-start | bytes 393220
  73.4 28.4 %all-to-all-start.1 = ((bf16[16,64,656]{2,1,0:T(8,128)(2,1)}), bf16[16,64,656]{2,1,0:T(8,128)(2,1)}, u32[]{:S(2)}, u32[]{:S(2)}) async-start(bf16[16,64,656]{2,1,0:T(8,128)(2,1)} %pack.1), calls=%async_computation.1 | async-start | bytes 3145728 | tf_op jit(solution)/shard_map/all_to_all | solution.py:624
  79.6 24.4 %collective-permute-start.8 = (bf16[64,1024]{1,0:T(8,128)(2,1)S(1)}, bf16[64,1024]{1,0:T(8,128)(2,1)S(1)}, u32[]{:S(2)}, u32[]{:S(2)}) collective-permute-start(bf16[64,1024]{1,0:T(8,128)(2,1)S(1)} %copy-done.10), channel_id=1, source_target_pairs={{0,31},{1,0},{2,1},{3,2},{4,3},{5,4},{6,5},{7,6},{8,7},{9,8},{10,9... | collective-permute-start | bytes 393224 | tf_op jit(solution)/shard_map/ppermute | solution.py:29
  80.3 23.7 %collective-permute-start.9 = (bf16[64,1024]{1,0:T(8,128)(2,1)S(1)}, bf16[64,1024]{1,0:T(8,128)(2,1)S(1)}, u32[]{:S(2)}, u32[]{:S(2)}) collective-permute-start(bf16[64,1024]{1,0:T(8,128)(2,1)S(1)} %copy-done.9), channel_id=1, source_target_pairs={{0,1},{1,2},{2,3},{3,4},{4,5},{5,6},{6,7},{7,8},{8,9},{9,10},{10,1... | collective-permute-start | bytes 393224 | tf_op jit(solution)/shard_map/ppermute | solution.py:29
  104.0 18.2 %all-to-all-start.2 = ((bf16[16,4,1040]{2,1,0:T(4,128)(2,1)}), bf16[16,4,1040]{2,1,0:T(4,128)(2,1)S(1)}, u32[]{:S(2)}, u32[]{:S(2)}) async-start(bf16[16,4,1040]{2,1,0:T(4,128)(2,1)} %join.1), calls=%async_computation.2 | async-start | bytes 294912 | tf_op jit(solution)/shard_map/all_to_all | solution.py:629

commit v16 on v15

--- a/solution.py
+++ b/solution.py
@@ -298,7 +298,9 @@
     )
     total = jnp.zeros(sum_refs[0].shape, f32)
     for d, sum_ref in enumerate(sum_refs):
-        other = dpred_of(every_ref[zh * near + (x + near - d) % near].astype(f32))
+        other = dpred
+        if d > 0:
+            other = dpred_of(every_ref[zh * near + (x + near - d) % near].astype(f32))
         dagg = lax.dot_general(other, quarter, first, preferred_element_type=f32)
         total = total + dagg * sum_ref[...].astype(f32)
     ddst[...] = (total * scale).astype(bf16)
@@ -401,10 +403,11 @@
     block_copy(step).wait()
     wide = size // slots
     base = pl.multiple_of(step * wide, wide)
-    node = lax.broadcasted_iota(jnp.int32, (nodes, wide), 0)
-    idx = idxt_ref[:, pl.ds(base, wide)]
+    node = lax.broadcasted_iota(jnp.int32, (nodes, wide), 0).astype(f32).astype(bf16)
+    idx = idxt_ref[:, pl.ds(base, wide)].astype(f32).astype(bf16)
+    one, zero = jnp.ones_like(node), jnp.zeros_like(node)
     for k in range(slots):
-        hot[:, k * wide : (k + 1) * wide] = jnp.where(node == idx[k : k + 1, :], 1.0, 0.0).astype(bf16)
+        hot[:, k * wide : (k + 1) * wide] = jnp.where(node == idx[k : k + 1, :], one, zero)
     for start in range(0, wide, TILE):
         some = lead[pl.ds(pl.multiple_of(base + start, TILE), TILE), :]
         for k in range(slots):
@@ -595,7 +598,8 @@
     gp, agg, pred, sent, kept, *pieces = forward(
         place, *feats, w_src, dst, idx_t, wout_t, members
     )
-    sums = [kept] + [shifted(piece, "x", d + 1) for d, piece in enumerate(pieces)]
+    two = shifted(pieces[1], "x", 2)
+    sums = [kept, shifted(pieces[0], "x", 1), two, shifted(pieces[2], "x", 3)]
     everyone = lax.all_to_all(sent, ENS, 0, 0, tiled=True)
     low = place[0] == 0
     edge = lax.ppermute(jnp.where(low, below, above), "c", swap)

time: 124 us -> 124 us (level)
  no operation moved by 1% of the time
where the time goes in v16:
time: 124 us
  starting transfers between devices  47.9 us (39%)
  Pallas kernels  35.8 us (29%)
  waiting for transfers between devices  29.3 us (24%)
  matrix products  6.5 us (5%)
  other arithmetic  2.66 us (2%)
    all_to_all x1, waiting for transfers between devices, body(): parts = lax.all_to_all(total, FIRST, 0, 0, tiled=True)  20.5 us
    pallas_call x1, Pallas kernels, forward(): pl.pallas_call(functools.partial(forward_kernel, slots, members), grid_sp...  19.3 us
    pallas_call x1, Pallas kernels, backward(): pl.pallas_call(functools.partial(backward_kernel, slots), grid_spec=prefe...  10.8 us
    ppermute x7, starting transfers between devices, shifted(): lax.ppermute(block, axes, [(i, (i + distance) % count) for i in range(cou...  10.2 us
    all_to_all x1, starting transfers between devices, body(): everyone = lax.all_to_all(sent, ENS, 0, 0, tiled=True)  8.96 us
    all_to_all x1, starting transfers between devices, body(): parts = lax.all_to_all(total, SECOND, 0, 0, tiled=True)  8.86 us
    ppermute x1, starting transfers between devices, body(): edge = lax.ppermute(jnp.where(low, below, above), 'c', swap)  7.95 us
    all_to_all x1, waiting for transfers between devices, body(): parts = lax.all_to_all(total, SECOND, 0, 0, tiled=True)  6.3 us
  transfers between devices with their start and end apart: 13, of which 5 were waited for; matrix products, arithmetic and copies ran while one was open for 7% of the time, Pallas kernels for 2%

profile of v16, /device:TPU:1, one launch (start us, length us, event | category | flops | bytes accessed | tf_op | source)
XLA Modules:
  0.0 123.6 jit_solution(13780879874617989963)
XLA Ops:
  0.6 0.0 copy-start
  0.6 3.3 %collective-permute-start.1 = (bf16[64,1024]{1,0:T(8,128)(2,1)}, bf16[64,1024]{1,0:T(8,128)(2,1)S(1)}, u32[]{:S(2)}, u32[]{:S(2)}) collective-permute-start(bf16[64,1024]{1,0:T(8,128)(2,1)} %bitcast.37), channel_id=1, source_target_pairs={{0,31},{1,0},{2,1},{3,2},{4,3},{5,4},{6,5},{7,6},{8,7},{9,8},{10,9... | collective-permute-start | bytes 393224 | tf_op jit(solution)/shard_map/ppermute | solution.py:29
  4.0 3.5 %convolution_convert_fusion.dst_ref = bf16[512,1024]{1,0:T(8,128)(2,1)} fusion(bf16[512,1024]{1,0:T(8,128)(2,1)} %grid_hbm.1, bf16[1024,1024]{1,0:T(8,128)(2,1)S(1)} %copy-done), kind=kOutput, calls=%fused_computation | convolution fusion | flops 1074266112 | bytes 4194304 | tf_op jit(solution)/shard_map/dot_general | solution.py:588
  7.5 0.6 fusion.2.idxt_ref
  8.1 0.7 pad_add_fusion.place_ref
  8.8 1.0 collective-permute-done.below_ref
  9.8 0.0 collective-permute-done.1.above_ref
  9.8 0.0 copy-start.8
  9.8 19.3 %forward.1 = (bf16[8192,1024]{1,0:T(8,128)(2,1)}, bf16[512,1024]{1,0:T(8,128)(2,1)}, f32[32,512]{1,0:T(8,128)}, bf16[8,32,512]{2,1,0:T(8,128)(2,1)}, bf16[512,25...) custom-call(s32[4]{0:T(128)} %pad_add_fusion.place_ref, ...), custom_call_target="tpu_custom_call" | custom-call | flops 4294967296 | bytes 16777216 | tf_op jit(solution)/shard_map/forward/pallas_call | solution.py:212
  29.1 9.0 %all-to-all-start = ((bf16[8,32,512]{2,1,0:T(8,128)(2,1)}), bf16[8,32,512]{2,1,0:T(8,128)(2,1)S(1)}, u32[]{:S(2)}, u32[]{:S(2)}) async-start(bf16[8,32,512]{2,1,0:T(8,128)(2,1)} %get-tuple-element.32), calls=%async_computation | async-start | bytes 524288 | tf_op jit(solution)/shard_map/all_to_all | solution.py:603
  38.1 1.5 %collective-permute-start.3 = (bf16[512,256]{1,0:T(8,128)(2,1)}, bf16[512,256]{1,0:T(8,128)(2,1)S(1)}, u32[]{:S(2)}, u32[]{:S(2)}) collective-permute-start(bf16[512,256]{1,0:T(8,128)(2,1)} %get-tuple-element.36), channel_id=1, source_target_pairs={{0,32},{32,64},{64,96},{96,0},{1,33},{33,65},{65,97},{97,1},{2,34}... | collective-permute-start | bytes 786440 | tf_op jit(solution)/shard_map/ppermute | solution.py:29
  39.5 2.4 %collective-permute-start.4 = (bf16[512,256]{1,0:T(8,128)(2,1)}, bf16[512,256]{1,0:T(8,128)(2,1)S(1)}, u32[]{:S(2)}, u32[]{:S(2)}) collective-permute-start(bf16[512,256]{1,0:T(8,128)(2,1)} %get-tuple-element.37), channel_id=1, source_target_pairs={{0,64},{32,96},{64,0},{96,32},{1,65},{33,97},{65,1},{97,33},{2,66}... | collective-permute-start | bytes 786440 | tf_op jit(solution)/shard_map/ppermute | solution.py:29
  41.9 1.2 collective-permute-start.5
  43.2 8.0 %collective-permute-start.2 = (bf16[64,1024]{1,0:T(8,128)(2,1)S(1)}, bf16[64,1024]{1,0:T(8,128)(2,1)S(1)}, u32[]{:S(2)}, u32[]{:S(2)}) collective-permute-start(bf16[64,1024]{1,0:T(8,128)(2,1)S(1)} %broadcast_select_fusion), channel_id=1, source_target_pairs={{0,1},{1,0},{2,3},{3,2},{4,5},{5,4},{6,7},{7,6},{8,9},{9,8},{10,11... | collective-permute-start | bytes 393224 | tf_op jit(solution)/shard_map/ppermute | solution.py:605
  51.2 0.7 copy.14.var_ref
  51.9 0.3 collective-permute-done.2.edge_ref
  52.2 10.8 %backward.1 = (bf16[64,1024]{1,0:T(8,128)(2,1)}, bf16[64,1024]{1,0:T(8,128)(2,1)}, bf16[64,1024]{1,0:T(8,128)(2,1)}, bf16[192,512]{1,0:T(8,128)(2,1)S(1)}, bf16[...) custom-call(s32[4]{0:T(128)} %pad_add_fusion.place_ref, ...), custom_call_target="tpu_custom_call" | custom-call | flops 4294967296 | bytes 16777216 | tf_op jit(solution)/shard_map/backward/pallas_call | solution.py:448
  63.0 5.5 %collective-permute-start.7 = (bf16[8,144,128]{2,1,0:T(8,128)(2,1)S(1)}, bf16[8,144,128]{2,1,0:T(8,128)(2,1)S(1)}, u32[]{:S(2)}, u32[]{:S(2)}) collective-permute-start(bf16[8,144,128]{2,1,0:T(8,128)(2,1)S(1)} %get-tuple-element.46), channel_id=1, source_target_pairs={{0,1},{1,0},{2,3},{3,2},{4,5},{5,4},{6,7},{7,6},{8,9},{9,8},{10,11... | collective-permute-start | bytes 884744 | tf_op jit(solution)/shard_map/ppermute | solution.py:622
  68.5 0.3 collective-permute-start.6
  68.8 1.2 collective-permute-done.6.far_ref
  70.0 3.5 %pack.1 = bf16[16,64,656]{2,1,0:T(8,128)(2,1)} custom-call(s32[4]{0:T(128)} %pad_add_fusion.place_ref, bf16[64,1024]{1,0:T(8,128)(2,1)} %copy-done.2, bf16[64,1024]{1,0:T(8,128)(2,1)} %bitcast.40, bf16[64,1024]{1,0:T(8,128)(2,1)} %copy-done.1, bf16[64,1024]{1,0:T(8,128)(2,1)} %copy-done.4, bf16[192,512]{1,0:T(8,128)(2,1)S(1)} %get-tuple-element.43.own_ref, ...), custom_call_target="tpu_custom_call" | custom-call | flops 402653184 | bytes 4194304 | tf_op jit(solution)/shard_map/pack/pallas_call | solution.py:510
  73.5 6.1 %all-to-all-start.1 = ((bf16[16,64,656]{2,1,0:T(8,128)(2,1)}), bf16[16,64,656]{2,1,0:T(8,128)(2,1)}, u32[]{:S(2)}, u32[]{:S(2)}) async-start(bf16[16,64,656]{2,1,0:T(8,128)(2,1)} %pack.1), calls=%async_computation.1 | async-start | bytes 3145728 | tf_op jit(solution)/shard_map/all_to_all | solution.py:628
  79.7 0.7 collective-permute-start.8
  80.4 1.1 collective-permute-start.9
  81.5 20.5 %all-to-all-done.1.parts_ref = bf16[16,64,656]{2,1,0:T(8,128)(2,1)} async-done(((bf16[16,64,656]{2,1,0:T(8,128)(2,1)}), bf16[16,64,656]{2,1,0:T(8,128)(2,1)}, u32[]{:S(2)}, u32[]{:S(2)}) %all-to-all-start.1) | async-done | bytes 1343520 | tf_op jit(solution)/shard_map/all_to_all | solution.py:628
  102.0 2.1 %join.1 = bf16[16,4,1040]{2,1,0:T(4,128)(2,1)} custom-call(bf16[16,64,656]{2,1,0:T(8,128)(2,1)} %all-to-all-done.1.parts_ref), custom_call_target="tpu_custom_call" | custom-call | flops 671744 | bytes 1343488 | tf_op jit(solution)/shard_map/join/pallas_call | solution.py:550
  104.1 8.9 %all-to-all-start.2 = ((bf16[16,4,1040]{2,1,0:T(4,128)(2,1)}), bf16[16,4,1040]{2,1,0:T(4,128)(2,1)S(1)}, u32[]{:S(2)}, u32[]{:S(2)}) async-start(bf16[16,4,1040]{2,1,0:T(4,128)(2,1)} %join.1), calls=%async_computation.2 | async-start | bytes 294912 | tf_op jit(solution)/shard_map/all_to_all | solution.py:633
  113.0 3.0 %fusion = bf16[1,64,1024]{2,1,0:T(8,128)(2,1)} fusion(bf16[1024,1024]{1,0:T(8,128)(2,1)} %wsrc_ref.1, bf16[64,1024]{1,0:T(8,128)(2,1)S(1)} %collective-permute-done.9, bf16[64,1024]{1,0:T(8,128)(2,1)S(1)} %collective-permute-done.8, bf16[64,1024]{1,0:T(8,128)(2,1)S(1)} %copy-done.3), kind=kOutput, calls=%fused_computation.2 | convolution fusion | flops 134676480 | bytes 2621440 | tf_op jit(solution)/shard_map/dot_general | solution.py:635
  116.0 6.3 %all-to-all-done.2 = bf16[16,4,1040]{2,1,0:T(4,128)(2,1)S(1)} async-done(((bf16[16,4,1040]{2,1,0:T(4,128)(2,1)}), bf16[16,4,1040]{2,1,0:T(4,128)(2,1)S(1)}, u32[]{:S(2)}, u32[]{:S(2)}) %all-to-all-start.2) | async-done | bytes 133152 | tf_op jit(solution)/shard_map/all_to_all | solution.py:633
  122.3 0.1 convert_reduce_fusion
  122.4 0.7 pad_maximum_fusion.2
  123.0 0.6 pad_maximum_fusion
  (31 shorter events, 0.1 us)
Async XLA Ops:
  0.6 3.3 %copy-start = (bf16[1024,1024]{1,0:T(8,128)(2,1)S(1)}, bf16[1024,1024]{1,0:T(8,128)(2,1)}, u32[]{:S(2)}) copy-start(bf16[1024,1024]{1,0:T(8,128)(2,1)} %param.13) | copy-start | bytes 6291460
  0.6 9.2 %collective-permute-start.1 = (bf16[64,1024]{1,0:T(8,128)(2,1)}, bf16[64,1024]{1,0:T(8,128)(2,1)S(1)}, u32[]{:S(2)}, u32[]{:S(2)}) collective-permute-start(bf16[64,1024]{1,0:T(8,128)(2,1)} %bitcast.37), channel_id=1, source_target_pairs={{0,31},{1,0},{2,1},{3,2},{4,3},{5,4},{6,5},{7,6},{8,7},{9,8},{10,9... | collective-permute-start | bytes 393224 | tf_op jit(solution)/shard_map/ppermute | solution.py:29
  4.0 5.8 %collective-permute-start = (bf16[64,1024]{1,0:T(8,128)(2,1)}, bf16[64,1024]{1,0:T(8,128)(2,1)S(1)}, u32[]{:S(2)}, u32[]{:S(2)}) collective-permute-start(bf16[64,1024]{1,0:T(8,128)(2,1)} %bitcast.38), channel_id=1, source_target_pairs={{0,1},{1,2},{2,3},{3,4},{4,5},{5,6},{6,7},{7,8},{8,9},{9,10},{10,1... | collective-permute-start | bytes 393224 | tf_op jit(solution)/shard_map/ppermute | solution.py:29
  4.0 3.5 %copy-start.5 = (s32[512,16]{0,1:T(8,128)S(1)}, s32[512,16]{0,1:T(8,128)}, u32[]{:S(2)}) copy-start(s32[512,16]{0,1:T(8,128)} %param.18) | copy-start | bytes 98308
  4.0 3.5 %copy-start.6 = (s32[512,16]{0,1:T(8,128)S(1)}, s32[512,16]{0,1:T(8,128)}, u32[]{:S(2)}) copy-start(s32[512,16]{0,1:T(8,128)} %param.19) | copy-start | bytes 98308
  9.8 33.4 %copy-start.2 = (bf16[64,1024]{1,0:T(8,128)(2,1)}, bf16[64,1024]{1,0:T(8,128)(2,1)S(1)}, u32[]{:S(2)}) copy-start(bf16[64,1024]{1,0:T(8,128)(2,1)S(1)} %collective-permute-done.below_ref) | copy-start | bytes 393220
  9.8 33.4 %copy-start.1 = (bf16[64,1024]{1,0:T(8,128)(2,1)}, bf16[64,1024]{1,0:T(8,128)(2,1)S(1)}, u32[]{:S(2)}) copy-start(bf16[64,1024]{1,0:T(8,128)(2,1)S(1)} %collective-permute-done.1.above_ref) | copy-start | bytes 393220
  9.8 33.3 %copy-start.7 = (s32[4]{0:T(128)S(1)}, s32[4]{0:T(128)}, u32[]{:S(2)}) copy-start(s32[4]{0:T(128)} %pad_add_fusion.place_ref) | copy-start | bytes 52
  9.8 41.4 %copy-start.8 = (f32[32]{0:T(128)S(1)}, f32[32]{0:T(128)}, u32[]{:S(2)}) copy-start(f32[32]{0:T(128)} %param.17) | copy-start | bytes 388
  29.1 23.0 %all-to-all-start = ((bf16[8,32,512]{2,1,0:T(8,128)(2,1)}), bf16[8,32,512]{2,1,0:T(8,128)(2,1)S(1)}, u32[]{:S(2)}, u32[]{:S(2)}) async-start(bf16[8,32,512]{2,1,0:T(8,128)(2,1)} %get-tuple-element.32), calls=%async_computation | async-start | bytes 524288 | tf_op jit(solution)/shard_map/all_to_all | solution.py:603
  38.1 14.1 %collective-permute-start.3 = (bf16[512,256]{1,0:T(8,128)(2,1)}, bf16[512,256]{1,0:T(8,128)(2,1)S(1)}, u32[]{:S(2)}, u32[]{:S(2)}) collective-permute-start(bf16[512,256]{1,0:T(8,128)(2,1)} %get-tuple-element.36), channel_id=1, source_target_pairs={{0,32},{32,64},{64,96},{96,0},{1,33},{33,65},{65,97},{97,1},{2,34}... | collective-permute-start | bytes 786440 | tf_op jit(solution)/shard_map/ppermute | solution.py:29
  39.5 12.6 %collective-permute-start.4 = (bf16[512,256]{1,0:T(8,128)(2,1)}, bf16[512,256]{1,0:T(8,128)(2,1)S(1)}, u32[]{:S(2)}, u32[]{:S(2)}) collective-permute-start(bf16[512,256]{1,0:T(8,128)(2,1)} %get-tuple-element.37), channel_id=1, source_target_pairs={{0,64},{32,96},{64,0},{96,32},{1,65},{33,97},{65,1},{97,33},{2,66}... | collective-permute-start | bytes 786440 | tf_op jit(solution)/shard_map/ppermute | solution.py:29
  41.9 10.2 %collective-permute-start.5 = (bf16[512,256]{1,0:T(8,128)(2,1)}, bf16[512,256]{1,0:T(8,128)(2,1)S(1)}, u32[]{:S(2)}, u32[]{:S(2)}) collective-permute-start(bf16[512,256]{1,0:T(8,128)(2,1)} %get-tuple-element.38), channel_id=1, source_target_pairs={{0,96},{32,0},{64,32},{96,64},{1,97},{33,1},{65,33},{97,65},{2,98}... | collective-permute-start | bytes 786440 | tf_op jit(solution)/shard_map/ppermute | solution.py:29
  43.2 8.9 %collective-permute-start.2 = (bf16[64,1024]{1,0:T(8,128)(2,1)S(1)}, bf16[64,1024]{1,0:T(8,128)(2,1)S(1)}, u32[]{:S(2)}, u32[]{:S(2)}) collective-permute-start(bf16[64,1024]{1,0:T(8,128)(2,1)S(1)} %broadcast_select_fusion), channel_id=1, source_target_pairs={{0,1},{1,0},{2,3},{3,2},{4,5},{5,4},{6,7},{7,6},{8,9},{9,8},{10,11... | collective-permute-start | bytes 393224 | tf_op jit(solution)/shard_map/ppermute | solution.py:605
  52.1 10.9 %copy-start.4 = (bf16[64,1024]{1,0:T(8,128)(2,1)}, bf16[64,1024]{1,0:T(8,128)(2,1)S(1)}, u32[]{:S(2)}) copy-start(bf16[64,1024]{1,0:T(8,128)(2,1)S(1)} %collective-permute-done.2.edge_ref) | copy-start | bytes 393220
  63.0 7.0 %collective-permute-start.7 = (bf16[8,144,128]{2,1,0:T(8,128)(2,1)S(1)}, bf16[8,144,128]{2,1,0:T(8,128)(2,1)S(1)}, u32[]{:S(2)}, u32[]{:S(2)}) collective-permute-start(bf16[8,144,128]{2,1,0:T(8,128)(2,1)S(1)} %get-tuple-element.46), channel_id=1, source_target_pairs={{0,1},{1,0},{2,3},{3,2},{4,5},{5,4},{6,7},{7,6},{8,9},{9,8},{10,11... | collective-permute-start | bytes 884744 | tf_op jit(solution)/shard_map/ppermute | solution.py:622
  68.5 1.5 %collective-permute-start.6 = (bf16[192,512]{1,0:T(8,128)(2,1)S(1)}, bf16[192,512]{1,0:T(8,128)(2,1)S(1)}, u32[]{:S(2)}, u32[]{:S(2)}) collective-permute-start(bf16[192,512]{1,0:T(8,128)(2,1)S(1)} %get-tuple-element.44), channel_id=1, source_target_pairs={{0,1},{1,0},{2,3},{3,2},{4,5},{5,4},{6,7},{7,6},{8,9},{9,8},{10,11... | collective-permute-start | bytes 589832 | tf_op jit(solution)/shard_map/ppermute | solution.py:623
  73.5 6.2 %copy-start.10 = (bf16[64,1024]{1,0:T(8,128)(2,1)S(1)}, bf16[64,1024]{1,0:T(8,128)(2,1)}, u32[]{:S(2)}) copy-start(bf16[64,1024]{1,0:T(8,128)(2,1)} %get-tuple-element.47) | copy-start | bytes 393220
  73.5 6.9 %copy-start.9 = (bf16[64,1024]{1,0:T(8,128)(2,1)S(1)}, bf16[64,1024]{1,0:T(8,128)(2,1)}, u32[]{:S(2)}) copy-start(bf16[64,1024]{1,0:T(8,128)(2,1)} %get-tuple-element.48) | copy-start | bytes 393220
  73.5 39.4 %copy-start.3 = (bf16[64,1024]{1,0:T(8,128)(2,1)S(1)}, bf16[64,1024]{1,0:T(8,128)(2,1)}, u32[]{:S(2)}) copy-start(bf16[64,1024]{1,0:T(8,128)(2,1)} %get-tuple-element.41) | copy-start | bytes 393220
  73.5 28.4 %all-to-all-start.1 = ((bf16[16,64,656]{2,1,0:T(8,128)(2,1)}), bf16[16,64,656]{2,1,0:T(8,128)(2,1)}, u32[]{:S(2)}, u32[]{:S(2)}) async-start(bf16[16,64,656]{2,1,0:T(8,128)(2,1)} %pack.1), calls=%async_computation.1 | async-start | bytes 3145728 | tf_op jit(solution)/shard_map/all_to_all | solution.py:628
  79.7 24.4 %collective-permute-start.8 = (bf16[64,1024]{1,0:T(8,128)(2,1)S(1)}, bf16[64,1024]{1,0:T(8,128)(2,1)S(1)}, u32[]{:S(2)}, u32[]{:S(2)}) collective-permute-start(bf16[64,1024]{1,0:T(8,128)(2,1)S(1)} %copy-done.10), channel_id=1, source_target_pairs={{0,31},{1,0},{2,1},{3,2},{4,3},{5,4},{6,5},{7,6},{8,7},{9,8},{10,9... | collective-permute-start | bytes 393224 | tf_op jit(solution)/shard_map/ppermute | solution.py:29
  80.4 23.7 %collective-permute-start.9 = (bf16[64,1024]{1,0:T(8,128)(2,1)S(1)}, bf16[64,1024]{1,0:T(8,128)(2,1)S(1)}, u32[]{:S(2)}, u32[]{:S(2)}) collective-permute-start(bf16[64,1024]{1,0:T(8,128)(2,1)S(1)} %copy-done.9), channel_id=1, source_target_pairs={{0,1},{1,2},{2,3},{3,4},{4,5},{5,6},{6,7},{7,8},{8,9},{9,10},{10,1... | collective-permute-start | bytes 393224 | tf_op jit(solution)/shard_map/ppermute | solution.py:29
  104.1 18.2 %all-to-all-start.2 = ((bf16[16,4,1040]{2,1,0:T(4,128)(2,1)}), bf16[16,4,1040]{2,1,0:T(4,128)(2,1)S(1)}, u32[]{:S(2)}, u32[]{:S(2)}) async-start(bf16[16,4,1040]{2,1,0:T(4,128)(2,1)} %join.1), calls=%async_computation.2 | async-start | bytes 294912 | tf_op jit(solution)/shard_map/all_to_all | solution.py:633

commit v17 on v15

--- a/solution.py
+++ b/solution.py
@@ -16,6 +16,7 @@
 BACK = 2
 GROUPS = 2
 QUARTERS = 4
+JOINS = 4
 f32 = jnp.float32
 bf16 = jnp.bfloat16
 SPACE = ("y", "zl", "c")
@@ -298,7 +299,9 @@
     )
     total = jnp.zeros(sum_refs[0].shape, f32)
     for d, sum_ref in enumerate(sum_refs):
-        other = dpred_of(every_ref[zh * near + (x + near - d) % near].astype(f32))
+        other = dpred
+        if d > 0:
+            other = dpred_of(every_ref[zh * near + (x + near - d) % near].astype(f32))
         dagg = lax.dot_general(other, quarter, first, preferred_element_type=f32)
         total = total + dagg * sum_ref[...].astype(f32)
     ddst[...] = (total * scale).astype(bf16)
@@ -546,9 +549,9 @@
     count = rows // rows_out
     return pl.pallas_call(
         join_kernel,
-        grid=(GROUPS,),
-        in_specs=[pl.BlockSpec((sources, rows // GROUPS, columns), lambda t: (0, t, 0))],
-        out_specs=pl.BlockSpec((count // GROUPS, rows_out, wide), lambda t: (t, 0, 0)),
+        grid=(JOINS,),
+        in_specs=[pl.BlockSpec((sources, rows // JOINS, columns), lambda t: (0, t, 0))],
+        out_specs=pl.BlockSpec((count // JOINS, rows_out, wide), lambda t: (t, 0, 0)),
         out_shape=jax.ShapeDtypeStruct((count, rows_out, wide), bf16),
         compiler_params=params(),
         cost_estimate=pl.CostEstimate(flops=parts.size, bytes_accessed=2 * parts.size, transcendentals=0),

time: 124 us -> 126 us (1.016)
  Pallas kernels: 35.6 us -> 37 us
  transfers between devices with their start and end apart: 13 -> 13, of which waited for: 5 -> 5; matrix products, arithmetic and copies ran while one was open for 7% -> 7% of each run, Pallas kernels for 2% -> 3%
where the time goes in v17:
time: 126 us; the launch traced here: 125 us
  starting transfers between devices  48 us (38%)
  Pallas kernels  37 us (29%)
  waiting for transfers between devices  29.2 us (23%)
  matrix products  6.5 us (5%)
  other arithmetic  2.66 us (2%)
    all_to_all x1, waiting for transfers between devices, body(): parts = lax.all_to_all(total, FIRST, 0, 0, tiled=True)  20.3 us
    pallas_call x1, Pallas kernels, forward(): pl.pallas_call(functools.partial(forward_kernel, slots, members), grid_sp...  19.3 us
    pallas_call x1, Pallas kernels, backward(): pl.pallas_call(functools.partial(backward_kernel, slots), grid_spec=prefe...  10.8 us
    ppermute x7, starting transfers between devices, shifted(): lax.ppermute(block, axes, [(i, (i + distance) % count) for i in range(cou...  10.2 us
    all_to_all x1, starting transfers between devices, body(): parts = lax.all_to_all(total, SECOND, 0, 0, tiled=True)  8.99 us
    all_to_all x1, starting transfers between devices, body(): everyone = lax.all_to_all(sent, ENS, 0, 0, tiled=True)  8.96 us
    ppermute x1, starting transfers between devices, body(): edge = lax.ppermute(jnp.where(low, below, above), 'c', swap)  7.95 us
    all_to_all x1, waiting for transfers between devices, body(): parts = lax.all_to_all(total, SECOND, 0, 0, tiled=True)  6.3 us
  transfers between devices with their start and end apart: 13, of which 5 were waited for; matrix products, arithmetic and copies ran while one was open for 7% of the time, Pallas kernels for 3%

profile of v17, /device:TPU:1, one launch (start us, length us, event | category | flops | bytes accessed | tf_op | source)
XLA Modules:
  0.0 124.9 jit_solution(12313477726042099586)
XLA Ops:
  0.6 0.0 copy-start
  0.6 3.3 %collective-permute-start.1 = (bf16[64,1024]{1,0:T(8,128)(2,1)}, bf16[64,1024]{1,0:T(8,128)(2,1)S(1)}, u32[]{:S(2)}, u32[]{:S(2)}) collective-permute-start(bf16[64,1024]{1,0:T(8,128)(2,1)} %bitcast.37), channel_id=1, source_target_pairs={{0,31},{1,0},{2,1},{3,2},{4,3},{5,4},{6,5},{7,6},{8,7},{9,8},{10,9... | collective-permute-start | bytes 393224 | tf_op jit(solution)/shard_map/ppermute | solution.py:30
  4.0 3.5 %convolution_convert_fusion.dst_ref = bf16[512,1024]{1,0:T(8,128)(2,1)} fusion(bf16[512,1024]{1,0:T(8,128)(2,1)} %grid_hbm.1, bf16[1024,1024]{1,0:T(8,128)(2,1)S(1)} %copy-done), kind=kOutput, calls=%fused_computation | convolution fusion | flops 1074266112 | bytes 4194304 | tf_op jit(solution)/shard_map/dot_general | solution.py:588
  7.5 0.6 fusion.2.idxt_ref
  8.1 0.7 pad_add_fusion.place_ref
  8.8 1.0 collective-permute-done.below_ref
  9.8 0.0 collective-permute-done.1.above_ref
  9.8 0.0 copy-start.8
  9.8 19.3 %forward.1 = (bf16[8192,1024]{1,0:T(8,128)(2,1)}, bf16[512,1024]{1,0:T(8,128)(2,1)}, f32[32,512]{1,0:T(8,128)}, bf16[8,32,512]{2,1,0:T(8,128)(2,1)}, bf16[512,25...) custom-call(s32[4]{0:T(128)} %pad_add_fusion.place_ref, ...), custom_call_target="tpu_custom_call" | custom-call | flops 4294967296 | bytes 16777216 | tf_op jit(solution)/shard_map/forward/pallas_call | solution.py:213
  29.1 9.0 %all-to-all-start = ((bf16[8,32,512]{2,1,0:T(8,128)(2,1)}), bf16[8,32,512]{2,1,0:T(8,128)(2,1)S(1)}, u32[]{:S(2)}, u32[]{:S(2)}) async-start(bf16[8,32,512]{2,1,0:T(8,128)(2,1)} %get-tuple-element.32), calls=%async_computation | async-start | bytes 524288 | tf_op jit(solution)/shard_map/all_to_all | solution.py:602
  38.1 1.5 %collective-permute-start.3 = (bf16[512,256]{1,0:T(8,128)(2,1)}, bf16[512,256]{1,0:T(8,128)(2,1)S(1)}, u32[]{:S(2)}, u32[]{:S(2)}) collective-permute-start(bf16[512,256]{1,0:T(8,128)(2,1)} %get-tuple-element.36), channel_id=1, source_target_pairs={{0,32},{32,64},{64,96},{96,0},{1,33},{33,65},{65,97},{97,1},{2,34}... | collective-permute-start | bytes 786440 | tf_op jit(solution)/shard_map/ppermute | solution.py:30
  39.5 2.4 %collective-permute-start.4 = (bf16[512,256]{1,0:T(8,128)(2,1)}, bf16[512,256]{1,0:T(8,128)(2,1)S(1)}, u32[]{:S(2)}, u32[]{:S(2)}) collective-permute-start(bf16[512,256]{1,0:T(8,128)(2,1)} %get-tuple-element.37), channel_id=1, source_target_pairs={{0,64},{32,96},{64,0},{96,32},{1,65},{33,97},{65,1},{97,33},{2,66}... | collective-permute-start | bytes 786440 | tf_op jit(solution)/shard_map/ppermute | solution.py:30
  41.9 1.2 collective-permute-start.5
  43.2 8.0 %collective-permute-start.2 = (bf16[64,1024]{1,0:T(8,128)(2,1)S(1)}, bf16[64,1024]{1,0:T(8,128)(2,1)S(1)}, u32[]{:S(2)}, u32[]{:S(2)}) collective-permute-start(bf16[64,1024]{1,0:T(8,128)(2,1)S(1)} %broadcast_select_fusion), channel_id=1, source_target_pairs={{0,1},{1,0},{2,3},{3,2},{4,5},{5,4},{6,7},{7,6},{8,9},{9,8},{10,11... | collective-permute-start | bytes 393224 | tf_op jit(solution)/shard_map/ppermute | solution.py:604
  51.2 0.7 copy.14.var_ref
  51.9 0.3 collective-permute-done.2.edge_ref
  52.2 10.8 %backward.1 = (bf16[64,1024]{1,0:T(8,128)(2,1)}, bf16[64,1024]{1,0:T(8,128)(2,1)}, bf16[64,1024]{1,0:T(8,128)(2,1)}, bf16[192,512]{1,0:T(8,128)(2,1)S(1)}, bf16[...) custom-call(s32[4]{0:T(128)} %pad_add_fusion.place_ref, ...), custom_call_target="tpu_custom_call" | custom-call | flops 4294967296 | bytes 16777216 | tf_op jit(solution)/shard_map/backward/pallas_call | solution.py:448
  63.0 5.5 %collective-permute-start.7 = (bf16[8,144,128]{2,1,0:T(8,128)(2,1)S(1)}, bf16[8,144,128]{2,1,0:T(8,128)(2,1)S(1)}, u32[]{:S(2)}, u32[]{:S(2)}) collective-permute-start(bf16[8,144,128]{2,1,0:T(8,128)(2,1)S(1)} %get-tuple-element.46), channel_id=1, source_target_pairs={{0,1},{1,0},{2,3},{3,2},{4,5},{5,4},{6,7},{7,6},{8,9},{9,8},{10,11... | collective-permute-start | bytes 884744 | tf_op jit(solution)/shard_map/ppermute | solution.py:621
  68.5 0.3 collective-permute-start.6
  68.8 1.2 collective-permute-done.6.far_ref
  70.0 3.5 %pack.1 = bf16[16,64,656]{2,1,0:T(8,128)(2,1)} custom-call(s32[4]{0:T(128)} %pad_add_fusion.place_ref, bf16[64,1024]{1,0:T(8,128)(2,1)} %copy-done.2, bf16[64,1024]{1,0:T(8,128)(2,1)} %bitcast.40, bf16[64,1024]{1,0:T(8,128)(2,1)} %copy-done.1, bf16[64,1024]{1,0:T(8,128)(2,1)} %copy-done.4, bf16[192,512]{1,0:T(8,128)(2,1)S(1)} %get-tuple-element.43.own_ref, ...), custom_call_target="tpu_custom_call" | custom-call | flops 402653184 | bytes 4194304 | tf_op jit(solution)/shard_map/pack/pallas_call | solution.py:510
  73.6 6.1 %all-to-all-start.1 = ((bf16[16,64,656]{2,1,0:T(8,128)(2,1)}), bf16[16,64,656]{2,1,0:T(8,128)(2,1)}, u32[]{:S(2)}, u32[]{:S(2)}) async-start(bf16[16,64,656]{2,1,0:T(8,128)(2,1)} %pack.1), calls=%async_computation.1 | async-start | bytes 3145728 | tf_op jit(solution)/shard_map/all_to_all | solution.py:627
  79.7 0.7 collective-permute-start.8
  80.5 1.1 collective-permute-start.9
  81.5 20.3 %all-to-all-done.1.parts_ref = bf16[16,64,656]{2,1,0:T(8,128)(2,1)} async-done(((bf16[16,64,656]{2,1,0:T(8,128)(2,1)}), bf16[16,64,656]{2,1,0:T(8,128)(2,1)}, u32[]{:S(2)}, u32[]{:S(2)}) %all-to-all-start.1) | async-done | bytes 1343520 | tf_op jit(solution)/shard_map/all_to_all | solution.py:627
  101.9 3.4 %join.1 = bf16[16,4,1040]{2,1,0:T(4,128)(2,1)} custom-call(bf16[16,64,656]{2,1,0:T(8,128)(2,1)} %all-to-all-done.1.parts_ref), custom_call_target="tpu_custom_call" | custom-call | flops 671744 | bytes 1343488 | tf_op jit(solution)/shard_map/join/pallas_call | solution.py:550
  105.3 9.0 %all-to-all-start.2 = ((bf16[16,4,1040]{2,1,0:T(4,128)(2,1)}), bf16[16,4,1040]{2,1,0:T(4,128)(2,1)S(1)}, u32[]{:S(2)}, u32[]{:S(2)}) async-start(bf16[16,4,1040]{2,1,0:T(4,128)(2,1)} %join.1), calls=%async_computation.2 | async-start | bytes 294912 | tf_op jit(solution)/shard_map/all_to_all | solution.py:632
  114.2 3.0 %fusion = bf16[1,64,1024]{2,1,0:T(8,128)(2,1)} fusion(bf16[1024,1024]{1,0:T(8,128)(2,1)} %wsrc_ref.1, bf16[64,1024]{1,0:T(8,128)(2,1)S(1)} %collective-permute-done.9, bf16[64,1024]{1,0:T(8,128)(2,1)S(1)} %collective-permute-done.8, bf16[64,1024]{1,0:T(8,128)(2,1)S(1)} %copy-done.3), kind=kOutput, calls=%fused_computation.2 | convolution fusion | flops 134676480 | bytes 2621440 | tf_op jit(solution)/shard_map/dot_general | solution.py:634
  117.3 6.3 %all-to-all-done.2 = bf16[16,4,1040]{2,1,0:T(4,128)(2,1)S(1)} async-done(((bf16[16,4,1040]{2,1,0:T(4,128)(2,1)}), bf16[16,4,1040]{2,1,0:T(4,128)(2,1)S(1)}, u32[]{:S(2)}, u32[]{:S(2)}) %all-to-all-start.2) | async-done | bytes 133152 | tf_op jit(solution)/shard_map/all_to_all | solution.py:632
  123.6 0.1 convert_reduce_fusion
  123.7 0.7 pad_maximum_fusion.2
  124.3 0.6 pad_maximum_fusion
  (31 shorter events, 0.1 us)
Async XLA Ops:
  0.6 3.3 %copy-start = (bf16[1024,1024]{1,0:T(8,128)(2,1)S(1)}, bf16[1024,1024]{1,0:T(8,128)(2,1)}, u32[]{:S(2)}) copy-start(bf16[1024,1024]{1,0:T(8,128)(2,1)} %param.13) | copy-start | bytes 6291460
  0.6 9.2 %collective-permute-start.1 = (bf16[64,1024]{1,0:T(8,128)(2,1)}, bf16[64,1024]{1,0:T(8,128)(2,1)S(1)}, u32[]{:S(2)}, u32[]{:S(2)}) collective-permute-start(bf16[64,1024]{1,0:T(8,128)(2,1)} %bitcast.37), channel_id=1, source_target_pairs={{0,31},{1,0},{2,1},{3,2},{4,3},{5,4},{6,5},{7,6},{8,7},{9,8},{10,9... | collective-permute-start | bytes 393224 | tf_op jit(solution)/shard_map/ppermute | solution.py:30
  4.0 5.8 %collective-permute-start = (bf16[64,1024]{1,0:T(8,128)(2,1)}, bf16[64,1024]{1,0:T(8,128)(2,1)S(1)}, u32[]{:S(2)}, u32[]{:S(2)}) collective-permute-start(bf16[64,1024]{1,0:T(8,128)(2,1)} %bitcast.38), channel_id=1, source_target_pairs={{0,1},{1,2},{2,3},{3,4},{4,5},{5,6},{6,7},{7,8},{8,9},{9,10},{10,1... | collective-permute-start | bytes 393224 | tf_op jit(solution)/shard_map/ppermute | solution.py:30
  4.0 3.5 %copy-start.5 = (s32[512,16]{0,1:T(8,128)S(1)}, s32[512,16]{0,1:T(8,128)}, u32[]{:S(2)}) copy-start(s32[512,16]{0,1:T(8,128)} %param.18) | copy-start | bytes 98308
  4.0 3.5 %copy-start.6 = (s32[512,16]{0,1:T(8,128)S(1)}, s32[512,16]{0,1:T(8,128)}, u32[]{:S(2)}) copy-start(s32[512,16]{0,1:T(8,128)} %param.19) | copy-start | bytes 98308
  9.8 33.4 %copy-start.2 = (bf16[64,1024]{1,0:T(8,128)(2,1)}, bf16[64,1024]{1,0:T(8,128)(2,1)S(1)}, u32[]{:S(2)}) copy-start(bf16[64,1024]{1,0:T(8,128)(2,1)S(1)} %collective-permute-done.below_ref) | copy-start | bytes 393220
  9.8 33.4 %copy-start.1 = (bf16[64,1024]{1,0:T(8,128)(2,1)}, bf16[64,1024]{1,0:T(8,128)(2,1)S(1)}, u32[]{:S(2)}) copy-start(bf16[64,1024]{1,0:T(8,128)(2,1)S(1)} %collective-permute-done.1.above_ref) | copy-start | bytes 393220
  9.8 33.3 %copy-start.7 = (s32[4]{0:T(128)S(1)}, s32[4]{0:T(128)}, u32[]{:S(2)}) copy-start(s32[4]{0:T(128)} %pad_add_fusion.place_ref) | copy-start | bytes 52
  9.8 41.4 %copy-start.8 = (f32[32]{0:T(128)S(1)}, f32[32]{0:T(128)}, u32[]{:S(2)}) copy-start(f32[32]{0:T(128)} %param.17) | copy-start | bytes 388
  29.1 23.0 %all-to-all-start = ((bf16[8,32,512]{2,1,0:T(8,128)(2,1)}), bf16[8,32,512]{2,1,0:T(8,128)(2,1)S(1)}, u32[]{:S(2)}, u32[]{:S(2)}) async-start(bf16[8,32,512]{2,1,0:T(8,128)(2,1)} %get-tuple-element.32), calls=%async_computation | async-start | bytes 524288 | tf_op jit(solution)/shard_map/all_to_all | solution.py:602
  38.1 14.1 %collective-permute-start.3 = (bf16[512,256]{1,0:T(8,128)(2,1)}, bf16[512,256]{1,0:T(8,128)(2,1)S(1)}, u32[]{:S(2)}, u32[]{:S(2)}) collective-permute-start(bf16[512,256]{1,0:T(8,128)(2,1)} %get-tuple-element.36), channel_id=1, source_target_pairs={{0,32},{32,64},{64,96},{96,0},{1,33},{33,65},{65,97},{97,1},{2,34}... | collective-permute-start | bytes 786440 | tf_op jit(solution)/shard_map/ppermute | solution.py:30
  39.5 12.6 %collective-permute-start.4 = (bf16[512,256]{1,0:T(8,128)(2,1)}, bf16[512,256]{1,0:T(8,128)(2,1)S(1)}, u32[]{:S(2)}, u32[]{:S(2)}) collective-permute-start(bf16[512,256]{1,0:T(8,128)(2,1)} %get-tuple-element.37), channel_id=1, source_target_pairs={{0,64},{32,96},{64,0},{96,32},{1,65},{33,97},{65,1},{97,33},{2,66}... | collective-permute-start | bytes 786440 | tf_op jit(solution)/shard_map/ppermute | solution.py:30
  41.9 10.2 %collective-permute-start.5 = (bf16[512,256]{1,0:T(8,128)(2,1)}, bf16[512,256]{1,0:T(8,128)(2,1)S(1)}, u32[]{:S(2)}, u32[]{:S(2)}) collective-permute-start(bf16[512,256]{1,0:T(8,128)(2,1)} %get-tuple-element.38), channel_id=1, source_target_pairs={{0,96},{32,0},{64,32},{96,64},{1,97},{33,1},{65,33},{97,65},{2,98}... | collective-permute-start | bytes 786440 | tf_op jit(solution)/shard_map/ppermute | solution.py:30
  43.2 8.9 %collective-permute-start.2 = (bf16[64,1024]{1,0:T(8,128)(2,1)S(1)}, bf16[64,1024]{1,0:T(8,128)(2,1)S(1)}, u32[]{:S(2)}, u32[]{:S(2)}) collective-permute-start(bf16[64,1024]{1,0:T(8,128)(2,1)S(1)} %broadcast_select_fusion), channel_id=1, source_target_pairs={{0,1},{1,0},{2,3},{3,2},{4,5},{5,4},{6,7},{7,6},{8,9},{9,8},{10,11... | collective-permute-start | bytes 393224 | tf_op jit(solution)/shard_map/ppermute | solution.py:604
  52.1 10.9 %copy-start.4 = (bf16[64,1024]{1,0:T(8,128)(2,1)}, bf16[64,1024]{1,0:T(8,128)(2,1)S(1)}, u32[]{:S(2)}) copy-start(bf16[64,1024]{1,0:T(8,128)(2,1)S(1)} %collective-permute-done.2.edge_ref) | copy-start | bytes 393220
  63.0 7.0 %collective-permute-start.7 = (bf16[8,144,128]{2,1,0:T(8,128)(2,1)S(1)}, bf16[8,144,128]{2,1,0:T(8,128)(2,1)S(1)}, u32[]{:S(2)}, u32[]{:S(2)}) collective-permute-start(bf16[8,144,128]{2,1,0:T(8,128)(2,1)S(1)} %get-tuple-element.46), channel_id=1, source_target_pairs={{0,1},{1,0},{2,3},{3,2},{4,5},{5,4},{6,7},{7,6},{8,9},{9,8},{10,11... | collective-permute-start | bytes 884744 | tf_op jit(solution)/shard_map/ppermute | solution.py:621
  68.5 1.5 %collective-permute-start.6 = (bf16[192,512]{1,0:T(8,128)(2,1)S(1)}, bf16[192,512]{1,0:T(8,128)(2,1)S(1)}, u32[]{:S(2)}, u32[]{:S(2)}) collective-permute-start(bf16[192,512]{1,0:T(8,128)(2,1)S(1)} %get-tuple-element.44), channel_id=1, source_target_pairs={{0,1},{1,0},{2,3},{3,2},{4,5},{5,4},{6,7},{7,6},{8,9},{9,8},{10,11... | collective-permute-start | bytes 589832 | tf_op jit(solution)/shard_map/ppermute | solution.py:622
  73.6 6.2 %copy-start.10 = (bf16[64,1024]{1,0:T(8,128)(2,1)S(1)}, bf16[64,1024]{1,0:T(8,128)(2,1)}, u32[]{:S(2)}) copy-start(bf16[64,1024]{1,0:T(8,128)(2,1)} %get-tuple-element.47) | copy-start | bytes 393220
  73.6 6.9 %copy-start.9 = (bf16[64,1024]{1,0:T(8,128)(2,1)S(1)}, bf16[64,1024]{1,0:T(8,128)(2,1)}, u32[]{:S(2)}) copy-start(bf16[64,1024]{1,0:T(8,128)(2,1)} %get-tuple-element.48) | copy-start | bytes 393220
  73.6 40.7 %copy-start.3 = (bf16[64,1024]{1,0:T(8,128)(2,1)S(1)}, bf16[64,1024]{1,0:T(8,128)(2,1)}, u32[]{:S(2)}) copy-start(bf16[64,1024]{1,0:T(8,128)(2,1)} %get-tuple-element.41) | copy-start | bytes 393220
  73.6 28.3 %all-to-all-start.1 = ((bf16[16,64,656]{2,1,0:T(8,128)(2,1)}), bf16[16,64,656]{2,1,0:T(8,128)(2,1)}, u32[]{:S(2)}, u32[]{:S(2)}) async-start(bf16[16,64,656]{2,1,0:T(8,128)(2,1)} %pack.1), calls=%async_computation.1 | async-start | bytes 3145728 | tf_op jit(solution)/shard_map/all_to_all | solution.py:627
  79.7 25.5 %collective-permute-start.8 = (bf16[64,1024]{1,0:T(8,128)(2,1)S(1)}, bf16[64,1024]{1,0:T(8,128)(2,1)S(1)}, u32[]{:S(2)}, u32[]{:S(2)}) collective-permute-start(bf16[64,1024]{1,0:T(8,128)(2,1)S(1)} %copy-done.10), channel_id=1, source_target_pairs={{0,31},{1,0},{2,1},{3,2},{4,3},{5,4},{6,5},{7,6},{8,7},{9,8},{10,9... | collective-permute-start | bytes 393224 | tf_op jit(solution)/shard_map/ppermute | solution.py:30
  80.5 24.8 %collective-permute-start.9 = (bf16[64,1024]{1,0:T(8,128)(2,1)S(1)}, bf16[64,1024]{1,0:T(8,128)(2,1)S(1)}, u32[]{:S(2)}, u32[]{:S(2)}) collective-permute-start(bf16[64,1024]{1,0:T(8,128)(2,1)S(1)} %copy-done.9), channel_id=1, source_target_pairs={{0,1},{1,2},{2,3},{3,4},{4,5},{5,6},{6,7},{7,8},{8,9},{9,10},{10,1... | collective-permute-start | bytes 393224 | tf_op jit(solution)/shard_map/ppermute | solution.py:30
  105.3 18.3 %all-to-all-start.2 = ((bf16[16,4,1040]{2,1,0:T(4,128)(2,1)}), bf16[16,4,1040]{2,1,0:T(4,128)(2,1)S(1)}, u32[]{:S(2)}, u32[]{:S(2)}) async-start(bf16[16,4,1040]{2,1,0:T(4,128)(2,1)} %join.1), calls=%async_computation.2 | async-start | bytes 294912 | tf_op jit(solution)/shard_map/all_to_all | solution.py:632
